TPU v7x, 32 devices: a whole 2x2x4 slice. The times are simulated.
32 devices in a mesh: prow: 4 (over x, core), pcol: 8 (over z, y).
Axes of the slice: x: 2, y: 2, z: 4, core: 2. Of those that a mesh axis runs over, the one named last changes fastest.
Arguments:
- matrix: bfloat16 [5, 2048, 2, 4096], P(None, 'prow', None, 'pcol'), may hold values from -6 to 6
- pivots: int32 [2, 512], replicated, may hold values from 0 to 10239, as said below
- lower_inverse: bfloat16 [2, 512, 512], replicated, as said below
- upper_inverse: bfloat16 [2, 512, 512], replicated, as said below
Outputs:
- factored: bfloat16 [5, 2048, 2, 4096], P(None, 'prow', None, 'pcol')
Inputs may be any that keep to these rules, and one draw needn't show every extreme that they name: `pivots`: for panel k, entry i is either k * 512 + i (the row stays) or a row from (k + 1) * 512 on; the entries of one panel are distinct; entry 511 of each panel is 10239, and entry 0 of panel 0 is 0. Each lower_inverse[k] is unit lower triangular. Each upper_inverse[k] is upper triangular with a positive diagonal.
All inputs are finite; a program needn't handle non-finite values.
Results may differ from a plain program's by a relative error of at most 0.0084.
Values may be sent and summed in bfloat16 or wider, within the bound.
No kernel may reach another device: no remote copies, remote signals or barrier semaphores. Data moves between devices by JAX's collectives and lax.ppermute only.
A program may use at most 128 MiB of HBM per device.

v0:
```python
import functools

import jax
import jax.numpy as jnp
from jax import lax
from jax.experimental import pallas as pl
from jax.experimental.pallas import tpu as pltpu
from jax.sharding import PartitionSpec as P

BF16 = jnp.bfloat16
F32 = jnp.float32
I32 = jnp.int32
SMEM = pl.BlockSpec(memory_space=pltpu.SMEM)
VMEM = pl.BlockSpec(memory_space=pltpu.VMEM)
ANY = pl.BlockSpec(memory_space=pl.ANY)
DMA = pltpu.SemaphoreType.DMA


def dot(a, b):
    return jnp.dot(a, b, preferred_element_type=F32)


def flat(rows):
    return rows.reshape(rows.shape[0], rows.shape[1] * rows.shape[2])


def bf16(*shape):
    return jax.ShapeDtypeStruct(shape, BF16)


def call(kernel, operands, outs, after=(), scratch=(), aliases=None, us=1.0, mib=8):
    count = len(operands)

    def ordered(*refs):
        kernel(*refs[:count], *refs[count + len(after) :])

    return pl.pallas_call(
        ordered,
        out_shape=tuple(shape for shape, _ in outs),
        in_specs=[spec for _, spec in operands] + [ANY] * len(after),
        out_specs=tuple(spec for _, spec in outs),
        scratch_shapes=list(scratch),
        input_output_aliases=aliases or {},
        compiler_params=pltpu.CompilerParams(vmem_limit_bytes=mib * 1024 * 1024),
        cost_estimate=pl.CostEstimate(flops=int(us * 1.1e9), bytes_accessed=0, transcendentals=0),
    )(*[array for array, _ in operands], *after)


def fill_indices(nb, rows, meta, pivots, spread, fetch, join, arrive, goal, hops):
    row, row_devices = meta[0], meta[3]
    chip, chips = row // 2, row_devices // 2
    lanes = spread.shape[2]
    tiles = nb // lanes
    slot = lax.broadcasted_iota(I32, (1, nb), 1)
    pivot0, pivot1 = pivots[0:1, :], pivots[1:2, :]

    def lookup(keys, entry, value):
        parts = [keys[:, t * lanes : (t + 1) * lanes] for t in range(tiles)]

        def add(i, totals):
            begin = pl.multiple_of(i * 8, 8)
            at = begin + lax.broadcasted_iota(I32, (8, lanes), 0)
            here, give = entry(begin, at), value(begin, at)
            return tuple(t + jnp.where(p == here, give, 0) for t, p in zip(totals, parts))

        zero = jnp.zeros((8, lanes), I32)
        totals = lax.fori_loop(0, nb // 8, add, (zero,) * tiles, unroll=8)
        return jnp.concatenate([jnp.sum(t, axis=0, keepdims=True) for t in totals], axis=1)

    def pivot_of(panel):
        return lambda begin, at: spread[panel, pl.ds(begin, 8), :]

    place = lambda begin, at: at + 1
    in_pivots0 = lookup(pivot1, pivot_of(0), place)
    in_pivots1 = lookup(pivot0, pivot_of(1), place)
    top1_in_pivots0 = lookup(nb + slot, pivot_of(0), place)
    over_top1 = lookup(pivot0, lambda begin, at: nb + at, pivot_of(1))
    chained = lookup(nb + in_pivots1 - 1, pivot_of(0), place)

    source0 = pivot0
    source1 = jnp.where(in_pivots0 > 0, in_pivots0 - 1, pivot1)
    second0 = jnp.where(in_pivots1 > 0, jnp.where(chained > 0, chained - 1, nb + in_pivots1 - 1), slot)
    second1 = jnp.where(top1_in_pivots0 > 0, top1_in_pivots0 - 1, nb + slot)
    target0 = jnp.where(over_top1 > 0, over_top1, jnp.where(in_pivots1 > 0, nb + in_pivots1 - 1, pivot0))
    target1 = jnp.where(top1_in_pivots0 > 0, top1_in_pivots0 - 1, pivot1)

    def holder(index):
        return lax.rem(lax.div(index, nb), row_devices)

    def local(index):
        return lax.div(index, nb * row_devices) * nb + lax.rem(index, nb)

    def placed(index):
        mine = (holder(index) == row) & (index >= 2 * nb)
        return jnp.where(mine, local(index), rows)

    for k, (source, second, target) in enumerate(((source0, second0, target0), (source1, second1, target1))):
        from_chip = lax.div(holder(source), 2)
        wanted = jnp.where(from_chip == chip, source, second)
        at = (slice(k, k + 1), slice(None))
        fetch[at] = local(wanted)
        join[at] = jnp.where(holder(wanted) == row, slot, nb)
        arrive[at] = placed(source)
        goal[at] = placed(target)
        hops[at] = lax.rem(chip + chips - from_chip, chips)


def copy_rows(count, target, target_at, origin, origin_at):
    def copy(i, carry):
        target[target_at(i)] = origin[origin_at(i)]
        return carry

    lax.fori_loop(0, count, copy, 0, unroll=16)


def first_kernel(tiles, piece, work, sem):
    load = pltpu.make_async_copy(tiles.at[pl.ds(0, piece.shape[0])], work, sem)
    load.start()
    load.wait()
    piece[...] = flat(work[...])[:, : piece.shape[1]]


def gather_kernel(meta, pivots, spread, tiles, *refs):
    *pieces, loaded, send, keep, block0, join, arrive, goal, hops, fetch, fetch_table, load_sem, table_sem = refs
    chunk, nb = pieces[0].shape
    rows = tiles.shape[0]
    core = meta[1]
    load = pltpu.make_async_copy(tiles, loaded.at[pl.ds(0, rows)], load_sem)
    load.start()
    fill_indices(nb, rows, meta, pivots, spread, fetch, join, arrive, goal, hops)
    table = pltpu.make_async_copy(fetch, fetch_table, table_sem)
    table.start()
    table.wait()
    load.wait()
    for i, piece in enumerate(pieces, 1):
        piece[...] = flat(loaded[i * chunk : (i + 1) * chunk])[:, :nb]
    copy_rows(nb, send, lambda i: i, loaded, lambda i: fetch_table[1 - core, i])
    copy_rows(nb, keep, lambda i: i, loaded, lambda i: fetch_table[core, i])
    block0[...] = loaded[0:nb]


def join_kernel(meta, join, keep, came, joined, work):
    count = came.shape[0]
    core = meta[1]
    work[0:count] = came[...]
    copy_rows(count, work, lambda i: join[core, i], keep, lambda i: i)
    joined[...] = work[0:count]


def scatter_kernel(meta, arrive, goal, came, came_sibling, old, old_sibling, tiles, out):
    core, chip = meta[1], meta[0] // 2
    count = old.shape[0]
    out[...] = tiles[...]

    def scatter(table, values, k):
        copy_rows(count, out, lambda i: table[k, i], values, lambda i: i)

    @pl.when(chip == 0)
    def _():
        scatter(goal, old, core)
        scatter(goal, old_sibling, 1 - core)

    @pl.when(chip != 0)
    def _():
        scatter(arrive, came, core)
        scatter(arrive, came_sibling, 1 - core)


def relay_kernel(meta, came, own, held):
    place = lax.div(meta[2], 2)

    @pl.when(place == 0)
    def _():
        held[...] = own[...]

    @pl.when(place != 0)
    def _():
        held[...] = came[...]


def pass_kernel(came, held):
    held[...] = came[...]


def old_kernel(line, meta, *refs):
    held, other, old = refs[: len(refs) // 2], refs[len(refs) // 2 : -1], refs[-1]
    place = lax.div(meta[2], 2)
    chunk = held[0].shape[0]
    for h in range(line):

        @pl.when(place == h)
        def _(h=h):
            for p in range(old.shape[1] // chunk):
                old[0, p * chunk : (p + 1) * chunk] = held[p + h][...]
                old[1, p * chunk : (p + 1) * chunk] = other[p + h][...]


def by_chip_kernel(meta, *refs):
    out = refs[-1]
    for h, choice in enumerate(refs[:-1]):

        @pl.when(meta[0] // 2 == h)
        def _(choice=choice):
            out[...] = choice[...]


def by_place_kernel(meta, *refs):
    out = refs[-1]
    for h, choice in enumerate(refs[:-1]):

        @pl.when(lax.div(meta[2], 2) == h)
        def _(choice=choice):
            out[...] = choice[...]


def head_kernel(meta, fresh, fresh_sibling, head):
    needed = 1 - lax.rem(meta[2], 2)
    half, nb = head.shape
    at = pl.ds(pl.multiple_of(meta[1] * half, half), half)

    @pl.when(meta[1] == needed)
    def _():
        head[...] = fresh[at, :nb]

    @pl.when(meta[1] != needed)
    def _():
        head[...] = fresh_sibling[at, :nb]


def choose(hop, choices):
    value = flat(choices[0]).astype(F32)
    for h, other in enumerate(choices[1:], 1):
        value = jnp.where(hop == h, flat(other).astype(F32), value)
    return value.astype(BF16)


def fresh_kernel(chips, meta, hops, *refs):
    choices, (fresh, brought) = refs[:chips], refs[chips:]
    nb = fresh.shape[0]
    core, chip = meta[1], meta[0] // 2
    hop = jnp.broadcast_to(hops[pl.ds(core, 1), :], (8, nb)).T[:, 0:1]
    fresh[...] = choose(hop, [c[...] for c in choices])
    if chips == 1:
        brought[...] = choices[0][...]
    for h in range(1, chips):

        @pl.when((chip == h) | ((chip == 0) & (h == 1)))
        def _(h=h):
            brought[...] = choices[h][...]


def raw(columns, nb):
    joined = jnp.concatenate(columns, axis=1)
    return joined.reshape(joined.shape[0], len(columns), nb)


def prep0_kernel(meta, lower, fresh, fresh_sibling, up0, top, work):
    core, column = meta[1], meta[2]
    nb = fresh.shape[0]

    @pl.when(core == 0)
    def _():
        work[...] = fresh[...]

    @pl.when(core != 0)
    def _():
        work[...] = fresh_sibling[...]

    shown = []
    for j in range(work.shape[1] // nb):
        cols = slice(j * nb, (j + 1) * nb)
        product = dot(lower[0], work[:, cols])
        show = product
        if j == 0:
            show = jnp.where(column == 0, work[:, cols].astype(F32), product)
            product = jnp.where(column == 0, 0.0, product)
        up0[:, cols] = product.astype(BF16)
        shown.append(show.astype(BF16))
    top[...] = raw(shown, nb)


def prep1_kernel(meta, lower, upper, fresh, fresh_sibling, up0, *refs):
    mine, mine_sibling, other, other_sibling, up1, up0_panel, top, work, head = refs
    core, column = meta[1], meta[2]
    side = lax.rem(column, 2)
    nb, half = fresh.shape[0], mine.shape[0]
    for which, who, piece in (
        (1 - side, core, mine), (1 - side, 1 - core, mine_sibling), (side, core, other), (side, 1 - core, other_sibling)
    ):
        head[which, pl.ds(pl.multiple_of(who * half, half), half)] = piece[...]

    @pl.when(core == 1)
    def _():
        work[...] = fresh[...]

    @pl.when(core != 1)
    def _():
        work[...] = fresh_sibling[...]

    up0_panel[...] = dot(lower[0], head[0]).astype(BF16)
    factor = dot(head[1], upper[0]).astype(BF16)
    in_panel, next_panel = column == 0, column == 1
    shown = []
    for j in range(work.shape[1] // nb):
        cols = slice(j * nb, (j + 1) * nb)
        updated = (work[:, cols].astype(F32) - dot(factor, up0[:, cols])).astype(BF16)
        last = dot(lower[1], updated)
        show = last
        if j == 0:
            show = jnp.where(next_panel, updated.astype(F32), show)
            show = jnp.where(in_panel, factor.astype(F32), show)
            last = jnp.where(in_panel | next_panel, 0.0, last)
        up1[:, cols] = last.astype(BF16)
        shown.append(show.astype(BF16))
    top[...] = raw(shown, nb)


def update_kernel(
    block_index, line, meta, goal, old, old_sibling, upper, up0, up1, up0_panel, tiles, top0, top1, *rest
):
    out, token, panels, block, result, panel_sem, block_sem, out_sem = rest[-8:]
    spans = (len(rest) - 8) // 2
    held, other = rest[:spans], rest[spans : 2 * spans]
    per_block = spans - line + 1
    row, core, column, row_devices = meta[0], meta[1], meta[2], meta[3]
    side, place = lax.rem(column, 2), lax.div(column, 2)
    nb, cb, _ = block.shape
    chunk = nb // per_block
    rows_of = pl.ds(block_index * nb, nb)

    def panel_copy(i, h, which):
        source = (held, other)[which][i + h]
        target = panels.at[lax.rem(side + which, 2), pl.ds(i * chunk, chunk)]
        return pltpu.make_async_copy(source, target, panel_sem.at[i, which])

    load = pltpu.make_async_copy(tiles.at[rows_of], block, block_sem)
    load.start()
    for h in range(line):

        @pl.when(place == h)
        def _(h=h):
            for i in range(per_block):
                panel_copy(i, h, 0).start()
                panel_copy(i, h, 1).start()

    def arrived():
        for i in range(per_block):
            panel_copy(i, 0, 0).wait()
            panel_copy(i, 0, 1).wait()

    def from_factors():
        here = block_index * nb + lax.broadcasted_iota(I32, (nb, nb), 0)
        pick = jnp.where(here == goal[pl.ds(core, 1), :], 1.0, 0.0)
        pick_sibling = jnp.where(here == goal[pl.ds(1 - core, 1), :], 1.0, 0.0)
        moved = jnp.sum(pick + pick_sibling, axis=1, keepdims=True) > 0.5
        pick, pick_sibling = pick.astype(BF16), pick_sibling.astype(BF16)
        arrived()
        whole = []
        for k in range(2):
            which = lax.rem(k + side, 2)
            brought = dot(pick, old[which]) + dot(pick_sibling, old_sibling[which])
            whole.append(jnp.where(moved, brought, panels[k].astype(F32)))
        factor0 = dot(whole[0].astype(BF16), upper[0]).astype(BF16)
        below = (whole[1] - dot(factor0, up0_panel[...])).astype(BF16)
        factor1 = dot(below, upper[1]).astype(BF16)
        load.wait()
        values = flat(block[...])
        columns = []
        for j in range(cb):
            cols = slice(j * nb, (j + 1) * nb)
            value = values[:, cols].astype(F32) - dot(factor0, up0[:, cols])
            value = value.astype(BF16).astype(F32) - dot(factor1, up1[:, cols])
            if j == 0:
                value = jnp.where(column == 0, factor0.astype(F32), value)
                value = jnp.where(column == 1, factor1.astype(F32), value)
            columns.append(value.astype(BF16))
        result[...] = raw(columns, nb)

    def from_top(top):
        arrived()
        load.wait()
        copy = pltpu.make_async_copy(top, result, block_sem)
        copy.start()
        copy.wait()

    if block_index == 0:
        pl.when(row == 0)(lambda: from_top(top0))
        pl.when(row == 1)(lambda: from_top(top1))
        pl.when(row >= 2)(from_factors)
    else:
        from_factors()
    store = pltpu.make_async_copy(result, out.at[rows_of], out_sem)
    store.start()
    token[...] = jnp.zeros(token.shape, F32)
    store.wait()


def body(matrix, pivots, lower, upper):
    rb, nb, cb, _ = matrix.shape
    rows = rb * nb
    chunk = nb // 2
    pieces = rows // chunk
    row_devices = lax.axis_size("prow")
    col_devices = lax.axis_size("pcol")
    chips, line = row_devices // 2, col_devices // 2
    row = lax.axis_index("prow").astype(I32)
    column = lax.axis_index("pcol").astype(I32)
    meta = jnp.stack([row, row % 2, column, jnp.int32(row_devices)])
    tiles = matrix.reshape(rows, cb, nb)

    def to_sibling(value):
        return lax.ppermute(value, "prow", [(r, r ^ 1) for r in range(row_devices)])

    def to_neighbour(value):
        return lax.ppermute(value, "pcol", [(c, c ^ 1) for c in range(col_devices)])

    def to_chip(value, h):
        return lax.ppermute(value, "prow", [(r, (r + 2 * h) % row_devices) for r in range(row_devices)])

    def to_next(value):
        return lax.ppermute(value, "pcol", [(c, c + 2) for c in range(col_devices - 2)])

    order = []

    def run(kernel, operands, outs, also=(), **kwargs):
        after = tuple(order[-1:]) + tuple(also)
        results = call(kernel, operands, outs, after=after, **kwargs)
        order.append(results[-1])
        return results

    last_step = pieces + line - 2
    piece_out = [(bf16(chunk, nb), VMEM)]
    own, held, other = [], [], []
    state = {}

    def turn_us(k):
        return 10.0 if k in (1, 6) or k > 8 else 0.2

    def step(k):
        if k == 0:
            own.extend(run(
                first_kernel, [(tiles, ANY)], piece_out, scratch=[pltpu.VMEM((chunk, cb, nb), BF16), DMA], mib=60,
            ))
            value = own[0]
        else:
            also = (other[k - 2],) if k >= 2 else ()
            came = state["came"]
            if k < pieces:
                operands = [(meta, SMEM), (came, VMEM), (own[k], VMEM)]
                (value,) = run(relay_kernel, operands, piece_out, also, us=turn_us(k))
            else:
                (value,) = run(pass_kernel, [(came, VMEM)], piece_out, also, us=turn_us(k))
        held.append(value)
        if k < last_step:
            state["came"] = to_next(value)
        other.append(to_neighbour(value))

    def gather():
        lanes = min(nb, 128)
        spread = jnp.broadcast_to(pivots[:, :, None], (2, nb, lanes))
        table = jax.ShapeDtypeStruct((2, nb), I32)
        results = run(
            gather_kernel,
            [(meta, SMEM), (pivots, VMEM), (spread, VMEM), (tiles, ANY)],
            piece_out * (pieces - 1) + [(bf16(rows + 8, cb, nb), VMEM)]
            + [(bf16(nb, cb, nb), VMEM)] * 3 + [(table, VMEM)] * 4,
            scratch=[pltpu.VMEM((2, nb), I32), pltpu.SMEM((2, nb), I32), DMA, DMA],
            us=8.0, mib=20,
        )
        own.extend(results[: pieces - 1])
        state["loaded"], send, *rest = results[pieces - 1 :]
        state.update(zip(("keep", "block0", "join", "arrive", "goal", "hops"), rest))
        state["sent"] = to_sibling(send)
        state["block0_sibling"] = to_sibling(state["block0"])

    def join():
        (joined,) = run(
            join_kernel,
            [(meta, SMEM), (state["join"], SMEM), (state["keep"], VMEM), (state["sent"], VMEM)],
            [(bf16(nb, cb, nb), VMEM)],
            scratch=[pltpu.VMEM((nb + 8, cb, nb), BF16)],
            us=2.0,
        )
        state["choices"] = [joined] + [to_chip(joined, h) for h in range(1, chips)]

    def fresh():
        new, brought = run(
            functools.partial(fresh_kernel, chips),
            [(meta, SMEM), (state["hops"], VMEM)] + [(c, VMEM) for c in state["choices"]],
            [(bf16(nb, cb * nb), VMEM), (bf16(nb, cb, nb), VMEM)],
            us=2.0, mib=16,
        )
        state["fresh"] = (new, to_sibling(new))
        state["brought"] = (brought, to_sibling(brought))

    def head():
        (mine,) = run(
            head_kernel, [(meta, SMEM)] + [(v, VMEM) for v in state["fresh"]], [(bf16(nb // 2, nb), VMEM)], us=0.1,
        )
        state["head"] = [mine] + [
            lax.ppermute(mine, "pcol", [(0, 2 * h), (1, 2 * h + 1)]) for h in range(1, line)
        ]

    def head_here():
        (mine,) = run(
            by_place_kernel, [(meta, SMEM)] + [(v, VMEM) for v in state["head"]], [(bf16(nb // 2, nb), VMEM)]
        )
        swapped = to_neighbour(mine)
        state["heads"] = (mine, to_sibling(mine), swapped, to_sibling(swapped))

    def old():
        spans = range(nb // chunk + line - 1)
        (mine,) = run(
            functools.partial(old_kernel, line),
            [(meta, SMEM)] + [(held[i], VMEM) for i in spans] + [(other[i], VMEM) for i in spans],
            [(bf16(2, nb, nb), VMEM)],
        )
        state["old"] = [mine] + [to_chip(mine, h) for h in range(1, chips)]

    def old_here():
        (mine,) = run(
            by_chip_kernel, [(meta, SMEM)] + [(v, VMEM) for v in state["old"]], [(bf16(2, nb, nb), VMEM)]
        )
        state["old"] = (mine, to_sibling(mine))

    def scatter():
        sources = state["brought"] + (state["block0"], state["block0_sibling"], state["loaded"])
        (state["moved"],) = run(
            scatter_kernel,
            [(meta, SMEM), (state["arrive"], SMEM), (state["goal"], SMEM)] + [(v, VMEM) for v in sources],
            [(bf16(rows + 8, cb, nb), VMEM)],
            us=0.1, mib=24,
        )

    def prep0():
        state["up0"], state["top0"] = run(
            prep0_kernel,
            [(meta, SMEM), (lower, VMEM)] + [(v, VMEM) for v in state["fresh"]],
            [(bf16(nb, cb * nb), VMEM), (bf16(nb, cb, nb), VMEM)],
            scratch=[pltpu.VMEM((nb, cb * nb), BF16)],
            us=0.1, mib=16,
        )

    def prep1():
        state["up1"], state["up0_panel"], state["top1"] = run(
            prep1_kernel,
            [(meta, SMEM), (lower, VMEM), (upper, VMEM)] + [(v, VMEM) for v in state["fresh"]]
            + [(state["up0"], VMEM)] + [(v, VMEM) for v in state["heads"]],
            [(bf16(nb, cb * nb), VMEM), (bf16(nb, nb), VMEM), (bf16(nb, cb, nb), VMEM)],
            scratch=[pltpu.VMEM((nb, cb * nb), BF16), pltpu.VMEM((2, nb, nb), BF16)],
            us=3.5, mib=16,
        )

    per_block = nb // chunk

    def update(b):
        spans = range(b * per_block, (b + 1) * per_block + line - 1)
        operands = [(meta, SMEM), (state["goal"], VMEM)] + [(v, VMEM) for v in state["old"]] + [(upper, VMEM)]
        operands += [(state[name], VMEM) for name in ("up0", "up1", "up0_panel")]
        operands += [(state[name], ANY) for name in ("moved", "top0", "top1")]
        operands += [(held[i], ANY) for i in spans] + [(other[i], ANY) for i in spans]
        aliases = {}
        if "result" in state:
            aliases = {len(operands): 0}
            operands.append((state["result"], ANY))
        kernel = functools.partial(update_kernel, b, line)
        if aliases:
            kernel = lambda *refs, kernel=kernel, at=len(operands) - 1: kernel(*refs[:at], *refs[at + 1 :])
        state["result"], _ = run(
            kernel,
            operands,
            [(bf16(rows, cb, nb), ANY), (jax.ShapeDtypeStruct((8, 128), F32), VMEM)],
            scratch=[
                pltpu.VMEM((2, nb, nb), BF16), pltpu.VMEM((nb, cb, nb), BF16), pltpu.VMEM((nb, cb, nb), BF16),
                DMA((per_block, 2)), DMA, DMA,
            ],
            aliases=aliases,
            us=5.0, mib=24,
        )

    plan = [(0, gather), (1, join), (5, fresh), (line + 1, old), (6, head), (6, scatter), (7, prep0), (8, head_here), (8, old_here), (9, prep1)]
    for b in range(rb):
        plan.append((max(9 + b, (b + 1) * per_block + line - 2), functools.partial(update, b)))
    for k in range(last_step + 1):
        step(k)
        while plan and (plan[0][0] <= k or k == last_step):
            plan.pop(0)[1]()
    return state["result"].reshape(matrix.shape)


def solution(mesh):
    placed = (P(None, "prow", None, "pcol"), P(), P(), P())
    return jax.shard_map(
        body, mesh=mesh, in_specs=placed, out_specs=P(None, "prow", None, "pcol"), check_vma=False
    )
```

profile of v0, /device:TPU:0, one launch (start us, length us, event | category | flops | bytes accessed | tf_op | source)
XLA Modules:
  0.0 161.5 jit_solution(8234031825474043125)
XLA Ops:
  0.0 1.8 %shard_map.46.refs_4_.refs_1_.refs_11_ = bf16[256,512]{1,0:T(8,128)(2,1)} custom-call(bf16[2560,2,512]{2,1,0:T(2,128)(2,1)} %bitcast.5), custom_call_target="tpu_custom_call" | custom-call | flops 1100000000 | tf_op jit(solution)/shard_map/pallas_call | solution.py:37
  1.8 4.9 %collective-permute-start = (bf16[256,512]{1,0:T(8,128)(2,1)}, bf16[256,512]{1,0:T(8,128)(2,1)S(1)}, u32[]{:S(2)}, u32[]{:S(2)}) collective-permute-start(bf16[256,512]{1,0:T(8,128)(2,1)} %shard_map.46.refs_4_.refs_1_.refs_11_), channel_id=1, source_target_pairs={{0,2},{1,3},{2,4},{3,5},{4,6},{5,7},{8,10},{9,11},{10,12},{11,13},... | collective-permute-start | bytes 786440 | tf_op jit(solution)/shard_map/ppermute | solution.py:421
  7.1 2.5 %copy-done.1 = bf16[5,512,2,512]{3,2,1,0:T(2,128)(2,1)S(1)} copy-done((bf16[5,512,2,512]{3,2,1,0:T(2,128)(2,1)S(1)}, bf16[5,512,2,512]{3,2,1,0:T(2,128)(2,1)}, u32[]{:S(2)}) %copy-start.1) | copy-done | bytes 5242904
  9.6 0.9 copy-done.3
  10.5 7.6 %shard_map.47 = (bf16[256,512]{1,0:T(8,128)(2,1)S(1)}, bf16[256,512]{1,0:T(8,128)(2,1)S(1)}, bf16[256,512]{1,0:T(8,128)(2,1)S(1)}, bf16[256,512]{1,0:T(8,128)(2,...) custom-call(s32[4]{0:T(128)S(1)} %pad_add_fusion.refs_0_, ...), custom_call_target="tpu_custom_call" | custom-call | flops 8800000000 | tf_op jit(solution)/shard_map/pallas_call | solution.py:37
  18.2 1.6 collective-permute-start.3
  20.4 3.5 %collective-permute-start.1 = (bf16[256,512]{1,0:T(8,128)(2,1)S(1)}, bf16[256,512]{1,0:T(8,128)(2,1)S(1)}, u32[]{:S(2)}, u32[]{:S(2)}) collective-permute-start(bf16[256,512]{1,0:T(8,128)(2,1)S(1)} %shard_map.48.refs_4_.refs_2_.refs_12_), channel_id=1, source_target_pairs={{0,2},{1,3},{2,4},{3,5},{4,6},{5,7},{8,10},{9,11},{10,12},{11,13},... | collective-permute-start | bytes 786440 | tf_op jit(solution)/shard_map/ppermute | solution.py:421
  23.9 2.3 %shard_map.49.refs_3_.refs_2_ = bf16[512,2,512]{2,1,0:T(2,128)(2,1)S(1)} custom-call(s32[4]{0:T(128)S(1)} %pad_add_fusion.refs_0_, s32[2,512]{1,0:T(2,128)S(1)} %get-tuple-element.42.refs_1_, bf16[512,2,512]{2,1,0:T(2,128)(2,1)S(1)} %get-tuple-element.43.refs_2_, bf16[512,2,512]{2,1,0:T(2,128)(2,1)S(1)} %collective-permute-done.2.refs_3_, ...), custom_call_target="tpu_custom_call" | custom-call | flops 2200000000 | tf_op jit(solution)/shard_map/pallas_call | solution.py:37
  26.1 1.6 collective-permute-start.10
  28.2 1.5 collective-permute-done.1.refs_1_
  30.3 4.4 %collective-permute-start.4 = (bf16[256,512]{1,0:T(8,128)(2,1)S(1)}, bf16[256,512]{1,0:T(8,128)(2,1)S(1)}, u32[]{:S(2)}, u32[]{:S(2)}) collective-permute-start(bf16[256,512]{1,0:T(8,128)(2,1)S(1)} %shard_map.50.refs_3_.refs_13_.refs_11_), channel_id=1, source_target_pairs={{0,2},{1,3},{2,4},{3,5},{4,6},{5,7},{8,10},{9,11},{10,12},{11,13},... | collective-permute-start | bytes 786440 | tf_op jit(solution)/shard_map/ppermute | solution.py:421
  35.5 4.2 %collective-permute-done.4.refs_1_ = bf16[256,512]{1,0:T(8,128)(2,1)S(1)} collective-permute-done((bf16[256,512]{1,0:T(8,128)(2,1)S(1)}, bf16[256,512]{1,0:T(8,128)(2,1)S(1)}, u32[]{:S(2)}, u32[]{:S(2)}) %collective-permute-start.4) | collective-permute-done | bytes 262176 | tf_op jit(solution)/shard_map/ppermute | solution.py:421
  40.3 4.4 %collective-permute-start.6 = (bf16[256,512]{1,0:T(8,128)(2,1)S(1)}, bf16[256,512]{1,0:T(8,128)(2,1)S(1)}, u32[]{:S(2)}, u32[]{:S(2)}) collective-permute-start(bf16[256,512]{1,0:T(8,128)(2,1)S(1)} %shard_map.51.refs_3_.refs_4_.refs_14_.refs_12_), channel_id=1, source_target_pairs={{0,2},{1,3},{2,4},{3,5},{4,6},{5,7},{8,10},{9,11},{10,12},{11,13},... | collective-permute-start | bytes 786440 | tf_op jit(solution)/shard_map/ppermute | solution.py:421
  45.3 3.5 %collective-permute-done.6.refs_1_ = bf16[256,512]{1,0:T(8,128)(2,1)S(1)} collective-permute-done((bf16[256,512]{1,0:T(8,128)(2,1)S(1)}, bf16[256,512]{1,0:T(8,128)(2,1)S(1)}, u32[]{:S(2)}, u32[]{:S(2)}) %collective-permute-start.6) | collective-permute-done | bytes 262176 | tf_op jit(solution)/shard_map/ppermute | solution.py:421
  49.4 4.4 %collective-permute-start.11 = (bf16[256,512]{1,0:T(8,128)(2,1)S(1)}, bf16[256,512]{1,0:T(8,128)(2,1)S(1)}, u32[]{:S(2)}, u32[]{:S(2)}) collective-permute-start(bf16[256,512]{1,0:T(8,128)(2,1)S(1)} %shard_map.52.refs_3_.refs_5_.refs_15_.refs_13_.refs_11_), channel_id=1, source_target_pairs={{0,2},{1,3},{2,4},{3,5},{4,6},{5,7},{8,10},{9,11},{10,12},{11,13},... | collective-permute-start | bytes 786440 | tf_op jit(solution)/shard_map/ppermute | solution.py:421
  54.4 3.3 %collective-permute-done.11.refs_1_ = bf16[256,512]{1,0:T(8,128)(2,1)S(1)} collective-permute-done((bf16[256,512]{1,0:T(8,128)(2,1)S(1)}, bf16[256,512]{1,0:T(8,128)(2,1)S(1)}, u32[]{:S(2)}, u32[]{:S(2)}) %collective-permute-start.11) | collective-permute-done | bytes 262176 | tf_op jit(solution)/shard_map/ppermute | solution.py:421
  58.3 4.4 %collective-permute-start.14 = (bf16[256,512]{1,0:T(8,128)(2,1)S(1)}, bf16[256,512]{1,0:T(8,128)(2,1)S(1)}, u32[]{:S(2)}, u32[]{:S(2)}) collective-permute-start(bf16[256,512]{1,0:T(8,128)(2,1)S(1)} %shard_map.53.refs_4_.refs_14_.refs_12_), channel_id=1, source_target_pairs={{0,2},{1,3},{2,4},{3,5},{4,6},{5,7},{8,10},{9,11},{10,12},{11,13},... | collective-permute-start | bytes 786440 | tf_op jit(solution)/shard_map/ppermute | solution.py:421
  63.3 1.6 shard_map.54
  65.4 0.6 shard_map.55.refs_3_.refs_1_
  66.5 1.5 collective-permute-start.12
  68.6 4.4 %collective-permute-start.18 = (bf16[256,512]{1,0:T(8,128)(2,1)S(1)}, bf16[256,512]{1,0:T(8,128)(2,1)S(1)}, u32[]{:S(2)}, u32[]{:S(2)}) collective-permute-start(bf16[256,512]{1,0:T(8,128)(2,1)S(1)} %shard_map.56.refs_3_.refs_15_.refs_13_.refs_11_), channel_id=1, source_target_pairs={{0,2},{1,3},{2,4},{3,5},{4,6},{5,7},{8,10},{9,11},{10,12},{11,13},... | collective-permute-start | bytes 786440 | tf_op jit(solution)/shard_map/ppermute | solution.py:421
  73.6 0.6 shard_map.57.refs_8_.refs_1_
  74.2 4.1 %shard_map.58.refs_3_.refs_8_ = bf16[2568,2,512]{2,1,0:T(2,128)(2,1)S(1)} custom-call(s32[4]{0:T(128)S(1)} %pad_add_fusion.refs_0_, s32[2,512]{1,0:T(2,128)S(1)} %get-tuple-element.52.refs_1_, s32[2,512]{1,0:T(2,128)S(1)} %get-tuple-element.38.refs_2_.refs_1_, bf16[512,2,512]{2,1,0:T(2,128)(2,1)S(1)} %get-tuple-element.48.refs_11_.refs_3_, ...), custom_call_target="tpu_custom_call" | custom-call | flops 110000000 | tf_op jit(solution)/shard_map/pallas_call | solution.py:37
  78.9 3.5 %collective-permute-start.22 = (bf16[256,512]{1,0:T(8,128)(2,1)S(1)}, bf16[256,512]{1,0:T(8,128)(2,1)S(1)}, u32[]{:S(2)}, u32[]{:S(2)}) collective-permute-start(bf16[256,512]{1,0:T(8,128)(2,1)S(1)} %shard_map.59.refs_4_.refs_14_.refs_12_), channel_id=1, source_target_pairs={{0,2},{1,3},{2,4},{3,5},{4,6},{5,7},{8,10},{9,11},{10,12},{11,13},... | collective-permute-start | bytes 786440 | tf_op jit(solution)/shard_map/ppermute | solution.py:421
  82.4 3.0 %collective-permute-start.15 = (bf16[256,512]{1,0:T(8,128)(2,1)S(1)}, bf16[256,512]{1,0:T(8,128)(2,1)S(1)}, u32[]{:S(2)}, u32[]{:S(2)}) collective-permute-start(bf16[256,512]{1,0:T(8,128)(2,1)S(1)} %shard_map.57.refs_8_.refs_1_), channel_id=1, source_target_pairs={{0,2},{1,3},{8,10},{9,11},{16,18},{17,19},{24,26},{25,27}} | collective-permute-start | bytes 786440 | tf_op jit(solution)/shard_map/ppermute | solution.py:501
  85.4 1.3 collective-permute-start.16
  86.7 1.3 collective-permute-start.17
  88.0 2.0 %shard_map.60 = (bf16[512,1024]{1,0:T(8,128)(2,1)S(1)}, bf16[512,2,512]{2,1,0:T(2,128)(2,1)S(1)}) custom-call(s32[4]{0:T(128)S(1)} %pad_add_fusion.refs_0_, bf16[2,512,512]{2,1,0:T(8,128)(2,1)S(1)} %copy-done.2, bf16[512,1024]{1,0:T(8,128)(2,1)S(1)} %get-tuple-element.49.refs_1_.refs_2_.refs_3_, ...), custom_call_target="tpu_custom_call" | custom-call | flops 110000000 | tf_op jit(solution)/shard_map/pallas_call | solution.py:37
  90.0 1.5 collective-permute-start.29
  92.0 2.7 %collective-permute-done.15.refs_2_ = bf16[256,512]{1,0:T(8,128)(2,1)S(1)} collective-permute-done((bf16[256,512]{1,0:T(8,128)(2,1)S(1)}, bf16[256,512]{1,0:T(8,128)(2,1)S(1)}, u32[]{:S(2)}, u32[]{:S(2)}) %collective-permute-start.15) | collective-permute-done | bytes 262176 | tf_op jit(solution)/shard_map/ppermute | solution.py:501
  94.7 5.6 %collective-permute-done.16.refs_3_ = bf16[256,512]{1,0:T(8,128)(2,1)S(1)} collective-permute-done((bf16[256,512]{1,0:T(8,128)(2,1)S(1)}, bf16[256,512]{1,0:T(8,128)(2,1)S(1)}, u32[]{:S(2)}, u32[]{:S(2)}) %collective-permute-start.16) | collective-permute-done | bytes 262176 | tf_op jit(solution)/shard_map/ppermute | solution.py:501
  100.3 2.9 %collective-permute-done.17.refs_4_ = bf16[256,512]{1,0:T(8,128)(2,1)S(1)} collective-permute-done((bf16[256,512]{1,0:T(8,128)(2,1)S(1)}, bf16[256,512]{1,0:T(8,128)(2,1)S(1)}, u32[]{:S(2)}, u32[]{:S(2)}) %collective-permute-start.17) | collective-permute-done | bytes 262176 | tf_op jit(solution)/shard_map/ppermute | solution.py:501
  103.3 0.6 shard_map.62.refs_3_.refs_6_
  103.9 1.7 %collective-permute-start.26 = (bf16[256,512]{1,0:T(8,128)(2,1)S(1)}, bf16[256,512]{1,0:T(8,128)(2,1)S(1)}, u32[]{:S(2)}, u32[]{:S(2)}) collective-permute-start(bf16[256,512]{1,0:T(8,128)(2,1)S(1)} %shard_map.62.refs_3_.refs_6_), channel_id=1, source_target_pairs={{0,1},{1,0},{2,3},{3,2},{4,5},{5,4},{6,7},{7,6},{8,9},{9,8},{10,11... | collective-permute-start | bytes 786440 | tf_op jit(solution)/shard_map/ppermute | solution.py:415
  105.5 1.3 collective-permute-start.28
  107.4 0.6 shard_map.63.refs_3_.refs_2_
  108.3 2.6 %collective-permute-done.26.refs_8_ = bf16[256,512]{1,0:T(8,128)(2,1)S(1)} collective-permute-done((bf16[256,512]{1,0:T(8,128)(2,1)S(1)}, bf16[256,512]{1,0:T(8,128)(2,1)S(1)}, u32[]{:S(2)}, u32[]{:S(2)}) %collective-permute-start.26) | collective-permute-done | bytes 262176 | tf_op jit(solution)/shard_map/ppermute | solution.py:415
  111.4 4.2 %collective-permute-start.30 = (bf16[256,512]{1,0:T(8,128)(2,1)S(1)}, bf16[256,512]{1,0:T(8,128)(2,1)S(1)}, u32[]{:S(2)}, u32[]{:S(2)}) collective-permute-start(bf16[256,512]{1,0:T(8,128)(2,1)S(1)} %shard_map.64.refs_10_.refs_14_.refs_12_), channel_id=1, source_target_pairs={{0,2},{1,3},{2,4},{3,5},{4,6},{5,7},{8,10},{9,11},{10,12},{11,13},... | collective-permute-start | bytes 786440 | tf_op jit(solution)/shard_map/ppermute | solution.py:421
  116.2 3.4 %shard_map.65 = (bf16[512,1024]{1,0:T(8,128)(2,1)S(1)}, bf16[512,512]{1,0:T(8,128)(2,1)S(1)}, bf16[512,2,512]{2,1,0:T(2,128)(2,1)S(1)}) custom-call(s32[4]{0:T(128)S(1)} %pad_add_fusion.refs_0_, bf16[2,512,512]{2,1,0:T(8,128)(2,1)S(1)} %copy-done.2, bf16[2,512,512]{2,1,0:T(8,128)(2,1)S(1)} %copy-done, ...), custom_call_target="tpu_custom_call" | custom-call | flops 3849999872 | tf_op jit(solution)/shard_map/pallas_call | solution.py:37
  119.7 1.8 %shard_map.66 = (bf16[2560,2,512]{2,1,0:T(2,128)(2,1)}, f32[8,128]{1,0:T(8,128)S(1)}) custom-call(s32[4]{0:T(128)S(1)} %pad_add_fusion.refs_0_, s32[2,512]{1,0:T(2,128)S(1)} %get-tuple-element.38.refs_2_.refs_1_, bf16[2,512,512]{2,1,0:T(8,128)(2,1)S(1)} %shard_map.63.refs_3_.refs_2_, bf16[2,512,512]{2,1,0:T(8,128)(2,1)S(1)} %collective-permute-done.24.refs_3_, ...), custom_call_target="tpu_custom_call" | custom-call | flops 5500000256 | tf_op jit(solution)/shard_map/pallas_call | solution.py:37
  121.6 5.5 %collective-permute-start.32 = (bf16[256,512]{1,0:T(8,128)(2,1)S(1)}, bf16[256,512]{1,0:T(8,128)(2,1)S(1)}, u32[]{:S(2)}, u32[]{:S(2)}) collective-permute-start(bf16[256,512]{1,0:T(8,128)(2,1)S(1)} %shard_map.67.refs_22_.refs_15_.refs_13_), channel_id=1, source_target_pairs={{0,2},{1,3},{2,4},{3,5},{4,6},{5,7},{8,10},{9,11},{10,12},{11,13},... | collective-permute-start | bytes 786440 | tf_op jit(solution)/shard_map/ppermute | solution.py:421
  127.1 1.7 %collective-permute-start.35 = (bf16[256,512]{1,0:T(8,128)(2,1)S(1)}, bf16[256,512]{1,0:T(8,128)(2,1)S(1)}, u32[]{:S(2)}, u32[]{:S(2)}) collective-permute-start(bf16[256,512]{1,0:T(8,128)(2,1)S(1)} %shard_map.67.refs_22_.refs_15_.refs_13_), channel_id=1, source_target_pairs={{0,1},{1,0},{2,3},{3,2},{4,5},{5,4},{6,7},{7,6},{8,9},{9,8},{10,11... | collective-permute-start | bytes 786440 | tf_op jit(solution)/shard_map/ppermute | solution.py:415
  128.8 6.2 %shard_map.68 = (bf16[2560,2,512]{2,1,0:T(2,128)(2,1)}, f32[8,128]{1,0:T(8,128)S(1)}) custom-call(s32[4]{0:T(128)S(1)} %pad_add_fusion.refs_0_, s32[2,512]{1,0:T(2,128)S(1)} %get-tuple-element.38.refs_2_.refs_1_, bf16[2,512,512]{2,1,0:T(8,128)(2,1)S(1)} %shard_map.63.refs_3_.refs_2_, ...), custom_call_target="tpu_custom_call", output_to_operand_aliasing={{0}: (21, {})} | custom-call | flops 5500000256 | tf_op jit(solution)/shard_map/pallas_call | solution.py:37
  135.0 4.4 %collective-permute-start.34 = (bf16[256,512]{1,0:T(8,128)(2,1)S(1)}, bf16[256,512]{1,0:T(8,128)(2,1)S(1)}, u32[]{:S(2)}, u32[]{:S(2)}) collective-permute-start(bf16[256,512]{1,0:T(8,128)(2,1)S(1)} %shard_map.69.refs_22_.refs_14_), channel_id=1, source_target_pairs={{0,2},{1,3},{2,4},{3,5},{4,6},{5,7},{8,10},{9,11},{10,12},{11,13},... | collective-permute-start | bytes 786440 | tf_op jit(solution)/shard_map/ppermute | solution.py:421
  139.9 6.4 %shard_map.70 = (bf16[2560,2,512]{2,1,0:T(2,128)(2,1)}, f32[8,128]{1,0:T(8,128)S(1)}) custom-call(s32[4]{0:T(128)S(1)} %pad_add_fusion.refs_0_, s32[2,512]{1,0:T(2,128)S(1)} %get-tuple-element.38.refs_2_.refs_1_, bf16[2,512,512]{2,1,0:T(8,128)(2,1)S(1)} %shard_map.63.refs_3_.refs_2_, ...), custom_call_target="tpu_custom_call", output_to_operand_aliasing={{0}: (21, {})} | custom-call | flops 5500000256 | tf_op jit(solution)/shard_map/pallas_call | solution.py:37
  146.4 1.7 %collective-permute-start.37 = (bf16[256,512]{1,0:T(8,128)(2,1)S(1)}, bf16[256,512]{1,0:T(8,128)(2,1)S(1)}, u32[]{:S(2)}, u32[]{:S(2)}) collective-permute-start(bf16[256,512]{1,0:T(8,128)(2,1)S(1)} %shard_map.71.refs_22_.refs_15_), channel_id=1, source_target_pairs={{0,1},{1,0},{2,3},{3,2},{4,5},{5,4},{6,7},{7,6},{8,9},{9,8},{10,11... | collective-permute-start | bytes 786440 | tf_op jit(solution)/shard_map/ppermute | solution.py:415
  148.1 6.2 %shard_map.72 = (bf16[2560,2,512]{2,1,0:T(2,128)(2,1)}, f32[8,128]{1,0:T(8,128)S(1)}) custom-call(s32[4]{0:T(128)S(1)} %pad_add_fusion.refs_0_, s32[2,512]{1,0:T(2,128)S(1)} %get-tuple-element.38.refs_2_.refs_1_, bf16[2,512,512]{2,1,0:T(8,128)(2,1)S(1)} %shard_map.63.refs_3_.refs_2_, ...), custom_call_target="tpu_custom_call", output_to_operand_aliasing={{0}: (21, {})} | custom-call | flops 5500000256 | tf_op jit(solution)/shard_map/pallas_call | solution.py:37
  154.3 7.1 %shard_map.73 = (bf16[2560,2,512]{2,1,0:T(2,128)(2,1)}, f32[8,128]{1,0:T(8,128)}) custom-call(s32[4]{0:T(128)S(1)} %pad_add_fusion.refs_0_, s32[2,512]{1,0:T(2,128)S(1)} %get-tuple-element.38.refs_2_.refs_1_, bf16[2,512,512]{2,1,0:T(8,128)(2,1)S(1)} %shard_map.63.refs_3_.refs_2_, ...), custom_call_target="tpu_custom_call", output_to_operand_aliasing={{0}: (21, {})} | custom-call | flops 5500000256 | tf_op jit(solution)/shard_map/pallas_call | solution.py:37
  (70 shorter events, 12.0 us)
Async XLA Ops:
  0.0 6.9 %copy-start.5 = (s32[2,512]{1,0:T(2,128)S(1)}, s32[2,512]{1,0:T(2,128)}, u32[]{:S(2)}) copy-start(s32[2,512]{1,0:T(2,128)} %refs_1_.3) | copy-start | bytes 12292
  1.8 18.0 %collective-permute-start = (bf16[256,512]{1,0:T(8,128)(2,1)}, bf16[256,512]{1,0:T(8,128)(2,1)S(1)}, u32[]{:S(2)}, u32[]{:S(2)}) collective-permute-start(bf16[256,512]{1,0:T(8,128)(2,1)} %shard_map.46.refs_4_.refs_1_.refs_11_), channel_id=1, source_target_pairs={{0,2},{1,3},{2,4},{3,5},{4,6},{5,7},{8,10},{9,11},{10,12},{11,13},... | collective-permute-start | bytes 786440 | tf_op jit(solution)/shard_map/ppermute | solution.py:421
  7.1 2.5 %copy-start.1 = (bf16[5,512,2,512]{3,2,1,0:T(2,128)(2,1)S(1)}, bf16[5,512,2,512]{3,2,1,0:T(2,128)(2,1)}, u32[]{:S(2)}) copy-start(bf16[5,512,2,512]{3,2,1,0:T(2,128)(2,1)} %param.4) | copy-start | bytes 15728644
  9.6 0.9 copy-start.3
  18.1 5.7 %collective-permute-start.2 = (bf16[512,2,512]{2,1,0:T(2,128)(2,1)S(1)}, bf16[512,2,512]{2,1,0:T(2,128)(2,1)S(1)}, u32[]{:S(2)}, u32[]{:S(2)}) collective-permute-start(bf16[512,2,512]{2,1,0:T(2,128)(2,1)S(1)} %get-tuple-element.44), channel_id=1, source_target_pairs={{0,8},{8,0},{16,24},{24,16},{1,9},{9,1},{17,25},{25,17},{2,10},{10... | collective-permute-start | bytes 3145736 | tf_op jit(solution)/shard_map/ppermute | solution.py:412
  18.2 10.0 %collective-permute-start.3 = (bf16[256,512]{1,0:T(8,128)(2,1)S(1)}, bf16[256,512]{1,0:T(8,128)(2,1)S(1)}, u32[]{:S(2)}, u32[]{:S(2)}) collective-permute-start(bf16[256,512]{1,0:T(8,128)(2,1)S(1)} %copy-done.3), channel_id=1, source_target_pairs={{0,1},{1,0},{2,3},{3,2},{4,5},{5,4},{6,7},{7,6},{8,9},{9,8},{10,11... | collective-permute-start | bytes 786440 | tf_op jit(solution)/shard_map/ppermute | solution.py:415
  20.4 9.4 %collective-permute-start.1 = (bf16[256,512]{1,0:T(8,128)(2,1)S(1)}, bf16[256,512]{1,0:T(8,128)(2,1)S(1)}, u32[]{:S(2)}, u32[]{:S(2)}) collective-permute-start(bf16[256,512]{1,0:T(8,128)(2,1)S(1)} %shard_map.48.refs_4_.refs_2_.refs_12_), channel_id=1, source_target_pairs={{0,2},{1,3},{2,4},{3,5},{4,6},{5,7},{8,10},{9,11},{10,12},{11,13},... | collective-permute-start | bytes 786440 | tf_op jit(solution)/shard_map/ppermute | solution.py:421
  26.1 37.1 %collective-permute-start.10 = (bf16[512,2,512]{2,1,0:T(2,128)(2,1)S(1)}, bf16[512,2,512]{2,1,0:T(2,128)(2,1)S(1)}, u32[]{:S(2)}, u32[]{:S(2)}) collective-permute-start(bf16[512,2,512]{2,1,0:T(2,128)(2,1)S(1)} %shard_map.49.refs_3_.refs_2_), channel_id=1, source_target_pairs={{0,16},{8,24},{16,0},{24,8},{1,17},{9,25},{17,1},{25,9},{2,18},{10... | collective-permute-start | bytes 3145736 | tf_op jit(solution)/shard_map/ppermute | solution.py:418
  27.7 7.8 %collective-permute-start.5 = (bf16[256,512]{1,0:T(8,128)(2,1)S(1)}, bf16[256,512]{1,0:T(8,128)(2,1)S(1)}, u32[]{:S(2)}, u32[]{:S(2)}) collective-permute-start(bf16[256,512]{1,0:T(8,128)(2,1)S(1)} %shard_map.48.refs_4_.refs_2_.refs_12_), channel_id=1, source_target_pairs={{0,1},{1,0},{2,3},{3,2},{4,5},{5,4},{6,7},{7,6},{8,9},{9,8},{10,11... | collective-permute-start | bytes 786440 | tf_op jit(solution)/shard_map/ppermute | solution.py:415
  30.3 9.4 %collective-permute-start.4 = (bf16[256,512]{1,0:T(8,128)(2,1)S(1)}, bf16[256,512]{1,0:T(8,128)(2,1)S(1)}, u32[]{:S(2)}, u32[]{:S(2)}) collective-permute-start(bf16[256,512]{1,0:T(8,128)(2,1)S(1)} %shard_map.50.refs_3_.refs_13_.refs_11_), channel_id=1, source_target_pairs={{0,2},{1,3},{2,4},{3,5},{4,6},{5,7},{8,10},{9,11},{10,12},{11,13},... | collective-permute-start | bytes 786440 | tf_op jit(solution)/shard_map/ppermute | solution.py:421
  34.7 10.6 %collective-permute-start.7 = (bf16[256,512]{1,0:T(8,128)(2,1)S(1)}, bf16[256,512]{1,0:T(8,128)(2,1)S(1)}, u32[]{:S(2)}, u32[]{:S(2)}) collective-permute-start(bf16[256,512]{1,0:T(8,128)(2,1)S(1)} %shard_map.50.refs_3_.refs_13_.refs_11_), channel_id=1, source_target_pairs={{0,1},{1,0},{2,3},{3,2},{4,5},{5,4},{6,7},{7,6},{8,9},{9,8},{10,11... | collective-permute-start | bytes 786440 | tf_op jit(solution)/shard_map/ppermute | solution.py:415
  40.3 8.5 %collective-permute-start.6 = (bf16[256,512]{1,0:T(8,128)(2,1)S(1)}, bf16[256,512]{1,0:T(8,128)(2,1)S(1)}, u32[]{:S(2)}, u32[]{:S(2)}) collective-permute-start(bf16[256,512]{1,0:T(8,128)(2,1)S(1)} %shard_map.51.refs_3_.refs_4_.refs_14_.refs_12_), channel_id=1, source_target_pairs={{0,2},{1,3},{2,4},{3,5},{4,6},{5,7},{8,10},{9,11},{10,12},{11,13},... | collective-permute-start | bytes 786440 | tf_op jit(solution)/shard_map/ppermute | solution.py:421
  44.7 9.7 %collective-permute-start.8 = (bf16[256,512]{1,0:T(8,128)(2,1)S(1)}, bf16[256,512]{1,0:T(8,128)(2,1)S(1)}, u32[]{:S(2)}, u32[]{:S(2)}) collective-permute-start(bf16[256,512]{1,0:T(8,128)(2,1)S(1)} %shard_map.51.refs_3_.refs_4_.refs_14_.refs_12_), channel_id=1, source_target_pairs={{0,1},{1,0},{2,3},{3,2},{4,5},{5,4},{6,7},{7,6},{8,9},{9,8},{10,11... | collective-permute-start | bytes 786440 | tf_op jit(solution)/shard_map/ppermute | solution.py:415
  49.4 8.3 %collective-permute-start.11 = (bf16[256,512]{1,0:T(8,128)(2,1)S(1)}, bf16[256,512]{1,0:T(8,128)(2,1)S(1)}, u32[]{:S(2)}, u32[]{:S(2)}) collective-permute-start(bf16[256,512]{1,0:T(8,128)(2,1)S(1)} %shard_map.52.refs_3_.refs_5_.refs_15_.refs_13_.refs_11_), channel_id=1, source_target_pairs={{0,2},{1,3},{2,4},{3,5},{4,6},{5,7},{8,10},{9,11},{10,12},{11,13},... | collective-permute-start | bytes 786440 | tf_op jit(solution)/shard_map/ppermute | solution.py:421
  53.8 11.1 %collective-permute-start.9 = (bf16[256,512]{1,0:T(8,128)(2,1)S(1)}, bf16[256,512]{1,0:T(8,128)(2,1)S(1)}, u32[]{:S(2)}, u32[]{:S(2)}) collective-permute-start(bf16[256,512]{1,0:T(8,128)(2,1)S(1)} %shard_map.52.refs_3_.refs_5_.refs_15_.refs_13_.refs_11_), channel_id=1, source_target_pairs={{0,1},{1,0},{2,3},{3,2},{4,5},{5,4},{6,7},{7,6},{8,9},{9,8},{10,11... | collective-permute-start | bytes 786440 | tf_op jit(solution)/shard_map/ppermute | solution.py:415
  54.4 14.2 %collective-permute-start.20 = (bf16[512,2,512]{2,1,0:T(2,128)(2,1)S(1)}, bf16[512,2,512]{2,1,0:T(2,128)(2,1)S(1)}, u32[]{:S(2)}, u32[]{:S(2)}) collective-permute-start(bf16[512,2,512]{2,1,0:T(2,128)(2,1)S(1)} %get-tuple-element.53.refs_5_), channel_id=1, source_target_pairs={{0,8},{8,0},{16,24},{24,16},{1,9},{9,1},{17,25},{25,17},{2,10},{10... | collective-permute-start | bytes 3145736 | tf_op jit(solution)/shard_map/ppermute | solution.py:412
  58.3 8.3 %collective-permute-start.14 = (bf16[256,512]{1,0:T(8,128)(2,1)S(1)}, bf16[256,512]{1,0:T(8,128)(2,1)S(1)}, u32[]{:S(2)}, u32[]{:S(2)}) collective-permute-start(bf16[256,512]{1,0:T(8,128)(2,1)S(1)} %shard_map.53.refs_4_.refs_14_.refs_12_), channel_id=1, source_target_pairs={{0,2},{1,3},{2,4},{3,5},{4,6},{5,7},{8,10},{9,11},{10,12},{11,13},... | collective-permute-start | bytes 786440 | tf_op jit(solution)/shard_map/ppermute | solution.py:421
  62.7 15.6 %collective-permute-start.21 = (bf16[256,512]{1,0:T(8,128)(2,1)S(1)}, bf16[256,512]{1,0:T(8,128)(2,1)S(1)}, u32[]{:S(2)}, u32[]{:S(2)}) collective-permute-start(bf16[256,512]{1,0:T(8,128)(2,1)S(1)} %shard_map.53.refs_4_.refs_14_.refs_12_), channel_id=1, source_target_pairs={{0,1},{1,0},{2,3},{3,2},{4,5},{5,4},{6,7},{7,6},{8,9},{9,8},{10,11... | collective-permute-start | bytes 786440 | tf_op jit(solution)/shard_map/ppermute | solution.py:415
  64.8 8.2 %collective-permute-start.13 = (bf16[512,1024]{1,0:T(8,128)(2,1)S(1)}, bf16[512,1024]{1,0:T(8,128)(2,1)S(1)}, u32[]{:S(2)}, u32[]{:S(2)}) collective-permute-start(bf16[512,1024]{1,0:T(8,128)(2,1)S(1)} %get-tuple-element.49.refs_1_.refs_2_.refs_3_), channel_id=1, source_target_pairs={{0,8},{8,0},{16,24},{24,16},{1,9},{9,1},{17,25},{25,17},{2,10},{10... | collective-permute-start | bytes 3145736 | tf_op jit(solution)/shard_map/ppermute | solution.py:412
  64.9 9.3 %collective-permute-start.19 = (bf16[512,2,512]{2,1,0:T(2,128)(2,1)S(1)}, bf16[512,2,512]{2,1,0:T(2,128)(2,1)S(1)}, u32[]{:S(2)}, u32[]{:S(2)}) collective-permute-start(bf16[512,2,512]{2,1,0:T(2,128)(2,1)S(1)} %get-tuple-element.48.refs_11_.refs_3_), channel_id=1, source_target_pairs={{0,8},{8,0},{16,24},{24,16},{1,9},{9,1},{17,25},{25,17},{2,10},{10... | collective-permute-start | bytes 3145736 | tf_op jit(solution)/shard_map/ppermute | solution.py:412
  66.5 40.4 %collective-permute-start.12 = (bf16[2,512,512]{2,1,0:T(8,128)(2,1)S(1)}, bf16[2,512,512]{2,1,0:T(8,128)(2,1)S(1)}, u32[]{:S(2)}, u32[]{:S(2)}) collective-permute-start(bf16[2,512,512]{2,1,0:T(8,128)(2,1)S(1)} %shard_map.55.refs_3_.refs_1_), channel_id=1, source_target_pairs={{0,16},{8,24},{16,0},{24,8},{1,17},{9,25},{17,1},{25,9},{2,18},{10... | collective-permute-start | bytes 3145736 | tf_op jit(solution)/shard_map/ppermute | solution.py:418
  68.6 9.7 %collective-permute-start.18 = (bf16[256,512]{1,0:T(8,128)(2,1)S(1)}, bf16[256,512]{1,0:T(8,128)(2,1)S(1)}, u32[]{:S(2)}, u32[]{:S(2)}) collective-permute-start(bf16[256,512]{1,0:T(8,128)(2,1)S(1)} %shard_map.56.refs_3_.refs_15_.refs_13_.refs_11_), channel_id=1, source_target_pairs={{0,2},{1,3},{2,4},{3,5},{4,6},{5,7},{8,10},{9,11},{10,12},{11,13},... | collective-permute-start | bytes 786440 | tf_op jit(solution)/shard_map/ppermute | solution.py:421
  73.0 13.6 %collective-permute-start.23 = (bf16[256,512]{1,0:T(8,128)(2,1)S(1)}, bf16[256,512]{1,0:T(8,128)(2,1)S(1)}, u32[]{:S(2)}, u32[]{:S(2)}) collective-permute-start(bf16[256,512]{1,0:T(8,128)(2,1)S(1)} %shard_map.56.refs_3_.refs_15_.refs_13_.refs_11_), channel_id=1, source_target_pairs={{0,1},{1,0},{2,3},{3,2},{4,5},{5,4},{6,7},{7,6},{8,9},{9,8},{10,11... | collective-permute-start | bytes 786440 | tf_op jit(solution)/shard_map/ppermute | solution.py:415
  78.3 9.7 %copy-start.2 = (bf16[2,512,512]{2,1,0:T(8,128)(2,1)S(1)}, bf16[2,512,512]{2,1,0:T(8,128)(2,1)}, u32[]{:S(2)}) copy-start(bf16[2,512,512]{2,1,0:T(8,128)(2,1)} %refs_1_.5) | copy-start | bytes 3145732
  78.9 11.1 %collective-permute-start.22 = (bf16[256,512]{1,0:T(8,128)(2,1)S(1)}, bf16[256,512]{1,0:T(8,128)(2,1)S(1)}, u32[]{:S(2)}, u32[]{:S(2)}) collective-permute-start(bf16[256,512]{1,0:T(8,128)(2,1)S(1)} %shard_map.59.refs_4_.refs_14_.refs_12_), channel_id=1, source_target_pairs={{0,2},{1,3},{2,4},{3,5},{4,6},{5,7},{8,10},{9,11},{10,12},{11,13},... | collective-permute-start | bytes 786440 | tf_op jit(solution)/shard_map/ppermute | solution.py:421
  82.4 12.3 %collective-permute-start.15 = (bf16[256,512]{1,0:T(8,128)(2,1)S(1)}, bf16[256,512]{1,0:T(8,128)(2,1)S(1)}, u32[]{:S(2)}, u32[]{:S(2)}) collective-permute-start(bf16[256,512]{1,0:T(8,128)(2,1)S(1)} %shard_map.57.refs_8_.refs_1_), channel_id=1, source_target_pairs={{0,2},{1,3},{8,10},{9,11},{16,18},{17,19},{24,26},{25,27}} | collective-permute-start | bytes 786440 | tf_op jit(solution)/shard_map/ppermute | solution.py:501
  85.4 15.0 %collective-permute-start.16 = (bf16[256,512]{1,0:T(8,128)(2,1)S(1)}, bf16[256,512]{1,0:T(8,128)(2,1)S(1)}, u32[]{:S(2)}, u32[]{:S(2)}) collective-permute-start(bf16[256,512]{1,0:T(8,128)(2,1)S(1)} %shard_map.57.refs_8_.refs_1_), channel_id=1, source_target_pairs={{0,4},{1,5},{8,12},{9,13},{16,20},{17,21},{24,28},{25,29}} | collective-permute-start | bytes 786440 | tf_op jit(solution)/shard_map/ppermute | solution.py:501
  86.7 16.6 %collective-permute-start.17 = (bf16[256,512]{1,0:T(8,128)(2,1)S(1)}, bf16[256,512]{1,0:T(8,128)(2,1)S(1)}, u32[]{:S(2)}, u32[]{:S(2)}) collective-permute-start(bf16[256,512]{1,0:T(8,128)(2,1)S(1)} %shard_map.57.refs_8_.refs_1_), channel_id=1, source_target_pairs={{0,6},{1,7},{8,14},{9,15},{16,22},{17,23},{24,30},{25,31}} | collective-permute-start | bytes 786440 | tf_op jit(solution)/shard_map/ppermute | solution.py:501
  90.0 18.1 %collective-permute-start.29 = (bf16[256,512]{1,0:T(8,128)(2,1)S(1)}, bf16[256,512]{1,0:T(8,128)(2,1)S(1)}, u32[]{:S(2)}, u32[]{:S(2)}) collective-permute-start(bf16[256,512]{1,0:T(8,128)(2,1)S(1)} %shard_map.59.refs_4_.refs_14_.refs_12_), channel_id=1, source_target_pairs={{0,1},{1,0},{2,3},{3,2},{4,5},{5,4},{6,7},{7,6},{8,9},{9,8},{10,11... | collective-permute-start | bytes 786440 | tf_op jit(solution)/shard_map/ppermute | solution.py:415
  103.9 7.0 %collective-permute-start.26 = (bf16[256,512]{1,0:T(8,128)(2,1)S(1)}, bf16[256,512]{1,0:T(8,128)(2,1)S(1)}, u32[]{:S(2)}, u32[]{:S(2)}) collective-permute-start(bf16[256,512]{1,0:T(8,128)(2,1)S(1)} %shard_map.62.refs_3_.refs_6_), channel_id=1, source_target_pairs={{0,1},{1,0},{2,3},{3,2},{4,5},{5,4},{6,7},{7,6},{8,9},{9,8},{10,11... | collective-permute-start | bytes 786440 | tf_op jit(solution)/shard_map/ppermute | solution.py:415
  105.5 5.3 %collective-permute-start.28 = (bf16[256,512]{1,0:T(8,128)(2,1)S(1)}, bf16[256,512]{1,0:T(8,128)(2,1)S(1)}, u32[]{:S(2)}, u32[]{:S(2)}) collective-permute-start(bf16[256,512]{1,0:T(8,128)(2,1)S(1)} %shard_map.61.refs_5_.refs_15_.refs_13_.refs_11_), channel_id=1, source_target_pairs={{0,2},{1,3},{2,4},{3,5},{4,6},{5,7},{8,10},{9,11},{10,12},{11,13},... | collective-permute-start | bytes 786440 | tf_op jit(solution)/shard_map/ppermute | solution.py:421
  106.8 8.8 %collective-permute-start.25 = (bf16[256,512]{1,0:T(8,128)(2,1)S(1)}, bf16[256,512]{1,0:T(8,128)(2,1)S(1)}, u32[]{:S(2)}, u32[]{:S(2)}) collective-permute-start(bf16[256,512]{1,0:T(8,128)(2,1)S(1)} %shard_map.62.refs_3_.refs_6_), channel_id=1, source_target_pairs={{0,8},{8,0},{16,24},{24,16},{1,9},{9,1},{17,25},{25,17},{2,10},{10... | collective-permute-start | bytes 786440 | tf_op jit(solution)/shard_map/ppermute | solution.py:412
  106.9 14.6 %collective-permute-start.31 = (bf16[256,512]{1,0:T(8,128)(2,1)S(1)}, bf16[256,512]{1,0:T(8,128)(2,1)S(1)}, u32[]{:S(2)}, u32[]{:S(2)}) collective-permute-start(bf16[256,512]{1,0:T(8,128)(2,1)S(1)} %shard_map.61.refs_5_.refs_15_.refs_13_.refs_11_), channel_id=1, source_target_pairs={{0,1},{1,0},{2,3},{3,2},{4,5},{5,4},{6,7},{7,6},{8,9},{9,8},{10,11... | collective-permute-start | bytes 786440 | tf_op jit(solution)/shard_map/ppermute | solution.py:415
  108.1 11.6 %collective-permute-start.24 = (bf16[2,512,512]{2,1,0:T(8,128)(2,1)S(1)}, bf16[2,512,512]{2,1,0:T(8,128)(2,1)S(1)}, u32[]{:S(2)}, u32[]{:S(2)}) collective-permute-start(bf16[2,512,512]{2,1,0:T(8,128)(2,1)S(1)} %shard_map.63.refs_3_.refs_2_), channel_id=1, source_target_pairs={{0,8},{8,0},{16,24},{24,16},{1,9},{9,1},{17,25},{25,17},{2,10},{10... | collective-permute-start | bytes 3145736 | tf_op jit(solution)/shard_map/ppermute | solution.py:412
  110.8 5.3 %collective-permute-start.27 = (bf16[256,512]{1,0:T(8,128)(2,1)S(1)}, bf16[256,512]{1,0:T(8,128)(2,1)S(1)}, u32[]{:S(2)}, u32[]{:S(2)}) collective-permute-start(bf16[256,512]{1,0:T(8,128)(2,1)S(1)} %collective-permute-done.26.refs_8_), channel_id=1, source_target_pairs={{0,8},{8,0},{16,24},{24,16},{1,9},{9,1},{17,25},{25,17},{2,10},{10... | collective-permute-start | bytes 786440 | tf_op jit(solution)/shard_map/ppermute | solution.py:412
  110.9 5.3 %copy-start = (bf16[2,512,512]{2,1,0:T(8,128)(2,1)S(1)}, bf16[2,512,512]{2,1,0:T(8,128)(2,1)}, u32[]{:S(2)}) copy-start(bf16[2,512,512]{2,1,0:T(8,128)(2,1)} %refs_4_.9) | copy-start | bytes 3145732
  111.4 10.1 %collective-permute-start.30 = (bf16[256,512]{1,0:T(8,128)(2,1)S(1)}, bf16[256,512]{1,0:T(8,128)(2,1)S(1)}, u32[]{:S(2)}, u32[]{:S(2)}) collective-permute-start(bf16[256,512]{1,0:T(8,128)(2,1)S(1)} %shard_map.64.refs_10_.refs_14_.refs_12_), channel_id=1, source_target_pairs={{0,2},{1,3},{2,4},{3,5},{4,6},{5,7},{8,10},{9,11},{10,12},{11,13},... | collective-permute-start | bytes 786440 | tf_op jit(solution)/shard_map/ppermute | solution.py:421
  115.7 19.3 %collective-permute-start.33 = (bf16[256,512]{1,0:T(8,128)(2,1)S(1)}, bf16[256,512]{1,0:T(8,128)(2,1)S(1)}, u32[]{:S(2)}, u32[]{:S(2)}) collective-permute-start(bf16[256,512]{1,0:T(8,128)(2,1)S(1)} %shard_map.64.refs_10_.refs_14_.refs_12_), channel_id=1, source_target_pairs={{0,1},{1,0},{2,3},{3,2},{4,5},{5,4},{6,7},{7,6},{8,9},{9,8},{10,11... | collective-permute-start | bytes 786440 | tf_op jit(solution)/shard_map/ppermute | solution.py:415
  116.2 3.5 %copy-start.4 = (bf16[256,512]{1,0:T(8,128)(2,1)S(1)}, bf16[256,512]{1,0:T(8,128)(2,1)}, u32[]{:S(2)}) copy-start(bf16[256,512]{1,0:T(8,128)(2,1)} %shard_map.46.refs_4_.refs_1_.refs_11_) | copy-start | bytes 786436
  121.6 13.4 %collective-permute-start.32 = (bf16[256,512]{1,0:T(8,128)(2,1)S(1)}, bf16[256,512]{1,0:T(8,128)(2,1)S(1)}, u32[]{:S(2)}, u32[]{:S(2)}) collective-permute-start(bf16[256,512]{1,0:T(8,128)(2,1)S(1)} %shard_map.67.refs_22_.refs_15_.refs_13_), channel_id=1, source_target_pairs={{0,2},{1,3},{2,4},{3,5},{4,6},{5,7},{8,10},{9,11},{10,12},{11,13},... | collective-permute-start | bytes 786440 | tf_op jit(solution)/shard_map/ppermute | solution.py:421
  127.1 19.2 %collective-permute-start.35 = (bf16[256,512]{1,0:T(8,128)(2,1)S(1)}, bf16[256,512]{1,0:T(8,128)(2,1)S(1)}, u32[]{:S(2)}, u32[]{:S(2)}) collective-permute-start(bf16[256,512]{1,0:T(8,128)(2,1)S(1)} %shard_map.67.refs_22_.refs_15_.refs_13_), channel_id=1, source_target_pairs={{0,1},{1,0},{2,3},{3,2},{4,5},{5,4},{6,7},{7,6},{8,9},{9,8},{10,11... | collective-permute-start | bytes 786440 | tf_op jit(solution)/shard_map/ppermute | solution.py:415
  135.0 11.3 %collective-permute-start.34 = (bf16[256,512]{1,0:T(8,128)(2,1)S(1)}, bf16[256,512]{1,0:T(8,128)(2,1)S(1)}, u32[]{:S(2)}, u32[]{:S(2)}) collective-permute-start(bf16[256,512]{1,0:T(8,128)(2,1)S(1)} %shard_map.69.refs_22_.refs_14_), channel_id=1, source_target_pairs={{0,2},{1,3},{2,4},{3,5},{4,6},{5,7},{8,10},{9,11},{10,12},{11,13},... | collective-permute-start | bytes 786440 | tf_op jit(solution)/shard_map/ppermute | solution.py:421
  139.4 14.8 %collective-permute-start.36 = (bf16[256,512]{1,0:T(8,128)(2,1)S(1)}, bf16[256,512]{1,0:T(8,128)(2,1)S(1)}, u32[]{:S(2)}, u32[]{:S(2)}) collective-permute-start(bf16[256,512]{1,0:T(8,128)(2,1)S(1)} %shard_map.69.refs_22_.refs_14_), channel_id=1, source_target_pairs={{0,1},{1,0},{2,3},{3,2},{4,5},{5,4},{6,7},{7,6},{8,9},{9,8},{10,11... | collective-permute-start | bytes 786440 | tf_op jit(solution)/shard_map/ppermute | solution.py:415
  146.4 7.9 %collective-permute-start.37 = (bf16[256,512]{1,0:T(8,128)(2,1)S(1)}, bf16[256,512]{1,0:T(8,128)(2,1)S(1)}, u32[]{:S(2)}, u32[]{:S(2)}) collective-permute-start(bf16[256,512]{1,0:T(8,128)(2,1)S(1)} %shard_map.71.refs_22_.refs_15_), channel_id=1, source_target_pairs={{0,1},{1,0},{2,3},{3,2},{4,5},{5,4},{6,7},{7,6},{8,9},{9,8},{10,11... | collective-permute-start | bytes 786440 | tf_op jit(solution)/shard_map/ppermute | solution.py:415
where the time goes:
time: 164 us; the launch traced here: 162 us
  starting transfers between devices  71.8 us (44%)
  Pallas kernels  58.1 us (35%)
  waiting for transfers between devices  27.1 us (17%)
  local copies, waits for them, and re-layouts  3.64 us (2%)
    pallas_call x28, Pallas kernels, call(): pl.pallas_call(ordered, out_shape=tuple((shape for shape, _ in outs)), in...  58.1 us
    ppermute x12, starting transfers between devices, to_next(): lax.ppermute(value, 'pcol', [(c, c + 2) for c in range(col_devices - 2)])  49.4 us
    ppermute x12, waiting for transfers between devices, to_next(): lax.ppermute(value, 'pcol', [(c, c + 2) for c in range(col_devices - 2)])  13.1 us
    ppermute x14, starting transfers between devices, to_neighbour(): return lax.ppermute(value, 'pcol', [(c, c ^ 1) for c in range(col_devices)])  12.9 us
    ppermute x3, waiting for transfers between devices, head(): lax.ppermute(mine, 'pcol', [(0, 2 * h), (1, 2 * h + 1)])  11.2 us
    ppermute x3, starting transfers between devices, head(): lax.ppermute(mine, 'pcol', [(0, 2 * h), (1, 2 * h + 1)])  5.59 us
    unnamed x12, local copies, waits for them, and re-layouts  3.45 us
  transfers between devices with their start and end apart: 38, of which 10 were waited for; matrix products, arithmetic and copies ran while one was open for 0% of the time, Pallas kernels for 30%

commit v1 on v0

--- a/solution.py
+++ b/solution.py
@@ -122,7 +122,7 @@
 
 def gather_kernel(meta, pivots, spread, tiles, *refs):
     *pieces, loaded, send, keep, block0, join, arrive, goal, hops, fetch, fetch_table, load_sem, table_sem = refs
-    chunk, nb = pieces[0].shape
+    nb = send.shape[0]
     rows = tiles.shape[0]
     core = meta[1]
     load = pltpu.make_async_copy(tiles, loaded.at[pl.ds(0, rows)], load_sem)
@@ -132,8 +132,11 @@
     table.start()
     table.wait()
     load.wait()
-    for i, piece in enumerate(pieces, 1):
-        piece[...] = flat(loaded[i * chunk : (i + 1) * chunk])[:, :nb]
+    begin = nb
+    for piece in pieces:
+        end = begin + piece.shape[0]
+        piece[...] = flat(loaded[begin:end])[:, :nb]
+        begin = end
     copy_rows(nb, send, lambda i: i, loaded, lambda i: fetch_table[1 - core, i])
     copy_rows(nb, keep, lambda i: i, loaded, lambda i: fetch_table[core, i])
     block0[...] = loaded[0:nb]
@@ -166,33 +169,29 @@
         scatter(arrive, came_sibling, 1 - core)
 
 
-def relay_kernel(meta, came, own, held):
+def relay_kernel(meta, came, *refs):
+    *own, held = refs
     place = lax.div(meta[2], 2)
-
-    @pl.when(place == 0)
-    def _():
-        held[...] = own[...]
+    for piece in own:
+
+        @pl.when(place == 0)
+        def _(piece=piece):
+            held[0 : piece.shape[0]] = piece[...]
 
     @pl.when(place != 0)
     def _():
-        held[...] = came[...]
-
-
-def pass_kernel(came, held):
-    held[...] = came[...]
+        count = min(came.shape[0], held.shape[0])
+        held[0:count] = came[0:count]
 
 
 def old_kernel(line, meta, *refs):
-    held, other, old = refs[: len(refs) // 2], refs[len(refs) // 2 : -1], refs[-1]
-    place = lax.div(meta[2], 2)
-    chunk = held[0].shape[0]
+    held, other, old = refs[:line], refs[line : 2 * line], refs[-1]
     for h in range(line):
 
-        @pl.when(place == h)
+        @pl.when(lax.div(meta[2], 2) == h)
         def _(h=h):
-            for p in range(old.shape[1] // chunk):
-                old[0, p * chunk : (p + 1) * chunk] = held[p + h][...]
-                old[1, p * chunk : (p + 1) * chunk] = other[p + h][...]
+            old[0] = held[h][0 : old.shape[1]]
+            old[1] = other[h][0 : old.shape[1]]
 
 
 def by_chip_kernel(meta, *refs):
@@ -215,8 +214,8 @@
 
 def head_kernel(meta, fresh, fresh_sibling, head):
     needed = 1 - lax.rem(meta[2], 2)
-    half, nb = head.shape
-    at = pl.ds(pl.multiple_of(meta[1] * half, half), half)
+    part, nb = head.shape
+    at = pl.ds(pl.multiple_of(meta[0] * part, part), part)
 
     @pl.when(meta[1] == needed)
     def _():
@@ -225,6 +224,12 @@
     @pl.when(meta[1] != needed)
     def _():
         head[...] = fresh_sibling[at, :nb]
+
+
+def stack_kernel(*refs):
+    *entries, out = refs
+    for i, entry in enumerate(entries):
+        out[i] = entry[...]
 
 
 def choose(hop, choices):
@@ -279,15 +284,16 @@
     top[...] = raw(shown, nb)
 
 
-def prep1_kernel(meta, lower, upper, fresh, fresh_sibling, up0, *refs):
-    mine, mine_sibling, other, other_sibling, up1, up0_panel, top, work, head = refs
-    core, column = meta[1], meta[2]
+def prep1_kernel(chips, meta, lower, upper, fresh, fresh_sibling, up0, *refs):
+    heads, heads_sibling, up1, up0_panel, top, work, head = refs
+    core, column, chip = meta[1], meta[2], meta[0] // 2
     side = lax.rem(column, 2)
-    nb, half = fresh.shape[0], mine.shape[0]
-    for which, who, piece in (
-        (1 - side, core, mine), (1 - side, 1 - core, mine_sibling), (side, core, other), (side, 1 - core, other_sibling)
-    ):
-        head[which, pl.ds(pl.multiple_of(who * half, half), half)] = piece[...]
+    nb, part = fresh.shape[0], heads.shape[2]
+    for who, parts in ((core, heads), (1 - core, heads_sibling)):
+        for h in range(chips):
+            at = pl.multiple_of((2 * lax.rem(chip + chips - h, chips) + who) * part, part)
+            head[1 - side, pl.ds(at, part)] = parts[h, 0]
+            head[side, pl.ds(at, part)] = parts[h, 1]
 
     @pl.when(core == 1)
     def _():
@@ -316,22 +322,18 @@
 
 
 def update_kernel(
-    block_index, line, meta, goal, old, old_sibling, upper, up0, up1, up0_panel, tiles, top0, top1, *rest
+    begin, line, meta, goal, old, old_sibling, upper, up0, up1, up0_panel, tiles, top0, top1, *rest
 ):
+    held, other = rest[:line], rest[line : 2 * line]
     out, token, panels, block, result, panel_sem, block_sem, out_sem = rest[-8:]
-    spans = (len(rest) - 8) // 2
-    held, other = rest[:spans], rest[spans : 2 * spans]
-    per_block = spans - line + 1
-    row, core, column, row_devices = meta[0], meta[1], meta[2], meta[3]
+    row, core, column = meta[0], meta[1], meta[2]
     side, place = lax.rem(column, 2), lax.div(column, 2)
-    nb, cb, _ = block.shape
-    chunk = nb // per_block
-    rows_of = pl.ds(block_index * nb, nb)
-
-    def panel_copy(i, h, which):
-        source = (held, other)[which][i + h]
-        target = panels.at[lax.rem(side + which, 2), pl.ds(i * chunk, chunk)]
-        return pltpu.make_async_copy(source, target, panel_sem.at[i, which])
+    count, cb, nb = block.shape
+    rows_of = pl.ds(begin, count)
+
+    def panel_copy(h, which):
+        source = (held, other)[which][h].at[pl.ds(0, count)]
+        return pltpu.make_async_copy(source, panels.at[lax.rem(side + which, 2)], panel_sem.at[which])
 
     load = pltpu.make_async_copy(tiles.at[rows_of], block, block_sem)
     load.start()
@@ -339,17 +341,15 @@
 
         @pl.when(place == h)
         def _(h=h):
-            for i in range(per_block):
-                panel_copy(i, h, 0).start()
-                panel_copy(i, h, 1).start()
+            panel_copy(h, 0).start()
+            panel_copy(h, 1).start()
 
     def arrived():
-        for i in range(per_block):
-            panel_copy(i, 0, 0).wait()
-            panel_copy(i, 0, 1).wait()
+        panel_copy(0, 0).wait()
+        panel_copy(0, 1).wait()
 
     def from_factors():
-        here = block_index * nb + lax.broadcasted_iota(I32, (nb, nb), 0)
+        here = begin + lax.broadcasted_iota(I32, (count, nb), 0)
         pick = jnp.where(here == goal[pl.ds(core, 1), :], 1.0, 0.0)
         pick_sibling = jnp.where(here == goal[pl.ds(1 - core, 1), :], 1.0, 0.0)
         moved = jnp.sum(pick + pick_sibling, axis=1, keepdims=True) > 0.5
@@ -379,11 +379,11 @@
     def from_top(top):
         arrived()
         load.wait()
-        copy = pltpu.make_async_copy(top, result, block_sem)
+        copy = pltpu.make_async_copy(top.at[rows_of], result, block_sem)
         copy.start()
         copy.wait()
 
-    if block_index == 0:
+    if begin < nb:
         pl.when(row == 0)(lambda: from_top(top0))
         pl.when(row == 1)(lambda: from_top(top1))
         pl.when(row >= 2)(from_factors)
@@ -398,8 +398,9 @@
 def body(matrix, pivots, lower, upper):
     rb, nb, cb, _ = matrix.shape
     rows = rb * nb
-    chunk = nb // 2
-    pieces = rows // chunk
+    sizes = [nb] * (rb - 1) + [nb // 2] * 2
+    begins = [sum(sizes[:i]) for i in range(len(sizes))]
+    pieces = len(sizes)
     row_devices = lax.axis_size("prow")
     col_devices = lax.axis_size("pcol")
     chips, line = row_devices // 2, col_devices // 2
@@ -429,27 +430,27 @@
         return results
 
     last_step = pieces + line - 2
-    piece_out = [(bf16(chunk, nb), VMEM)]
+
+    def piece_out(i):
+        return (bf16(sizes[i], nb), VMEM)
+
+    def step_out(k):
+        return (bf16(max(sizes[k - p] for p in range(line) if 0 <= k - p < pieces), nb), VMEM)
+
     own, held, other = [], [], []
     state = {}
-
-    def turn_us(k):
-        return 10.0 if k in (1, 6) or k > 8 else 0.2
 
     def step(k):
         if k == 0:
             own.extend(run(
-                first_kernel, [(tiles, ANY)], piece_out, scratch=[pltpu.VMEM((chunk, cb, nb), BF16), DMA], mib=60,
+                first_kernel, [(tiles, ANY)], [piece_out(0)],
+                scratch=[pltpu.VMEM((sizes[0], cb, nb), BF16), DMA], mib=60,
             ))
             value = own[0]
         else:
             also = (other[k - 2],) if k >= 2 else ()
-            came = state["came"]
-            if k < pieces:
-                operands = [(meta, SMEM), (came, VMEM), (own[k], VMEM)]
-                (value,) = run(relay_kernel, operands, piece_out, also, us=turn_us(k))
-            else:
-                (value,) = run(pass_kernel, [(came, VMEM)], piece_out, also, us=turn_us(k))
+            operands = [(meta, SMEM), (state["came"], VMEM)] + [(v, VMEM) for v in own[k : k + 1]]
+            (value,) = run(relay_kernel, operands, [step_out(k)], also, us=0.2 if k in (3, 4, 5) else 12.0)
         held.append(value)
         if k < last_step:
             state["came"] = to_next(value)
@@ -462,7 +463,7 @@
         results = run(
             gather_kernel,
             [(meta, SMEM), (pivots, VMEM), (spread, VMEM), (tiles, ANY)],
-            piece_out * (pieces - 1) + [(bf16(rows + 8, cb, nb), VMEM)]
+            [piece_out(i) for i in range(1, pieces)] + [(bf16(rows + 8, cb, nb), VMEM)]
             + [(bf16(nb, cb, nb), VMEM)] * 3 + [(table, VMEM)] * 4,
             scratch=[pltpu.VMEM((2, nb), I32), pltpu.SMEM((2, nb), I32), DMA, DMA],
             us=8.0, mib=20,
@@ -493,9 +494,11 @@
         state["fresh"] = (new, to_sibling(new))
         state["brought"] = (brought, to_sibling(brought))
 
+    part = nb // row_devices
+
     def head():
         (mine,) = run(
-            head_kernel, [(meta, SMEM)] + [(v, VMEM) for v in state["fresh"]], [(bf16(nb // 2, nb), VMEM)], us=0.1,
+            head_kernel, [(meta, SMEM)] + [(v, VMEM) for v in state["fresh"]], [(bf16(part, nb), VMEM)], us=0.1
         )
         state["head"] = [mine] + [
             lax.ppermute(mine, "pcol", [(0, 2 * h), (1, 2 * h + 1)]) for h in range(1, line)
@@ -503,18 +506,23 @@
 
     def head_here():
         (mine,) = run(
-            by_place_kernel, [(meta, SMEM)] + [(v, VMEM) for v in state["head"]], [(bf16(nb // 2, nb), VMEM)]
-        )
-        swapped = to_neighbour(mine)
-        state["heads"] = (mine, to_sibling(mine), swapped, to_sibling(swapped))
+            by_place_kernel, [(meta, SMEM)] + [(v, VMEM) for v in state["head"]], [(bf16(part, nb), VMEM)]
+        )
+        state["head"] = (mine, to_neighbour(mine))
+
+    def head_pair():
+        (pair,) = run(stack_kernel, [(v, VMEM) for v in state["head"]], [(bf16(2, part, nb), VMEM)])
+        state["head"] = [pair] + [to_chip(pair, h) for h in range(1, chips)]
+
+    def head_all():
+        (mine,) = run(
+            stack_kernel, [(v, VMEM) for v in state["head"]], [(bf16(chips, 2, part, nb), VMEM)], us=0.1
+        )
+        state["heads"] = (mine, to_sibling(mine))
 
     def old():
-        spans = range(nb // chunk + line - 1)
-        (mine,) = run(
-            functools.partial(old_kernel, line),
-            [(meta, SMEM)] + [(held[i], VMEM) for i in spans] + [(other[i], VMEM) for i in spans],
-            [(bf16(2, nb, nb), VMEM)],
-        )
+        operands = [(meta, SMEM)] + [(v, VMEM) for v in held[:line] + other[:line]]
+        (mine,) = run(functools.partial(old_kernel, line), operands, [(bf16(2, nb, nb), VMEM)], us=0.6)
         state["old"] = [mine] + [to_chip(mine, h) for h in range(1, chips)]
 
     def old_here():
@@ -543,7 +551,7 @@
 
     def prep1():
         state["up1"], state["up0_panel"], state["top1"] = run(
-            prep1_kernel,
+            functools.partial(prep1_kernel, chips),
             [(meta, SMEM), (lower, VMEM), (upper, VMEM)] + [(v, VMEM) for v in state["fresh"]]
             + [(state["up0"], VMEM)] + [(v, VMEM) for v in state["heads"]],
             [(bf16(nb, cb * nb), VMEM), (bf16(nb, nb), VMEM), (bf16(nb, cb, nb), VMEM)],
@@ -551,36 +559,31 @@
             us=3.5, mib=16,
         )
 
-    per_block = nb // chunk
-
-    def update(b):
-        spans = range(b * per_block, (b + 1) * per_block + line - 1)
+    def update(i):
         operands = [(meta, SMEM), (state["goal"], VMEM)] + [(v, VMEM) for v in state["old"]] + [(upper, VMEM)]
         operands += [(state[name], VMEM) for name in ("up0", "up1", "up0_panel")]
         operands += [(state[name], ANY) for name in ("moved", "top0", "top1")]
-        operands += [(held[i], ANY) for i in spans] + [(other[i], ANY) for i in spans]
+        operands += [(v, ANY) for v in held[i : i + line] + other[i : i + line]]
         aliases = {}
         if "result" in state:
             aliases = {len(operands): 0}
             operands.append((state["result"], ANY))
-        kernel = functools.partial(update_kernel, b, line)
-        if aliases:
-            kernel = lambda *refs, kernel=kernel, at=len(operands) - 1: kernel(*refs[:at], *refs[at + 1 :])
+        count = sizes[i]
         state["result"], _ = run(
-            kernel,
+            functools.partial(update_kernel, begins[i], line),
             operands,
             [(bf16(rows, cb, nb), ANY), (jax.ShapeDtypeStruct((8, 128), F32), VMEM)],
             scratch=[
-                pltpu.VMEM((2, nb, nb), BF16), pltpu.VMEM((nb, cb, nb), BF16), pltpu.VMEM((nb, cb, nb), BF16),
-                DMA((per_block, 2)), DMA, DMA,
+                pltpu.VMEM((2, count, nb), BF16), pltpu.VMEM((count, cb, nb), BF16),
+                pltpu.VMEM((count, cb, nb), BF16), DMA((2,)), DMA, DMA,
             ],
             aliases=aliases,
             us=5.0, mib=24,
         )
 
-    plan = [(0, gather), (1, join), (5, fresh), (line + 1, old), (6, head), (6, scatter), (7, prep0), (8, head_here), (8, old_here), (9, prep1)]
-    for b in range(rb):
-        plan.append((max(9 + b, (b + 1) * per_block + line - 2), functools.partial(update, b)))
+    plan = [(0, gather), (1, join), (3, fresh), (line - 1, old), (3, head), (4, head_here), (4, head_pair), (5, old_here), (5, head_all), (5, scatter), (5, prep0), (5, prep1)]
+    for i in range(pieces):
+        plan.append((max(6 + i, i + line - 1), functools.partial(update, i)))
     for k in range(last_step + 1):
         step(k)
         while plan and (plan[0][0] <= k or k == last_step):

time: 164 us -> 179 us (1.091); the launches traced: 162 us -> 179 us
  waiting for transfers between devices: 27.1 us -> 59.6 us
  starting transfers between devices: 71.8 us -> 54.3 us
  Pallas kernels: 58.1 us -> 60.6 us
    ppermute x14 -> x10, waiting for transfers between devices: 2.82 us -> 23.9 us  [to_neighbour(): return lax.ppermute(value, 'pcol', [(c, c ^ 1) for c in range(col_devices)])]
    ppermute x12 -> x8, starting transfers between devices: 49.4 us -> 31.4 us  [to_next(): lax.ppermute(value, 'pcol', [(c, c + 2) for c in range(col_devices - 2)])]
    ppermute x12 -> x8, waiting for transfers between devices: 13.1 us -> 28 us  [to_next(): lax.ppermute(value, 'pcol', [(c, c + 2) for c in range(col_devices - 2)])]
    ppermute x3, waiting for transfers between devices: 11.2 us -> 4.42 us  [head(): lax.ppermute(mine, 'pcol', [(0, 2 * h), (1, 2 * h + 1)])]
    ppermute x2 -> x3, waiting for transfers between devices: 0.01 us -> 3.29 us  [to_chip(): lax.ppermute(value, 'prow', [(r, (r + 2 * h) % row_devices) for r in rang...]
    pallas_call x28 -> x27, Pallas kernels: 58.1 us -> 60.6 us  [call(): pl.pallas_call(ordered, out_shape=tuple((shape for shape, _ in outs)), in...]
    ppermute x14 -> x10, starting transfers between devices: 12.9 us -> 11.4 us  [to_neighbour(): return lax.ppermute(value, 'pcol', [(c, c ^ 1) for c in range(col_devices)])]
    ppermute x2 -> x3, starting transfers between devices: 3.05 us -> 3.71 us  [to_chip(): lax.ppermute(value, 'prow', [(r, (r + 2 * h) % row_devices) for r in rang...]
  transfers between devices with their start and end apart: 38 -> 30, of which waited for: 10 -> 11; matrix products, arithmetic and copies ran while one was open for 0% -> 0% of each run, Pallas kernels for 30% -> 29%
where the time goes in v1:
time: 179 us
  Pallas kernels  60.6 us (34%)
  waiting for transfers between devices  59.6 us (33%)
  starting transfers between devices  54.3 us (30%)
  local copies, waits for them, and re-layouts  3.73 us (2%)
    pallas_call x27, Pallas kernels, call(): pl.pallas_call(ordered, out_shape=tuple((shape for shape, _ in outs)), in...  60.6 us
    ppermute x8, starting transfers between devices, to_next(): lax.ppermute(value, 'pcol', [(c, c + 2) for c in range(col_devices - 2)])  31.4 us
    ppermute x8, waiting for transfers between devices, to_next(): lax.ppermute(value, 'pcol', [(c, c + 2) for c in range(col_devices - 2)])  28 us
    ppermute x10, waiting for transfers between devices, to_neighbour(): return lax.ppermute(value, 'pcol', [(c, c ^ 1) for c in range(col_devices)])  23.9 us
    ppermute x10, starting transfers between devices, to_neighbour(): return lax.ppermute(value, 'pcol', [(c, c ^ 1) for c in range(col_devices)])  11.4 us
    ppermute x3, starting transfers between devices, head(): lax.ppermute(mine, 'pcol', [(0, 2 * h), (1, 2 * h + 1)])  7.37 us
    ppermute x3, waiting for transfers between devices, head(): lax.ppermute(mine, 'pcol', [(0, 2 * h), (1, 2 * h + 1)])  4.42 us
    ppermute x3, starting transfers between devices, to_chip(): lax.ppermute(value, 'prow', [(r, (r + 2 * h) % row_devices) for r in rang...  3.71 us
  transfers between devices with their start and end apart: 30, of which 11 were waited for; matrix products, arithmetic and copies ran while one was open for 0% of the time, Pallas kernels for 29%

profile of v1, /device:TPU:0, one launch (start us, length us, event | category | flops | bytes accessed | tf_op | source)
XLA Modules:
  0.0 179.0 jit_solution(16965188667590379942)
XLA Ops:
  0.0 2.2 %shard_map.46.refs_4_.refs_1_.refs_11_ = bf16[512,512]{1,0:T(8,128)(2,1)} custom-call(bf16[2560,2,512]{2,1,0:T(2,128)(2,1)} %bitcast.5), custom_call_target="tpu_custom_call" | custom-call | flops 1100000000 | tf_op jit(solution)/shard_map/pallas_call | solution.py:37
  2.2 5.0 %collective-permute-start = (bf16[512,512]{1,0:T(8,128)(2,1)}, bf16[512,512]{1,0:T(8,128)(2,1)S(1)}, u32[]{:S(2)}, u32[]{:S(2)}) collective-permute-start(bf16[512,512]{1,0:T(8,128)(2,1)} %shard_map.46.refs_4_.refs_1_.refs_11_), channel_id=1, source_target_pairs={{0,2},{1,3},{2,4},{3,5},{4,6},{5,7},{8,10},{9,11},{10,12},{11,13},... | collective-permute-start | bytes 1572872 | tf_op jit(solution)/shard_map/ppermute | solution.py:422
  7.1 1.6 collective-permute-start.3
  9.0 2.5 %copy-done.1 = bf16[5,512,2,512]{3,2,1,0:T(2,128)(2,1)S(1)} copy-done((bf16[5,512,2,512]{3,2,1,0:T(2,128)(2,1)S(1)}, bf16[5,512,2,512]{3,2,1,0:T(2,128)(2,1)}, u32[]{:S(2)}) %copy-start.1) | copy-done | bytes 5242904
  11.5 1.0 copy-done.2
  12.5 7.5 %shard_map.47 = (bf16[512,512]{1,0:T(8,128)(2,1)S(1)}, bf16[512,512]{1,0:T(8,128)(2,1)S(1)}, bf16[512,512]{1,0:T(8,128)(2,1)S(1)}, bf16[256,512]{1,0:T(8,128)(2,...) custom-call(s32[4]{0:T(128)S(1)} %pad_add_fusion.refs_0_, ...), custom_call_target="tpu_custom_call" | custom-call | flops 8800000000 | tf_op jit(solution)/shard_map/pallas_call | solution.py:37
  20.7 3.5 %collective-permute-start.1 = (bf16[512,512]{1,0:T(8,128)(2,1)S(1)}, bf16[512,512]{1,0:T(8,128)(2,1)S(1)}, u32[]{:S(2)}, u32[]{:S(2)}) collective-permute-start(bf16[512,512]{1,0:T(8,128)(2,1)S(1)} %shard_map.48.refs_4_.refs_2_.refs_12_.refs_11_), channel_id=1, source_target_pairs={{0,2},{1,3},{2,4},{3,5},{4,6},{5,7},{8,10},{9,11},{10,12},{11,13},... | collective-permute-start | bytes 1572872 | tf_op jit(solution)/shard_map/ppermute | solution.py:422
  24.2 0.9 collective-permute-start.5
  25.1 2.3 %shard_map.49.refs_3_.refs_2_ = bf16[512,2,512]{2,1,0:T(2,128)(2,1)S(1)} custom-call(s32[4]{0:T(128)S(1)} %pad_add_fusion.refs_0_, s32[2,512]{1,0:T(2,128)S(1)} %get-tuple-element.40.refs_1_, bf16[512,2,512]{2,1,0:T(2,128)(2,1)S(1)} %get-tuple-element.41.refs_2_, bf16[512,2,512]{2,1,0:T(2,128)(2,1)S(1)} %collective-permute-done.2.refs_3_, ...), custom_call_target="tpu_custom_call" | custom-call | flops 2200000000 | tf_op jit(solution)/shard_map/pallas_call | solution.py:37
  27.4 1.6 collective-permute-start.8
  28.9 7.1 %collective-permute-done.1.refs_1_ = bf16[512,512]{1,0:T(8,128)(2,1)S(1)} collective-permute-done((bf16[512,512]{1,0:T(8,128)(2,1)S(1)}, bf16[512,512]{1,0:T(8,128)(2,1)S(1)}, u32[]{:S(2)}, u32[]{:S(2)}) %collective-permute-start.1) | collective-permute-done | bytes 524320 | tf_op jit(solution)/shard_map/ppermute | solution.py:422
  36.6 4.4 %collective-permute-start.4 = (bf16[512,512]{1,0:T(8,128)(2,1)S(1)}, bf16[512,512]{1,0:T(8,128)(2,1)S(1)}, u32[]{:S(2)}, u32[]{:S(2)}) collective-permute-start(bf16[512,512]{1,0:T(8,128)(2,1)S(1)} %shard_map.50.refs_3_.refs_13_.refs_12_.refs_11_), channel_id=1, source_target_pairs={{0,2},{1,3},{2,4},{3,5},{4,6},{5,7},{8,10},{9,11},{10,12},{11,13},... | collective-permute-start | bytes 1572872 | tf_op jit(solution)/shard_map/ppermute | solution.py:422
  41.1 11.0 %collective-permute-done.4.refs_1_ = bf16[512,512]{1,0:T(8,128)(2,1)S(1)} collective-permute-done((bf16[512,512]{1,0:T(8,128)(2,1)S(1)}, bf16[512,512]{1,0:T(8,128)(2,1)S(1)}, u32[]{:S(2)}, u32[]{:S(2)}) %collective-permute-start.4) | collective-permute-done | bytes 524320 | tf_op jit(solution)/shard_map/ppermute | solution.py:422
  52.7 1.6 shard_map.52
  54.3 1.1 collective-permute-start.6
  55.4 1.0 collective-permute-start.7
  56.4 4.4 %collective-permute-start.10 = (bf16[512,512]{1,0:T(8,128)(2,1)S(1)}, bf16[512,512]{1,0:T(8,128)(2,1)S(1)}, u32[]{:S(2)}, u32[]{:S(2)}) collective-permute-start(bf16[512,512]{1,0:T(8,128)(2,1)S(1)} %shard_map.51.refs_4_.refs_14_.refs_13_.refs_12_.refs_11_), channel_id=1, source_target_pairs={{0,2},{1,3},{2,4},{3,5},{4,6},{5,7},{8,10},{9,11},{10,12},{11,13},... | collective-permute-start | bytes 1572872 | tf_op jit(solution)/shard_map/ppermute | solution.py:422
  60.8 8.3 %collective-permute-done.6.refs_7_.refs_4_.refs_17_.refs_16_.refs_15_ = bf16[512,512]{1,0:T(8,128)(2,1)S(1)} collective-permute-done((bf16[512,512]{1,0:T(8,128)(2,1)S(1)}, bf16[512,512]{1,0:T(8,128)(2,1)S(1)}, u32[]{:S(2)}, u32[]{:S(2)}) %collective-permute-start.6) | collective-permute-done | bytes 524320 | tf_op jit(solution)/shard_map/ppermute | solution.py:416
  69.1 10.8 %collective-permute-done.7.refs_8_.refs_4_.refs_18_.refs_17_.refs_16_.refs_15_ = bf16[512,512]{1,0:T(8,128)(2,1)S(1)} collective-permute-done((bf16[512,512]{1,0:T(8,128)(2,1)S(1)}, bf16[512,512]{1,0:T(8,128)(2,1)S(1)}, u32[]{:S(2)}, u32[]{:S(2)}) %collective-permute-start.7) | collective-permute-done | bytes 524320 | tf_op jit(solution)/shard_map/ppermute | solution.py:416
  79.9 1.2 shard_map.53.refs_3_.refs_1_
  81.1 1.6 collective-permute-start.9
  83.2 4.4 %collective-permute-start.13 = (bf16[128,512]{1,0:T(8,128)(2,1)S(1)}, bf16[128,512]{1,0:T(8,128)(2,1)S(1)}, u32[]{:S(2)}, u32[]{:S(2)}) collective-permute-start(bf16[128,512]{1,0:T(8,128)(2,1)S(1)} %shard_map.54.refs_3_.refs_1_), channel_id=1, source_target_pairs={{0,2},{1,3},{8,10},{9,11},{16,18},{17,19},{24,26},{25,27}} | collective-permute-start | bytes 393224 | tf_op jit(solution)/shard_map/ppermute | solution.py:504
  87.6 1.7 collective-permute-start.14
  89.3 1.3 collective-permute-start.15
  91.2 1.3 collective-permute-start.12
  92.6 1.6 collective-permute-done.14.refs_3_
  94.2 2.8 %collective-permute-done.15.refs_4_ = bf16[128,512]{1,0:T(8,128)(2,1)S(1)} collective-permute-done((bf16[128,512]{1,0:T(8,128)(2,1)S(1)}, bf16[128,512]{1,0:T(8,128)(2,1)S(1)}, u32[]{:S(2)}, u32[]{:S(2)}) %collective-permute-start.15) | collective-permute-done | bytes 131104 | tf_op jit(solution)/shard_map/ppermute | solution.py:504
  97.8 4.8 %collective-permute-done.16.refs_1_ = bf16[128,512]{1,0:T(8,128)(2,1)S(1)} collective-permute-done((bf16[128,512]{1,0:T(8,128)(2,1)S(1)}, bf16[128,512]{1,0:T(8,128)(2,1)S(1)}, u32[]{:S(2)}, u32[]{:S(2)}) %collective-permute-start.16) | collective-permute-done | bytes 131104 | tf_op jit(solution)/shard_map/ppermute | solution.py:416
  103.3 3.7 %collective-permute-done.12.refs_1_ = bf16[512,512]{1,0:T(8,128)(2,1)S(1)} collective-permute-done((bf16[512,512]{1,0:T(8,128)(2,1)S(1)}, bf16[512,512]{1,0:T(8,128)(2,1)S(1)}, u32[]{:S(2)}, u32[]{:S(2)}) %collective-permute-start.12) | collective-permute-done | bytes 524320 | tf_op jit(solution)/shard_map/ppermute | solution.py:422
  107.5 0.6 shard_map.59.refs_2_
  108.2 3.3 %collective-permute-done.20.refs_1_ = bf16[2,128,512]{2,1,0:T(8,128)(2,1)S(1)} collective-permute-done((bf16[2,128,512]{2,1,0:T(8,128)(2,1)S(1)}, bf16[2,128,512]{2,1,0:T(8,128)(2,1)S(1)}, u32[]{:S(2)}, u32[]{:S(2)}) %collective-permute-start.20) | collective-permute-done | bytes 262176 | tf_op jit(solution)/shard_map/ppermute | solution.py:419
  111.6 1.1 collective-permute-start.23
  112.6 3.8 %collective-permute-start.22 = (bf16[512,512]{1,0:T(8,128)(2,1)S(1)}, bf16[512,512]{1,0:T(8,128)(2,1)S(1)}, u32[]{:S(2)}, u32[]{:S(2)}) collective-permute-start(bf16[512,512]{1,0:T(8,128)(2,1)S(1)} %shard_map.58.refs_3_.refs_14_.refs_13_.refs_12_.refs_11_), channel_id=1, source_target_pairs={{0,2},{1,3},{2,4},{3,5},{4,6},{5,7},{8,10},{9,11},{10,12},{11,13},... | collective-permute-start | bytes 1572872 | tf_op jit(solution)/shard_map/ppermute | solution.py:422
  116.5 1.7 collective-permute-start.25
  118.3 4.1 %shard_map.61.refs_4_.refs_8_ = bf16[2568,2,512]{2,1,0:T(2,128)(2,1)S(1)} custom-call(s32[4]{0:T(128)S(1)} %pad_add_fusion.refs_0_, s32[2,512]{1,0:T(2,128)S(1)} %get-tuple-element.48.refs_1_, s32[2,512]{1,0:T(2,128)S(1)} %get-tuple-element.36.refs_2_.refs_1_, bf16[512,2,512]{2,1,0:T(2,128)(2,1)S(1)} %get-tuple-element.44.refs_9_.refs_3_, ...), custom_call_target="tpu_custom_call" | custom-call | flops 110000000 | tf_op jit(solution)/shard_map/pallas_call | solution.py:37
  122.3 2.0 %shard_map.62 = (bf16[512,1024]{1,0:T(8,128)(2,1)S(1)}, bf16[512,2,512]{2,1,0:T(2,128)(2,1)S(1)}) custom-call(s32[4]{0:T(128)S(1)} %pad_add_fusion.refs_0_, bf16[2,512,512]{2,1,0:T(8,128)(2,1)S(1)} %copy-done.4, bf16[512,1024]{1,0:T(8,128)(2,1)S(1)} %get-tuple-element.46.refs_1_.refs_2_.refs_3_, ...), custom_call_target="tpu_custom_call" | custom-call | flops 110000000 | tf_op jit(solution)/shard_map/pallas_call | solution.py:37
  124.3 3.3 %shard_map.63 = (bf16[512,1024]{1,0:T(8,128)(2,1)S(1)}, bf16[512,512]{1,0:T(8,128)(2,1)S(1)}, bf16[512,2,512]{2,1,0:T(2,128)(2,1)S(1)}) custom-call(s32[4]{0:T(128)S(1)} %pad_add_fusion.refs_0_, bf16[2,512,512]{2,1,0:T(8,128)(2,1)S(1)} %copy-done.4, bf16[2,512,512]{2,1,0:T(8,128)(2,1)S(1)} %copy-done, ...), custom_call_target="tpu_custom_call" | custom-call | flops 3849999872 | tf_op jit(solution)/shard_map/pallas_call | solution.py:37
  128.5 4.6 %collective-permute-start.24 = (bf16[512,512]{1,0:T(8,128)(2,1)S(1)}, bf16[512,512]{1,0:T(8,128)(2,1)S(1)}, u32[]{:S(2)}, u32[]{:S(2)}) collective-permute-start(bf16[512,512]{1,0:T(8,128)(2,1)S(1)} %shard_map.64.refs_19_.refs_14_.refs_13_.refs_12_), channel_id=1, source_target_pairs={{0,2},{1,3},{2,4},{3,5},{4,6},{5,7},{8,10},{9,11},{10,12},{11,13},... | collective-permute-start | bytes 1572872 | tf_op jit(solution)/shard_map/ppermute | solution.py:422
  133.1 1.7 collective-permute-start.27
  134.8 2.8 %shard_map.65 = (bf16[2560,2,512]{2,1,0:T(2,128)(2,1)}, f32[8,128]{1,0:T(8,128)S(1)}) custom-call(s32[4]{0:T(128)S(1)} %pad_add_fusion.refs_0_, s32[2,512]{1,0:T(2,128)S(1)} %get-tuple-element.36.refs_2_.refs_1_, bf16[2,512,512]{2,1,0:T(8,128)(2,1)S(1)} %shard_map.59.refs_2_, bf16[2,512,512]{2,1,0:T(8,128)(2,1)S(1)} %collective-permute-done.17.refs_3_, ...), custom_call_target="tpu_custom_call" | custom-call | flops 5500000256 | tf_op jit(solution)/shard_map/pallas_call | solution.py:37
  137.6 5.9 %collective-permute-done.24.refs_1_ = bf16[512,512]{1,0:T(8,128)(2,1)S(1)} collective-permute-done((bf16[512,512]{1,0:T(8,128)(2,1)S(1)}, bf16[512,512]{1,0:T(8,128)(2,1)S(1)}, u32[]{:S(2)}, u32[]{:S(2)}) %collective-permute-start.24) | collective-permute-done | bytes 524320 | tf_op jit(solution)/shard_map/ppermute | solution.py:422
  144.1 4.4 %collective-permute-start.26 = (bf16[256,512]{1,0:T(8,128)(2,1)S(1)}, bf16[256,512]{1,0:T(8,128)(2,1)S(1)}, u32[]{:S(2)}, u32[]{:S(2)}) collective-permute-start(bf16[256,512]{1,0:T(8,128)(2,1)S(1)} %shard_map.66.refs_20_.refs_14_.refs_13_), channel_id=1, source_target_pairs={{0,2},{1,3},{2,4},{3,5},{4,6},{5,7},{8,10},{9,11},{10,12},{11,13},... | collective-permute-start | bytes 786440 | tf_op jit(solution)/shard_map/ppermute | solution.py:422
  148.5 1.7 collective-permute-start.28
  150.2 6.2 %shard_map.67 = (bf16[2560,2,512]{2,1,0:T(2,128)(2,1)}, f32[8,128]{1,0:T(8,128)S(1)}) custom-call(s32[4]{0:T(128)S(1)} %pad_add_fusion.refs_0_, s32[2,512]{1,0:T(2,128)S(1)} %get-tuple-element.36.refs_2_.refs_1_, bf16[2,512,512]{2,1,0:T(8,128)(2,1)S(1)} %shard_map.59.refs_2_, ...), custom_call_target="tpu_custom_call", output_to_operand_aliasing={{0}: (19, {})} | custom-call | flops 5500000256 | tf_op jit(solution)/shard_map/pallas_call | solution.py:37
  157.4 6.4 %shard_map.69 = (bf16[2560,2,512]{2,1,0:T(2,128)(2,1)}, f32[8,128]{1,0:T(8,128)S(1)}) custom-call(s32[4]{0:T(128)S(1)} %pad_add_fusion.refs_0_, s32[2,512]{1,0:T(2,128)S(1)} %get-tuple-element.36.refs_2_.refs_1_, bf16[2,512,512]{2,1,0:T(8,128)(2,1)S(1)} %shard_map.59.refs_2_, ...), custom_call_target="tpu_custom_call", output_to_operand_aliasing={{0}: (19, {})} | custom-call | flops 5500000256 | tf_op jit(solution)/shard_map/pallas_call | solution.py:37
  163.9 6.2 %shard_map.70 = (bf16[2560,2,512]{2,1,0:T(2,128)(2,1)}, f32[8,128]{1,0:T(8,128)S(1)}) custom-call(s32[4]{0:T(128)S(1)} %pad_add_fusion.refs_0_, s32[2,512]{1,0:T(2,128)S(1)} %get-tuple-element.36.refs_2_.refs_1_, bf16[2,512,512]{2,1,0:T(8,128)(2,1)S(1)} %shard_map.59.refs_2_, ...), custom_call_target="tpu_custom_call", output_to_operand_aliasing={{0}: (19, {})} | custom-call | flops 5500000256 | tf_op jit(solution)/shard_map/pallas_call | solution.py:37
  170.1 4.1 %shard_map.71 = (bf16[2560,2,512]{2,1,0:T(2,128)(2,1)}, f32[8,128]{1,0:T(8,128)S(1)}) custom-call(s32[4]{0:T(128)S(1)} %pad_add_fusion.refs_0_, s32[2,512]{1,0:T(2,128)S(1)} %get-tuple-element.36.refs_2_.refs_1_, bf16[2,512,512]{2,1,0:T(8,128)(2,1)S(1)} %shard_map.59.refs_2_, ...), custom_call_target="tpu_custom_call", output_to_operand_aliasing={{0}: (19, {})} | custom-call | flops 5500000256 | tf_op jit(solution)/shard_map/pallas_call | solution.py:37
  174.2 4.6 %shard_map.72 = (bf16[2560,2,512]{2,1,0:T(2,128)(2,1)}, f32[8,128]{1,0:T(8,128)}) custom-call(s32[4]{0:T(128)S(1)} %pad_add_fusion.refs_0_, s32[2,512]{1,0:T(2,128)S(1)} %get-tuple-element.36.refs_2_.refs_1_, bf16[2,512,512]{2,1,0:T(8,128)(2,1)S(1)} %shard_map.59.refs_2_, ...), custom_call_target="tpu_custom_call", output_to_operand_aliasing={{0}: (19, {})} | custom-call | flops 5500000256 | tf_op jit(solution)/shard_map/pallas_call | solution.py:37
  (53 shorter events, 8.0 us)
Async XLA Ops:
  0.0 8.8 %copy-start.5 = (s32[2,512]{1,0:T(2,128)S(1)}, s32[2,512]{1,0:T(2,128)}, u32[]{:S(2)}) copy-start(s32[2,512]{1,0:T(2,128)} %refs_1_.3) | copy-start | bytes 12292
  2.2 18.0 %collective-permute-start = (bf16[512,512]{1,0:T(8,128)(2,1)}, bf16[512,512]{1,0:T(8,128)(2,1)S(1)}, u32[]{:S(2)}, u32[]{:S(2)}) collective-permute-start(bf16[512,512]{1,0:T(8,128)(2,1)} %shard_map.46.refs_4_.refs_1_.refs_11_), channel_id=1, source_target_pairs={{0,2},{1,3},{2,4},{3,5},{4,6},{5,7},{8,10},{9,11},{10,12},{11,13},... | collective-permute-start | bytes 1572872 | tf_op jit(solution)/shard_map/ppermute | solution.py:422
  7.1 21.8 %collective-permute-start.3 = (bf16[512,512]{1,0:T(8,128)(2,1)}, bf16[512,512]{1,0:T(8,128)(2,1)}, u32[]{:S(2)}, u32[]{:S(2)}) collective-permute-start(bf16[512,512]{1,0:T(8,128)(2,1)} %shard_map.46.refs_4_.refs_1_.refs_11_), channel_id=1, source_target_pairs={{0,1},{1,0},{2,3},{3,2},{4,5},{5,4},{6,7},{7,6},{8,9},{9,8},{10,11... | collective-permute-start | bytes 1572872 | tf_op jit(solution)/shard_map/ppermute | solution.py:416
  9.0 2.5 %copy-start.1 = (bf16[5,512,2,512]{3,2,1,0:T(2,128)(2,1)S(1)}, bf16[5,512,2,512]{3,2,1,0:T(2,128)(2,1)}, u32[]{:S(2)}) copy-start(bf16[5,512,2,512]{3,2,1,0:T(2,128)(2,1)} %param.4) | copy-start | bytes 15728644
  11.5 1.0 copy-start.2
  20.1 5.0 %collective-permute-start.2 = (bf16[512,2,512]{2,1,0:T(2,128)(2,1)S(1)}, bf16[512,2,512]{2,1,0:T(2,128)(2,1)S(1)}, u32[]{:S(2)}, u32[]{:S(2)}) collective-permute-start(bf16[512,2,512]{2,1,0:T(2,128)(2,1)S(1)} %get-tuple-element.42), channel_id=1, source_target_pairs={{0,8},{8,0},{16,24},{24,16},{1,9},{9,1},{17,25},{25,17},{2,10},{10... | collective-permute-start | bytes 3145736 | tf_op jit(solution)/shard_map/ppermute | solution.py:413
  20.7 15.3 %collective-permute-start.1 = (bf16[512,512]{1,0:T(8,128)(2,1)S(1)}, bf16[512,512]{1,0:T(8,128)(2,1)S(1)}, u32[]{:S(2)}, u32[]{:S(2)}) collective-permute-start(bf16[512,512]{1,0:T(8,128)(2,1)S(1)} %shard_map.48.refs_4_.refs_2_.refs_12_.refs_11_), channel_id=1, source_target_pairs={{0,2},{1,3},{2,4},{3,5},{4,6},{5,7},{8,10},{9,11},{10,12},{11,13},... | collective-permute-start | bytes 1572872 | tf_op jit(solution)/shard_map/ppermute | solution.py:422
  24.2 16.8 %collective-permute-start.5 = (bf16[512,512]{1,0:T(8,128)(2,1)S(1)}, bf16[512,512]{1,0:T(8,128)(2,1)S(1)}, u32[]{:S(2)}, u32[]{:S(2)}) collective-permute-start(bf16[512,512]{1,0:T(8,128)(2,1)S(1)} %shard_map.48.refs_4_.refs_2_.refs_12_.refs_11_), channel_id=1, source_target_pairs={{0,1},{1,0},{2,3},{3,2},{4,5},{5,4},{6,7},{7,6},{8,9},{9,8},{10,11... | collective-permute-start | bytes 1572872 | tf_op jit(solution)/shard_map/ppermute | solution.py:416
  27.4 25.3 %collective-permute-start.8 = (bf16[512,2,512]{2,1,0:T(2,128)(2,1)S(1)}, bf16[512,2,512]{2,1,0:T(2,128)(2,1)S(1)}, u32[]{:S(2)}, u32[]{:S(2)}) collective-permute-start(bf16[512,2,512]{2,1,0:T(2,128)(2,1)S(1)} %shard_map.49.refs_3_.refs_2_), channel_id=1, source_target_pairs={{0,16},{8,24},{16,0},{24,8},{1,17},{9,25},{17,1},{25,9},{2,18},{10... | collective-permute-start | bytes 3145736 | tf_op jit(solution)/shard_map/ppermute | solution.py:419
  36.6 15.4 %collective-permute-start.4 = (bf16[512,512]{1,0:T(8,128)(2,1)S(1)}, bf16[512,512]{1,0:T(8,128)(2,1)S(1)}, u32[]{:S(2)}, u32[]{:S(2)}) collective-permute-start(bf16[512,512]{1,0:T(8,128)(2,1)S(1)} %shard_map.50.refs_3_.refs_13_.refs_12_.refs_11_), channel_id=1, source_target_pairs={{0,2},{1,3},{2,4},{3,5},{4,6},{5,7},{8,10},{9,11},{10,12},{11,13},... | collective-permute-start | bytes 1572872 | tf_op jit(solution)/shard_map/ppermute | solution.py:422
  54.2 28.4 %collective-permute-start.11 = (bf16[512,1024]{1,0:T(8,128)(2,1)S(1)}, bf16[512,1024]{1,0:T(8,128)(2,1)S(1)}, u32[]{:S(2)}, u32[]{:S(2)}) collective-permute-start(bf16[512,1024]{1,0:T(8,128)(2,1)S(1)} %get-tuple-element.46.refs_1_.refs_2_.refs_3_), channel_id=1, source_target_pairs={{0,8},{8,0},{16,24},{24,16},{1,9},{9,1},{17,25},{25,17},{2,10},{10... | collective-permute-start | bytes 3145736 | tf_op jit(solution)/shard_map/ppermute | solution.py:413
  54.3 14.8 %collective-permute-start.6 = (bf16[512,512]{1,0:T(8,128)(2,1)S(1)}, bf16[512,512]{1,0:T(8,128)(2,1)S(1)}, u32[]{:S(2)}, u32[]{:S(2)}) collective-permute-start(bf16[512,512]{1,0:T(8,128)(2,1)S(1)} %shard_map.50.refs_3_.refs_13_.refs_12_.refs_11_), channel_id=1, source_target_pairs={{0,1},{1,0},{2,3},{3,2},{4,5},{5,4},{6,7},{7,6},{8,9},{9,8},{10,11... | collective-permute-start | bytes 1572872 | tf_op jit(solution)/shard_map/ppermute | solution.py:416
  55.4 24.5 %collective-permute-start.7 = (bf16[512,512]{1,0:T(8,128)(2,1)S(1)}, bf16[512,512]{1,0:T(8,128)(2,1)S(1)}, u32[]{:S(2)}, u32[]{:S(2)}) collective-permute-start(bf16[512,512]{1,0:T(8,128)(2,1)S(1)} %shard_map.51.refs_4_.refs_14_.refs_13_.refs_12_.refs_11_), channel_id=1, source_target_pairs={{0,1},{1,0},{2,3},{3,2},{4,5},{5,4},{6,7},{7,6},{8,9},{9,8},{10,11... | collective-permute-start | bytes 1572872 | tf_op jit(solution)/shard_map/ppermute | solution.py:416
  56.4 34.2 %collective-permute-start.10 = (bf16[512,512]{1,0:T(8,128)(2,1)S(1)}, bf16[512,512]{1,0:T(8,128)(2,1)S(1)}, u32[]{:S(2)}, u32[]{:S(2)}) collective-permute-start(bf16[512,512]{1,0:T(8,128)(2,1)S(1)} %shard_map.51.refs_4_.refs_14_.refs_13_.refs_12_.refs_11_), channel_id=1, source_target_pairs={{0,2},{1,3},{2,4},{3,5},{4,6},{5,7},{8,10},{9,11},{10,12},{11,13},... | collective-permute-start | bytes 1572872 | tf_op jit(solution)/shard_map/ppermute | solution.py:422
  81.1 26.5 %collective-permute-start.9 = (bf16[2,512,512]{2,1,0:T(8,128)(2,1)S(1)}, bf16[2,512,512]{2,1,0:T(8,128)(2,1)S(1)}, u32[]{:S(2)}, u32[]{:S(2)}) collective-permute-start(bf16[2,512,512]{2,1,0:T(8,128)(2,1)S(1)} %shard_map.53.refs_3_.refs_1_), channel_id=1, source_target_pairs={{0,16},{8,24},{16,0},{24,8},{1,17},{9,25},{17,1},{25,9},{2,18},{10... | collective-permute-start | bytes 3145736 | tf_op jit(solution)/shard_map/ppermute | solution.py:419
  83.2 9.3 %collective-permute-start.13 = (bf16[128,512]{1,0:T(8,128)(2,1)S(1)}, bf16[128,512]{1,0:T(8,128)(2,1)S(1)}, u32[]{:S(2)}, u32[]{:S(2)}) collective-permute-start(bf16[128,512]{1,0:T(8,128)(2,1)S(1)} %shard_map.54.refs_3_.refs_1_), channel_id=1, source_target_pairs={{0,2},{1,3},{8,10},{9,11},{16,18},{17,19},{24,26},{25,27}} | collective-permute-start | bytes 393224 | tf_op jit(solution)/shard_map/ppermute | solution.py:504
  87.6 6.6 %collective-permute-start.14 = (bf16[128,512]{1,0:T(8,128)(2,1)S(1)}, bf16[128,512]{1,0:T(8,128)(2,1)S(1)}, u32[]{:S(2)}, u32[]{:S(2)}) collective-permute-start(bf16[128,512]{1,0:T(8,128)(2,1)S(1)} %shard_map.54.refs_3_.refs_1_), channel_id=1, source_target_pairs={{0,4},{1,5},{8,12},{9,13},{16,20},{17,21},{24,28},{25,29}} | collective-permute-start | bytes 393224 | tf_op jit(solution)/shard_map/ppermute | solution.py:504
  89.3 7.7 %collective-permute-start.15 = (bf16[128,512]{1,0:T(8,128)(2,1)S(1)}, bf16[128,512]{1,0:T(8,128)(2,1)S(1)}, u32[]{:S(2)}, u32[]{:S(2)}) collective-permute-start(bf16[128,512]{1,0:T(8,128)(2,1)S(1)} %shard_map.54.refs_3_.refs_1_), channel_id=1, source_target_pairs={{0,6},{1,7},{8,14},{9,15},{16,22},{17,23},{24,30},{25,31}} | collective-permute-start | bytes 393224 | tf_op jit(solution)/shard_map/ppermute | solution.py:504
  91.2 15.8 %collective-permute-start.12 = (bf16[512,512]{1,0:T(8,128)(2,1)S(1)}, bf16[512,512]{1,0:T(8,128)(2,1)S(1)}, u32[]{:S(2)}, u32[]{:S(2)}) collective-permute-start(bf16[512,512]{1,0:T(8,128)(2,1)S(1)} %shard_map.55.refs_5_.refs_14_.refs_13_.refs_12_.refs_11_), channel_id=1, source_target_pairs={{0,2},{1,3},{2,4},{3,5},{4,6},{5,7},{8,10},{9,11},{10,12},{11,13},... | collective-permute-start | bytes 1572872 | tf_op jit(solution)/shard_map/ppermute | solution.py:422
  92.5 23.9 %collective-permute-start.19 = (bf16[512,2,512]{2,1,0:T(2,128)(2,1)S(1)}, bf16[512,2,512]{2,1,0:T(2,128)(2,1)S(1)}, u32[]{:S(2)}, u32[]{:S(2)}) collective-permute-start(bf16[512,2,512]{2,1,0:T(2,128)(2,1)S(1)} %get-tuple-element.49.refs_5_), channel_id=1, source_target_pairs={{0,8},{8,0},{16,24},{24,16},{1,9},{9,1},{17,25},{25,17},{2,10},{10... | collective-permute-start | bytes 3145736 | tf_op jit(solution)/shard_map/ppermute | solution.py:413
  94.2 22.3 %collective-permute-start.18 = (bf16[512,2,512]{2,1,0:T(2,128)(2,1)S(1)}, bf16[512,2,512]{2,1,0:T(2,128)(2,1)S(1)}, u32[]{:S(2)}, u32[]{:S(2)}) collective-permute-start(bf16[512,2,512]{2,1,0:T(2,128)(2,1)S(1)} %get-tuple-element.44.refs_9_.refs_3_), channel_id=1, source_target_pairs={{0,8},{8,0},{16,24},{24,16},{1,9},{9,1},{17,25},{25,17},{2,10},{10... | collective-permute-start | bytes 3145736 | tf_op jit(solution)/shard_map/ppermute | solution.py:413
  97.6 5.0 %collective-permute-start.16 = (bf16[128,512]{1,0:T(8,128)(2,1)S(1)}, bf16[128,512]{1,0:T(8,128)(2,1)S(1)}, u32[]{:S(2)}, u32[]{:S(2)}) collective-permute-start(bf16[128,512]{1,0:T(8,128)(2,1)S(1)} %shard_map.56.refs_0_.refs_2_), channel_id=1, source_target_pairs={{0,1},{1,0},{2,3},{3,2},{4,5},{5,4},{6,7},{7,6},{8,9},{9,8},{10,11... | collective-permute-start | bytes 393224 | tf_op jit(solution)/shard_map/ppermute | solution.py:416
  102.7 8.8 %collective-permute-start.20 = (bf16[2,128,512]{2,1,0:T(8,128)(2,1)S(1)}, bf16[2,128,512]{2,1,0:T(8,128)(2,1)S(1)}, u32[]{:S(2)}, u32[]{:S(2)}) collective-permute-start(bf16[2,128,512]{2,1,0:T(8,128)(2,1)S(1)} %shard_map.57.refs_3_.refs_0_), channel_id=1, source_target_pairs={{0,16},{8,24},{16,0},{24,8},{1,17},{9,25},{17,1},{25,9},{2,18},{10... | collective-permute-start | bytes 786440 | tf_op jit(solution)/shard_map/ppermute | solution.py:419
  111.5 12.8 %collective-permute-start.21 = (bf16[2,2,128,512]{3,2,1,0:T(8,128)(2,1)S(1)}, bf16[2,2,128,512]{3,2,1,0:T(8,128)(2,1)S(1)}, u32[]{:S(2)}, u32[]{:S(2)}) collective-permute-start(bf16[2,2,128,512]{3,2,1,0:T(8,128)(2,1)S(1)} %shard_map.60.refs_8_.refs_6_), channel_id=1, source_target_pairs={{0,8},{8,0},{16,24},{24,16},{1,9},{9,1},{17,25},{25,17},{2,10},{10... | collective-permute-start | bytes 1572872 | tf_op jit(solution)/shard_map/ppermute | solution.py:413
  111.6 16.1 %collective-permute-start.23 = (bf16[512,512]{1,0:T(8,128)(2,1)S(1)}, bf16[512,512]{1,0:T(8,128)(2,1)S(1)}, u32[]{:S(2)}, u32[]{:S(2)}) collective-permute-start(bf16[512,512]{1,0:T(8,128)(2,1)S(1)} %shard_map.55.refs_5_.refs_14_.refs_13_.refs_12_.refs_11_), channel_id=1, source_target_pairs={{0,1},{1,0},{2,3},{3,2},{4,5},{5,4},{6,7},{7,6},{8,9},{9,8},{10,11... | collective-permute-start | bytes 1572872 | tf_op jit(solution)/shard_map/ppermute | solution.py:416
  112.6 15.3 %collective-permute-start.22 = (bf16[512,512]{1,0:T(8,128)(2,1)S(1)}, bf16[512,512]{1,0:T(8,128)(2,1)S(1)}, u32[]{:S(2)}, u32[]{:S(2)}) collective-permute-start(bf16[512,512]{1,0:T(8,128)(2,1)S(1)} %shard_map.58.refs_3_.refs_14_.refs_13_.refs_12_.refs_11_), channel_id=1, source_target_pairs={{0,2},{1,3},{2,4},{3,5},{4,6},{5,7},{8,10},{9,11},{10,12},{11,13},... | collective-permute-start | bytes 1572872 | tf_op jit(solution)/shard_map/ppermute | solution.py:422
  116.4 18.4 %collective-permute-start.17 = (bf16[2,512,512]{2,1,0:T(8,128)(2,1)S(1)}, bf16[2,512,512]{2,1,0:T(8,128)(2,1)S(1)}, u32[]{:S(2)}, u32[]{:S(2)}) collective-permute-start(bf16[2,512,512]{2,1,0:T(8,128)(2,1)S(1)} %shard_map.59.refs_2_), channel_id=1, source_target_pairs={{0,8},{8,0},{16,24},{24,16},{1,9},{9,1},{17,25},{25,17},{2,10},{10... | collective-permute-start | bytes 3145736 | tf_op jit(solution)/shard_map/ppermute | solution.py:413
  116.5 21.1 %collective-permute-start.25 = (bf16[512,512]{1,0:T(8,128)(2,1)S(1)}, bf16[512,512]{1,0:T(8,128)(2,1)S(1)}, u32[]{:S(2)}, u32[]{:S(2)}) collective-permute-start(bf16[512,512]{1,0:T(8,128)(2,1)S(1)} %shard_map.58.refs_3_.refs_14_.refs_13_.refs_12_.refs_11_), channel_id=1, source_target_pairs={{0,1},{1,0},{2,3},{3,2},{4,5},{5,4},{6,7},{7,6},{8,9},{9,8},{10,11... | collective-permute-start | bytes 1572872 | tf_op jit(solution)/shard_map/ppermute | solution.py:416
  118.3 4.1 %copy-start.4 = (bf16[2,512,512]{2,1,0:T(8,128)(2,1)S(1)}, bf16[2,512,512]{2,1,0:T(8,128)(2,1)}, u32[]{:S(2)}) copy-start(bf16[2,512,512]{2,1,0:T(8,128)(2,1)} %refs_1_.5) | copy-start | bytes 3145732
  122.3 2.0 %copy-start = (bf16[2,512,512]{2,1,0:T(8,128)(2,1)S(1)}, bf16[2,512,512]{2,1,0:T(8,128)(2,1)}, u32[]{:S(2)}) copy-start(bf16[2,512,512]{2,1,0:T(8,128)(2,1)} %refs_4_.11) | copy-start | bytes 3145732
  127.9 6.9 %copy-start.3 = (bf16[512,512]{1,0:T(8,128)(2,1)S(1)}, bf16[512,512]{1,0:T(8,128)(2,1)}, u32[]{:S(2)}) copy-start(bf16[512,512]{1,0:T(8,128)(2,1)} %shard_map.46.refs_4_.refs_1_.refs_11_) | copy-start | bytes 1572868
  128.5 15.1 %collective-permute-start.24 = (bf16[512,512]{1,0:T(8,128)(2,1)S(1)}, bf16[512,512]{1,0:T(8,128)(2,1)S(1)}, u32[]{:S(2)}, u32[]{:S(2)}) collective-permute-start(bf16[512,512]{1,0:T(8,128)(2,1)S(1)} %shard_map.64.refs_19_.refs_14_.refs_13_.refs_12_), channel_id=1, source_target_pairs={{0,2},{1,3},{2,4},{3,5},{4,6},{5,7},{8,10},{9,11},{10,12},{11,13},... | collective-permute-start | bytes 1572872 | tf_op jit(solution)/shard_map/ppermute | solution.py:422
  133.1 23.3 %collective-permute-start.27 = (bf16[512,512]{1,0:T(8,128)(2,1)S(1)}, bf16[512,512]{1,0:T(8,128)(2,1)S(1)}, u32[]{:S(2)}, u32[]{:S(2)}) collective-permute-start(bf16[512,512]{1,0:T(8,128)(2,1)S(1)} %shard_map.64.refs_19_.refs_14_.refs_13_.refs_12_), channel_id=1, source_target_pairs={{0,1},{1,0},{2,3},{3,2},{4,5},{5,4},{6,7},{7,6},{8,9},{9,8},{10,11... | collective-permute-start | bytes 1572872 | tf_op jit(solution)/shard_map/ppermute | solution.py:416
  144.1 12.3 %collective-permute-start.26 = (bf16[256,512]{1,0:T(8,128)(2,1)S(1)}, bf16[256,512]{1,0:T(8,128)(2,1)S(1)}, u32[]{:S(2)}, u32[]{:S(2)}) collective-permute-start(bf16[256,512]{1,0:T(8,128)(2,1)S(1)} %shard_map.66.refs_20_.refs_14_.refs_13_), channel_id=1, source_target_pairs={{0,2},{1,3},{2,4},{3,5},{4,6},{5,7},{8,10},{9,11},{10,12},{11,13},... | collective-permute-start | bytes 786440 | tf_op jit(solution)/shard_map/ppermute | solution.py:422
  148.5 21.5 %collective-permute-start.28 = (bf16[256,512]{1,0:T(8,128)(2,1)S(1)}, bf16[256,512]{1,0:T(8,128)(2,1)S(1)}, u32[]{:S(2)}, u32[]{:S(2)}) collective-permute-start(bf16[256,512]{1,0:T(8,128)(2,1)S(1)} %shard_map.66.refs_20_.refs_14_.refs_13_), channel_id=1, source_target_pairs={{0,1},{1,0},{2,3},{3,2},{4,5},{5,4},{6,7},{7,6},{8,9},{9,8},{10,11... | collective-permute-start | bytes 786440 | tf_op jit(solution)/shard_map/ppermute | solution.py:416
  157.0 17.1 %collective-permute-start.29 = (bf16[256,512]{1,0:T(8,128)(2,1)S(1)}, bf16[256,512]{1,0:T(8,128)(2,1)S(1)}, u32[]{:S(2)}, u32[]{:S(2)}) collective-permute-start(bf16[256,512]{1,0:T(8,128)(2,1)S(1)} %shard_map.68.refs_20_.refs_14_), channel_id=1, source_target_pairs={{0,1},{1,0},{2,3},{3,2},{4,5},{5,4},{6,7},{7,6},{8,9},{9,8},{10,11... | collective-permute-start | bytes 786440 | tf_op jit(solution)/shard_map/ppermute | solution.py:416

commit v2 on v1

--- a/solution.py
+++ b/solution.py
@@ -170,37 +170,28 @@
 
 
 def relay_kernel(meta, came, *refs):
-    *own, held = refs
+    *own, sent = refs
     place = lax.div(meta[2], 2)
     for piece in own:
 
         @pl.when(place == 0)
         def _(piece=piece):
-            held[0 : piece.shape[0]] = piece[...]
+            sent[0 : piece.shape[0]] = piece[...]
 
     @pl.when(place != 0)
     def _():
-        count = min(came.shape[0], held.shape[0])
-        held[0:count] = came[0:count]
-
-
-def old_kernel(line, meta, *refs):
-    held, other, old = refs[:line], refs[line : 2 * line], refs[-1]
-    for h in range(line):
-
-        @pl.when(lax.div(meta[2], 2) == h)
+        count = min(came.shape[0], sent.shape[0])
+        sent[0:count] = came[0:count]
+
+
+def old_kernel(meta, *refs):
+    *choices, old = refs
+    for h in range(len(choices) // 2):
+
+        @pl.when(meta[0] // 2 == h)
         def _(h=h):
-            old[0] = held[h][0 : old.shape[1]]
-            old[1] = other[h][0 : old.shape[1]]
-
-
-def by_chip_kernel(meta, *refs):
-    out = refs[-1]
-    for h, choice in enumerate(refs[:-1]):
-
-        @pl.when(meta[0] // 2 == h)
-        def _(choice=choice):
-            out[...] = choice[...]
+            old[0] = choices[2 * h][...]
+            old[1] = choices[2 * h + 1][...]
 
 
 def by_place_kernel(meta, *refs):
@@ -209,13 +200,13 @@
 
         @pl.when(lax.div(meta[2], 2) == h)
         def _(choice=choice):
-            out[...] = choice[...]
+            out[...] = choice[0 : out.shape[0]]
 
 
 def head_kernel(meta, fresh, fresh_sibling, head):
     needed = 1 - lax.rem(meta[2], 2)
-    part, nb = head.shape
-    at = pl.ds(pl.multiple_of(meta[0] * part, part), part)
+    half, nb = head.shape
+    at = pl.ds(pl.multiple_of(meta[1] * half, half), half)
 
     @pl.when(meta[1] == needed)
     def _():
@@ -224,12 +215,6 @@
     @pl.when(meta[1] != needed)
     def _():
         head[...] = fresh_sibling[at, :nb]
-
-
-def stack_kernel(*refs):
-    *entries, out = refs
-    for i, entry in enumerate(entries):
-        out[i] = entry[...]
 
 
 def choose(hop, choices):
@@ -284,16 +269,15 @@
     top[...] = raw(shown, nb)
 
 
-def prep1_kernel(chips, meta, lower, upper, fresh, fresh_sibling, up0, *refs):
-    heads, heads_sibling, up1, up0_panel, top, work, head = refs
-    core, column, chip = meta[1], meta[2], meta[0] // 2
+def prep1_kernel(meta, lower, upper, fresh, fresh_sibling, up0, *refs):
+    mine, mine_sibling, other, other_sibling, up1, up0_panel, top, work, head = refs
+    core, column = meta[1], meta[2]
     side = lax.rem(column, 2)
-    nb, part = fresh.shape[0], heads.shape[2]
-    for who, parts in ((core, heads), (1 - core, heads_sibling)):
-        for h in range(chips):
-            at = pl.multiple_of((2 * lax.rem(chip + chips - h, chips) + who) * part, part)
-            head[1 - side, pl.ds(at, part)] = parts[h, 0]
-            head[side, pl.ds(at, part)] = parts[h, 1]
+    nb, half = fresh.shape[0], mine.shape[0]
+    for which, who, piece in (
+        (1 - side, core, mine), (1 - side, 1 - core, mine_sibling), (side, core, other), (side, 1 - core, other_sibling)
+    ):
+        head[which, pl.ds(pl.multiple_of(who * half, half), half)] = piece[...]
 
     @pl.when(core == 1)
     def _():
@@ -322,31 +306,28 @@
 
 
 def update_kernel(
-    begin, line, meta, goal, old, old_sibling, upper, up0, up1, up0_panel, tiles, top0, top1, *rest
+    begin, meta, goal, old, old_sibling, upper, up0, up1, up0_panel, tiles, top0, top1, *rest
 ):
-    held, other = rest[:line], rest[line : 2 * line]
+    held, other = rest[:2]
     out, token, panels, block, result, panel_sem, block_sem, out_sem = rest[-8:]
     row, core, column = meta[0], meta[1], meta[2]
-    side, place = lax.rem(column, 2), lax.div(column, 2)
+    side = lax.rem(column, 2)
     count, cb, nb = block.shape
     rows_of = pl.ds(begin, count)
 
-    def panel_copy(h, which):
-        source = (held, other)[which][h].at[pl.ds(0, count)]
-        return pltpu.make_async_copy(source, panels.at[lax.rem(side + which, 2)], panel_sem.at[which])
+    def panel_copy(which):
+        return pltpu.make_async_copy(
+            (held, other)[which], panels.at[lax.rem(side + which, 2)], panel_sem.at[which]
+        )
 
     load = pltpu.make_async_copy(tiles.at[rows_of], block, block_sem)
     load.start()
-    for h in range(line):
-
-        @pl.when(place == h)
-        def _(h=h):
-            panel_copy(h, 0).start()
-            panel_copy(h, 1).start()
+    panel_copy(0).start()
+    panel_copy(1).start()
 
     def arrived():
-        panel_copy(0, 0).wait()
-        panel_copy(0, 1).wait()
+        panel_copy(0).wait()
+        panel_copy(1).wait()
 
     def from_factors():
         here = begin + lax.broadcasted_iota(I32, (count, nb), 0)
@@ -418,8 +399,9 @@
     def to_chip(value, h):
         return lax.ppermute(value, "prow", [(r, (r + 2 * h) % row_devices) for r in range(row_devices)])
 
-    def to_next(value):
-        return lax.ppermute(value, "pcol", [(c, c + 2) for c in range(col_devices - 2)])
+    def along(value, begin):
+        pairs = [(p, (p + (1 if (p - begin) % 2 == 0 else -1)) % line) for p in range(line)]
+        return lax.ppermute(value, "pcol", [(2 * p + y, 2 * q + y) for p, q in pairs for y in range(2)])
 
     order = []
 
@@ -429,32 +411,64 @@
         order.append(results[-1])
         return results
 
-    last_step = pieces + line - 2
+    lag = 2
+    behind = lag * ((line - 2) // 2)
+    even_turns = pieces + behind
+    odd_turns = pieces + lag * ((line - 3) // 2) if line > 2 else 0
+    last_turn = pieces + behind
 
     def piece_out(i):
         return (bf16(sizes[i], nb), VMEM)
 
-    def step_out(k):
-        return (bf16(max(sizes[k - p] for p in range(line) if 0 <= k - p < pieces), nb), VMEM)
-
-    own, held, other = [], [], []
+    def even_out(k):
+        return (bf16(max(sizes[k - h] for h in range(0, behind + 1, lag) if 0 <= k - h < pieces), nb), VMEM)
+
+    own, even_came, odd_came, held, other = [], [], [], [], []
     state = {}
-
-    def step(k):
+    awaited = []
+
+    def wait(k, value):
+        awaited.append((k, value))
+        return value
+
+    def due(k):
+        values = [value for at, value in awaited if at <= k]
+        awaited[:] = [entry for entry in awaited if entry[0] > k]
+        return values
+
+    def turn(k):
+        state["turn"] = k
         if k == 0:
             own.extend(run(
                 first_kernel, [(tiles, ANY)], [piece_out(0)],
                 scratch=[pltpu.VMEM((sizes[0], cb, nb), BF16), DMA], mib=60,
             ))
-            value = own[0]
-        else:
-            also = (other[k - 2],) if k >= 2 else ()
-            operands = [(meta, SMEM), (state["came"], VMEM)] + [(v, VMEM) for v in own[k : k + 1]]
-            (value,) = run(relay_kernel, operands, [step_out(k)], also, us=0.2 if k in (3, 4, 5) else 12.0)
-        held.append(value)
-        if k < last_step:
-            state["came"] = to_next(value)
-        other.append(to_neighbour(value))
+        if k < even_turns:
+            if k == 0:
+                value = own[0]
+            else:
+                also = due(k)
+                operands = [(meta, SMEM)]
+                if k >= lag and odd_turns:
+                    operands += [(odd_came[k - lag], VMEM)] + [(v, VMEM) for v in own[k : k + 1]]
+                else:
+                    operands += [(own[k], VMEM), (own[k], VMEM)]
+                (value,) = run(relay_kernel, operands, [even_out(k)], also, us=0.2 if k in (2, 4, 5) else 12.0)
+            even_came.append(wait(k + 1, along(value, 0)))
+        if 0 < k <= odd_turns:
+            carried = [sizes[k - 1 - h] for h in range(0, behind, lag) if 0 <= k - 1 - h < pieces]
+            odd_came.append(wait(k + 1, along(even_came[k - 1][: max(carried)], 1)))
+        m = k - 1 - behind
+        if 0 <= m < pieces:
+            choices = [own[m]]
+            for p in range(1, line):
+                choices.append((odd_came, even_came)[p % 2][m + lag * ((p - 1) // 2)])
+            (value,) = run(
+                by_place_kernel, [(meta, SMEM)] + [(c, VMEM) for c in choices], [piece_out(m)],
+                due(k) if k >= even_turns else (), us=0.2 if k in (2, 4, 5) else 12.0 if k >= even_turns else 0.6,
+            )
+            held.append(value)
+            other.append(wait(k + 1, to_neighbour(value)))
 
     def gather():
         lanes = min(nb, 128)
@@ -472,7 +486,7 @@
         state["loaded"], send, *rest = results[pieces - 1 :]
         state.update(zip(("keep", "block0", "join", "arrive", "goal", "hops"), rest))
         state["sent"] = to_sibling(send)
-        state["block0_sibling"] = to_sibling(state["block0"])
+        state["block0_sibling"] = wait(state["turn"] + 2, to_sibling(state["block0"]))
 
     def join():
         (joined,) = run(
@@ -482,7 +496,7 @@
             scratch=[pltpu.VMEM((nb + 8, cb, nb), BF16)],
             us=2.0,
         )
-        state["choices"] = [joined] + [to_chip(joined, h) for h in range(1, chips)]
+        state["choices"] = [joined] + [wait(state["turn"] + 2, to_chip(joined, h)) for h in range(1, chips)]
 
     def fresh():
         new, brought = run(
@@ -491,45 +505,40 @@
             [(bf16(nb, cb * nb), VMEM), (bf16(nb, cb, nb), VMEM)],
             us=2.0, mib=16,
         )
-        state["fresh"] = (new, to_sibling(new))
-        state["brought"] = (brought, to_sibling(brought))
-
-    part = nb // row_devices
+        state["fresh"] = (new, wait(state["turn"] + 1, to_sibling(new)))
+        state["brought"] = (brought, wait(state["turn"] + 1, to_sibling(brought)))
 
     def head():
         (mine,) = run(
-            head_kernel, [(meta, SMEM)] + [(v, VMEM) for v in state["fresh"]], [(bf16(part, nb), VMEM)], us=0.1
+            head_kernel, [(meta, SMEM)] + [(v, VMEM) for v in state["fresh"]], [(bf16(nb // 2, nb), VMEM)], us=0.1
         )
         state["head"] = [mine] + [
-            lax.ppermute(mine, "pcol", [(0, 2 * h), (1, 2 * h + 1)]) for h in range(1, line)
+            wait(state["turn"] + 1, lax.ppermute(mine, "pcol", [(0, 2 * h), (1, 2 * h + 1)])) for h in range(1, line)
         ]
 
     def head_here():
         (mine,) = run(
-            by_place_kernel, [(meta, SMEM)] + [(v, VMEM) for v in state["head"]], [(bf16(part, nb), VMEM)]
-        )
-        state["head"] = (mine, to_neighbour(mine))
-
-    def head_pair():
-        (pair,) = run(stack_kernel, [(v, VMEM) for v in state["head"]], [(bf16(2, part, nb), VMEM)])
-        state["head"] = [pair] + [to_chip(pair, h) for h in range(1, chips)]
-
-    def head_all():
+            by_place_kernel, [(meta, SMEM)] + [(v, VMEM) for v in state["head"]], [(bf16(nb // 2, nb), VMEM)]
+        )
+        swapped = to_neighbour(mine)
+        state["heads"] = [mine, to_sibling(mine), swapped, to_sibling(swapped)]
+        wait(state["turn"] + 1, state["heads"][1])
+        wait(state["turn"] + 1, state["heads"][3])
+
+    def old_here():
+        first = [(held[0], other[0])]
+        first += zip(state["held_x"], state["other_x"])
         (mine,) = run(
-            stack_kernel, [(v, VMEM) for v in state["head"]], [(bf16(chips, 2, part, nb), VMEM)], us=0.1
-        )
-        state["heads"] = (mine, to_sibling(mine))
-
-    def old():
-        operands = [(meta, SMEM)] + [(v, VMEM) for v in held[:line] + other[:line]]
-        (mine,) = run(functools.partial(old_kernel, line), operands, [(bf16(2, nb, nb), VMEM)], us=0.6)
-        state["old"] = [mine] + [to_chip(mine, h) for h in range(1, chips)]
-
-    def old_here():
-        (mine,) = run(
-            by_chip_kernel, [(meta, SMEM)] + [(v, VMEM) for v in state["old"]], [(bf16(2, nb, nb), VMEM)]
-        )
-        state["old"] = (mine, to_sibling(mine))
+            old_kernel, [(meta, SMEM)] + [(v, VMEM) for pair in first for v in pair], [(bf16(2, nb, nb), VMEM)],
+            us=0.6,
+        )
+        state["old"] = (mine, wait(state["turn"] + 1, to_sibling(mine)))
+
+    def old_held():
+        state["held_x"] = [wait(state["turn"] + 3, to_chip(held[0], h)) for h in range(1, chips)]
+
+    def old_other():
+        state["other_x"] = [wait(state["turn"] + 2, to_chip(other[0], h)) for h in range(1, chips)]
 
     def scatter():
         sources = state["brought"] + (state["block0"], state["block0_sibling"], state["loaded"])
@@ -551,7 +560,7 @@
 
     def prep1():
         state["up1"], state["up0_panel"], state["top1"] = run(
-            functools.partial(prep1_kernel, chips),
+            prep1_kernel,
             [(meta, SMEM), (lower, VMEM), (upper, VMEM)] + [(v, VMEM) for v in state["fresh"]]
             + [(state["up0"], VMEM)] + [(v, VMEM) for v in state["heads"]],
             [(bf16(nb, cb * nb), VMEM), (bf16(nb, nb), VMEM), (bf16(nb, cb, nb), VMEM)],
@@ -563,14 +572,14 @@
         operands = [(meta, SMEM), (state["goal"], VMEM)] + [(v, VMEM) for v in state["old"]] + [(upper, VMEM)]
         operands += [(state[name], VMEM) for name in ("up0", "up1", "up0_panel")]
         operands += [(state[name], ANY) for name in ("moved", "top0", "top1")]
-        operands += [(v, ANY) for v in held[i : i + line] + other[i : i + line]]
+        operands += [(held[i], ANY), (other[i], ANY)]
         aliases = {}
         if "result" in state:
             aliases = {len(operands): 0}
             operands.append((state["result"], ANY))
         count = sizes[i]
         state["result"], _ = run(
-            functools.partial(update_kernel, begins[i], line),
+            functools.partial(update_kernel, begins[i]),
             operands,
             [(bf16(rows, cb, nb), ANY), (jax.ShapeDtypeStruct((8, 128), F32), VMEM)],
             scratch=[
@@ -581,12 +590,12 @@
             us=5.0, mib=24,
         )
 
-    plan = [(0, gather), (1, join), (3, fresh), (line - 1, old), (3, head), (4, head_here), (4, head_pair), (5, old_here), (5, head_all), (5, scatter), (5, prep0), (5, prep1)]
+    plan = [(0, gather), (1, join), (behind + 1, old_held), (3, fresh), (4, head), (behind + 2, old_other), (4, scatter), (5, head_here), (5, prep0), (6, old_here), (6, prep1)]
     for i in range(pieces):
-        plan.append((max(6 + i, i + line - 1), functools.partial(update, i)))
-    for k in range(last_step + 1):
-        step(k)
-        while plan and (plan[0][0] <= k or k == last_step):
+        plan.append((max(6 + i // 2, i + behind + 2), functools.partial(update, i)))
+    for k in range(last_turn + 1):
+        turn(k)
+        while plan and (plan[0][0] <= k or k == last_turn):
             plan.pop(0)[1]()
     return state["result"].reshape(matrix.shape)
 

time: 179 us -> 212 us (1.18); the launches traced: 179 us -> 209 us
  waiting for transfers between devices: 59.6 us -> 85.9 us
    ppermute x8 -> x14, waiting for transfers between devices: 28 us -> 64 us  [along(): lax.ppermute(value, 'pcol', [(2 * p + y, 2 * q + y) for p, q in pairs for...]
    ppermute x10 -> x7, waiting for transfers between devices: 23.9 us -> 5.79 us  [to_neighbour(): return lax.ppermute(value, 'pcol', [(c, c ^ 1) for c in range(col_devices)])]
    ppermute x3, waiting for transfers between devices: 4.42 us -> 15.8 us  [head(): lax.ppermute(mine, 'pcol', [(0, 2 * h), (1, 2 * h + 1)])]
    ppermute x8 -> x14, starting transfers between devices: 31.4 us -> 38 us  [along(): lax.ppermute(value, 'pcol', [(2 * p + y, 2 * q + y) for p, q in pairs for...]
    ppermute x10 -> x7, starting transfers between devices: 11.4 us -> 7.92 us  [to_neighbour(): return lax.ppermute(value, 'pcol', [(c, c ^ 1) for c in range(col_devices)])]
    ppermute x3, waiting for transfers between devices: 3.29 us -> 0.36 us  [to_chip(): lax.ppermute(value, 'prow', [(r, (r + 2 * h) % row_devices) for r in rang...]
    ppermute x3, starting transfers between devices: 7.37 us -> 4.53 us  [head(): lax.ppermute(mine, 'pcol', [(0, 2 * h), (1, 2 * h + 1)])]
    pallas_call x27 -> x29, Pallas kernels: 60.6 us -> 61.9 us  [call(): pl.pallas_call(ordered, out_shape=tuple((shape for shape, _ in outs)), in...]
  transfers between devices with their start and end apart: 30 -> 34, of which waited for: 11 -> 13; matrix products, arithmetic and copies ran while one was open for 0% -> 0% of each run, Pallas kernels for 29% -> 24%
where the time goes in v2:
time: 212 us; the launch traced here: 209 us
  waiting for transfers between devices  85.9 us (41%)
  Pallas kernels  61.9 us (29%)
  starting transfers between devices  56.3 us (27%)
  local copies, waits for them, and re-layouts  3.77 us (2%)
    ppermute x14, waiting for transfers between devices, along(): lax.ppermute(value, 'pcol', [(2 * p + y, 2 * q + y) for p, q in pairs for...  64 us
    pallas_call x29, Pallas kernels, call(): pl.pallas_call(ordered, out_shape=tuple((shape for shape, _ in outs)), in...  61.9 us
    ppermute x14, starting transfers between devices, along(): lax.ppermute(value, 'pcol', [(2 * p + y, 2 * q + y) for p, q in pairs for...  38 us
    ppermute x3, waiting for transfers between devices, head(): lax.ppermute(mine, 'pcol', [(0, 2 * h), (1, 2 * h + 1)])  15.8 us
    ppermute x7, starting transfers between devices, to_neighbour(): return lax.ppermute(value, 'pcol', [(c, c ^ 1) for c in range(col_devices)])  7.92 us
    ppermute x7, waiting for transfers between devices, to_neighbour(): return lax.ppermute(value, 'pcol', [(c, c ^ 1) for c in range(col_devices)])  5.79 us
    ppermute x3, starting transfers between devices, to_chip(): lax.ppermute(value, 'prow', [(r, (r + 2 * h) % row_devices) for r in rang...  4.54 us
    ppermute x3, starting transfers between devices, head(): lax.ppermute(mine, 'pcol', [(0, 2 * h), (1, 2 * h + 1)])  4.53 us
  transfers between devices with their start and end apart: 34, of which 13 were waited for; matrix products, arithmetic and copies ran while one was open for 0% of the time, Pallas kernels for 24%

profile of v2, /device:TPU:0, one launch (start us, length us, event | category | flops | bytes accessed | tf_op | source)
XLA Modules:
  0.0 208.6 jit_solution(17754374499662495011)
XLA Ops:
  0.0 2.2 %shard_map.46.refs_4_.refs_1_ = bf16[512,512]{1,0:T(8,128)(2,1)} custom-call(bf16[2560,2,512]{2,1,0:T(2,128)(2,1)} %bitcast.5), custom_call_target="tpu_custom_call" | custom-call | flops 1100000000 | tf_op jit(solution)/shard_map/pallas_call | solution.py:37
  2.2 3.1 %collective-permute-start = (bf16[512,512]{1,0:T(8,128)(2,1)}, bf16[512,512]{1,0:T(8,128)(2,1)S(1)}, u32[]{:S(2)}, u32[]{:S(2)}) collective-permute-start(bf16[512,512]{1,0:T(8,128)(2,1)} %shard_map.46.refs_4_.refs_1_), channel_id=1, source_target_pairs={{0,2},{1,3},{2,0},{3,1},{4,6},{5,7},{6,4},{7,5},{8,10},{9,11},{10,... | collective-permute-start | bytes 1572872 | tf_op jit(solution)/shard_map/ppermute | solution.py:404
  5.6 2.5 %copy-done = bf16[5,512,2,512]{3,2,1,0:T(2,128)(2,1)S(1)} copy-done((bf16[5,512,2,512]{3,2,1,0:T(2,128)(2,1)S(1)}, bf16[5,512,2,512]{3,2,1,0:T(2,128)(2,1)}, u32[]{:S(2)}) %copy-start) | copy-done | bytes 5242904
  8.0 1.0 copy-done.1
  9.1 7.5 %shard_map.47 = (bf16[512,512]{1,0:T(8,128)(2,1)S(1)}, bf16[512,512]{1,0:T(8,128)(2,1)S(1)}, bf16[512,512]{1,0:T(8,128)(2,1)S(1)}, bf16[256,512]{1,0:T(8,128)(2,...) custom-call(s32[4]{0:T(128)S(1)} %pad_add_fusion.refs_0_, ...), custom_call_target="tpu_custom_call" | custom-call | flops 8800000000 | tf_op jit(solution)/shard_map/pallas_call | solution.py:37
  18.0 1.8 collective-permute-start.4
  19.8 2.5 %collective-permute-start.1 = (bf16[512,512]{1,0:T(8,128)(2,1)S(1)}, bf16[512,512]{1,0:T(8,128)(2,1)S(1)}, u32[]{:S(2)}, u32[]{:S(2)}) collective-permute-start(bf16[512,512]{1,0:T(8,128)(2,1)S(1)} %collective-permute-done.refs_4_.refs_2_), channel_id=1, source_target_pairs={{0,6},{1,7},{2,4},{3,5},{4,2},{5,3},{6,0},{7,1},{8,14},{9,15},{10,... | collective-permute-start | bytes 1572872 | tf_op jit(solution)/shard_map/ppermute | solution.py:404
  22.3 2.3 %shard_map.49.refs_3_.refs_2_ = bf16[512,2,512]{2,1,0:T(2,128)(2,1)S(1)} custom-call(s32[4]{0:T(128)S(1)} %pad_add_fusion.refs_0_, s32[2,512]{1,0:T(2,128)S(1)} %get-tuple-element.38.refs_1_, bf16[512,2,512]{2,1,0:T(2,128)(2,1)S(1)} %get-tuple-element.39.refs_2_, bf16[512,2,512]{2,1,0:T(2,128)(2,1)S(1)} %collective-permute-done.2.refs_3_, ...), custom_call_target="tpu_custom_call" | custom-call | flops 2200000000 | tf_op jit(solution)/shard_map/pallas_call | solution.py:37
  24.5 1.6 collective-permute-start.7
  26.1 6.1 %collective-permute-done.4.refs_5_.refs_2_ = bf16[512,512]{1,0:T(8,128)(2,1)S(1)} collective-permute-done((bf16[512,512]{1,0:T(8,128)(2,1)S(1)}, bf16[512,512]{1,0:T(8,128)(2,1)S(1)}, u32[]{:S(2)}, u32[]{:S(2)}) %collective-permute-start.4) | collective-permute-done | bytes 524320 | tf_op jit(solution)/shard_map/ppermute | solution.py:404
  32.2 12.8 %collective-permute-done.1.refs_1_.refs_6_.refs_3_ = bf16[512,512]{1,0:T(8,128)(2,1)S(1)} collective-permute-done((bf16[512,512]{1,0:T(8,128)(2,1)S(1)}, bf16[512,512]{1,0:T(8,128)(2,1)S(1)}, u32[]{:S(2)}, u32[]{:S(2)}) %collective-permute-start.1) | collective-permute-done | bytes 524320 | tf_op jit(solution)/shard_map/ppermute | solution.py:404
  45.7 2.6 %collective-permute-start.6 = (bf16[512,512]{1,0:T(8,128)(2,1)S(1)}, bf16[512,512]{1,0:T(8,128)(2,1)S(1)}, u32[]{:S(2)}, u32[]{:S(2)}) collective-permute-start(bf16[512,512]{1,0:T(8,128)(2,1)S(1)} %collective-permute-done.4.refs_5_.refs_2_), channel_id=1, source_target_pairs={{0,6},{1,7},{2,4},{3,5},{4,2},{5,3},{6,0},{7,1},{8,14},{9,15},{10,... | collective-permute-start | bytes 1572872 | tf_op jit(solution)/shard_map/ppermute | solution.py:404
  48.3 21.3 %collective-permute-done.5.refs_5_.refs_4_.refs_2_ = bf16[512,512]{1,0:T(8,128)(2,1)S(1)} collective-permute-done((bf16[512,512]{1,0:T(8,128)(2,1)S(1)}, bf16[512,512]{1,0:T(8,128)(2,1)S(1)}, u32[]{:S(2)}, u32[]{:S(2)}) %collective-permute-start.5) | collective-permute-done | bytes 524320 | tf_op jit(solution)/shard_map/ppermute | solution.py:404
  70.7 1.6 shard_map.53
  72.9 1.7 collective-permute-start.11
  74.7 1.2 collective-permute-start.15
  75.8 1.5 collective-permute-start.8
  77.4 9.6 %collective-permute-done.11.refs_4_.refs_2_ = bf16[512,512]{1,0:T(8,128)(2,1)S(1)} collective-permute-done((bf16[512,512]{1,0:T(8,128)(2,1)S(1)}, bf16[512,512]{1,0:T(8,128)(2,1)S(1)}, u32[]{:S(2)}, u32[]{:S(2)}) %collective-permute-start.11) | collective-permute-done | bytes 524320 | tf_op jit(solution)/shard_map/ppermute | solution.py:404
  86.9 2.1 collective-permute-start.12
  89.0 10.9 %collective-permute-done.15.refs_1_.refs_5_.refs_3_ = bf16[512,512]{1,0:T(8,128)(2,1)S(1)} collective-permute-done((bf16[512,512]{1,0:T(8,128)(2,1)S(1)}, bf16[512,512]{1,0:T(8,128)(2,1)S(1)}, u32[]{:S(2)}, u32[]{:S(2)}) %collective-permute-start.15) | collective-permute-done | bytes 524320 | tf_op jit(solution)/shard_map/ppermute | solution.py:404
  101.1 1.6 collective-permute-start.17
  102.7 10.7 %collective-permute-start.16 = (bf16[512,512]{1,0:T(8,128)(2,1)S(1)}, bf16[512,512]{1,0:T(8,128)(2,1)S(1)}, u32[]{:S(2)}, u32[]{:S(2)}) collective-permute-start(bf16[512,512]{1,0:T(8,128)(2,1)S(1)} %shard_map.54.refs_5_), channel_id=1, source_target_pairs={{0,2},{1,3},{2,0},{3,1},{4,6},{5,7},{6,4},{7,5},{8,10},{9,11},{10,... | collective-permute-start | bytes 1572872 | tf_op jit(solution)/shard_map/ppermute | solution.py:404
  114.0 1.9 collective-permute-start.18
  115.9 1.3 collective-permute-start.19
  117.2 1.3 collective-permute-start.20
  118.5 12.6 %collective-permute-done.18.refs_7_.refs_2_ = bf16[256,512]{1,0:T(8,128)(2,1)S(1)} collective-permute-done((bf16[256,512]{1,0:T(8,128)(2,1)S(1)}, bf16[256,512]{1,0:T(8,128)(2,1)S(1)}, u32[]{:S(2)}, u32[]{:S(2)}) %collective-permute-start.18) | collective-permute-done | bytes 262176 | tf_op jit(solution)/shard_map/ppermute | solution.py:516
  131.1 1.5 collective-permute-start.9
  132.6 3.2 %collective-permute-done.19.refs_8_.refs_3_ = bf16[256,512]{1,0:T(8,128)(2,1)S(1)} collective-permute-done((bf16[256,512]{1,0:T(8,128)(2,1)S(1)}, bf16[256,512]{1,0:T(8,128)(2,1)S(1)}, u32[]{:S(2)}, u32[]{:S(2)}) %collective-permute-start.19) | collective-permute-done | bytes 262176 | tf_op jit(solution)/shard_map/ppermute | solution.py:516
  135.8 1.5 collective-permute-start.10
  137.3 4.1 %shard_map.57.refs_3_.refs_8_ = bf16[2568,2,512]{2,1,0:T(2,128)(2,1)S(1)} custom-call(s32[4]{0:T(128)S(1)} %pad_add_fusion.refs_0_, s32[2,512]{1,0:T(2,128)S(1)} %get-tuple-element.46.refs_1_, s32[2,512]{1,0:T(2,128)S(1)} %get-tuple-element.36.refs_2_.refs_1_, bf16[512,2,512]{2,1,0:T(2,128)(2,1)S(1)} %get-tuple-element.47.refs_3_, ...), custom_call_target="tpu_custom_call" | custom-call | flops 110000000 | tf_op jit(solution)/shard_map/pallas_call | solution.py:37
  143.9 1.6 collective-permute-start.25
  145.9 4.5 %collective-permute-start.22 = (bf16[256,512]{1,0:T(8,128)(2,1)S(1)}, bf16[256,512]{1,0:T(8,128)(2,1)S(1)}, u32[]{:S(2)}, u32[]{:S(2)}) collective-permute-start(bf16[256,512]{1,0:T(8,128)(2,1)S(1)} %slice.8), channel_id=1, source_target_pairs={{0,6},{1,7},{2,4},{3,5},{4,2},{5,3},{6,0},{7,1},{8,14},{9,15},{10,... | collective-permute-start | bytes 786440 | tf_op jit(solution)/shard_map/ppermute | solution.py:404
  150.4 4.3 %collective-permute-done.25.refs_8_ = bf16[256,512]{1,0:T(8,128)(2,1)S(1)} collective-permute-done((bf16[256,512]{1,0:T(8,128)(2,1)S(1)}, bf16[256,512]{1,0:T(8,128)(2,1)S(1)}, u32[]{:S(2)}, u32[]{:S(2)}) %collective-permute-start.25) | collective-permute-done | bytes 262176 | tf_op jit(solution)/shard_map/ppermute | solution.py:397
  154.7 2.0 shard_map.61
  156.7 3.0 %collective-permute-done.22.refs_1_.refs_6_.refs_3_ = bf16[256,512]{1,0:T(8,128)(2,1)S(1)} collective-permute-done((bf16[256,512]{1,0:T(8,128)(2,1)S(1)}, bf16[256,512]{1,0:T(8,128)(2,1)S(1)}, u32[]{:S(2)}, u32[]{:S(2)}) %collective-permute-start.22) | collective-permute-done | bytes 262176 | tf_op jit(solution)/shard_map/ppermute | solution.py:404
  161.7 2.4 %collective-permute-start.28 = (bf16[256,512]{1,0:T(8,128)(2,1)S(1)}, bf16[256,512]{1,0:T(8,128)(2,1)S(1)}, u32[]{:S(2)}, u32[]{:S(2)}) collective-permute-start(bf16[256,512]{1,0:T(8,128)(2,1)S(1)} %slice.9), channel_id=1, source_target_pairs={{0,6},{1,7},{2,4},{3,5},{4,2},{5,3},{6,0},{7,1},{8,14},{9,15},{10,... | collective-permute-start | bytes 786440 | tf_op jit(solution)/shard_map/ppermute | solution.py:404
  164.6 3.3 %collective-permute-start.29 = (bf16[256,512]{1,0:T(8,128)(2,1)S(1)}, bf16[256,512]{1,0:T(8,128)(2,1)S(1)}, u32[]{:S(2)}, u32[]{:S(2)}) collective-permute-start(bf16[256,512]{1,0:T(8,128)(2,1)S(1)} %shard_map.62.refs_5_), channel_id=1, source_target_pairs={{0,2},{1,3},{2,0},{3,1},{4,6},{5,7},{6,4},{7,5},{8,10},{9,11},{10,... | collective-permute-start | bytes 786440 | tf_op jit(solution)/shard_map/ppermute | solution.py:404
  167.9 3.4 %shard_map.65 = (bf16[512,1024]{1,0:T(8,128)(2,1)S(1)}, bf16[512,512]{1,0:T(8,128)(2,1)S(1)}, bf16[512,2,512]{2,1,0:T(2,128)(2,1)S(1)}) custom-call(s32[4]{0:T(128)S(1)} %pad_add_fusion.refs_0_, bf16[2,512,512]{2,1,0:T(8,128)(2,1)S(1)} %copy-done.2, bf16[2,512,512]{2,1,0:T(8,128)(2,1)S(1)} %copy-done.4, ...), custom_call_target="tpu_custom_call" | custom-call | flops 3849999872 | tf_op jit(solution)/shard_map/pallas_call | solution.py:37
  171.3 1.8 shard_map.66
  173.1 6.2 %shard_map.67 = (bf16[2560,2,512]{2,1,0:T(2,128)(2,1)}, f32[8,128]{1,0:T(8,128)S(1)}) custom-call(s32[4]{0:T(128)S(1)} %pad_add_fusion.refs_0_, s32[2,512]{1,0:T(2,128)S(1)} %get-tuple-element.36.refs_2_.refs_1_, bf16[2,512,512]{2,1,0:T(8,128)(2,1)S(1)} %shard_map.64.refs_10_.refs_2_, ...), custom_call_target="tpu_custom_call", output_to_operand_aliasing={{0}: (13, {})} | custom-call | flops 5500000256 | tf_op jit(solution)/shard_map/pallas_call | solution.py:37
  179.9 2.1 %collective-permute-start.31 = (bf16[256,512]{1,0:T(8,128)(2,1)S(1)}, bf16[256,512]{1,0:T(8,128)(2,1)S(1)}, u32[]{:S(2)}, u32[]{:S(2)}) collective-permute-start(bf16[256,512]{1,0:T(8,128)(2,1)S(1)} %shard_map.68.refs_5_), channel_id=1, source_target_pairs={{0,2},{1,3},{2,0},{3,1},{4,6},{5,7},{6,4},{7,5},{8,10},{9,11},{10,... | collective-permute-start | bytes 786440 | tf_op jit(solution)/shard_map/ppermute | solution.py:404
  183.4 6.2 %shard_map.70 = (bf16[2560,2,512]{2,1,0:T(2,128)(2,1)}, f32[8,128]{1,0:T(8,128)S(1)}) custom-call(s32[4]{0:T(128)S(1)} %pad_add_fusion.refs_0_, s32[2,512]{1,0:T(2,128)S(1)} %get-tuple-element.36.refs_2_.refs_1_, bf16[2,512,512]{2,1,0:T(8,128)(2,1)S(1)} %shard_map.64.refs_10_.refs_2_, ...), custom_call_target="tpu_custom_call", output_to_operand_aliasing={{0}: (13, {})} | custom-call | flops 5500000256 | tf_op jit(solution)/shard_map/pallas_call | solution.py:37
  189.6 6.2 %shard_map.71 = (bf16[2560,2,512]{2,1,0:T(2,128)(2,1)}, f32[8,128]{1,0:T(8,128)S(1)}) custom-call(s32[4]{0:T(128)S(1)} %pad_add_fusion.refs_0_, s32[2,512]{1,0:T(2,128)S(1)} %get-tuple-element.36.refs_2_.refs_1_, bf16[2,512,512]{2,1,0:T(8,128)(2,1)S(1)} %shard_map.64.refs_10_.refs_2_, ...), custom_call_target="tpu_custom_call", output_to_operand_aliasing={{0}: (13, {})} | custom-call | flops 5500000256 | tf_op jit(solution)/shard_map/pallas_call | solution.py:37
  195.8 0.9 shard_map.72.refs_14_.refs_11_
  196.6 1.6 collective-permute-start.33
  198.2 4.0 %shard_map.73 = (bf16[2560,2,512]{2,1,0:T(2,128)(2,1)}, f32[8,128]{1,0:T(8,128)S(1)}) custom-call(s32[4]{0:T(128)S(1)} %pad_add_fusion.refs_0_, s32[2,512]{1,0:T(2,128)S(1)} %get-tuple-element.36.refs_2_.refs_1_, bf16[2,512,512]{2,1,0:T(8,128)(2,1)S(1)} %shard_map.64.refs_10_.refs_2_, ...), custom_call_target="tpu_custom_call", output_to_operand_aliasing={{0}: (13, {})} | custom-call | flops 5500000256 | tf_op jit(solution)/shard_map/pallas_call | solution.py:37
  202.3 1.5 collective-permute-done.33.refs_12_
  203.8 4.6 %shard_map.74 = (bf16[2560,2,512]{2,1,0:T(2,128)(2,1)}, f32[8,128]{1,0:T(8,128)}) custom-call(s32[4]{0:T(128)S(1)} %pad_add_fusion.refs_0_, s32[2,512]{1,0:T(2,128)S(1)} %get-tuple-element.36.refs_2_.refs_1_, bf16[2,512,512]{2,1,0:T(8,128)(2,1)S(1)} %shard_map.64.refs_10_.refs_2_, ...), custom_call_target="tpu_custom_call", output_to_operand_aliasing={{0}: (13, {})} | custom-call | flops 5500000256 | tf_op jit(solution)/shard_map/pallas_call | solution.py:37
  (63 shorter events, 13.2 us)
Async XLA Ops:
  0.0 5.3 %copy-start.3 = (s32[2,512]{1,0:T(2,128)S(1)}, s32[2,512]{1,0:T(2,128)}, u32[]{:S(2)}) copy-start(s32[2,512]{1,0:T(2,128)} %refs_1_.3) | copy-start | bytes 12292
  2.2 15.2 %collective-permute-start = (bf16[512,512]{1,0:T(8,128)(2,1)}, bf16[512,512]{1,0:T(8,128)(2,1)S(1)}, u32[]{:S(2)}, u32[]{:S(2)}) collective-permute-start(bf16[512,512]{1,0:T(8,128)(2,1)} %shard_map.46.refs_4_.refs_1_), channel_id=1, source_target_pairs={{0,2},{1,3},{2,0},{3,1},{4,6},{5,7},{6,4},{7,5},{8,10},{9,11},{10,... | collective-permute-start | bytes 1572872 | tf_op jit(solution)/shard_map/ppermute | solution.py:404
  5.5 2.5 %copy-start = (bf16[5,512,2,512]{3,2,1,0:T(2,128)(2,1)S(1)}, bf16[5,512,2,512]{3,2,1,0:T(2,128)(2,1)}, u32[]{:S(2)}) copy-start(bf16[5,512,2,512]{3,2,1,0:T(2,128)(2,1)} %param.4) | copy-start | bytes 15728644
  8.0 1.0 copy-start.1
  16.6 5.7 %collective-permute-start.2 = (bf16[512,2,512]{2,1,0:T(2,128)(2,1)S(1)}, bf16[512,2,512]{2,1,0:T(2,128)(2,1)S(1)}, u32[]{:S(2)}, u32[]{:S(2)}) collective-permute-start(bf16[512,2,512]{2,1,0:T(2,128)(2,1)S(1)} %get-tuple-element.40), channel_id=1, source_target_pairs={{0,8},{8,0},{16,24},{24,16},{1,9},{9,1},{17,25},{25,17},{2,10},{10... | collective-permute-start | bytes 3145736 | tf_op jit(solution)/shard_map/ppermute | solution.py:394
  16.7 15.5 %collective-permute-start.3 = (bf16[512,2,512]{2,1,0:T(2,128)(2,1)S(1)}, bf16[512,2,512]{2,1,0:T(2,128)(2,1)S(1)}, u32[]{:S(2)}, u32[]{:S(2)}) collective-permute-start(bf16[512,2,512]{2,1,0:T(2,128)(2,1)S(1)} %get-tuple-element.43.refs_5_), channel_id=1, source_target_pairs={{0,8},{8,0},{16,24},{24,16},{1,9},{9,1},{17,25},{25,17},{2,10},{10... | collective-permute-start | bytes 3145736 | tf_op jit(solution)/shard_map/ppermute | solution.py:394
  18.0 14.2 %collective-permute-start.4 = (bf16[512,512]{1,0:T(8,128)(2,1)S(1)}, bf16[512,512]{1,0:T(8,128)(2,1)S(1)}, u32[]{:S(2)}, u32[]{:S(2)}) collective-permute-start(bf16[512,512]{1,0:T(8,128)(2,1)S(1)} %shard_map.48.refs_4_), channel_id=1, source_target_pairs={{0,2},{1,3},{2,0},{3,1},{4,6},{5,7},{6,4},{7,5},{8,10},{9,11},{10,... | collective-permute-start | bytes 1572872 | tf_op jit(solution)/shard_map/ppermute | solution.py:404
  19.8 25.2 %collective-permute-start.1 = (bf16[512,512]{1,0:T(8,128)(2,1)S(1)}, bf16[512,512]{1,0:T(8,128)(2,1)S(1)}, u32[]{:S(2)}, u32[]{:S(2)}) collective-permute-start(bf16[512,512]{1,0:T(8,128)(2,1)S(1)} %collective-permute-done.refs_4_.refs_2_), channel_id=1, source_target_pairs={{0,6},{1,7},{2,4},{3,5},{4,2},{5,3},{6,0},{7,1},{8,14},{9,15},{10,... | collective-permute-start | bytes 1572872 | tf_op jit(solution)/shard_map/ppermute | solution.py:404
  24.5 45.0 %collective-permute-start.7 = (bf16[512,2,512]{2,1,0:T(2,128)(2,1)S(1)}, bf16[512,2,512]{2,1,0:T(2,128)(2,1)S(1)}, u32[]{:S(2)}, u32[]{:S(2)}) collective-permute-start(bf16[512,2,512]{2,1,0:T(2,128)(2,1)S(1)} %shard_map.49.refs_3_.refs_2_), channel_id=1, source_target_pairs={{0,16},{8,24},{16,0},{24,8},{1,17},{9,25},{17,1},{25,9},{2,18},{10... | collective-permute-start | bytes 3145736 | tf_op jit(solution)/shard_map/ppermute | solution.py:400
  45.6 23.9 %collective-permute-start.5 = (bf16[512,512]{1,0:T(8,128)(2,1)S(1)}, bf16[512,512]{1,0:T(8,128)(2,1)S(1)}, u32[]{:S(2)}, u32[]{:S(2)}) collective-permute-start(bf16[512,512]{1,0:T(8,128)(2,1)S(1)} %shard_map.50.refs_3_), channel_id=1, source_target_pairs={{0,2},{1,3},{2,0},{3,1},{4,6},{5,7},{6,4},{7,5},{8,10},{9,11},{10,... | collective-permute-start | bytes 1572872 | tf_op jit(solution)/shard_map/ppermute | solution.py:404
  45.7 23.8 %collective-permute-start.6 = (bf16[512,512]{1,0:T(8,128)(2,1)S(1)}, bf16[512,512]{1,0:T(8,128)(2,1)S(1)}, u32[]{:S(2)}, u32[]{:S(2)}) collective-permute-start(bf16[512,512]{1,0:T(8,128)(2,1)S(1)} %collective-permute-done.4.refs_5_.refs_2_), channel_id=1, source_target_pairs={{0,6},{1,7},{2,4},{3,5},{4,2},{5,3},{6,0},{7,1},{8,14},{9,15},{10,... | collective-permute-start | bytes 1572872 | tf_op jit(solution)/shard_map/ppermute | solution.py:404
  72.3 27.6 %collective-permute-start.13 = (bf16[512,2,512]{2,1,0:T(2,128)(2,1)S(1)}, bf16[512,2,512]{2,1,0:T(2,128)(2,1)S(1)}, u32[]{:S(2)}, u32[]{:S(2)}) collective-permute-start(bf16[512,2,512]{2,1,0:T(2,128)(2,1)S(1)} %get-tuple-element.47.refs_3_), channel_id=1, source_target_pairs={{0,8},{8,0},{16,24},{24,16},{1,9},{9,1},{17,25},{25,17},{2,10},{10... | collective-permute-start | bytes 3145736 | tf_op jit(solution)/shard_map/ppermute | solution.py:394
  72.4 27.5 %collective-permute-start.14 = (bf16[512,1024]{1,0:T(8,128)(2,1)S(1)}, bf16[512,1024]{1,0:T(8,128)(2,1)S(1)}, u32[]{:S(2)}, u32[]{:S(2)}) collective-permute-start(bf16[512,1024]{1,0:T(8,128)(2,1)S(1)} %get-tuple-element.49.refs_1_.refs_2_.refs_3_), channel_id=1, source_target_pairs={{0,8},{8,0},{16,24},{24,16},{1,9},{9,1},{17,25},{25,17},{2,10},{10... | collective-permute-start | bytes 3145736 | tf_op jit(solution)/shard_map/ppermute | solution.py:394
  72.9 14.0 %collective-permute-start.11 = (bf16[512,512]{1,0:T(8,128)(2,1)S(1)}, bf16[512,512]{1,0:T(8,128)(2,1)S(1)}, u32[]{:S(2)}, u32[]{:S(2)}) collective-permute-start(bf16[512,512]{1,0:T(8,128)(2,1)S(1)} %shard_map.51.refs_5_), channel_id=1, source_target_pairs={{0,2},{1,3},{2,0},{3,1},{4,6},{5,7},{6,4},{7,5},{8,10},{9,11},{10,... | collective-permute-start | bytes 1572872 | tf_op jit(solution)/shard_map/ppermute | solution.py:404
  74.7 25.3 %collective-permute-start.15 = (bf16[512,512]{1,0:T(8,128)(2,1)S(1)}, bf16[512,512]{1,0:T(8,128)(2,1)S(1)}, u32[]{:S(2)}, u32[]{:S(2)}) collective-permute-start(bf16[512,512]{1,0:T(8,128)(2,1)S(1)} %collective-permute-done.5.refs_5_.refs_4_.refs_2_), channel_id=1, source_target_pairs={{0,6},{1,7},{2,4},{3,5},{4,2},{5,3},{6,0},{7,1},{8,14},{9,15},{10,... | collective-permute-start | bytes 1572872 | tf_op jit(solution)/shard_map/ppermute | solution.py:404
  75.8 24.1 %collective-permute-start.8 = (bf16[512,512]{1,0:T(8,128)(2,1)S(1)}, bf16[512,512]{1,0:T(8,128)(2,1)S(1)}, u32[]{:S(2)}, u32[]{:S(2)}) collective-permute-start(bf16[512,512]{1,0:T(8,128)(2,1)S(1)} %shard_map.52.refs_4_.refs_1_.refs_11_), channel_id=1, source_target_pairs={{0,1},{1,0},{2,3},{3,2},{4,5},{5,4},{6,7},{7,6},{8,9},{9,8},{10,11... | collective-permute-start | bytes 1572872 | tf_op jit(solution)/shard_map/ppermute | solution.py:397
  86.9 30.3 %collective-permute-start.12 = (bf16[512,512]{1,0:T(8,128)(2,1)S(1)}, bf16[512,512]{1,0:T(8,128)(2,1)S(1)}, u32[]{:S(2)}, u32[]{:S(2)}) collective-permute-start(bf16[512,512]{1,0:T(8,128)(2,1)S(1)} %collective-permute-done.11.refs_4_.refs_2_), channel_id=1, source_target_pairs={{0,6},{1,7},{2,4},{3,5},{4,2},{5,3},{6,0},{7,1},{8,14},{9,15},{10,... | collective-permute-start | bytes 1572872 | tf_op jit(solution)/shard_map/ppermute | solution.py:404
  101.1 40.3 %collective-permute-start.17 = (bf16[512,512]{1,0:T(8,128)(2,1)S(1)}, bf16[512,512]{1,0:T(8,128)(2,1)S(1)}, u32[]{:S(2)}, u32[]{:S(2)}) collective-permute-start(bf16[512,512]{1,0:T(8,128)(2,1)S(1)} %shard_map.55.refs_3_.refs_11_), channel_id=1, source_target_pairs={{0,1},{1,0},{2,3},{3,2},{4,5},{5,4},{6,7},{7,6},{8,9},{9,8},{10,11... | collective-permute-start | bytes 1572872 | tf_op jit(solution)/shard_map/ppermute | solution.py:397
  102.7 38.7 %collective-permute-start.16 = (bf16[512,512]{1,0:T(8,128)(2,1)S(1)}, bf16[512,512]{1,0:T(8,128)(2,1)S(1)}, u32[]{:S(2)}, u32[]{:S(2)}) collective-permute-start(bf16[512,512]{1,0:T(8,128)(2,1)S(1)} %shard_map.54.refs_5_), channel_id=1, source_target_pairs={{0,2},{1,3},{2,0},{3,1},{4,6},{5,7},{6,4},{7,5},{8,10},{9,11},{10,... | collective-permute-start | bytes 1572872 | tf_op jit(solution)/shard_map/ppermute | solution.py:404
  114.0 17.1 %collective-permute-start.18 = (bf16[256,512]{1,0:T(8,128)(2,1)S(1)}, bf16[256,512]{1,0:T(8,128)(2,1)S(1)}, u32[]{:S(2)}, u32[]{:S(2)}) collective-permute-start(bf16[256,512]{1,0:T(8,128)(2,1)S(1)} %shard_map.56.refs_8_.refs_1_), channel_id=1, source_target_pairs={{0,2},{1,3},{8,10},{9,11},{16,18},{17,19},{24,26},{25,27}} | collective-permute-start | bytes 786440 | tf_op jit(solution)/shard_map/ppermute | solution.py:516
  115.9 19.9 %collective-permute-start.19 = (bf16[256,512]{1,0:T(8,128)(2,1)S(1)}, bf16[256,512]{1,0:T(8,128)(2,1)S(1)}, u32[]{:S(2)}, u32[]{:S(2)}) collective-permute-start(bf16[256,512]{1,0:T(8,128)(2,1)S(1)} %shard_map.56.refs_8_.refs_1_), channel_id=1, source_target_pairs={{0,4},{1,5},{8,12},{9,13},{16,20},{17,21},{24,28},{25,29}} | collective-permute-start | bytes 786440 | tf_op jit(solution)/shard_map/ppermute | solution.py:516
  117.2 24.2 %collective-permute-start.20 = (bf16[256,512]{1,0:T(8,128)(2,1)S(1)}, bf16[256,512]{1,0:T(8,128)(2,1)S(1)}, u32[]{:S(2)}, u32[]{:S(2)}) collective-permute-start(bf16[256,512]{1,0:T(8,128)(2,1)S(1)} %shard_map.56.refs_8_.refs_1_), channel_id=1, source_target_pairs={{0,6},{1,7},{8,14},{9,15},{16,22},{17,23},{24,30},{25,31}} | collective-permute-start | bytes 786440 | tf_op jit(solution)/shard_map/ppermute | solution.py:516
  131.1 14.4 %collective-permute-start.9 = (bf16[512,512]{1,0:T(8,128)(2,1)S(1)}, bf16[512,512]{1,0:T(8,128)(2,1)S(1)}, u32[]{:S(2)}, u32[]{:S(2)}) collective-permute-start(bf16[512,512]{1,0:T(8,128)(2,1)S(1)} %shard_map.52.refs_4_.refs_1_.refs_11_), channel_id=1, source_target_pairs={{0,16},{8,24},{16,0},{24,8},{1,17},{9,25},{17,1},{25,9},{2,18},{10... | collective-permute-start | bytes 1572872 | tf_op jit(solution)/shard_map/ppermute | solution.py:400
  135.8 10.1 %collective-permute-start.10 = (bf16[512,512]{1,0:T(8,128)(2,1)S(1)}, bf16[512,512]{1,0:T(8,128)(2,1)S(1)}, u32[]{:S(2)}, u32[]{:S(2)}) collective-permute-start(bf16[512,512]{1,0:T(8,128)(2,1)S(1)} %collective-permute-done.8.refs_6_.refs_2_.refs_12_), channel_id=1, source_target_pairs={{0,16},{8,24},{16,0},{24,8},{1,17},{9,25},{17,1},{25,9},{2,18},{10... | collective-permute-start | bytes 1572872 | tf_op jit(solution)/shard_map/ppermute | solution.py:400
  142.0 12.8 %copy-start.2 = (bf16[2,512,512]{2,1,0:T(8,128)(2,1)S(1)}, bf16[2,512,512]{2,1,0:T(8,128)(2,1)}, u32[]{:S(2)}) copy-start(bf16[2,512,512]{2,1,0:T(8,128)(2,1)} %refs_1_.5) | copy-start | bytes 3145732
  142.0 17.8 %collective-permute-start.21 = (bf16[512,512]{1,0:T(8,128)(2,1)S(1)}, bf16[512,512]{1,0:T(8,128)(2,1)S(1)}, u32[]{:S(2)}, u32[]{:S(2)}) collective-permute-start(bf16[512,512]{1,0:T(8,128)(2,1)S(1)} %shard_map.58.refs_5_), channel_id=1, source_target_pairs={{0,2},{1,3},{2,0},{3,1},{4,6},{5,7},{6,4},{7,5},{8,10},{9,11},{10,... | collective-permute-start | bytes 1572872 | tf_op jit(solution)/shard_map/ppermute | solution.py:404
  142.7 17.1 %collective-permute-start.23 = (bf16[512,512]{1,0:T(8,128)(2,1)S(1)}, bf16[512,512]{1,0:T(8,128)(2,1)S(1)}, u32[]{:S(2)}, u32[]{:S(2)}) collective-permute-start(bf16[512,512]{1,0:T(8,128)(2,1)S(1)} %shard_map.59.refs_5_.refs_11_), channel_id=1, source_target_pairs={{0,1},{1,0},{2,3},{3,2},{4,5},{5,4},{6,7},{7,6},{8,9},{9,8},{10,11... | collective-permute-start | bytes 1572872 | tf_op jit(solution)/shard_map/ppermute | solution.py:397
  143.9 10.9 %collective-permute-start.25 = (bf16[256,512]{1,0:T(8,128)(2,1)S(1)}, bf16[256,512]{1,0:T(8,128)(2,1)S(1)}, u32[]{:S(2)}, u32[]{:S(2)}) collective-permute-start(bf16[256,512]{1,0:T(8,128)(2,1)S(1)} %shard_map.60.refs_4_.refs_6_), channel_id=1, source_target_pairs={{0,1},{1,0},{2,3},{3,2},{4,5},{5,4},{6,7},{7,6},{8,9},{9,8},{10,11... | collective-permute-start | bytes 786440 | tf_op jit(solution)/shard_map/ppermute | solution.py:397
  145.5 11.2 %collective-permute-start.24 = (bf16[256,512]{1,0:T(8,128)(2,1)S(1)}, bf16[256,512]{1,0:T(8,128)(2,1)S(1)}, u32[]{:S(2)}, u32[]{:S(2)}) collective-permute-start(bf16[256,512]{1,0:T(8,128)(2,1)S(1)} %shard_map.60.refs_4_.refs_6_), channel_id=1, source_target_pairs={{0,8},{8,0},{16,24},{24,16},{1,9},{9,1},{17,25},{25,17},{2,10},{10... | collective-permute-start | bytes 786440 | tf_op jit(solution)/shard_map/ppermute | solution.py:394
  145.9 13.9 %collective-permute-start.22 = (bf16[256,512]{1,0:T(8,128)(2,1)S(1)}, bf16[256,512]{1,0:T(8,128)(2,1)S(1)}, u32[]{:S(2)}, u32[]{:S(2)}) collective-permute-start(bf16[256,512]{1,0:T(8,128)(2,1)S(1)} %slice.8), channel_id=1, source_target_pairs={{0,6},{1,7},{2,4},{3,5},{4,2},{5,3},{6,0},{7,1},{8,14},{9,15},{10,... | collective-permute-start | bytes 786440 | tf_op jit(solution)/shard_map/ppermute | solution.py:404
  154.7 5.0 %collective-permute-start.26 = (bf16[256,512]{1,0:T(8,128)(2,1)S(1)}, bf16[256,512]{1,0:T(8,128)(2,1)S(1)}, u32[]{:S(2)}, u32[]{:S(2)}) collective-permute-start(bf16[256,512]{1,0:T(8,128)(2,1)S(1)} %collective-permute-done.25.refs_8_), channel_id=1, source_target_pairs={{0,8},{8,0},{16,24},{24,16},{1,9},{9,1},{17,25},{25,17},{2,10},{10... | collective-permute-start | bytes 786440 | tf_op jit(solution)/shard_map/ppermute | solution.py:394
  160.3 7.5 %copy-start.4 = (bf16[2,512,512]{2,1,0:T(8,128)(2,1)S(1)}, bf16[2,512,512]{2,1,0:T(8,128)(2,1)}, u32[]{:S(2)}) copy-start(bf16[2,512,512]{2,1,0:T(8,128)(2,1)} %refs_4_.11) | copy-start | bytes 3145732
  161.6 9.7 %collective-permute-start.27 = (bf16[2,512,512]{2,1,0:T(8,128)(2,1)S(1)}, bf16[2,512,512]{2,1,0:T(8,128)(2,1)S(1)}, u32[]{:S(2)}, u32[]{:S(2)}) collective-permute-start(bf16[2,512,512]{2,1,0:T(8,128)(2,1)S(1)} %shard_map.64.refs_10_.refs_2_), channel_id=1, source_target_pairs={{0,8},{8,0},{16,24},{24,16},{1,9},{9,1},{17,25},{25,17},{2,10},{10... | collective-permute-start | bytes 3145736 | tf_op jit(solution)/shard_map/ppermute | solution.py:394
  161.7 17.6 %collective-permute-start.28 = (bf16[256,512]{1,0:T(8,128)(2,1)S(1)}, bf16[256,512]{1,0:T(8,128)(2,1)S(1)}, u32[]{:S(2)}, u32[]{:S(2)}) collective-permute-start(bf16[256,512]{1,0:T(8,128)(2,1)S(1)} %slice.9), channel_id=1, source_target_pairs={{0,6},{1,7},{2,4},{3,5},{4,2},{5,3},{6,0},{7,1},{8,14},{9,15},{10,... | collective-permute-start | bytes 786440 | tf_op jit(solution)/shard_map/ppermute | solution.py:404
  164.1 15.2 %collective-permute-start.30 = (bf16[512,512]{1,0:T(8,128)(2,1)S(1)}, bf16[512,512]{1,0:T(8,128)(2,1)S(1)}, u32[]{:S(2)}, u32[]{:S(2)}) collective-permute-start(bf16[512,512]{1,0:T(8,128)(2,1)S(1)} %shard_map.63.refs_5_.refs_11_), channel_id=1, source_target_pairs={{0,1},{1,0},{2,3},{3,2},{4,5},{5,4},{6,7},{7,6},{8,9},{9,8},{10,11... | collective-permute-start | bytes 1572872 | tf_op jit(solution)/shard_map/ppermute | solution.py:397
  164.6 14.7 %collective-permute-start.29 = (bf16[256,512]{1,0:T(8,128)(2,1)S(1)}, bf16[256,512]{1,0:T(8,128)(2,1)S(1)}, u32[]{:S(2)}, u32[]{:S(2)}) collective-permute-start(bf16[256,512]{1,0:T(8,128)(2,1)S(1)} %shard_map.62.refs_5_), channel_id=1, source_target_pairs={{0,2},{1,3},{2,0},{3,1},{4,6},{5,7},{6,4},{7,5},{8,10},{9,11},{10,... | collective-permute-start | bytes 786440 | tf_op jit(solution)/shard_map/ppermute | solution.py:404
  179.9 15.9 %collective-permute-start.31 = (bf16[256,512]{1,0:T(8,128)(2,1)S(1)}, bf16[256,512]{1,0:T(8,128)(2,1)S(1)}, u32[]{:S(2)}, u32[]{:S(2)}) collective-permute-start(bf16[256,512]{1,0:T(8,128)(2,1)S(1)} %shard_map.68.refs_5_), channel_id=1, source_target_pairs={{0,2},{1,3},{2,0},{3,1},{4,6},{5,7},{6,4},{7,5},{8,10},{9,11},{10,... | collective-permute-start | bytes 786440 | tf_op jit(solution)/shard_map/ppermute | solution.py:404
  182.9 12.9 %collective-permute-start.32 = (bf16[256,512]{1,0:T(8,128)(2,1)S(1)}, bf16[256,512]{1,0:T(8,128)(2,1)S(1)}, u32[]{:S(2)}, u32[]{:S(2)}) collective-permute-start(bf16[256,512]{1,0:T(8,128)(2,1)S(1)} %shard_map.69.refs_14_.refs_11_), channel_id=1, source_target_pairs={{0,1},{1,0},{2,3},{3,2},{4,5},{5,4},{6,7},{7,6},{8,9},{9,8},{10,11... | collective-permute-start | bytes 786440 | tf_op jit(solution)/shard_map/ppermute | solution.py:397
  196.6 7.1 %collective-permute-start.33 = (bf16[256,512]{1,0:T(8,128)(2,1)S(1)}, bf16[256,512]{1,0:T(8,128)(2,1)S(1)}, u32[]{:S(2)}, u32[]{:S(2)}) collective-permute-start(bf16[256,512]{1,0:T(8,128)(2,1)S(1)} %shard_map.72.refs_14_.refs_11_), channel_id=1, source_target_pairs={{0,1},{1,0},{2,3},{3,2},{4,5},{5,4},{6,7},{7,6},{8,9},{9,8},{10,11... | collective-permute-start | bytes 786440 | tf_op jit(solution)/shard_map/ppermute | solution.py:397

commit v3 on v1

--- a/solution.py
+++ b/solution.py
@@ -99,7 +99,7 @@
         wanted = jnp.where(from_chip == chip, source, second)
         at = (slice(k, k + 1), slice(None))
         fetch[at] = local(wanted)
-        join[at] = jnp.where(holder(wanted) == row, slot, nb)
+        join[at] = jnp.where(holder(wanted) == row, lax.rem(slot, nb // 2), nb // 2)
         arrive[at] = placed(source)
         goal[at] = placed(target)
         hops[at] = lax.rem(chip + chips - from_chip, chips)
@@ -137,36 +137,42 @@
         end = begin + piece.shape[0]
         piece[...] = flat(loaded[begin:end])[:, :nb]
         begin = end
-    copy_rows(nb, send, lambda i: i, loaded, lambda i: fetch_table[1 - core, i])
-    copy_rows(nb, keep, lambda i: i, loaded, lambda i: fetch_table[core, i])
+    half, side = nb // 2, lax.rem(meta[2], 2)
+    for turn, b in enumerate((1 - side, side)):
+        to = lambda i, turn=turn: turn * half + i
+        copy_rows(half, send, to, loaded, lambda i, b=b: fetch_table[b, (1 - core) * half + i])
+        copy_rows(half, keep, to, loaded, lambda i, b=b: fetch_table[b, core * half + i])
     block0[...] = loaded[0:nb]
 
 
-def join_kernel(meta, join, keep, came, joined, work):
-    count = came.shape[0]
-    core = meta[1]
-    work[0:count] = came[...]
-    copy_rows(count, work, lambda i: join[core, i], keep, lambda i: i)
-    joined[...] = work[0:count]
-
-
-def scatter_kernel(meta, arrive, goal, came, came_sibling, old, old_sibling, tiles, out):
-    core, chip = meta[1], meta[0] // 2
-    count = old.shape[0]
+def join_kernel(meta, join, keep, came, joined0, joined1, work0, work1):
+    half = joined0.shape[0]
+    core, side = meta[1], lax.rem(meta[2], 2)
+    for turn, (b, work, joined) in enumerate(((1 - side, work0, joined0), (side, work1, joined1))):
+        work[0:half] = came[turn * half : (turn + 1) * half]
+        copy_rows(
+            half, work, lambda i, b=b: join[b, core * half + i], keep, lambda i, turn=turn: turn * half + i
+        )
+        joined[...] = work[0:half]
+
+
+def scatter_kernel(meta, arrive, goal, *refs):
+    *came, old, old_sibling, tiles, out = refs
+    core, side, chip = meta[1], lax.rem(meta[2], 2), meta[0] // 2
+    nb = old.shape[0]
+    half = nb // 2
     out[...] = tiles[...]
-
-    def scatter(table, values, k):
-        copy_rows(count, out, lambda i: table[k, i], values, lambda i: i)
 
     @pl.when(chip == 0)
     def _():
-        scatter(goal, old, core)
-        scatter(goal, old_sibling, 1 - core)
+        copy_rows(nb, out, lambda i: goal[core, i], old, lambda i: i)
+        copy_rows(nb, out, lambda i: goal[1 - core, i], old_sibling, lambda i: i)
 
     @pl.when(chip != 0)
     def _():
-        scatter(arrive, came, core)
-        scatter(arrive, came_sibling, 1 - core)
+        for turn, b in enumerate((1 - side, side)):
+            for values, who in ((came[2 * turn], core), (came[2 * turn + 1], 1 - core)):
+                copy_rows(half, out, lambda i, b=b, who=who: arrive[b, who * half + i], values, lambda i: i)
 
 
 def relay_kernel(meta, came, *refs):
@@ -185,51 +191,22 @@
 
 
 def old_kernel(line, meta, *refs):
-    held, other, old = refs[:line], refs[line : 2 * line], refs[-1]
+    *choices, old = refs
     for h in range(line):
 
         @pl.when(lax.div(meta[2], 2) == h)
         def _(h=h):
-            old[0] = held[h][0 : old.shape[1]]
-            old[1] = other[h][0 : old.shape[1]]
+            old[...] = choices[h][0 : old.shape[0]]
 
 
 def by_chip_kernel(meta, *refs):
-    out = refs[-1]
-    for h, choice in enumerate(refs[:-1]):
+    *choices, out = refs
+    for h in range(len(choices) // 2):
 
         @pl.when(meta[0] // 2 == h)
-        def _(choice=choice):
-            out[...] = choice[...]
-
-
-def by_place_kernel(meta, *refs):
-    out = refs[-1]
-    for h, choice in enumerate(refs[:-1]):
-
-        @pl.when(lax.div(meta[2], 2) == h)
-        def _(choice=choice):
-            out[...] = choice[...]
-
-
-def head_kernel(meta, fresh, fresh_sibling, head):
-    needed = 1 - lax.rem(meta[2], 2)
-    part, nb = head.shape
-    at = pl.ds(pl.multiple_of(meta[0] * part, part), part)
-
-    @pl.when(meta[1] == needed)
-    def _():
-        head[...] = fresh[at, :nb]
-
-    @pl.when(meta[1] != needed)
-    def _():
-        head[...] = fresh_sibling[at, :nb]
-
-
-def stack_kernel(*refs):
-    *entries, out = refs
-    for i, entry in enumerate(entries):
-        out[i] = entry[...]
+        def _(h=h):
+            out[0] = choices[2 * h][...]
+            out[1] = choices[2 * h + 1][...]
 
 
 def choose(hop, choices):
@@ -239,12 +216,17 @@
     return value.astype(BF16)
 
 
-def fresh_kernel(chips, meta, hops, *refs):
-    choices, (fresh, brought) = refs[:chips], refs[chips:]
-    nb = fresh.shape[0]
-    core, chip = meta[1], meta[0] // 2
-    hop = jnp.broadcast_to(hops[pl.ds(core, 1), :], (8, nb)).T[:, 0:1]
+def fresh_kernel(turn, chips, meta, hops, *refs):
+    choices, (fresh, brought, *head) = refs[:chips], refs[chips:]
+    half = fresh.shape[0]
+    core, side, chip = meta[1], lax.rem(meta[2], 2), meta[0] // 2
+    b = side if turn else 1 - side
+    hop = jnp.broadcast_to(hops[pl.ds(b, 1), :], (8, 2 * half)).T[:, 0:1]
+    hop = jnp.where(core == 0, hop[:half], hop[half:])
     fresh[...] = choose(hop, [c[...] for c in choices])
+    if head:
+        part, nb = head[0].shape
+        head[0][...] = fresh[pl.ds(pl.multiple_of(chip * part, part), part), :nb]
     if chips == 1:
         brought[...] = choices[0][...]
     for h in range(1, chips):
@@ -254,23 +236,27 @@
             brought[...] = choices[h][...]
 
 
+def assemble(meta, b, fresh, work):
+    core, side = meta[1], lax.rem(meta[2], 2)
+    half = work.shape[0] // 2
+    for turn, which in enumerate((1 - side, side)):
+
+        @pl.when(which == b)
+        def _(turn=turn):
+            work[pl.ds(pl.multiple_of(core * half, half), half)] = fresh[2 * turn][...]
+            work[pl.ds(pl.multiple_of((1 - core) * half, half), half)] = fresh[2 * turn + 1][...]
+
+
 def raw(columns, nb):
     joined = jnp.concatenate(columns, axis=1)
     return joined.reshape(joined.shape[0], len(columns), nb)
 
 
-def prep0_kernel(meta, lower, fresh, fresh_sibling, up0, top, work):
-    core, column = meta[1], meta[2]
-    nb = fresh.shape[0]
-
-    @pl.when(core == 0)
-    def _():
-        work[...] = fresh[...]
-
-    @pl.when(core != 0)
-    def _():
-        work[...] = fresh_sibling[...]
-
+def prep0_kernel(meta, lower, *refs):
+    *fresh, up0, top, work = refs
+    column = meta[2]
+    nb = work.shape[0]
+    assemble(meta, 0, fresh, work)
     shown = []
     for j in range(work.shape[1] // nb):
         cols = slice(j * nb, (j + 1) * nb)
@@ -284,25 +270,15 @@
     top[...] = raw(shown, nb)
 
 
-def prep1_kernel(chips, meta, lower, upper, fresh, fresh_sibling, up0, *refs):
-    heads, heads_sibling, up1, up0_panel, top, work, head = refs
-    core, column, chip = meta[1], meta[2], meta[0] // 2
-    side = lax.rem(column, 2)
-    nb, part = fresh.shape[0], heads.shape[2]
-    for who, parts in ((core, heads), (1 - core, heads_sibling)):
-        for h in range(chips):
-            at = pl.multiple_of((2 * lax.rem(chip + chips - h, chips) + who) * part, part)
-            head[1 - side, pl.ds(at, part)] = parts[h, 0]
-            head[side, pl.ds(at, part)] = parts[h, 1]
-
-    @pl.when(core == 1)
-    def _():
-        work[...] = fresh[...]
-
-    @pl.when(core != 1)
-    def _():
-        work[...] = fresh_sibling[...]
-
+def prep1_kernel(meta, lower, upper, up0, heads, *refs):
+    *fresh, up1, up0_panel, top, work, head = refs
+    column = meta[2]
+    row_devices, _, part, nb = heads.shape
+    for r in range(row_devices):
+        at = (r % 2 * (row_devices // 2) + r // 2) * part
+        head[1, at : at + part] = heads[r, 0]
+        head[0, at : at + part] = heads[r, 1]
+    assemble(meta, 1, fresh, work)
     up0_panel[...] = dot(lower[0], head[0]).astype(BF16)
     factor = dot(head[1], upper[0]).astype(BF16)
     in_panel, next_panel = column == 0, column == 1
@@ -448,9 +424,9 @@
             ))
             value = own[0]
         else:
-            also = (other[k - 2],) if k >= 2 else ()
+            also = [other[k - 1]] + state.pop('awaited', [])
             operands = [(meta, SMEM), (state["came"], VMEM)] + [(v, VMEM) for v in own[k : k + 1]]
-            (value,) = run(relay_kernel, operands, [step_out(k)], also, us=0.2 if k in (3, 4, 5) else 12.0)
+            (value,) = run(relay_kernel, operands, [step_out(k)], also, us=0.2 if k in (2, 3, 5) else 12.0)
         held.append(value)
         if k < last_step:
             state["came"] = to_next(value)
@@ -474,65 +450,49 @@
         state["sent"] = to_sibling(send)
         state["block0_sibling"] = to_sibling(state["block0"])
 
+    half = nb // 2
+    part = half // chips
+
     def join():
-        (joined,) = run(
+        joined = run(
             join_kernel,
             [(meta, SMEM), (state["join"], SMEM), (state["keep"], VMEM), (state["sent"], VMEM)],
-            [(bf16(nb, cb, nb), VMEM)],
-            scratch=[pltpu.VMEM((nb + 8, cb, nb), BF16)],
+            [(bf16(half, cb, nb), VMEM)] * 2,
+            scratch=[pltpu.VMEM((half + 8, cb, nb), BF16)] * 2,
             us=2.0,
         )
-        state["choices"] = [joined] + [to_chip(joined, h) for h in range(1, chips)]
-
-    def fresh():
-        new, brought = run(
-            functools.partial(fresh_kernel, chips),
-            [(meta, SMEM), (state["hops"], VMEM)] + [(c, VMEM) for c in state["choices"]],
-            [(bf16(nb, cb * nb), VMEM), (bf16(nb, cb, nb), VMEM)],
-            us=2.0, mib=16,
-        )
-        state["fresh"] = (new, to_sibling(new))
-        state["brought"] = (brought, to_sibling(brought))
-
-    part = nb // row_devices
-
-    def head():
+        state["choices"] = [[v] + [to_chip(v, h) for h in range(1, chips)] for v in joined]
+        state["fresh"], state["brought"] = [], []
+
+    def fresh(turn):
+        new, brought, *head = run(
+            functools.partial(fresh_kernel, turn, chips),
+            [(meta, SMEM), (state["hops"], VMEM)] + [(c, VMEM) for c in state["choices"][turn]],
+            [(bf16(half, cb * nb), VMEM), (bf16(half, cb, nb), VMEM)]
+            + [(bf16(part, nb), VMEM)] * (1 - turn),
+            us=1.5, mib=16,
+        )
+        state["fresh"] += [new, to_sibling(new)]
+        state["brought"] += [brought, to_sibling(brought)]
+        if head:
+            parts = lax.all_gather(head[0], "pcol")[:2]
+            state["heads"] = lax.all_gather(parts, "prow")
+
+    def old(values, name):
+        operands = [(meta, SMEM)] + [(v, VMEM) for v in values[:line]]
+        (mine,) = run(functools.partial(old_kernel, line), operands, [(bf16(nb, nb), VMEM)], us=0.1)
+        state[name] = [mine] + [to_chip(mine, h) for h in range(1, chips)]
+        state["awaited"] = state.get("awaited", []) + state[name][1:]
+
+    def old_here():
+        choices = [v for pair in zip(state["old_held"], state["old_other"]) for v in pair]
         (mine,) = run(
-            head_kernel, [(meta, SMEM)] + [(v, VMEM) for v in state["fresh"]], [(bf16(part, nb), VMEM)], us=0.1
-        )
-        state["head"] = [mine] + [
-            lax.ppermute(mine, "pcol", [(0, 2 * h), (1, 2 * h + 1)]) for h in range(1, line)
-        ]
-
-    def head_here():
-        (mine,) = run(
-            by_place_kernel, [(meta, SMEM)] + [(v, VMEM) for v in state["head"]], [(bf16(part, nb), VMEM)]
-        )
-        state["head"] = (mine, to_neighbour(mine))
-
-    def head_pair():
-        (pair,) = run(stack_kernel, [(v, VMEM) for v in state["head"]], [(bf16(2, part, nb), VMEM)])
-        state["head"] = [pair] + [to_chip(pair, h) for h in range(1, chips)]
-
-    def head_all():
-        (mine,) = run(
-            stack_kernel, [(v, VMEM) for v in state["head"]], [(bf16(chips, 2, part, nb), VMEM)], us=0.1
-        )
-        state["heads"] = (mine, to_sibling(mine))
-
-    def old():
-        operands = [(meta, SMEM)] + [(v, VMEM) for v in held[:line] + other[:line]]
-        (mine,) = run(functools.partial(old_kernel, line), operands, [(bf16(2, nb, nb), VMEM)], us=0.6)
-        state["old"] = [mine] + [to_chip(mine, h) for h in range(1, chips)]
-
-    def old_here():
-        (mine,) = run(
-            by_chip_kernel, [(meta, SMEM)] + [(v, VMEM) for v in state["old"]], [(bf16(2, nb, nb), VMEM)]
+            by_chip_kernel, [(meta, SMEM)] + [(v, VMEM) for v in choices], [(bf16(2, nb, nb), VMEM)], us=0.1
         )
         state["old"] = (mine, to_sibling(mine))
 
     def scatter():
-        sources = state["brought"] + (state["block0"], state["block0_sibling"], state["loaded"])
+        sources = state["brought"] + [state["block0"], state["block0_sibling"], state["loaded"]]
         (state["moved"],) = run(
             scatter_kernel,
             [(meta, SMEM), (state["arrive"], SMEM), (state["goal"], SMEM)] + [(v, VMEM) for v in sources],
@@ -546,14 +506,14 @@
             [(meta, SMEM), (lower, VMEM)] + [(v, VMEM) for v in state["fresh"]],
             [(bf16(nb, cb * nb), VMEM), (bf16(nb, cb, nb), VMEM)],
             scratch=[pltpu.VMEM((nb, cb * nb), BF16)],
-            us=0.1, mib=16,
+            us=2.0, mib=16,
         )
 
     def prep1():
         state["up1"], state["up0_panel"], state["top1"] = run(
-            functools.partial(prep1_kernel, chips),
-            [(meta, SMEM), (lower, VMEM), (upper, VMEM)] + [(v, VMEM) for v in state["fresh"]]
-            + [(state["up0"], VMEM)] + [(v, VMEM) for v in state["heads"]],
+            prep1_kernel,
+            [(meta, SMEM), (lower, VMEM), (upper, VMEM), (state["up0"], VMEM), (state["heads"], VMEM)]
+            + [(v, VMEM) for v in state["fresh"]],
             [(bf16(nb, cb * nb), VMEM), (bf16(nb, nb), VMEM), (bf16(nb, cb, nb), VMEM)],
             scratch=[pltpu.VMEM((nb, cb * nb), BF16), pltpu.VMEM((2, nb, nb), BF16)],
             us=3.5, mib=16,
@@ -581,9 +541,9 @@
             us=5.0, mib=24,
         )
 
-    plan = [(0, gather), (1, join), (3, fresh), (line - 1, old), (3, head), (4, head_here), (4, head_pair), (5, old_here), (5, head_all), (5, scatter), (5, prep0), (5, prep1)]
+    plan = [(0, gather), (1, join), (2, functools.partial(fresh, 0)), (3, functools.partial(fresh, 1)), (line - 1, functools.partial(old, held, "old_held")), (line, functools.partial(old, other, "old_other")), (4, scatter), (4, prep0), (5, prep1), (5, old_here)]
     for i in range(pieces):
-        plan.append((max(6 + i, i + line - 1), functools.partial(update, i)))
+        plan.append((max((5, 5, 6, 7, 8, 8)[min(i, 5)], i + line - 1), functools.partial(update, i)))
     for k in range(last_step + 1):
         step(k)
         while plan and (plan[0][0] <= k or k == last_step):

time: 179 us -> 206 us (1.15)
  local copies, waits for them, and re-layouts: 3.73 us -> 28.6 us
  waiting for transfers between devices: 59.6 us -> 45.3 us
  between operations: 0.68 us -> 14.3 us
  Pallas kernels: 60.6 us -> 67.5 us
  starting transfers between devices: 54.3 us -> 48.9 us
    unnamed x12 -> x120, local copies, waits for them, and re-layouts: 3.54 us -> 26.7 us
    ppermute x10 -> x9, waiting for transfers between devices: 23.9 us -> 8.78 us  [to_neighbour(): return lax.ppermute(value, 'pcol', [(c, c ^ 1) for c in range(col_devices)])]
    all_gather x0 -> x2, waiting for transfers between devices: none -> 13.2 us  [the longest x1 13.2 us: fresh(): parts = lax.all_gather(head[0], 'pcol')[:2]]
    ppermute x8, waiting for transfers between devices: 28 us -> 19.4 us  [to_next(): lax.ppermute(value, 'pcol', [(c, c + 2) for c in range(col_devices - 2)])]
    ppermute x3 -> x0, starting transfers between devices: 7.37 us -> none  [head(): lax.ppermute(mine, 'pcol', [(0, 2 * h), (1, 2 * h + 1)])]
    pallas_call x27 -> x25, Pallas kernels: 60.6 us -> 67.5 us  [call(): pl.pallas_call(ordered, out_shape=tuple((shape for shape, _ in outs)), in...]
    ppermute x3 -> x0, waiting for transfers between devices: 4.42 us -> none  [head(): lax.ppermute(mine, 'pcol', [(0, 2 * h), (1, 2 * h + 1)])]
    ppermute x8, starting transfers between devices: 31.4 us -> 28.7 us  [to_next(): lax.ppermute(value, 'pcol', [(c, c + 2) for c in range(col_devices - 2)])]
  transfers between devices with their start and end apart: 30 -> 30, of which waited for: 11 -> 12; matrix products, arithmetic and copies ran while one was open for 0% -> 1% of each run, Pallas kernels for 29% -> 26%
where the time goes in v3:
time: 206 us; the launch traced here: 205 us
  Pallas kernels  67.5 us (33%)
  starting transfers between devices  48.9 us (24%)
  waiting for transfers between devices  45.3 us (22%)
  local copies, waits for them, and re-layouts  28.6 us (14%)
  between operations  14.3 us (7%)
    pallas_call x25, Pallas kernels, call(): pl.pallas_call(ordered, out_shape=tuple((shape for shape, _ in outs)), in...  67.5 us
    ppermute x8, starting transfers between devices, to_next(): lax.ppermute(value, 'pcol', [(c, c + 2) for c in range(col_devices - 2)])  28.7 us
    unnamed x120, local copies, waits for them, and re-layouts  26.7 us
    ppermute x8, waiting for transfers between devices, to_next(): lax.ppermute(value, 'pcol', [(c, c + 2) for c in range(col_devices - 2)])  19.4 us
    ppermute x9, starting transfers between devices, to_neighbour(): return lax.ppermute(value, 'pcol', [(c, c ^ 1) for c in range(col_devices)])  13.7 us
    all_gather x1, waiting for transfers between devices, fresh(): parts = lax.all_gather(head[0], 'pcol')[:2]  13.2 us
    ppermute x9, waiting for transfers between devices, to_neighbour(): return lax.ppermute(value, 'pcol', [(c, c ^ 1) for c in range(col_devices)])  8.78 us
    ppermute x4, starting transfers between devices, to_chip(): lax.ppermute(value, 'prow', [(r, (r + 2 * h) % row_devices) for r in rang...  5.21 us
  transfers between devices with their start and end apart: 30, of which 12 were waited for; matrix products, arithmetic and copies ran while one was open for 1% of the time, Pallas kernels for 26%

profile of v3, /device:TPU:0, one launch (start us, length us, event | category | flops | bytes accessed | tf_op | source)
XLA Modules:
  0.0 204.7 jit_solution(1312440928405332362)
XLA Ops:
  6.5 2.2 %shard_map.46.refs_4_.refs_1_.refs_11_ = bf16[512,512]{1,0:T(8,128)(2,1)} custom-call(bf16[2560,2,512]{2,1,0:T(2,128)(2,1)} %bitcast.9), custom_call_target="tpu_custom_call" | custom-call | flops 1100000000 | tf_op jit(solution)/shard_map/pallas_call | solution.py:37
  8.8 3.0 %collective-permute-start.1 = (bf16[512,512]{1,0:T(8,128)(2,1)}, bf16[512,512]{1,0:T(8,128)(2,1)S(1)}, u32[]{:S(2)}, u32[]{:S(2)}) collective-permute-start(bf16[512,512]{1,0:T(8,128)(2,1)} %shard_map.46.refs_4_.refs_1_.refs_11_), channel_id=1, source_target_pairs={{0,1},{1,0},{2,3},{3,2},{4,5},{5,4},{6,7},{7,6},{8,9},{9,8},{10,11... | collective-permute-start | bytes 1572872 | tf_op jit(solution)/shard_map/ppermute | solution.py:392
  11.8 3.5 %collective-permute-start = (bf16[512,512]{1,0:T(8,128)(2,1)}, bf16[512,512]{1,0:T(8,128)(2,1)S(1)}, u32[]{:S(2)}, u32[]{:S(2)}) collective-permute-start(bf16[512,512]{1,0:T(8,128)(2,1)} %shard_map.46.refs_4_.refs_1_.refs_11_), channel_id=1, source_target_pairs={{0,2},{1,3},{2,4},{3,5},{4,6},{5,7},{8,10},{9,11},{10,12},{11,13},... | collective-permute-start | bytes 1572872 | tf_op jit(solution)/shard_map/ppermute | solution.py:398
  15.6 2.5 %copy-done.19 = bf16[5,512,2,512]{3,2,1,0:T(2,128)(2,1)S(1)} copy-done((bf16[5,512,2,512]{3,2,1,0:T(2,128)(2,1)S(1)}, bf16[5,512,2,512]{3,2,1,0:T(2,128)(2,1)}, u32[]{:S(2)}) %copy-start.19) | copy-done | bytes 5242904
  19.1 8.7 %shard_map.47 = (bf16[512,512]{1,0:T(8,128)(2,1)S(1)}, bf16[512,512]{1,0:T(8,128)(2,1)S(1)}, bf16[512,512]{1,0:T(8,128)(2,1)S(1)}, bf16[256,512]{1,0:T(8,128)(2,...) custom-call(s32[4]{0:T(128)S(1)} %pad_add_fusion.refs_0_, ...), custom_call_target="tpu_custom_call" | custom-call | flops 8800000000 | tf_op jit(solution)/shard_map/pallas_call | solution.py:37
  28.6 1.6 copy-done.17
  30.4 3.5 %collective-permute-start.2 = (bf16[512,512]{1,0:T(8,128)(2,1)S(1)}, bf16[512,512]{1,0:T(8,128)(2,1)S(1)}, u32[]{:S(2)}, u32[]{:S(2)}) collective-permute-start(bf16[512,512]{1,0:T(8,128)(2,1)S(1)} %shard_map.48.refs_4_.refs_2_.refs_12_.refs_11_), channel_id=1, source_target_pairs={{0,2},{1,3},{2,4},{3,5},{4,6},{5,7},{8,10},{9,11},{10,12},{11,13},... | collective-permute-start | bytes 1572872 | tf_op jit(solution)/shard_map/ppermute | solution.py:398
  34.5 3.2 %shard_map.49 = (bf16[256,2,512]{2,1,0:T(2,128)(2,1)S(1)}, bf16[256,2,512]{2,1,0:T(2,128)(2,1)}) custom-call(s32[4]{0:T(128)S(1)} %pad_add_fusion.refs_0_, s32[2,512]{1,0:T(2,128)S(1)} %get-tuple-element.45.refs_1_, bf16[512,2,512]{2,1,0:T(2,128)(2,1)S(1)} %get-tuple-element.46.refs_2_, bf16[512,2,512]{2,1,0:T(2,128)(2,1)S(1)} %collective-permute-done.3.refs_3_, ...), custom_call_target="tpu_custom_call" | custom-call | flops 2200000000 | tf_op jit(solution)/shard_map/pallas_call | solution.py:37
  37.7 1.5 collective-permute-start.6
  39.2 5.3 %collective-permute-done.2.refs_1_ = bf16[512,512]{1,0:T(8,128)(2,1)S(1)} collective-permute-done((bf16[512,512]{1,0:T(8,128)(2,1)S(1)}, bf16[512,512]{1,0:T(8,128)(2,1)S(1)}, u32[]{:S(2)}, u32[]{:S(2)}) %collective-permute-start.2) | collective-permute-done | bytes 524320 | tf_op jit(solution)/shard_map/ppermute | solution.py:398
  44.5 2.3 %collective-permute-done.4.refs_4_.refs_2_.refs_16_.refs_15_ = bf16[512,512]{1,0:T(8,128)(2,1)S(1)} collective-permute-done((bf16[512,512]{1,0:T(8,128)(2,1)S(1)}, bf16[512,512]{1,0:T(8,128)(2,1)S(1)}, u32[]{:S(2)}, u32[]{:S(2)}) %collective-permute-start.4) | collective-permute-done | bytes 524320 | tf_op jit(solution)/shard_map/ppermute | solution.py:392
  47.4 2.9 %collective-permute-done.6.refs_3_ = bf16[256,2,512]{2,1,0:T(2,128)(2,1)S(1)} collective-permute-done((bf16[256,2,512]{2,1,0:T(2,128)(2,1)S(1)}, bf16[256,2,512]{2,1,0:T(2,128)(2,1)S(1)}, u32[]{:S(2)}, u32[]{:S(2)}) %collective-permute-start.6) | collective-permute-done | bytes 524320 | tf_op jit(solution)/shard_map/ppermute | solution.py:395
  50.3 1.8 shard_map.51
  53.8 3.6 %collective-permute-start.5 = (bf16[512,512]{1,0:T(8,128)(2,1)S(1)}, bf16[512,512]{1,0:T(8,128)(2,1)S(1)}, u32[]{:S(2)}, u32[]{:S(2)}) collective-permute-start(bf16[512,512]{1,0:T(8,128)(2,1)S(1)} %shard_map.50.refs_4_.refs_3_.refs_13_.refs_12_.refs_11_), channel_id=1, source_target_pairs={{0,2},{1,3},{2,4},{3,5},{4,6},{5,7},{8,10},{9,11},{10,12},{11,13},... | collective-permute-start | bytes 1572872 | tf_op jit(solution)/shard_map/ppermute | solution.py:398
  57.4 1.6 collective-permute-start.7
  59.0 1.5 collective-permute-start.8
  60.5 9.1 %collective-permute-done.5.refs_1_ = bf16[512,512]{1,0:T(8,128)(2,1)S(1)} collective-permute-done((bf16[512,512]{1,0:T(8,128)(2,1)S(1)}, bf16[512,512]{1,0:T(8,128)(2,1)S(1)}, u32[]{:S(2)}, u32[]{:S(2)}) %collective-permute-start.5) | collective-permute-done | bytes 524320 | tf_op jit(solution)/shard_map/ppermute | solution.py:398
  70.8 2.6 %shard_map.53 = (bf16[256,1024]{1,0:T(8,128)(2,1)S(1)}, bf16[256,2,512]{2,1,0:T(2,128)(2,1)}) custom-call(s32[4]{0:T(128)S(1)} %pad_add_fusion.refs_0_, s32[2,512]{1,0:T(2,128)S(1)} %get-tuple-element.43.refs_3_.refs_1_, bf16[256,2,512]{2,1,0:T(2,128)(2,1)} %get-tuple-element.48.refs_3_.refs_2_, bf16[256,2,512]{2,1,0:T(2,128)(2,1)S(1)} %collective-permute-done.8.refs_3_, ...), custom_call_target="tpu_custom_call" | custom-call | flops 1650000000 | tf_op jit(solution)/shard_map/pallas_call | solution.py:37
  75.3 1.6 collective-permute-start.11
  76.9 4.5 %collective-permute-start.10 = (bf16[512,512]{1,0:T(8,128)(2,1)S(1)}, bf16[512,512]{1,0:T(8,128)(2,1)}, u32[]{:S(2)}, u32[]{:S(2)}) collective-permute-start(bf16[512,512]{1,0:T(8,128)(2,1)S(1)} %shard_map.52.refs_4_.refs_14_.refs_13_.refs_12_.refs_11_), channel_id=1, source_target_pairs={{0,2},{1,3},{2,4},{3,5},{4,6},{5,7},{8,10},{9,11},{10,12},{11,13},... | collective-permute-start | bytes 1572872 | tf_op jit(solution)/shard_map/ppermute | solution.py:398
  81.5 1.8 collective-permute-start.9
  83.7 13.2 %all-gather.5.cloned.1.call-done = bf16[1024,512]{1,0:T(8,128)(2,1)} async-done(((bf16[128,512]{1,0:T(8,128)(2,1)}), bf16[1024,512]{1,0:T(8,128)(2,1)}) %all-gather.5.cloned.1.call-update) | async-done | bytes 1048592 | tf_op jit(solution)/shard_map/all_gather | solution.py:478
  96.9 1.7 slice.5
  104.1 3.4 %collective-permute-start.18 = (bf16[512,512]{1,0:T(8,128)(2,1)S(1)}, bf16[512,512]{1,0:T(8,128)(2,1)S(1)}, u32[]{:S(2)}, u32[]{:S(2)}) collective-permute-start(bf16[512,512]{1,0:T(8,128)(2,1)S(1)} %shard_map.55.refs_5_.refs_14_.refs_13_.refs_12_.refs_11_), channel_id=1, source_target_pairs={{0,2},{1,3},{2,4},{3,5},{4,6},{5,7},{8,10},{9,11},{10,12},{11,13},... | collective-permute-start | bytes 1572872 | tf_op jit(solution)/shard_map/ppermute | solution.py:398
  108.2 1.6 collective-permute-start.19
  109.7 2.5 %copy-done.18 = bf16[2568,2,512]{2,1,0:T(2,128)(2,1)S(1)} copy-done((bf16[2568,2,512]{2,1,0:T(2,128)(2,1)S(1)}, bf16[2568,2,512]{2,1,0:T(2,128)(2,1)}, u32[]{:S(2)}) %copy-start.18) | copy-done | bytes 5259288
  112.3 5.4 %shard_map.57.refs_6_.refs_8_ = bf16[2568,2,512]{2,1,0:T(2,128)(2,1)S(1)} custom-call(s32[4]{0:T(128)S(1)} %pad_add_fusion.refs_0_, s32[2,512]{1,0:T(2,128)S(1)} %get-tuple-element.56.refs_1_, s32[2,512]{1,0:T(2,128)S(1)} %get-tuple-element.41.refs_2_.refs_1_, bf16[256,2,512]{2,1,0:T(2,128)(2,1)S(1)} %copy-done.40, ...), custom_call_target="tpu_custom_call" | custom-call | flops 110000000 | tf_op jit(solution)/shard_map/pallas_call | solution.py:37
  117.8 2.0 shard_map.58
  119.8 2.4 %copy-done = bf16[2568,2,512]{2,1,0:T(2,128)(2,1)} copy-done((bf16[2568,2,512]{2,1,0:T(2,128)(2,1)}, bf16[2568,2,512]{2,1,0:T(2,128)(2,1)S(1)}, u32[]{:S(2)}) %copy-start) | copy-done | bytes 5259288
  124.1 1.4 shard_map.59.refs_9_.refs_14_.refs_13_.refs_12_.refs_11_
  127.2 1.2 copy-done.3
  135.2 3.5 %shard_map.60 = (bf16[512,1024]{1,0:T(8,128)(2,1)S(1)}, bf16[512,512]{1,0:T(8,128)(2,1)S(1)}, bf16[512,2,512]{2,1,0:T(2,128)(2,1)S(1)}) custom-call(s32[4]{0:T(128)S(1)} %pad_add_fusion.refs_0_, bf16[2,512,512]{2,1,0:T(8,128)(2,1)S(1)} %copy-done.35, bf16[2,512,512]{2,1,0:T(8,128)(2,1)S(1)} %copy-done.1, bf16[512,1024]{1,0:T(8,128)(2,1)S(1)} %copy-done.3, ...), custom_call_target="tpu_custom_call" | custom-call | flops 3849999872 | tf_op jit(solution)/shard_map/pallas_call | solution.py:37
  139.4 3.4 %collective-permute-start.21 = (bf16[512,512]{1,0:T(8,128)(2,1)}, bf16[512,512]{1,0:T(8,128)(2,1)S(1)}, u32[]{:S(2)}, u32[]{:S(2)}) collective-permute-start(bf16[512,512]{1,0:T(8,128)(2,1)} %shard_map.59.refs_9_.refs_14_.refs_13_.refs_12_.refs_11_), channel_id=1, source_target_pairs={{0,2},{1,3},{2,4},{3,5},{4,6},{5,7},{8,10},{9,11},{10,12},{11,13},... | collective-permute-start | bytes 1572872 | tf_op jit(solution)/shard_map/ppermute | solution.py:398
  142.9 1.5 collective-permute-start.22
  144.5 1.8 shard_map.62
  146.4 6.2 %shard_map.63 = (bf16[2560,2,512]{2,1,0:T(2,128)(2,1)}, f32[8,128]{1,0:T(8,128)S(1)}) custom-call(s32[4]{0:T(128)S(1)} %pad_add_fusion.refs_0_, s32[2,512]{1,0:T(2,128)S(1)} %get-tuple-element.41.refs_2_.refs_1_, bf16[2,512,512]{2,1,0:T(8,128)(2,1)S(1)} %shard_map.61.refs_2_.refs_19_, ...), custom_call_target="tpu_custom_call", output_to_operand_aliasing={{0}: (19, {})} | custom-call | flops 5500000256 | tf_op jit(solution)/shard_map/pallas_call | solution.py:37
  152.6 2.3 %collective-permute-done.21.refs_1_ = bf16[512,512]{1,0:T(8,128)(2,1)S(1)} collective-permute-done((bf16[512,512]{1,0:T(8,128)(2,1)}, bf16[512,512]{1,0:T(8,128)(2,1)S(1)}, u32[]{:S(2)}, u32[]{:S(2)}) %collective-permute-start.21) | collective-permute-done | bytes 524320 | tf_op jit(solution)/shard_map/ppermute | solution.py:398
  155.0 2.2 %collective-permute-done.22.refs_3_.refs_18_.refs_17_.refs_16_.refs_15_ = bf16[512,512]{1,0:T(8,128)(2,1)S(1)} collective-permute-done((bf16[512,512]{1,0:T(8,128)(2,1)}, bf16[512,512]{1,0:T(8,128)(2,1)S(1)}, u32[]{:S(2)}, u32[]{:S(2)}) %collective-permute-start.22) | collective-permute-done | bytes 524320 | tf_op jit(solution)/shard_map/ppermute | solution.py:392
  157.7 3.4 %collective-permute-start.23 = (bf16[512,512]{1,0:T(8,128)(2,1)S(1)}, bf16[512,512]{1,0:T(8,128)(2,1)S(1)}, u32[]{:S(2)}, u32[]{:S(2)}) collective-permute-start(bf16[512,512]{1,0:T(8,128)(2,1)S(1)} %shard_map.64.refs_20_.refs_14_.refs_13_.refs_12_), channel_id=1, source_target_pairs={{0,2},{1,3},{2,4},{3,5},{4,6},{5,7},{8,10},{9,11},{10,12},{11,13},... | collective-permute-start | bytes 1572872 | tf_op jit(solution)/shard_map/ppermute | solution.py:398
  161.2 1.5 collective-permute-start.24
  162.7 6.4 %shard_map.65 = (bf16[2560,2,512]{2,1,0:T(2,128)(2,1)}, f32[8,128]{1,0:T(8,128)S(1)}) custom-call(s32[4]{0:T(128)S(1)} %pad_add_fusion.refs_0_, s32[2,512]{1,0:T(2,128)S(1)} %get-tuple-element.41.refs_2_.refs_1_, bf16[2,512,512]{2,1,0:T(8,128)(2,1)S(1)} %shard_map.61.refs_2_.refs_19_, ...), custom_call_target="tpu_custom_call", output_to_operand_aliasing={{0}: (19, {})} | custom-call | flops 5500000256 | tf_op jit(solution)/shard_map/pallas_call | solution.py:37
  169.2 2.7 %collective-permute-done.23.refs_1_ = bf16[512,512]{1,0:T(8,128)(2,1)S(1)} collective-permute-done((bf16[512,512]{1,0:T(8,128)(2,1)S(1)}, bf16[512,512]{1,0:T(8,128)(2,1)S(1)}, u32[]{:S(2)}, u32[]{:S(2)}) %collective-permute-start.23) | collective-permute-done | bytes 524320 | tf_op jit(solution)/shard_map/ppermute | solution.py:398
  171.8 2.3 %collective-permute-done.24.refs_3_.refs_18_.refs_17_.refs_16_ = bf16[512,512]{1,0:T(8,128)(2,1)S(1)} collective-permute-done((bf16[512,512]{1,0:T(8,128)(2,1)S(1)}, bf16[512,512]{1,0:T(8,128)(2,1)S(1)}, u32[]{:S(2)}, u32[]{:S(2)}) %collective-permute-start.24) | collective-permute-done | bytes 524320 | tf_op jit(solution)/shard_map/ppermute | solution.py:392
  174.7 3.3 %collective-permute-start.25 = (bf16[256,512]{1,0:T(8,128)(2,1)S(1)}, bf16[256,512]{1,0:T(8,128)(2,1)S(1)}, u32[]{:S(2)}, u32[]{:S(2)}) collective-permute-start(bf16[256,512]{1,0:T(8,128)(2,1)S(1)} %shard_map.66.refs_20_.refs_14_.refs_13_), channel_id=1, source_target_pairs={{0,2},{1,3},{2,4},{3,5},{4,6},{5,7},{8,10},{9,11},{10,12},{11,13},... | collective-permute-start | bytes 786440 | tf_op jit(solution)/shard_map/ppermute | solution.py:398
  179.1 6.2 %shard_map.67 = (bf16[2560,2,512]{2,1,0:T(2,128)(2,1)}, f32[8,128]{1,0:T(8,128)S(1)}) custom-call(s32[4]{0:T(128)S(1)} %pad_add_fusion.refs_0_, s32[2,512]{1,0:T(2,128)S(1)} %get-tuple-element.41.refs_2_.refs_1_, bf16[2,512,512]{2,1,0:T(8,128)(2,1)S(1)} %shard_map.61.refs_2_.refs_19_, ...), custom_call_target="tpu_custom_call", output_to_operand_aliasing={{0}: (19, {})} | custom-call | flops 5500000256 | tf_op jit(solution)/shard_map/pallas_call | solution.py:37
  187.0 4.1 %shard_map.69 = (bf16[2560,2,512]{2,1,0:T(2,128)(2,1)}, f32[8,128]{1,0:T(8,128)S(1)}) custom-call(s32[4]{0:T(128)S(1)} %pad_add_fusion.refs_0_, s32[2,512]{1,0:T(2,128)S(1)} %get-tuple-element.41.refs_2_.refs_1_, bf16[2,512,512]{2,1,0:T(8,128)(2,1)S(1)} %shard_map.61.refs_2_.refs_19_, ...), custom_call_target="tpu_custom_call", output_to_operand_aliasing={{0}: (19, {})} | custom-call | flops 5500000256 | tf_op jit(solution)/shard_map/pallas_call | solution.py:37
  191.1 1.3 collective-permute-done.27.refs_18_
  192.4 5.4 %shard_map.70 = (bf16[2560,2,512]{2,1,0:T(2,128)(2,1)}, f32[8,128]{1,0:T(8,128)}) custom-call(s32[4]{0:T(128)S(1)} %pad_add_fusion.refs_0_, s32[2,512]{1,0:T(2,128)S(1)} %get-tuple-element.41.refs_2_.refs_1_, bf16[2,512,512]{2,1,0:T(8,128)(2,1)S(1)} %shard_map.61.refs_2_.refs_19_, ...), custom_call_target="tpu_custom_call", output_to_operand_aliasing={{0}: (19, {})} | custom-call | flops 5500000256 | tf_op jit(solution)/shard_map/pallas_call | solution.py:37
  (163 shorter events, 29.6 us)
Async XLA Ops:
  6.5 90.4 %all-gather.5.cloned.1.call-start = ((), (), s32[]{:S(2)}) async-start(), calls=%async_computation | async-start | bytes 1179648 | tf_op jit(solution)/shard_map/all_gather | solution.py:478
  8.8 19.2 %collective-permute-start.1 = (bf16[512,512]{1,0:T(8,128)(2,1)}, bf16[512,512]{1,0:T(8,128)(2,1)S(1)}, u32[]{:S(2)}, u32[]{:S(2)}) collective-permute-start(bf16[512,512]{1,0:T(8,128)(2,1)} %shard_map.46.refs_4_.refs_1_.refs_11_), channel_id=1, source_target_pairs={{0,1},{1,0},{2,3},{3,2},{4,5},{5,4},{6,7},{7,6},{8,9},{9,8},{10,11... | collective-permute-start | bytes 1572872 | tf_op jit(solution)/shard_map/ppermute | solution.py:392
  11.8 16.2 %collective-permute-start = (bf16[512,512]{1,0:T(8,128)(2,1)}, bf16[512,512]{1,0:T(8,128)(2,1)S(1)}, u32[]{:S(2)}, u32[]{:S(2)}) collective-permute-start(bf16[512,512]{1,0:T(8,128)(2,1)} %shard_map.46.refs_4_.refs_1_.refs_11_), channel_id=1, source_target_pairs={{0,2},{1,3},{2,4},{3,5},{4,6},{5,7},{8,10},{9,11},{10,12},{11,13},... | collective-permute-start | bytes 1572872 | tf_op jit(solution)/shard_map/ppermute | solution.py:398
  27.9 6.6 %collective-permute-start.3 = (bf16[512,2,512]{2,1,0:T(2,128)(2,1)S(1)}, bf16[512,2,512]{2,1,0:T(2,128)(2,1)S(1)}, u32[]{:S(2)}, u32[]{:S(2)}) collective-permute-start(bf16[512,2,512]{2,1,0:T(2,128)(2,1)S(1)} %get-tuple-element.47), channel_id=1, source_target_pairs={{0,8},{8,0},{16,24},{24,16},{1,9},{9,1},{17,25},{25,17},{2,10},{10... | collective-permute-start | bytes 3145736 | tf_op jit(solution)/shard_map/ppermute | solution.py:389
  30.4 17.0 %copy-start.31 = (bf16[512,512]{1,0:T(8,128)(2,1)}, bf16[512,512]{1,0:T(8,128)(2,1)S(1)}, u32[]{:S(2)}) copy-start(bf16[512,512]{1,0:T(8,128)(2,1)S(1)} %shard_map.48.refs_4_.refs_2_.refs_12_.refs_11_) | copy-start | bytes 1572868
  30.4 14.1 %collective-permute-start.2 = (bf16[512,512]{1,0:T(8,128)(2,1)S(1)}, bf16[512,512]{1,0:T(8,128)(2,1)S(1)}, u32[]{:S(2)}, u32[]{:S(2)}) collective-permute-start(bf16[512,512]{1,0:T(8,128)(2,1)S(1)} %shard_map.48.refs_4_.refs_2_.refs_12_.refs_11_), channel_id=1, source_target_pairs={{0,2},{1,3},{2,4},{3,5},{4,6},{5,7},{8,10},{9,11},{10,12},{11,13},... | collective-permute-start | bytes 1572872 | tf_op jit(solution)/shard_map/ppermute | solution.py:398
  33.9 12.9 %collective-permute-start.4 = (bf16[512,512]{1,0:T(8,128)(2,1)S(1)}, bf16[512,512]{1,0:T(8,128)(2,1)S(1)}, u32[]{:S(2)}, u32[]{:S(2)}) collective-permute-start(bf16[512,512]{1,0:T(8,128)(2,1)S(1)} %shard_map.48.refs_4_.refs_2_.refs_12_.refs_11_), channel_id=1, source_target_pairs={{0,1},{1,0},{2,3},{3,2},{4,5},{5,4},{6,7},{7,6},{8,9},{9,8},{10,11... | collective-permute-start | bytes 1572872 | tf_op jit(solution)/shard_map/ppermute | solution.py:392
  37.7 12.5 %collective-permute-start.6 = (bf16[256,2,512]{2,1,0:T(2,128)(2,1)S(1)}, bf16[256,2,512]{2,1,0:T(2,128)(2,1)S(1)}, u32[]{:S(2)}, u32[]{:S(2)}) collective-permute-start(bf16[256,2,512]{2,1,0:T(2,128)(2,1)S(1)} %get-tuple-element.50.refs_2_), channel_id=1, source_target_pairs={{0,16},{8,24},{16,0},{24,8},{1,17},{9,25},{17,1},{25,9},{2,18},{10... | collective-permute-start | bytes 1572872 | tf_op jit(solution)/shard_map/ppermute | solution.py:395
  46.8 56.6 %copy-start.22 = (bf16[512,512]{1,0:T(8,128)(2,1)}, bf16[512,512]{1,0:T(8,128)(2,1)S(1)}, u32[]{:S(2)}) copy-start(bf16[512,512]{1,0:T(8,128)(2,1)S(1)} %collective-permute-done.4.refs_4_.refs_2_.refs_16_.refs_15_) | copy-start | bytes 1572868
  47.4 26.1 %copy-start.15 = (bf16[512,512]{1,0:T(8,128)(2,1)}, bf16[512,512]{1,0:T(8,128)(2,1)S(1)}, u32[]{:S(2)}) copy-start(bf16[512,512]{1,0:T(8,128)(2,1)S(1)} %shard_map.50.refs_4_.refs_3_.refs_13_.refs_12_.refs_11_) | copy-start | bytes 1572868
  53.7 19.8 %copy-start.29 = (bf16[512,512]{1,0:T(8,128)(2,1)S(1)}, bf16[512,512]{1,0:T(8,128)(2,1)}, u32[]{:S(2)}) copy-start(bf16[512,512]{1,0:T(8,128)(2,1)} %shard_map.46.refs_4_.refs_1_.refs_11_) | copy-start | bytes 1572868
  53.7 73.5 %all-gather.7.cloned.1.call-start = ((), (), s32[]{:S(2)}) async-start(), calls=%async_computation.1 | async-start | bytes 1310720 | tf_op jit(solution)/shard_map/all_gather | solution.py:479
  53.8 15.8 %collective-permute-start.5 = (bf16[512,512]{1,0:T(8,128)(2,1)S(1)}, bf16[512,512]{1,0:T(8,128)(2,1)S(1)}, u32[]{:S(2)}, u32[]{:S(2)}) collective-permute-start(bf16[512,512]{1,0:T(8,128)(2,1)S(1)} %shard_map.50.refs_4_.refs_3_.refs_13_.refs_12_.refs_11_), channel_id=1, source_target_pairs={{0,2},{1,3},{2,4},{3,5},{4,6},{5,7},{8,10},{9,11},{10,12},{11,13},... | collective-permute-start | bytes 1572872 | tf_op jit(solution)/shard_map/ppermute | solution.py:398
  57.4 12.8 %collective-permute-start.7 = (bf16[512,512]{1,0:T(8,128)(2,1)S(1)}, bf16[512,512]{1,0:T(8,128)(2,1)S(1)}, u32[]{:S(2)}, u32[]{:S(2)}) collective-permute-start(bf16[512,512]{1,0:T(8,128)(2,1)S(1)} %shard_map.50.refs_4_.refs_3_.refs_13_.refs_12_.refs_11_), channel_id=1, source_target_pairs={{0,1},{1,0},{2,3},{3,2},{4,5},{5,4},{6,7},{7,6},{8,9},{9,8},{10,11... | collective-permute-start | bytes 1572872 | tf_op jit(solution)/shard_map/ppermute | solution.py:392
  59.0 11.8 %collective-permute-start.8 = (bf16[256,2,512]{2,1,0:T(2,128)(2,1)}, bf16[256,2,512]{2,1,0:T(2,128)(2,1)S(1)}, u32[]{:S(2)}, u32[]{:S(2)}) collective-permute-start(bf16[256,2,512]{2,1,0:T(2,128)(2,1)} %get-tuple-element.48.refs_3_.refs_2_), channel_id=1, source_target_pairs={{0,16},{8,24},{16,0},{24,8},{1,17},{9,25},{17,1},{25,9},{2,18},{10... | collective-permute-start | bytes 1572872 | tf_op jit(solution)/shard_map/ppermute | solution.py:395
  70.2 33.1 %copy-start.11 = (bf16[512,512]{1,0:T(8,128)(2,1)}, bf16[512,512]{1,0:T(8,128)(2,1)S(1)}, u32[]{:S(2)}) copy-start(bf16[512,512]{1,0:T(8,128)(2,1)S(1)} %collective-permute-done.7.refs_4_.refs_3_.refs_17_.refs_16_.refs_15_) | copy-start | bytes 1572868
  70.8 32.6 %copy-start.5 = (bf16[512,512]{1,0:T(8,128)(2,1)}, bf16[512,512]{1,0:T(8,128)(2,1)S(1)}, u32[]{:S(2)}) copy-start(bf16[512,512]{1,0:T(8,128)(2,1)S(1)} %shard_map.52.refs_4_.refs_14_.refs_13_.refs_12_.refs_11_) | copy-start | bytes 1572868
  75.3 28.1 %copy-start.24 = (bf16[512,512]{1,0:T(8,128)(2,1)}, bf16[512,512]{1,0:T(8,128)(2,1)S(1)}, u32[]{:S(2)}) copy-start(bf16[512,512]{1,0:T(8,128)(2,1)S(1)} %shard_map.54.refs_3_.refs_1_) | copy-start | bytes 1572868
  75.3 23.3 %collective-permute-start.11 = (bf16[512,512]{1,0:T(8,128)(2,1)S(1)}, bf16[512,512]{1,0:T(8,128)(2,1)S(1)}, u32[]{:S(2)}, u32[]{:S(2)}) collective-permute-start(bf16[512,512]{1,0:T(8,128)(2,1)S(1)} %shard_map.54.refs_3_.refs_1_), channel_id=1, source_target_pairs={{0,16},{8,24},{16,0},{24,8},{1,17},{9,25},{17,1},{25,9},{2,18},{10... | collective-permute-start | bytes 1572872 | tf_op jit(solution)/shard_map/ppermute | solution.py:395
  76.9 22.6 %collective-permute-start.10 = (bf16[512,512]{1,0:T(8,128)(2,1)S(1)}, bf16[512,512]{1,0:T(8,128)(2,1)}, u32[]{:S(2)}, u32[]{:S(2)}) collective-permute-start(bf16[512,512]{1,0:T(8,128)(2,1)S(1)} %shard_map.52.refs_4_.refs_14_.refs_13_.refs_12_.refs_11_), channel_id=1, source_target_pairs={{0,2},{1,3},{2,4},{3,5},{4,6},{5,7},{8,10},{9,11},{10,12},{11,13},... | collective-permute-start | bytes 1572872 | tf_op jit(solution)/shard_map/ppermute | solution.py:398
  81.5 18.5 %collective-permute-start.9 = (bf16[512,512]{1,0:T(8,128)(2,1)S(1)}, bf16[512,512]{1,0:T(8,128)(2,1)S(1)}, u32[]{:S(2)}, u32[]{:S(2)}) collective-permute-start(bf16[512,512]{1,0:T(8,128)(2,1)S(1)} %shard_map.52.refs_4_.refs_14_.refs_13_.refs_12_.refs_11_), channel_id=1, source_target_pairs={{0,1},{1,0},{2,3},{3,2},{4,5},{5,4},{6,7},{7,6},{8,9},{9,8},{10,11... | collective-permute-start | bytes 1572872 | tf_op jit(solution)/shard_map/ppermute | solution.py:392
  83.2 20.9 %collective-permute-start.17 = (bf16[512,2,512]{2,1,0:T(2,128)(2,1)}, bf16[512,2,512]{2,1,0:T(2,128)(2,1)}, u32[]{:S(2)}, u32[]{:S(2)}) collective-permute-start(bf16[512,2,512]{2,1,0:T(2,128)(2,1)} %get-tuple-element.58.refs_7_), channel_id=1, source_target_pairs={{0,8},{8,0},{16,24},{24,16},{1,9},{9,1},{17,25},{25,17},{2,10},{10... | collective-permute-start | bytes 3145736 | tf_op jit(solution)/shard_map/ppermute | solution.py:389
  83.2 24.3 %collective-permute-start.16 = (bf16[256,2,512]{2,1,0:T(2,128)(2,1)}, bf16[256,2,512]{2,1,0:T(2,128)(2,1)}, u32[]{:S(2)}, u32[]{:S(2)}) collective-permute-start(bf16[256,2,512]{2,1,0:T(2,128)(2,1)} %get-tuple-element.52.refs_5_), channel_id=1, source_target_pairs={{0,8},{8,0},{16,24},{24,16},{1,9},{9,1},{17,25},{25,17},{2,10},{10... | collective-permute-start | bytes 1572872 | tf_op jit(solution)/shard_map/ppermute | solution.py:389
  99.5 8.7 %collective-permute-start.15 = (bf16[256,2,512]{2,1,0:T(2,128)(2,1)}, bf16[256,2,512]{2,1,0:T(2,128)(2,1)S(1)}, u32[]{:S(2)}, u32[]{:S(2)}) collective-permute-start(bf16[256,2,512]{2,1,0:T(2,128)(2,1)} %copy-done.39), channel_id=1, source_target_pairs={{0,8},{8,0},{16,24},{24,16},{1,9},{9,1},{17,25},{25,17},{2,10},{10... | collective-permute-start | bytes 1572872 | tf_op jit(solution)/shard_map/ppermute | solution.py:389
  99.5 18.3 %collective-permute-start.14 = (bf16[256,1024]{1,0:T(8,128)(2,1)}, bf16[256,1024]{1,0:T(8,128)(2,1)S(1)}, u32[]{:S(2)}, u32[]{:S(2)}) collective-permute-start(bf16[256,1024]{1,0:T(8,128)(2,1)} %copy-done.41), channel_id=1, source_target_pairs={{0,8},{8,0},{16,24},{24,16},{1,9},{9,1},{17,25},{25,17},{2,10},{10... | collective-permute-start | bytes 1572872 | tf_op jit(solution)/shard_map/ppermute | solution.py:389
  100.0 17.8 %collective-permute-start.13 = (bf16[256,1024]{1,0:T(8,128)(2,1)}, bf16[256,1024]{1,0:T(8,128)(2,1)S(1)}, u32[]{:S(2)}, u32[]{:S(2)}) collective-permute-start(bf16[256,1024]{1,0:T(8,128)(2,1)} %copy-done.36), channel_id=1, source_target_pairs={{0,8},{8,0},{16,24},{24,16},{1,9},{9,1},{17,25},{25,17},{2,10},{10... | collective-permute-start | bytes 1572872 | tf_op jit(solution)/shard_map/ppermute | solution.py:389
  103.4 14.3 %copy-start.7 = (bf16[512,512]{1,0:T(8,128)(2,1)}, bf16[512,512]{1,0:T(8,128)(2,1)S(1)}, u32[]{:S(2)}) copy-start(bf16[512,512]{1,0:T(8,128)(2,1)S(1)} %shard_map.55.refs_5_.refs_14_.refs_13_.refs_12_.refs_11_) | copy-start | bytes 1572868
  104.1 13.6 %copy-start.20 = (bf16[512,512]{1,0:T(8,128)(2,1)}, bf16[512,512]{1,0:T(8,128)(2,1)S(1)}, u32[]{:S(2)}) copy-start(bf16[512,512]{1,0:T(8,128)(2,1)S(1)} %shard_map.56.refs_10_.refs_2_) | copy-start | bytes 1572868
  104.1 20.0 %collective-permute-start.18 = (bf16[512,512]{1,0:T(8,128)(2,1)S(1)}, bf16[512,512]{1,0:T(8,128)(2,1)S(1)}, u32[]{:S(2)}, u32[]{:S(2)}) collective-permute-start(bf16[512,512]{1,0:T(8,128)(2,1)S(1)} %shard_map.55.refs_5_.refs_14_.refs_13_.refs_12_.refs_11_), channel_id=1, source_target_pairs={{0,2},{1,3},{2,4},{3,5},{4,6},{5,7},{8,10},{9,11},{10,12},{11,13},... | collective-permute-start | bytes 1572872 | tf_op jit(solution)/shard_map/ppermute | solution.py:398
  107.5 16.6 %collective-permute-start.12 = (bf16[512,512]{1,0:T(8,128)(2,1)S(1)}, bf16[512,512]{1,0:T(8,128)(2,1)S(1)}, u32[]{:S(2)}, u32[]{:S(2)}) collective-permute-start(bf16[512,512]{1,0:T(8,128)(2,1)S(1)} %shard_map.56.refs_10_.refs_2_), channel_id=1, source_target_pairs={{0,16},{8,24},{16,0},{24,8},{1,17},{9,25},{17,1},{25,9},{2,18},{10... | collective-permute-start | bytes 1572872 | tf_op jit(solution)/shard_map/ppermute | solution.py:395
  108.2 15.9 %collective-permute-start.19 = (bf16[512,512]{1,0:T(8,128)(2,1)S(1)}, bf16[512,512]{1,0:T(8,128)(2,1)S(1)}, u32[]{:S(2)}, u32[]{:S(2)}) collective-permute-start(bf16[512,512]{1,0:T(8,128)(2,1)S(1)} %shard_map.55.refs_5_.refs_14_.refs_13_.refs_12_.refs_11_), channel_id=1, source_target_pairs={{0,1},{1,0},{2,3},{3,2},{4,5},{5,4},{6,7},{7,6},{8,9},{9,8},{10,11... | collective-permute-start | bytes 1572872 | tf_op jit(solution)/shard_map/ppermute | solution.py:392
  117.7 9.5 %copy-start.1 = (bf16[2,512,512]{2,1,0:T(8,128)(2,1)S(1)}, bf16[2,512,512]{2,1,0:T(8,128)(2,1)}, u32[]{:S(2)}) copy-start(bf16[2,512,512]{2,1,0:T(8,128)(2,1)} %refs_4_.11) | copy-start | bytes 3145732
  124.1 20.3 %slice-start = ((s8[5259264]{0:T(1024)(128)(4,1)}), s8[1064960]{0:T(1024)(128)(4,1)S(1)}, s32[]{:S(2)}) async-start(s8[5259264]{0:T(1024)(128)(4,1)} %bitcast.7), calls=%async_computation.2 | async-start | bytes 2129920
  135.1 9.3 %slice-start.1 = ((s8[5259264]{0:T(1024)(128)(4,1)}), s8[4194304]{0:T(1024)(128)(4,1)S(1)}, s32[]{:S(2)}) async-start(s8[5259264]{0:T(1024)(128)(4,1)} %bitcast.7), calls=%async_computation.3 | async-start | bytes 8388608
  135.1 9.3 %copy-start.4 = (bf16[512,1024]{1,0:T(8,128)(2,1)S(1)}, bf16[512,1024]{1,0:T(8,128)(2,1)}, u32[]{:S(2)}) copy-start(bf16[512,1024]{1,0:T(8,128)(2,1)} %copy-done.2) | copy-start | bytes 3145732
  135.1 9.3 %copy-start.6 = (bf16[512,512]{1,0:T(8,128)(2,1)S(1)}, bf16[512,512]{1,0:T(8,128)(2,1)}, u32[]{:S(2)}) copy-start(bf16[512,512]{1,0:T(8,128)(2,1)} %copy-done.5) | copy-start | bytes 1572868
  135.1 9.3 %copy-start.12 = (bf16[512,512]{1,0:T(8,128)(2,1)S(1)}, bf16[512,512]{1,0:T(8,128)(2,1)}, u32[]{:S(2)}) copy-start(bf16[512,512]{1,0:T(8,128)(2,1)} %copy-done.11) | copy-start | bytes 1572868
  135.1 9.3 %copy-start.14 = (bf16[512,512]{1,0:T(8,128)(2,1)S(1)}, bf16[512,512]{1,0:T(8,128)(2,1)}, u32[]{:S(2)}) copy-start(bf16[512,512]{1,0:T(8,128)(2,1)} %copy-done.13) | copy-start | bytes 1572868
  135.1 9.3 %copy-start.16 = (bf16[512,512]{1,0:T(8,128)(2,1)S(1)}, bf16[512,512]{1,0:T(8,128)(2,1)}, u32[]{:S(2)}) copy-start(bf16[512,512]{1,0:T(8,128)(2,1)} %copy-done.15) | copy-start | bytes 1572868
  135.1 9.3 %copy-start.23 = (bf16[512,512]{1,0:T(8,128)(2,1)S(1)}, bf16[512,512]{1,0:T(8,128)(2,1)}, u32[]{:S(2)}) copy-start(bf16[512,512]{1,0:T(8,128)(2,1)} %copy-done.22) | copy-start | bytes 1572868
  139.3 5.1 %collective-permute-start.20 = (bf16[2,512,512]{2,1,0:T(8,128)(2,1)S(1)}, bf16[2,512,512]{2,1,0:T(8,128)(2,1)S(1)}, u32[]{:S(2)}, u32[]{:S(2)}) collective-permute-start(bf16[2,512,512]{2,1,0:T(8,128)(2,1)S(1)} %shard_map.61.refs_2_.refs_19_), channel_id=1, source_target_pairs={{0,8},{8,0},{16,24},{24,16},{1,9},{9,1},{17,25},{25,17},{2,10},{10... | collective-permute-start | bytes 3145736 | tf_op jit(solution)/shard_map/ppermute | solution.py:389
  139.4 15.5 %collective-permute-start.21 = (bf16[512,512]{1,0:T(8,128)(2,1)}, bf16[512,512]{1,0:T(8,128)(2,1)S(1)}, u32[]{:S(2)}, u32[]{:S(2)}) collective-permute-start(bf16[512,512]{1,0:T(8,128)(2,1)} %shard_map.59.refs_9_.refs_14_.refs_13_.refs_12_.refs_11_), channel_id=1, source_target_pairs={{0,2},{1,3},{2,4},{3,5},{4,6},{5,7},{8,10},{9,11},{10,12},{11,13},... | collective-permute-start | bytes 1572872 | tf_op jit(solution)/shard_map/ppermute | solution.py:398
  142.9 14.3 %collective-permute-start.22 = (bf16[512,512]{1,0:T(8,128)(2,1)}, bf16[512,512]{1,0:T(8,128)(2,1)S(1)}, u32[]{:S(2)}, u32[]{:S(2)}) collective-permute-start(bf16[512,512]{1,0:T(8,128)(2,1)} %shard_map.59.refs_9_.refs_14_.refs_13_.refs_12_.refs_11_), channel_id=1, source_target_pairs={{0,1},{1,0},{2,3},{3,2},{4,5},{5,4},{6,7},{7,6},{8,9},{9,8},{10,11... | collective-permute-start | bytes 1572872 | tf_op jit(solution)/shard_map/ppermute | solution.py:392
  157.7 14.1 %collective-permute-start.23 = (bf16[512,512]{1,0:T(8,128)(2,1)S(1)}, bf16[512,512]{1,0:T(8,128)(2,1)S(1)}, u32[]{:S(2)}, u32[]{:S(2)}) collective-permute-start(bf16[512,512]{1,0:T(8,128)(2,1)S(1)} %shard_map.64.refs_20_.refs_14_.refs_13_.refs_12_), channel_id=1, source_target_pairs={{0,2},{1,3},{2,4},{3,5},{4,6},{5,7},{8,10},{9,11},{10,12},{11,13},... | collective-permute-start | bytes 1572872 | tf_op jit(solution)/shard_map/ppermute | solution.py:398
  161.2 13.0 %collective-permute-start.24 = (bf16[512,512]{1,0:T(8,128)(2,1)S(1)}, bf16[512,512]{1,0:T(8,128)(2,1)S(1)}, u32[]{:S(2)}, u32[]{:S(2)}) collective-permute-start(bf16[512,512]{1,0:T(8,128)(2,1)S(1)} %shard_map.64.refs_20_.refs_14_.refs_13_.refs_12_), channel_id=1, source_target_pairs={{0,1},{1,0},{2,3},{3,2},{4,5},{5,4},{6,7},{7,6},{8,9},{9,8},{10,11... | collective-permute-start | bytes 1572872 | tf_op jit(solution)/shard_map/ppermute | solution.py:392
  174.7 10.7 %collective-permute-start.25 = (bf16[256,512]{1,0:T(8,128)(2,1)S(1)}, bf16[256,512]{1,0:T(8,128)(2,1)S(1)}, u32[]{:S(2)}, u32[]{:S(2)}) collective-permute-start(bf16[256,512]{1,0:T(8,128)(2,1)S(1)} %shard_map.66.refs_20_.refs_14_.refs_13_), channel_id=1, source_target_pairs={{0,2},{1,3},{2,4},{3,5},{4,6},{5,7},{8,10},{9,11},{10,12},{11,13},... | collective-permute-start | bytes 786440 | tf_op jit(solution)/shard_map/ppermute | solution.py:398
  178.0 7.4 %collective-permute-start.26 = (bf16[256,512]{1,0:T(8,128)(2,1)S(1)}, bf16[256,512]{1,0:T(8,128)(2,1)S(1)}, u32[]{:S(2)}, u32[]{:S(2)}) collective-permute-start(bf16[256,512]{1,0:T(8,128)(2,1)S(1)} %shard_map.66.refs_20_.refs_14_.refs_13_), channel_id=1, source_target_pairs={{0,1},{1,0},{2,3},{3,2},{4,5},{5,4},{6,7},{7,6},{8,9},{9,8},{10,11... | collective-permute-start | bytes 786440 | tf_op jit(solution)/shard_map/ppermute | solution.py:392
  186.0 6.4 %collective-permute-start.27 = (bf16[256,512]{1,0:T(8,128)(2,1)S(1)}, bf16[256,512]{1,0:T(8,128)(2,1)S(1)}, u32[]{:S(2)}, u32[]{:S(2)}) collective-permute-start(bf16[256,512]{1,0:T(8,128)(2,1)S(1)} %shard_map.68.refs_20_.refs_14_), channel_id=1, source_target_pairs={{0,1},{1,0},{2,3},{3,2},{4,5},{5,4},{6,7},{7,6},{8,9},{9,8},{10,11... | collective-permute-start | bytes 786440 | tf_op jit(solution)/shard_map/ppermute | solution.py:392
  (42 other events, 131.8 us)
Sparse Core Ops, SparseCore 0:
  53.9 43.0 all-gather.4
  98.8 18.1 all-gather.6

commit v4 on v3

--- a/solution.py
+++ b/solution.py
@@ -209,6 +209,21 @@
             out[1] = choices[2 * h + 1][...]
 
 
+def by_place_kernel(meta, *refs):
+    out = refs[-1]
+    for h, choice in enumerate(refs[:-1]):
+
+        @pl.when(lax.div(meta[2], 2) == h)
+        def _(choice=choice):
+            out[...] = choice[...]
+
+
+def stack_kernel(*refs):
+    *entries, out = refs
+    for i, entry in enumerate(entries):
+        out[i] = entry[...]
+
+
 def choose(hop, choices):
     value = flat(choices[0]).astype(F32)
     for h, other in enumerate(choices[1:], 1):
@@ -270,14 +285,16 @@
     top[...] = raw(shown, nb)
 
 
-def prep1_kernel(meta, lower, upper, up0, heads, *refs):
+def prep1_kernel(chips, meta, lower, upper, up0, heads, heads_sibling, *refs):
     *fresh, up1, up0_panel, top, work, head = refs
-    column = meta[2]
-    row_devices, _, part, nb = heads.shape
-    for r in range(row_devices):
-        at = (r % 2 * (row_devices // 2) + r // 2) * part
-        head[1, at : at + part] = heads[r, 0]
-        head[0, at : at + part] = heads[r, 1]
+    core, column, chip = meta[1], meta[2], meta[0] // 2
+    side = lax.rem(column, 2)
+    nb, part = work.shape[0], heads.shape[2]
+    for who, parts in ((core, heads), (1 - core, heads_sibling)):
+        for h in range(chips):
+            at = pl.multiple_of((who * chips + lax.rem(chip + chips - h, chips)) * part, part)
+            head[1 - side, pl.ds(at, part)] = parts[h, 0]
+            head[side, pl.ds(at, part)] = parts[h, 1]
     assemble(meta, 1, fresh, work)
     up0_panel[...] = dot(lower[0], head[0]).astype(BF16)
     factor = dot(head[1], upper[0]).astype(BF16)
@@ -449,6 +466,7 @@
         state.update(zip(("keep", "block0", "join", "arrive", "goal", "hops"), rest))
         state["sent"] = to_sibling(send)
         state["block0_sibling"] = to_sibling(state["block0"])
+        state["awaited"] = [state["block0_sibling"]]
 
     half = nb // 2
     part = half // chips
@@ -475,8 +493,26 @@
         state["fresh"] += [new, to_sibling(new)]
         state["brought"] += [brought, to_sibling(brought)]
         if head:
-            parts = lax.all_gather(head[0], "pcol")[:2]
-            state["heads"] = lax.all_gather(parts, "prow")
+            state["head"] = head + [
+                lax.ppermute(head[0], "pcol", [(0, 2 * h), (1, 2 * h + 1)]) for h in range(1, line)
+            ]
+            state["awaited"] = state.get("awaited", []) + state["head"][1:]
+
+    def head_here():
+        (mine,) = run(
+            by_place_kernel, [(meta, SMEM)] + [(v, VMEM) for v in state["head"]], [(bf16(part, nb), VMEM)], us=0.1
+        )
+        state["head"] = (mine, to_neighbour(mine))
+
+    def head_pair():
+        (pair,) = run(stack_kernel, [(v, VMEM) for v in state["head"]], [(bf16(2, part, nb), VMEM)], us=0.1)
+        state["head"] = [pair] + [to_chip(pair, h) for h in range(1, chips)]
+
+    def head_all():
+        (mine,) = run(
+            stack_kernel, [(v, VMEM) for v in state["head"]], [(bf16(chips, 2, part, nb), VMEM)], us=0.1
+        )
+        state["heads"] = (mine, to_sibling(mine))
 
     def old(values, name):
         operands = [(meta, SMEM)] + [(v, VMEM) for v in values[:line]]
@@ -511,9 +547,9 @@
 
     def prep1():
         state["up1"], state["up0_panel"], state["top1"] = run(
-            prep1_kernel,
-            [(meta, SMEM), (lower, VMEM), (upper, VMEM), (state["up0"], VMEM), (state["heads"], VMEM)]
-            + [(v, VMEM) for v in state["fresh"]],
+            functools.partial(prep1_kernel, chips),
+            [(meta, SMEM), (lower, VMEM), (upper, VMEM), (state["up0"], VMEM)]
+            + [(v, VMEM) for v in state["heads"]] + [(v, VMEM) for v in state["fresh"]],
             [(bf16(nb, cb * nb), VMEM), (bf16(nb, nb), VMEM), (bf16(nb, cb, nb), VMEM)],
             scratch=[pltpu.VMEM((nb, cb * nb), BF16), pltpu.VMEM((2, nb, nb), BF16)],
             us=3.5, mib=16,
@@ -541,7 +577,7 @@
             us=5.0, mib=24,
         )
 
-    plan = [(0, gather), (1, join), (2, functools.partial(fresh, 0)), (3, functools.partial(fresh, 1)), (line - 1, functools.partial(old, held, "old_held")), (line, functools.partial(old, other, "old_other")), (4, scatter), (4, prep0), (5, prep1), (5, old_here)]
+    plan = [(0, gather), (1, join), (2, functools.partial(fresh, 0)), (3, head_here), (line - 1, functools.partial(old, held, "old_held")), (3, head_pair), (3, functools.partial(fresh, 1)), (line, functools.partial(old, other, "old_other")), (4, head_all), (4, scatter), (4, prep0), (5, prep1), (5, old_here)]
     for i in range(pieces):
         plan.append((max((5, 5, 6, 7, 8, 8)[min(i, 5)], i + line - 1), functools.partial(update, i)))
     for k in range(last_step + 1):

time: 206 us -> 173 us (0.84)
  local copies, waits for them, and re-layouts: 28.6 us -> 3.74 us
  between operations: 14.3 us -> 0.66 us
  waiting for transfers between devices: 45.3 us -> 54.8 us
  Pallas kernels: 67.5 us -> 60.7 us
  starting transfers between devices: 48.9 us -> 52.8 us
    unnamed x120 -> x12, local copies, waits for them, and re-layouts: 26.7 us -> 3.55 us
    ppermute x9 -> x10, waiting for transfers between devices: 8.78 us -> 24.9 us  [to_neighbour(): return lax.ppermute(value, 'pcol', [(c, c ^ 1) for c in range(col_devices)])]
    all_gather x2 -> x0, waiting for transfers between devices: 13.2 us -> none  [the longest x1 13.2 us: fresh(): parts = lax.all_gather(head[0], 'pcol')[:2]]
    ppermute x0 -> x3, waiting for transfers between devices: none -> 8.95 us  [fresh(): lax.ppermute(head[0], 'pcol', [(0, 2 * h), (1, 2 * h + 1)])]
    pallas_call x25 -> x28, Pallas kernels: 67.5 us -> 60.7 us  [call(): pl.pallas_call(ordered, out_shape=tuple((shape for shape, _ in outs)), in...]
    ppermute x0 -> x3, starting transfers between devices: none -> 5.69 us  [fresh(): lax.ppermute(head[0], 'pcol', [(0, 2 * h), (1, 2 * h + 1)])]
    ppermute x9 -> x10, starting transfers between devices: 13.7 us -> 9.77 us  [to_neighbour(): return lax.ppermute(value, 'pcol', [(c, c ^ 1) for c in range(col_devices)])]
    ppermute x8, waiting for transfers between devices: 19.4 us -> 15.5 us  [to_next(): lax.ppermute(value, 'pcol', [(c, c + 2) for c in range(col_devices - 2)])]
  transfers between devices with their start and end apart: 30 -> 34, of which waited for: 12 -> 14; matrix products, arithmetic and copies ran while one was open for 1% -> 0% of each run, Pallas kernels for 26% -> 23%
where the time goes in v4:
time: 173 us
  Pallas kernels  60.7 us (35%)
  waiting for transfers between devices  54.8 us (32%)
  starting transfers between devices  52.8 us (31%)
  local copies, waits for them, and re-layouts  3.74 us (2%)
    pallas_call x28, Pallas kernels, call(): pl.pallas_call(ordered, out_shape=tuple((shape for shape, _ in outs)), in...  60.7 us
    ppermute x8, starting transfers between devices, to_next(): lax.ppermute(value, 'pcol', [(c, c + 2) for c in range(col_devices - 2)])  28.8 us
    ppermute x10, waiting for transfers between devices, to_neighbour(): return lax.ppermute(value, 'pcol', [(c, c ^ 1) for c in range(col_devices)])  24.9 us
    ppermute x8, waiting for transfers between devices, to_next(): lax.ppermute(value, 'pcol', [(c, c + 2) for c in range(col_devices - 2)])  15.5 us
    ppermute x10, starting transfers between devices, to_neighbour(): return lax.ppermute(value, 'pcol', [(c, c ^ 1) for c in range(col_devices)])  9.77 us
    ppermute x3, waiting for transfers between devices, fresh(): lax.ppermute(head[0], 'pcol', [(0, 2 * h), (1, 2 * h + 1)])  8.95 us
    ppermute x5, starting transfers between devices, to_chip(): lax.ppermute(value, 'prow', [(r, (r + 2 * h) % row_devices) for r in rang...  6.76 us
    ppermute x3, starting transfers between devices, fresh(): lax.ppermute(head[0], 'pcol', [(0, 2 * h), (1, 2 * h + 1)])  5.69 us
  transfers between devices with their start and end apart: 34, of which 14 were waited for; matrix products, arithmetic and copies ran while one was open for 0% of the time, Pallas kernels for 23%

profile of v4, /device:TPU:0, one launch (start us, length us, event | category | flops | bytes accessed | tf_op | source)
XLA Modules:
  0.0 172.8 jit_solution(2300404706745828855)
XLA Ops:
  0.0 2.2 %shard_map.46.refs_4_.refs_1_.refs_11_ = bf16[512,512]{1,0:T(8,128)(2,1)} custom-call(bf16[2560,2,512]{2,1,0:T(2,128)(2,1)} %bitcast.5), custom_call_target="tpu_custom_call" | custom-call | flops 1100000000 | tf_op jit(solution)/shard_map/pallas_call | solution.py:37
  2.5 2.5 %copy-done.1 = bf16[5,512,2,512]{3,2,1,0:T(2,128)(2,1)S(1)} copy-done((bf16[5,512,2,512]{3,2,1,0:T(2,128)(2,1)S(1)}, bf16[5,512,2,512]{3,2,1,0:T(2,128)(2,1)}, u32[]{:S(2)}) %copy-start.1) | copy-done | bytes 5242904
  5.0 1.0 copy-done.2
  6.0 7.7 %shard_map.47 = (bf16[512,512]{1,0:T(8,128)(2,1)S(1)}, bf16[512,512]{1,0:T(8,128)(2,1)S(1)}, bf16[512,512]{1,0:T(8,128)(2,1)S(1)}, bf16[256,512]{1,0:T(8,128)(2,...) custom-call(s32[4]{0:T(128)S(1)} %pad_add_fusion.refs_0_, ...), custom_call_target="tpu_custom_call" | custom-call | flops 8800000000 | tf_op jit(solution)/shard_map/pallas_call | solution.py:37
  14.3 2.6 %collective-permute-start.1 = (bf16[512,512]{1,0:T(8,128)(2,1)S(1)}, bf16[512,512]{1,0:T(8,128)(2,1)S(1)}, u32[]{:S(2)}, u32[]{:S(2)}) collective-permute-start(bf16[512,512]{1,0:T(8,128)(2,1)S(1)} %copy-done.2), channel_id=1, source_target_pairs={{0,1},{1,0},{2,3},{3,2},{4,5},{5,4},{6,7},{7,6},{8,9},{9,8},{10,11... | collective-permute-start | bytes 1572872 | tf_op jit(solution)/shard_map/ppermute | solution.py:409
  16.9 3.5 %collective-permute-start = (bf16[512,512]{1,0:T(8,128)(2,1)S(1)}, bf16[512,512]{1,0:T(8,128)(2,1)S(1)}, u32[]{:S(2)}, u32[]{:S(2)}) collective-permute-start(bf16[512,512]{1,0:T(8,128)(2,1)S(1)} %copy-done.2), channel_id=1, source_target_pairs={{0,2},{1,3},{2,4},{3,5},{4,6},{5,7},{8,10},{9,11},{10,12},{11,13},... | collective-permute-start | bytes 1572872 | tf_op jit(solution)/shard_map/ppermute | solution.py:415
  20.5 8.9 %collective-permute-done.1.refs_4_.refs_1_.refs_15_ = bf16[512,512]{1,0:T(8,128)(2,1)S(1)} collective-permute-done((bf16[512,512]{1,0:T(8,128)(2,1)S(1)}, bf16[512,512]{1,0:T(8,128)(2,1)S(1)}, u32[]{:S(2)}, u32[]{:S(2)}) %collective-permute-start.1) | collective-permute-done | bytes 524320 | tf_op jit(solution)/shard_map/ppermute | solution.py:409
  29.4 2.5 %collective-permute-done.refs_1_ = bf16[512,512]{1,0:T(8,128)(2,1)S(1)} collective-permute-done((bf16[512,512]{1,0:T(8,128)(2,1)S(1)}, bf16[512,512]{1,0:T(8,128)(2,1)S(1)}, u32[]{:S(2)}, u32[]{:S(2)}) %collective-permute-start) | collective-permute-done | bytes 524320 | tf_op jit(solution)/shard_map/ppermute | solution.py:415
  32.4 4.4 %collective-permute-start.3 = (bf16[512,512]{1,0:T(8,128)(2,1)S(1)}, bf16[512,512]{1,0:T(8,128)(2,1)S(1)}, u32[]{:S(2)}, u32[]{:S(2)}) collective-permute-start(bf16[512,512]{1,0:T(8,128)(2,1)S(1)} %shard_map.48.refs_4_.refs_2_.refs_12_.refs_11_), channel_id=1, source_target_pairs={{0,2},{1,3},{2,4},{3,5},{4,6},{5,7},{8,10},{9,11},{10,12},{11,13},... | collective-permute-start | bytes 1572872 | tf_op jit(solution)/shard_map/ppermute | solution.py:415
  37.4 2.4 %shard_map.49 = (bf16[256,2,512]{2,1,0:T(2,128)(2,1)S(1)}, bf16[256,2,512]{2,1,0:T(2,128)(2,1)S(1)}) custom-call(s32[4]{0:T(128)S(1)} %pad_add_fusion.refs_0_, s32[2,512]{1,0:T(2,128)S(1)} %get-tuple-element.46.refs_1_, bf16[512,2,512]{2,1,0:T(2,128)(2,1)S(1)} %get-tuple-element.47.refs_2_, bf16[512,2,512]{2,1,0:T(2,128)(2,1)S(1)} %collective-permute-done.4.refs_3_, ...), custom_call_target="tpu_custom_call" | custom-call | flops 2200000000 | tf_op jit(solution)/shard_map/pallas_call | solution.py:37
  39.8 1.6 collective-permute-start.7
  41.4 6.1 %collective-permute-done.3.refs_1_ = bf16[512,512]{1,0:T(8,128)(2,1)S(1)} collective-permute-done((bf16[512,512]{1,0:T(8,128)(2,1)S(1)}, bf16[512,512]{1,0:T(8,128)(2,1)S(1)}, u32[]{:S(2)}, u32[]{:S(2)}) %collective-permute-start.3) | collective-permute-done | bytes 524320 | tf_op jit(solution)/shard_map/ppermute | solution.py:415
  47.5 2.3 %collective-permute-done.5.refs_4_.refs_2_.refs_16_.refs_15_ = bf16[512,512]{1,0:T(8,128)(2,1)S(1)} collective-permute-done((bf16[512,512]{1,0:T(8,128)(2,1)S(1)}, bf16[512,512]{1,0:T(8,128)(2,1)S(1)}, u32[]{:S(2)}, u32[]{:S(2)}) %collective-permute-start.5) | collective-permute-done | bytes 524320 | tf_op jit(solution)/shard_map/ppermute | solution.py:409
  50.4 3.5 %collective-permute-start.6 = (bf16[512,512]{1,0:T(8,128)(2,1)S(1)}, bf16[512,512]{1,0:T(8,128)(2,1)S(1)}, u32[]{:S(2)}, u32[]{:S(2)}) collective-permute-start(bf16[512,512]{1,0:T(8,128)(2,1)S(1)} %shard_map.50.refs_4_.refs_3_.refs_13_.refs_12_.refs_11_), channel_id=1, source_target_pairs={{0,2},{1,3},{2,4},{3,5},{4,6},{5,7},{8,10},{9,11},{10,12},{11,13},... | collective-permute-start | bytes 1572872 | tf_op jit(solution)/shard_map/ppermute | solution.py:415
  54.5 1.1 shard_map.51
  55.6 3.1 %collective-permute-start.10 = (bf16[128,512]{1,0:T(8,128)(2,1)S(1)}, bf16[128,512]{1,0:T(8,128)(2,1)S(1)}, u32[]{:S(2)}, u32[]{:S(2)}) collective-permute-start(bf16[128,512]{1,0:T(8,128)(2,1)S(1)} %get-tuple-element.52.refs_3_.refs_1_), channel_id=1, source_target_pairs={{0,4},{1,5},{8,12},{9,13},{16,20},{17,21},{24,28},{25,29}} | collective-permute-start | bytes 393224 | tf_op jit(solution)/shard_map/ppermute | solution.py:497
  58.7 1.3 collective-permute-start.11
  60.0 1.3 collective-permute-start.9
  61.3 7.6 %collective-permute-done.10.refs_6_.refs_3_ = bf16[128,512]{1,0:T(8,128)(2,1)S(1)} collective-permute-done((bf16[128,512]{1,0:T(8,128)(2,1)S(1)}, bf16[128,512]{1,0:T(8,128)(2,1)S(1)}, u32[]{:S(2)}, u32[]{:S(2)}) %collective-permute-start.10) | collective-permute-done | bytes 131104 | tf_op jit(solution)/shard_map/ppermute | solution.py:497
  68.9 1.5 collective-permute-start.14
  70.4 1.3 collective-permute-done.9.refs_5_.refs_2_
  73.6 1.6 collective-permute-start.16
  75.6 4.4 %collective-permute-start.13 = (bf16[512,512]{1,0:T(8,128)(2,1)S(1)}, bf16[512,512]{1,0:T(8,128)(2,1)S(1)}, u32[]{:S(2)}, u32[]{:S(2)}) collective-permute-start(bf16[512,512]{1,0:T(8,128)(2,1)S(1)} %shard_map.52.refs_5_.refs_4_.refs_14_.refs_13_.refs_12_.refs_11_), channel_id=1, source_target_pairs={{0,2},{1,3},{2,4},{3,5},{4,6},{5,7},{8,10},{9,11},{10,12},{11,13},... | collective-permute-start | bytes 1572872 | tf_op jit(solution)/shard_map/ppermute | solution.py:415
  80.1 1.6 collective-permute-start.15
  81.6 7.1 %collective-permute-done.15.refs_1_ = bf16[128,512]{1,0:T(8,128)(2,1)S(1)} collective-permute-done((bf16[128,512]{1,0:T(8,128)(2,1)S(1)}, bf16[128,512]{1,0:T(8,128)(2,1)S(1)}, u32[]{:S(2)}, u32[]{:S(2)}) %collective-permute-start.15) | collective-permute-done | bytes 131104 | tf_op jit(solution)/shard_map/ppermute | solution.py:409
  89.3 1.1 shard_map.56
  92.8 4.4 %collective-permute-start.24 = (bf16[512,512]{1,0:T(8,128)(2,1)S(1)}, bf16[512,512]{1,0:T(8,128)(2,1)S(1)}, u32[]{:S(2)}, u32[]{:S(2)}) collective-permute-start(bf16[512,512]{1,0:T(8,128)(2,1)S(1)} %shard_map.57.refs_5_.refs_14_.refs_13_.refs_12_.refs_11_), channel_id=1, source_target_pairs={{0,2},{1,3},{2,4},{3,5},{4,6},{5,7},{8,10},{9,11},{10,12},{11,13},... | collective-permute-start | bytes 1572872 | tf_op jit(solution)/shard_map/ppermute | solution.py:415
  97.2 1.6 collective-permute-start.17
  99.4 4.1 %shard_map.60.refs_6_.refs_8_ = bf16[2568,2,512]{2,1,0:T(2,128)(2,1)S(1)} custom-call(s32[4]{0:T(128)S(1)} %pad_add_fusion.refs_0_, s32[2,512]{1,0:T(2,128)S(1)} %get-tuple-element.57.refs_1_, s32[2,512]{1,0:T(2,128)S(1)} %get-tuple-element.41.refs_2_.refs_1_, bf16[256,2,512]{2,1,0:T(2,128)(2,1)S(1)} %get-tuple-element.58.refs_3_, ...), custom_call_target="tpu_custom_call" | custom-call | flops 110000000 | tf_op jit(solution)/shard_map/pallas_call | solution.py:37
  103.6 2.0 %shard_map.61 = (bf16[512,1024]{1,0:T(8,128)(2,1)S(1)}, bf16[512,2,512]{2,1,0:T(2,128)(2,1)S(1)}) custom-call(s32[4]{0:T(128)S(1)} %pad_add_fusion.refs_0_, bf16[2,512,512]{2,1,0:T(8,128)(2,1)S(1)} %copy-done.4, bf16[256,1024]{1,0:T(8,128)(2,1)S(1)} %get-tuple-element.55.refs_2_.refs_6_, bf16[256,1024]{1,0:T(8,128)(2,1)S(1)} %collective-permute-done.18.refs_3_.refs_7_, ...), custom_call_target="tpu_custom_call" | custom-call | flops 2200000000 | tf_op jit(solution)/shard_map/pallas_call | solution.py:37
  105.5 5.3 %collective-permute-done.17.refs_5_.refs_4_ = bf16[512,512]{1,0:T(8,128)(2,1)S(1)} collective-permute-done((bf16[512,512]{1,0:T(8,128)(2,1)S(1)}, bf16[512,512]{1,0:T(8,128)(2,1)S(1)}, u32[]{:S(2)}, u32[]{:S(2)}) %collective-permute-start.17) | collective-permute-done | bytes 524320 | tf_op jit(solution)/shard_map/ppermute | solution.py:412
  110.9 1.2 collective-permute-done.25.refs_4_.refs_18_.refs_17_.refs_16_.refs_15_
  112.7 3.5 %shard_map.63 = (bf16[512,1024]{1,0:T(8,128)(2,1)S(1)}, bf16[512,512]{1,0:T(8,128)(2,1)S(1)}, bf16[512,2,512]{2,1,0:T(2,128)(2,1)S(1)}) custom-call(s32[4]{0:T(128)S(1)} %pad_add_fusion.refs_0_, bf16[2,512,512]{2,1,0:T(8,128)(2,1)S(1)} %copy-done.4, bf16[2,512,512]{2,1,0:T(8,128)(2,1)S(1)} %copy-done, ...), custom_call_target="tpu_custom_call" | custom-call | flops 3849999872 | tf_op jit(solution)/shard_map/pallas_call | solution.py:37
  116.9 4.0 %collective-permute-start.27 = (bf16[512,512]{1,0:T(8,128)(2,1)S(1)}, bf16[512,512]{1,0:T(8,128)(2,1)S(1)}, u32[]{:S(2)}, u32[]{:S(2)}) collective-permute-start(bf16[512,512]{1,0:T(8,128)(2,1)S(1)} %shard_map.62.refs_10_.refs_14_.refs_13_.refs_12_.refs_11_), channel_id=1, source_target_pairs={{0,2},{1,3},{2,4},{3,5},{4,6},{5,7},{8,10},{9,11},{10,12},{11,13},... | collective-permute-start | bytes 1572872 | tf_op jit(solution)/shard_map/ppermute | solution.py:415
  121.6 1.8 %shard_map.65 = (bf16[2560,2,512]{2,1,0:T(2,128)(2,1)}, f32[8,128]{1,0:T(8,128)S(1)}) custom-call(s32[4]{0:T(128)S(1)} %pad_add_fusion.refs_0_, s32[2,512]{1,0:T(2,128)S(1)} %get-tuple-element.41.refs_2_.refs_1_, bf16[2,512,512]{2,1,0:T(8,128)(2,1)S(1)} %shard_map.64.refs_2_.refs_19_, bf16[2,512,512]{2,1,0:T(8,128)(2,1)S(1)} %collective-permute-done.26.refs_3_, ...), custom_call_target="tpu_custom_call" | custom-call | flops 5500000256 | tf_op jit(solution)/shard_map/pallas_call | solution.py:37
  123.4 6.3 %shard_map.66 = (bf16[2560,2,512]{2,1,0:T(2,128)(2,1)}, f32[8,128]{1,0:T(8,128)S(1)}) custom-call(s32[4]{0:T(128)S(1)} %pad_add_fusion.refs_0_, s32[2,512]{1,0:T(2,128)S(1)} %get-tuple-element.41.refs_2_.refs_1_, bf16[2,512,512]{2,1,0:T(8,128)(2,1)S(1)} %shard_map.64.refs_2_.refs_19_, ...), custom_call_target="tpu_custom_call", output_to_operand_aliasing={{0}: (19, {})} | custom-call | flops 5500000256 | tf_op jit(solution)/shard_map/pallas_call | solution.py:37
  129.7 3.1 %collective-permute-done.27.refs_1_ = bf16[512,512]{1,0:T(8,128)(2,1)S(1)} collective-permute-done((bf16[512,512]{1,0:T(8,128)(2,1)S(1)}, bf16[512,512]{1,0:T(8,128)(2,1)S(1)}, u32[]{:S(2)}, u32[]{:S(2)}) %collective-permute-start.27) | collective-permute-done | bytes 524320 | tf_op jit(solution)/shard_map/ppermute | solution.py:415
  132.7 2.3 %collective-permute-done.28.refs_3_.refs_18_.refs_17_.refs_16_.refs_15_ = bf16[512,512]{1,0:T(8,128)(2,1)S(1)} collective-permute-done((bf16[512,512]{1,0:T(8,128)(2,1)S(1)}, bf16[512,512]{1,0:T(8,128)(2,1)S(1)}, u32[]{:S(2)}, u32[]{:S(2)}) %collective-permute-start.28) | collective-permute-done | bytes 524320 | tf_op jit(solution)/shard_map/ppermute | solution.py:409
  135.6 2.2 %collective-permute-start.29 = (bf16[512,512]{1,0:T(8,128)(2,1)S(1)}, bf16[512,512]{1,0:T(8,128)(2,1)S(1)}, u32[]{:S(2)}, u32[]{:S(2)}) collective-permute-start(bf16[512,512]{1,0:T(8,128)(2,1)S(1)} %shard_map.67.refs_20_.refs_14_.refs_13_.refs_12_), channel_id=1, source_target_pairs={{0,2},{1,3},{2,4},{3,5},{4,6},{5,7},{8,10},{9,11},{10,12},{11,13},... | collective-permute-start | bytes 1572872 | tf_op jit(solution)/shard_map/ppermute | solution.py:415
  138.5 6.5 %shard_map.68 = (bf16[2560,2,512]{2,1,0:T(2,128)(2,1)}, f32[8,128]{1,0:T(8,128)S(1)}) custom-call(s32[4]{0:T(128)S(1)} %pad_add_fusion.refs_0_, s32[2,512]{1,0:T(2,128)S(1)} %get-tuple-element.41.refs_2_.refs_1_, bf16[2,512,512]{2,1,0:T(8,128)(2,1)S(1)} %shard_map.64.refs_2_.refs_19_, ...), custom_call_target="tpu_custom_call", output_to_operand_aliasing={{0}: (19, {})} | custom-call | flops 5500000256 | tf_op jit(solution)/shard_map/pallas_call | solution.py:37
  144.9 3.9 %collective-permute-done.29.refs_1_ = bf16[512,512]{1,0:T(8,128)(2,1)S(1)} collective-permute-done((bf16[512,512]{1,0:T(8,128)(2,1)S(1)}, bf16[512,512]{1,0:T(8,128)(2,1)S(1)}, u32[]{:S(2)}, u32[]{:S(2)}) %collective-permute-start.29) | collective-permute-done | bytes 524320 | tf_op jit(solution)/shard_map/ppermute | solution.py:415
  148.8 2.3 %collective-permute-done.30.refs_3_.refs_18_.refs_17_.refs_16_ = bf16[512,512]{1,0:T(8,128)(2,1)S(1)} collective-permute-done((bf16[512,512]{1,0:T(8,128)(2,1)S(1)}, bf16[512,512]{1,0:T(8,128)(2,1)S(1)}, u32[]{:S(2)}, u32[]{:S(2)}) %collective-permute-start.30) | collective-permute-done | bytes 524320 | tf_op jit(solution)/shard_map/ppermute | solution.py:409
  151.7 2.3 %collective-permute-start.31 = (bf16[256,512]{1,0:T(8,128)(2,1)S(1)}, bf16[256,512]{1,0:T(8,128)(2,1)S(1)}, u32[]{:S(2)}, u32[]{:S(2)}) collective-permute-start(bf16[256,512]{1,0:T(8,128)(2,1)S(1)} %shard_map.69.refs_20_.refs_14_.refs_13_), channel_id=1, source_target_pairs={{0,2},{1,3},{2,4},{3,5},{4,6},{5,7},{8,10},{9,11},{10,12},{11,13},... | collective-permute-start | bytes 786440 | tf_op jit(solution)/shard_map/ppermute | solution.py:415
  154.6 6.2 %shard_map.70 = (bf16[2560,2,512]{2,1,0:T(2,128)(2,1)}, f32[8,128]{1,0:T(8,128)S(1)}) custom-call(s32[4]{0:T(128)S(1)} %pad_add_fusion.refs_0_, s32[2,512]{1,0:T(2,128)S(1)} %get-tuple-element.41.refs_2_.refs_1_, bf16[2,512,512]{2,1,0:T(8,128)(2,1)S(1)} %shard_map.64.refs_2_.refs_19_, ...), custom_call_target="tpu_custom_call", output_to_operand_aliasing={{0}: (19, {})} | custom-call | flops 5500000256 | tf_op jit(solution)/shard_map/pallas_call | solution.py:37
  161.5 1.5 collective-permute-start.33
  163.0 4.1 %shard_map.72 = (bf16[2560,2,512]{2,1,0:T(2,128)(2,1)}, f32[8,128]{1,0:T(8,128)S(1)}) custom-call(s32[4]{0:T(128)S(1)} %pad_add_fusion.refs_0_, s32[2,512]{1,0:T(2,128)S(1)} %get-tuple-element.41.refs_2_.refs_1_, bf16[2,512,512]{2,1,0:T(8,128)(2,1)S(1)} %shard_map.64.refs_2_.refs_19_, ...), custom_call_target="tpu_custom_call", output_to_operand_aliasing={{0}: (19, {})} | custom-call | flops 5500000256 | tf_op jit(solution)/shard_map/pallas_call | solution.py:37
  167.1 0.8 collective-permute-done.33.refs_18_
  167.9 4.7 %shard_map.73 = (bf16[2560,2,512]{2,1,0:T(2,128)(2,1)}, f32[8,128]{1,0:T(8,128)}) custom-call(s32[4]{0:T(128)S(1)} %pad_add_fusion.refs_0_, s32[2,512]{1,0:T(2,128)S(1)} %get-tuple-element.41.refs_2_.refs_1_, bf16[2,512,512]{2,1,0:T(8,128)(2,1)S(1)} %shard_map.64.refs_2_.refs_19_, ...), custom_call_target="tpu_custom_call", output_to_operand_aliasing={{0}: (19, {})} | custom-call | flops 5500000256 | tf_op jit(solution)/shard_map/pallas_call | solution.py:37
  (62 shorter events, 13.9 us)
Async XLA Ops:
  0.0 2.3 %copy-start.5 = (s32[2,512]{1,0:T(2,128)S(1)}, s32[2,512]{1,0:T(2,128)}, u32[]{:S(2)}) copy-start(s32[2,512]{1,0:T(2,128)} %refs_1_.3) | copy-start | bytes 12292
  2.5 2.5 %copy-start.1 = (bf16[5,512,2,512]{3,2,1,0:T(2,128)(2,1)S(1)}, bf16[5,512,2,512]{3,2,1,0:T(2,128)(2,1)}, u32[]{:S(2)}) copy-start(bf16[5,512,2,512]{3,2,1,0:T(2,128)(2,1)} %param.4) | copy-start | bytes 15728644
  5.0 1.0 copy-start.2
  13.8 18.1 %collective-permute-start.2 = (bf16[512,2,512]{2,1,0:T(2,128)(2,1)S(1)}, bf16[512,2,512]{2,1,0:T(2,128)(2,1)S(1)}, u32[]{:S(2)}, u32[]{:S(2)}) collective-permute-start(bf16[512,2,512]{2,1,0:T(2,128)(2,1)S(1)} %get-tuple-element.44.refs_7_), channel_id=1, source_target_pairs={{0,8},{8,0},{16,24},{24,16},{1,9},{9,1},{17,25},{25,17},{2,10},{10... | collective-permute-start | bytes 3145736 | tf_op jit(solution)/shard_map/ppermute | solution.py:406
  14.3 15.1 %collective-permute-start.1 = (bf16[512,512]{1,0:T(8,128)(2,1)S(1)}, bf16[512,512]{1,0:T(8,128)(2,1)S(1)}, u32[]{:S(2)}, u32[]{:S(2)}) collective-permute-start(bf16[512,512]{1,0:T(8,128)(2,1)S(1)} %copy-done.2), channel_id=1, source_target_pairs={{0,1},{1,0},{2,3},{3,2},{4,5},{5,4},{6,7},{7,6},{8,9},{9,8},{10,11... | collective-permute-start | bytes 1572872 | tf_op jit(solution)/shard_map/ppermute | solution.py:409
  16.9 15.0 %collective-permute-start = (bf16[512,512]{1,0:T(8,128)(2,1)S(1)}, bf16[512,512]{1,0:T(8,128)(2,1)S(1)}, u32[]{:S(2)}, u32[]{:S(2)}) collective-permute-start(bf16[512,512]{1,0:T(8,128)(2,1)S(1)} %copy-done.2), channel_id=1, source_target_pairs={{0,2},{1,3},{2,4},{3,5},{4,6},{5,7},{8,10},{9,11},{10,12},{11,13},... | collective-permute-start | bytes 1572872 | tf_op jit(solution)/shard_map/ppermute | solution.py:415
  20.4 17.1 %collective-permute-start.4 = (bf16[512,2,512]{2,1,0:T(2,128)(2,1)S(1)}, bf16[512,2,512]{2,1,0:T(2,128)(2,1)S(1)}, u32[]{:S(2)}, u32[]{:S(2)}) collective-permute-start(bf16[512,2,512]{2,1,0:T(2,128)(2,1)S(1)} %get-tuple-element.48), channel_id=1, source_target_pairs={{0,8},{8,0},{16,24},{24,16},{1,9},{9,1},{17,25},{25,17},{2,10},{10... | collective-permute-start | bytes 3145736 | tf_op jit(solution)/shard_map/ppermute | solution.py:406
  32.4 15.1 %collective-permute-start.3 = (bf16[512,512]{1,0:T(8,128)(2,1)S(1)}, bf16[512,512]{1,0:T(8,128)(2,1)S(1)}, u32[]{:S(2)}, u32[]{:S(2)}) collective-permute-start(bf16[512,512]{1,0:T(8,128)(2,1)S(1)} %shard_map.48.refs_4_.refs_2_.refs_12_.refs_11_), channel_id=1, source_target_pairs={{0,2},{1,3},{2,4},{3,5},{4,6},{5,7},{8,10},{9,11},{10,12},{11,13},... | collective-permute-start | bytes 1572872 | tf_op jit(solution)/shard_map/ppermute | solution.py:415
  36.9 13.0 %collective-permute-start.5 = (bf16[512,512]{1,0:T(8,128)(2,1)S(1)}, bf16[512,512]{1,0:T(8,128)(2,1)S(1)}, u32[]{:S(2)}, u32[]{:S(2)}) collective-permute-start(bf16[512,512]{1,0:T(8,128)(2,1)S(1)} %shard_map.48.refs_4_.refs_2_.refs_12_.refs_11_), channel_id=1, source_target_pairs={{0,1},{1,0},{2,3},{3,2},{4,5},{5,4},{6,7},{7,6},{8,9},{9,8},{10,11... | collective-permute-start | bytes 1572872 | tf_op jit(solution)/shard_map/ppermute | solution.py:409
  39.8 14.6 %collective-permute-start.7 = (bf16[256,2,512]{2,1,0:T(2,128)(2,1)S(1)}, bf16[256,2,512]{2,1,0:T(2,128)(2,1)S(1)}, u32[]{:S(2)}, u32[]{:S(2)}) collective-permute-start(bf16[256,2,512]{2,1,0:T(2,128)(2,1)S(1)} %get-tuple-element.51.refs_2_), channel_id=1, source_target_pairs={{0,16},{8,24},{16,0},{24,8},{1,17},{9,25},{17,1},{25,9},{2,18},{10... | collective-permute-start | bytes 1572872 | tf_op jit(solution)/shard_map/ppermute | solution.py:412
  50.4 21.4 %collective-permute-start.6 = (bf16[512,512]{1,0:T(8,128)(2,1)S(1)}, bf16[512,512]{1,0:T(8,128)(2,1)S(1)}, u32[]{:S(2)}, u32[]{:S(2)}) collective-permute-start(bf16[512,512]{1,0:T(8,128)(2,1)S(1)} %shard_map.50.refs_4_.refs_3_.refs_13_.refs_12_.refs_11_), channel_id=1, source_target_pairs={{0,2},{1,3},{2,4},{3,5},{4,6},{5,7},{8,10},{9,11},{10,12},{11,13},... | collective-permute-start | bytes 1572872 | tf_op jit(solution)/shard_map/ppermute | solution.py:415
  53.9 17.9 %collective-permute-start.8 = (bf16[512,512]{1,0:T(8,128)(2,1)S(1)}, bf16[512,512]{1,0:T(8,128)(2,1)S(1)}, u32[]{:S(2)}, u32[]{:S(2)}) collective-permute-start(bf16[512,512]{1,0:T(8,128)(2,1)S(1)} %shard_map.50.refs_4_.refs_3_.refs_13_.refs_12_.refs_11_), channel_id=1, source_target_pairs={{0,1},{1,0},{2,3},{3,2},{4,5},{5,4},{6,7},{7,6},{8,9},{9,8},{10,11... | collective-permute-start | bytes 1572872 | tf_op jit(solution)/shard_map/ppermute | solution.py:409
  55.6 13.3 %collective-permute-start.10 = (bf16[128,512]{1,0:T(8,128)(2,1)S(1)}, bf16[128,512]{1,0:T(8,128)(2,1)S(1)}, u32[]{:S(2)}, u32[]{:S(2)}) collective-permute-start(bf16[128,512]{1,0:T(8,128)(2,1)S(1)} %get-tuple-element.52.refs_3_.refs_1_), channel_id=1, source_target_pairs={{0,4},{1,5},{8,12},{9,13},{16,20},{17,21},{24,28},{25,29}} | collective-permute-start | bytes 393224 | tf_op jit(solution)/shard_map/ppermute | solution.py:497
  58.7 11.7 %collective-permute-start.11 = (bf16[128,512]{1,0:T(8,128)(2,1)S(1)}, bf16[128,512]{1,0:T(8,128)(2,1)S(1)}, u32[]{:S(2)}, u32[]{:S(2)}) collective-permute-start(bf16[128,512]{1,0:T(8,128)(2,1)S(1)} %get-tuple-element.52.refs_3_.refs_1_), channel_id=1, source_target_pairs={{0,6},{1,7},{8,14},{9,15},{16,22},{17,23},{24,30},{25,31}} | collective-permute-start | bytes 393224 | tf_op jit(solution)/shard_map/ppermute | solution.py:497
  60.0 11.7 %collective-permute-start.9 = (bf16[128,512]{1,0:T(8,128)(2,1)S(1)}, bf16[128,512]{1,0:T(8,128)(2,1)S(1)}, u32[]{:S(2)}, u32[]{:S(2)}) collective-permute-start(bf16[128,512]{1,0:T(8,128)(2,1)S(1)} %get-tuple-element.52.refs_3_.refs_1_), channel_id=1, source_target_pairs={{0,2},{1,3},{8,10},{9,11},{16,18},{17,19},{24,26},{25,27}} | collective-permute-start | bytes 393224 | tf_op jit(solution)/shard_map/ppermute | solution.py:497
  68.9 19.8 %collective-permute-start.14 = (bf16[256,2,512]{2,1,0:T(2,128)(2,1)S(1)}, bf16[256,2,512]{2,1,0:T(2,128)(2,1)S(1)}, u32[]{:S(2)}, u32[]{:S(2)}) collective-permute-start(bf16[256,2,512]{2,1,0:T(2,128)(2,1)S(1)} %get-tuple-element.49.refs_3_.refs_2_), channel_id=1, source_target_pairs={{0,16},{8,24},{16,0},{24,8},{1,17},{9,25},{17,1},{25,9},{2,18},{10... | collective-permute-start | bytes 1572872 | tf_op jit(solution)/shard_map/ppermute | solution.py:412
  73.6 16.9 %collective-permute-start.16 = (bf16[512,512]{1,0:T(8,128)(2,1)S(1)}, bf16[512,512]{1,0:T(8,128)(2,1)S(1)}, u32[]{:S(2)}, u32[]{:S(2)}) collective-permute-start(bf16[512,512]{1,0:T(8,128)(2,1)S(1)} %shard_map.54.refs_2_.refs_1_), channel_id=1, source_target_pairs={{0,16},{8,24},{16,0},{24,8},{1,17},{9,25},{17,1},{25,9},{2,18},{10... | collective-permute-start | bytes 1572872 | tf_op jit(solution)/shard_map/ppermute | solution.py:412
  75.1 15.9 %collective-permute-start.12 = (bf16[512,512]{1,0:T(8,128)(2,1)S(1)}, bf16[512,512]{1,0:T(8,128)(2,1)S(1)}, u32[]{:S(2)}, u32[]{:S(2)}) collective-permute-start(bf16[512,512]{1,0:T(8,128)(2,1)S(1)} %shard_map.52.refs_5_.refs_4_.refs_14_.refs_13_.refs_12_.refs_11_), channel_id=1, source_target_pairs={{0,1},{1,0},{2,3},{3,2},{4,5},{5,4},{6,7},{7,6},{8,9},{9,8},{10,11... | collective-permute-start | bytes 1572872 | tf_op jit(solution)/shard_map/ppermute | solution.py:409
  75.6 15.4 %collective-permute-start.13 = (bf16[512,512]{1,0:T(8,128)(2,1)S(1)}, bf16[512,512]{1,0:T(8,128)(2,1)S(1)}, u32[]{:S(2)}, u32[]{:S(2)}) collective-permute-start(bf16[512,512]{1,0:T(8,128)(2,1)S(1)} %shard_map.52.refs_5_.refs_4_.refs_14_.refs_13_.refs_12_.refs_11_), channel_id=1, source_target_pairs={{0,2},{1,3},{2,4},{3,5},{4,6},{5,7},{8,10},{9,11},{10,12},{11,13},... | collective-permute-start | bytes 1572872 | tf_op jit(solution)/shard_map/ppermute | solution.py:415
  80.1 8.7 %collective-permute-start.15 = (bf16[128,512]{1,0:T(8,128)(2,1)S(1)}, bf16[128,512]{1,0:T(8,128)(2,1)S(1)}, u32[]{:S(2)}, u32[]{:S(2)}) collective-permute-start(bf16[128,512]{1,0:T(8,128)(2,1)S(1)} %shard_map.53.refs_5_.refs_0_), channel_id=1, source_target_pairs={{0,1},{1,0},{2,3},{3,2},{4,5},{5,4},{6,7},{7,6},{8,9},{9,8},{10,11... | collective-permute-start | bytes 393224 | tf_op jit(solution)/shard_map/ppermute | solution.py:409
  88.7 4.1 %collective-permute-start.20 = (bf16[256,2,512]{2,1,0:T(2,128)(2,1)S(1)}, bf16[256,2,512]{2,1,0:T(2,128)(2,1)S(1)}, u32[]{:S(2)}, u32[]{:S(2)}) collective-permute-start(bf16[256,2,512]{2,1,0:T(2,128)(2,1)S(1)} %get-tuple-element.58.refs_3_), channel_id=1, source_target_pairs={{0,8},{8,0},{16,24},{24,16},{1,9},{9,1},{17,25},{25,17},{2,10},{10... | collective-permute-start | bytes 1572872 | tf_op jit(solution)/shard_map/ppermute | solution.py:406
  88.7 8.4 %collective-permute-start.18 = (bf16[256,1024]{1,0:T(8,128)(2,1)S(1)}, bf16[256,1024]{1,0:T(8,128)(2,1)S(1)}, u32[]{:S(2)}, u32[]{:S(2)}) collective-permute-start(bf16[256,1024]{1,0:T(8,128)(2,1)S(1)} %get-tuple-element.55.refs_2_.refs_6_), channel_id=1, source_target_pairs={{0,8},{8,0},{16,24},{24,16},{1,9},{9,1},{17,25},{25,17},{2,10},{10... | collective-permute-start | bytes 1572872 | tf_op jit(solution)/shard_map/ppermute | solution.py:406
  90.4 8.3 %collective-permute-start.22 = (bf16[2,128,512]{2,1,0:T(8,128)(2,1)S(1)}, bf16[2,128,512]{2,1,0:T(8,128)(2,1)S(1)}, u32[]{:S(2)}, u32[]{:S(2)}) collective-permute-start(bf16[2,128,512]{2,1,0:T(8,128)(2,1)S(1)} %shard_map.55.refs_4_.refs_0_), channel_id=1, source_target_pairs={{0,16},{8,24},{16,0},{24,8},{1,17},{9,25},{17,1},{25,9},{2,18},{10... | collective-permute-start | bytes 786440 | tf_op jit(solution)/shard_map/ppermute | solution.py:412
  91.0 8.3 %collective-permute-start.21 = (bf16[256,2,512]{2,1,0:T(2,128)(2,1)S(1)}, bf16[256,2,512]{2,1,0:T(2,128)(2,1)S(1)}, u32[]{:S(2)}, u32[]{:S(2)}) collective-permute-start(bf16[256,2,512]{2,1,0:T(2,128)(2,1)S(1)} %get-tuple-element.54.refs_3_.refs_5_), channel_id=1, source_target_pairs={{0,8},{8,0},{16,24},{24,16},{1,9},{9,1},{17,25},{25,17},{2,10},{10... | collective-permute-start | bytes 1572872 | tf_op jit(solution)/shard_map/ppermute | solution.py:406
  91.1 12.5 %collective-permute-start.19 = (bf16[256,1024]{1,0:T(8,128)(2,1)S(1)}, bf16[256,1024]{1,0:T(8,128)(2,1)S(1)}, u32[]{:S(2)}, u32[]{:S(2)}) collective-permute-start(bf16[256,1024]{1,0:T(8,128)(2,1)S(1)} %get-tuple-element.56.refs_4_.refs_8_), channel_id=1, source_target_pairs={{0,8},{8,0},{16,24},{24,16},{1,9},{9,1},{17,25},{25,17},{2,10},{10... | collective-permute-start | bytes 1572872 | tf_op jit(solution)/shard_map/ppermute | solution.py:406
  92.8 18.1 %collective-permute-start.24 = (bf16[512,512]{1,0:T(8,128)(2,1)S(1)}, bf16[512,512]{1,0:T(8,128)(2,1)S(1)}, u32[]{:S(2)}, u32[]{:S(2)}) collective-permute-start(bf16[512,512]{1,0:T(8,128)(2,1)S(1)} %shard_map.57.refs_5_.refs_14_.refs_13_.refs_12_.refs_11_), channel_id=1, source_target_pairs={{0,2},{1,3},{2,4},{3,5},{4,6},{5,7},{8,10},{9,11},{10,12},{11,13},... | collective-permute-start | bytes 1572872 | tf_op jit(solution)/shard_map/ppermute | solution.py:415
  97.2 13.7 %collective-permute-start.17 = (bf16[512,512]{1,0:T(8,128)(2,1)S(1)}, bf16[512,512]{1,0:T(8,128)(2,1)S(1)}, u32[]{:S(2)}, u32[]{:S(2)}) collective-permute-start(bf16[512,512]{1,0:T(8,128)(2,1)S(1)} %shard_map.58.refs_2_), channel_id=1, source_target_pairs={{0,16},{8,24},{16,0},{24,8},{1,17},{9,25},{17,1},{25,9},{2,18},{10... | collective-permute-start | bytes 1572872 | tf_op jit(solution)/shard_map/ppermute | solution.py:412
  98.7 13.3 %collective-permute-start.25 = (bf16[512,512]{1,0:T(8,128)(2,1)S(1)}, bf16[512,512]{1,0:T(8,128)(2,1)S(1)}, u32[]{:S(2)}, u32[]{:S(2)}) collective-permute-start(bf16[512,512]{1,0:T(8,128)(2,1)S(1)} %shard_map.57.refs_5_.refs_14_.refs_13_.refs_12_.refs_11_), channel_id=1, source_target_pairs={{0,1},{1,0},{2,3},{3,2},{4,5},{5,4},{6,7},{7,6},{8,9},{9,8},{10,11... | collective-permute-start | bytes 1572872 | tf_op jit(solution)/shard_map/ppermute | solution.py:409
  99.3 13.3 %collective-permute-start.23 = (bf16[2,2,128,512]{3,2,1,0:T(8,128)(2,1)S(1)}, bf16[2,2,128,512]{3,2,1,0:T(8,128)(2,1)S(1)}, u32[]{:S(2)}, u32[]{:S(2)}) collective-permute-start(bf16[2,2,128,512]{3,2,1,0:T(8,128)(2,1)S(1)} %shard_map.59.refs_10_.refs_4_), channel_id=1, source_target_pairs={{0,8},{8,0},{16,24},{24,16},{1,9},{9,1},{17,25},{25,17},{2,10},{10... | collective-permute-start | bytes 1572872 | tf_op jit(solution)/shard_map/ppermute | solution.py:406
  99.4 4.1 %copy-start.4 = (bf16[2,512,512]{2,1,0:T(8,128)(2,1)S(1)}, bf16[2,512,512]{2,1,0:T(8,128)(2,1)}, u32[]{:S(2)}) copy-start(bf16[2,512,512]{2,1,0:T(8,128)(2,1)} %refs_1_.5) | copy-start | bytes 3145732
  103.5 9.1 %copy-start = (bf16[2,512,512]{2,1,0:T(8,128)(2,1)S(1)}, bf16[2,512,512]{2,1,0:T(8,128)(2,1)}, u32[]{:S(2)}) copy-start(bf16[2,512,512]{2,1,0:T(8,128)(2,1)} %refs_4_.11) | copy-start | bytes 3145732
  112.7 8.9 %copy-start.3 = (bf16[512,512]{1,0:T(8,128)(2,1)S(1)}, bf16[512,512]{1,0:T(8,128)(2,1)}, u32[]{:S(2)}) copy-start(bf16[512,512]{1,0:T(8,128)(2,1)} %shard_map.46.refs_4_.refs_1_.refs_11_) | copy-start | bytes 1572868
  116.8 4.8 %collective-permute-start.26 = (bf16[2,512,512]{2,1,0:T(8,128)(2,1)S(1)}, bf16[2,512,512]{2,1,0:T(8,128)(2,1)S(1)}, u32[]{:S(2)}, u32[]{:S(2)}) collective-permute-start(bf16[2,512,512]{2,1,0:T(8,128)(2,1)S(1)} %shard_map.64.refs_2_.refs_19_), channel_id=1, source_target_pairs={{0,8},{8,0},{16,24},{24,16},{1,9},{9,1},{17,25},{25,17},{2,10},{10... | collective-permute-start | bytes 3145736 | tf_op jit(solution)/shard_map/ppermute | solution.py:406
  116.9 15.8 %collective-permute-start.27 = (bf16[512,512]{1,0:T(8,128)(2,1)S(1)}, bf16[512,512]{1,0:T(8,128)(2,1)S(1)}, u32[]{:S(2)}, u32[]{:S(2)}) collective-permute-start(bf16[512,512]{1,0:T(8,128)(2,1)S(1)} %shard_map.62.refs_10_.refs_14_.refs_13_.refs_12_.refs_11_), channel_id=1, source_target_pairs={{0,2},{1,3},{2,4},{3,5},{4,6},{5,7},{8,10},{9,11},{10,12},{11,13},... | collective-permute-start | bytes 1572872 | tf_op jit(solution)/shard_map/ppermute | solution.py:415
  120.9 14.1 %collective-permute-start.28 = (bf16[512,512]{1,0:T(8,128)(2,1)S(1)}, bf16[512,512]{1,0:T(8,128)(2,1)S(1)}, u32[]{:S(2)}, u32[]{:S(2)}) collective-permute-start(bf16[512,512]{1,0:T(8,128)(2,1)S(1)} %shard_map.62.refs_10_.refs_14_.refs_13_.refs_12_.refs_11_), channel_id=1, source_target_pairs={{0,1},{1,0},{2,3},{3,2},{4,5},{5,4},{6,7},{7,6},{8,9},{9,8},{10,11... | collective-permute-start | bytes 1572872 | tf_op jit(solution)/shard_map/ppermute | solution.py:409
  135.6 13.2 %collective-permute-start.29 = (bf16[512,512]{1,0:T(8,128)(2,1)S(1)}, bf16[512,512]{1,0:T(8,128)(2,1)S(1)}, u32[]{:S(2)}, u32[]{:S(2)}) collective-permute-start(bf16[512,512]{1,0:T(8,128)(2,1)S(1)} %shard_map.67.refs_20_.refs_14_.refs_13_.refs_12_), channel_id=1, source_target_pairs={{0,2},{1,3},{2,4},{3,5},{4,6},{5,7},{8,10},{9,11},{10,12},{11,13},... | collective-permute-start | bytes 1572872 | tf_op jit(solution)/shard_map/ppermute | solution.py:415
  137.8 13.3 %collective-permute-start.30 = (bf16[512,512]{1,0:T(8,128)(2,1)S(1)}, bf16[512,512]{1,0:T(8,128)(2,1)S(1)}, u32[]{:S(2)}, u32[]{:S(2)}) collective-permute-start(bf16[512,512]{1,0:T(8,128)(2,1)S(1)} %shard_map.67.refs_20_.refs_14_.refs_13_.refs_12_), channel_id=1, source_target_pairs={{0,1},{1,0},{2,3},{3,2},{4,5},{5,4},{6,7},{7,6},{8,9},{9,8},{10,11... | collective-permute-start | bytes 1572872 | tf_op jit(solution)/shard_map/ppermute | solution.py:409
  151.7 9.2 %collective-permute-start.31 = (bf16[256,512]{1,0:T(8,128)(2,1)S(1)}, bf16[256,512]{1,0:T(8,128)(2,1)S(1)}, u32[]{:S(2)}, u32[]{:S(2)}) collective-permute-start(bf16[256,512]{1,0:T(8,128)(2,1)S(1)} %shard_map.69.refs_20_.refs_14_.refs_13_), channel_id=1, source_target_pairs={{0,2},{1,3},{2,4},{3,5},{4,6},{5,7},{8,10},{9,11},{10,12},{11,13},... | collective-permute-start | bytes 786440 | tf_op jit(solution)/shard_map/ppermute | solution.py:415
  154.0 6.9 %collective-permute-start.32 = (bf16[256,512]{1,0:T(8,128)(2,1)S(1)}, bf16[256,512]{1,0:T(8,128)(2,1)S(1)}, u32[]{:S(2)}, u32[]{:S(2)}) collective-permute-start(bf16[256,512]{1,0:T(8,128)(2,1)S(1)} %shard_map.69.refs_20_.refs_14_.refs_13_), channel_id=1, source_target_pairs={{0,1},{1,0},{2,3},{3,2},{4,5},{5,4},{6,7},{7,6},{8,9},{9,8},{10,11... | collective-permute-start | bytes 786440 | tf_op jit(solution)/shard_map/ppermute | solution.py:409
  161.5 6.4 %collective-permute-start.33 = (bf16[256,512]{1,0:T(8,128)(2,1)S(1)}, bf16[256,512]{1,0:T(8,128)(2,1)S(1)}, u32[]{:S(2)}, u32[]{:S(2)}) collective-permute-start(bf16[256,512]{1,0:T(8,128)(2,1)S(1)} %shard_map.71.refs_20_.refs_14_), channel_id=1, source_target_pairs={{0,1},{1,0},{2,3},{3,2},{4,5},{5,4},{6,7},{7,6},{8,9},{9,8},{10,11... | collective-permute-start | bytes 786440 | tf_op jit(solution)/shard_map/ppermute | solution.py:409

commit v5 on v4

--- a/solution.py
+++ b/solution.py
@@ -446,7 +446,8 @@
             (value,) = run(relay_kernel, operands, [step_out(k)], also, us=0.2 if k in (2, 3, 5) else 12.0)
         held.append(value)
         if k < last_step:
-            state["came"] = to_next(value)
+            sent = max(sizes[k - p] for p in range(line - 1) if 0 <= k - p < pieces)
+            state["came"] = to_next(value[:sent])
         other.append(to_neighbour(value))
 
     def gather():
@@ -466,7 +467,6 @@
         state.update(zip(("keep", "block0", "join", "arrive", "goal", "hops"), rest))
         state["sent"] = to_sibling(send)
         state["block0_sibling"] = to_sibling(state["block0"])
-        state["awaited"] = [state["block0_sibling"]]
 
     half = nb // 2
     part = half // chips
@@ -481,6 +481,7 @@
         )
         state["choices"] = [[v] + [to_chip(v, h) for h in range(1, chips)] for v in joined]
         state["fresh"], state["brought"] = [], []
+        state["awaited"] = [state["block0_sibling"]]
 
     def fresh(turn):
         new, brought, *head = run(
@@ -518,7 +519,8 @@
         operands = [(meta, SMEM)] + [(v, VMEM) for v in values[:line]]
         (mine,) = run(functools.partial(old_kernel, line), operands, [(bf16(nb, nb), VMEM)], us=0.1)
         state[name] = [mine] + [to_chip(mine, h) for h in range(1, chips)]
-        state["awaited"] = state.get("awaited", []) + state[name][1:]
+        if name == "old_held":
+            state["awaited"] = state.get("awaited", []) + state[name][1:]
 
     def old_here():
         choices = [v for pair in zip(state["old_held"], state["old_other"]) for v in pair]
@@ -579,7 +581,7 @@
 
     plan = [(0, gather), (1, join), (2, functools.partial(fresh, 0)), (3, head_here), (line - 1, functools.partial(old, held, "old_held")), (3, head_pair), (3, functools.partial(fresh, 1)), (line, functools.partial(old, other, "old_other")), (4, head_all), (4, scatter), (4, prep0), (5, prep1), (5, old_here)]
     for i in range(pieces):
-        plan.append((max((5, 5, 6, 7, 8, 8)[min(i, 5)], i + line - 1), functools.partial(update, i)))
+        plan.append((max((6, 6, 7, 7, 8, 8)[min(i, 5)], i + line - 1), functools.partial(update, i)))
     for k in range(last_step + 1):
         step(k)
         while plan and (plan[0][0] <= k or k == last_step):

time: 173 us -> 164 us (0.948); the launches traced: 173 us -> 161 us
  waiting for transfers between devices: 54.8 us -> 47.7 us
  starting transfers between devices: 52.8 us -> 48.8 us
    ppermute x10, waiting for transfers between devices: 24.9 us -> 16.3 us  [to_neighbour(): return lax.ppermute(value, 'pcol', [(c, c ^ 1) for c in range(col_devices)])]
    ppermute x8, waiting for transfers between devices: 15.5 us -> 19.8 us  [to_next(): lax.ppermute(value, 'pcol', [(c, c + 2) for c in range(col_devices - 2)])]
    ppermute x3, waiting for transfers between devices: 8.95 us -> 4.82 us  [fresh(): lax.ppermute(head[0], 'pcol', [(0, 2 * h), (1, 2 * h + 1)])]
    ppermute x8, starting transfers between devices: 28.8 us -> 26.5 us  [to_next(): lax.ppermute(value, 'pcol', [(c, c + 2) for c in range(col_devices - 2)])]
  transfers between devices with their start and end apart: 34 -> 34, of which waited for: 14 -> 14; matrix products, arithmetic and copies ran while one was open for 0% -> 0% of each run, Pallas kernels for 23% -> 33%
where the time goes in v5:
time: 164 us; the launch traced here: 161 us
  Pallas kernels  60.4 us (37%)
  starting transfers between devices  48.8 us (30%)
  waiting for transfers between devices  47.7 us (29%)
  local copies, waits for them, and re-layouts  3.76 us (2%)
    pallas_call x28, Pallas kernels, call(): pl.pallas_call(ordered, out_shape=tuple((shape for shape, _ in outs)), in...  60.4 us
    ppermute x8, starting transfers between devices, to_next(): lax.ppermute(value, 'pcol', [(c, c + 2) for c in range(col_devices - 2)])  26.5 us
    ppermute x8, waiting for transfers between devices, to_next(): lax.ppermute(value, 'pcol', [(c, c + 2) for c in range(col_devices - 2)])  19.8 us
    ppermute x10, waiting for transfers between devices, to_neighbour(): return lax.ppermute(value, 'pcol', [(c, c ^ 1) for c in range(col_devices)])  16.3 us
    ppermute x10, starting transfers between devices, to_neighbour(): return lax.ppermute(value, 'pcol', [(c, c ^ 1) for c in range(col_devices)])  10.1 us
    ppermute x5, waiting for transfers between devices, to_chip(): lax.ppermute(value, 'prow', [(r, (r + 2 * h) % row_devices) for r in rang...  6.8 us
    ppermute x5, starting transfers between devices, to_chip(): lax.ppermute(value, 'prow', [(r, (r + 2 * h) % row_devices) for r in rang...  6.03 us
    ppermute x3, waiting for transfers between devices, fresh(): lax.ppermute(head[0], 'pcol', [(0, 2 * h), (1, 2 * h + 1)])  4.82 us
  transfers between devices with their start and end apart: 34, of which 14 were waited for; matrix products, arithmetic and copies ran while one was open for 0% of the time, Pallas kernels for 33%

profile of v5, /device:TPU:0, one launch (start us, length us, event | category | flops | bytes accessed | tf_op | source)
XLA Modules:
  0.0 161.4 jit_solution(306273562892889135)
XLA Ops:
  0.0 2.2 %shard_map.46.refs_4_.refs_1_.refs_11_ = bf16[512,512]{1,0:T(8,128)(2,1)} custom-call(bf16[2560,2,512]{2,1,0:T(2,128)(2,1)} %bitcast.5), custom_call_target="tpu_custom_call" | custom-call | flops 1100000000 | tf_op jit(solution)/shard_map/pallas_call | solution.py:37
  2.2 3.0 %collective-permute-start.1 = (bf16[512,512]{1,0:T(8,128)(2,1)}, bf16[512,512]{1,0:T(8,128)(2,1)S(1)}, u32[]{:S(2)}, u32[]{:S(2)}) collective-permute-start(bf16[512,512]{1,0:T(8,128)(2,1)} %shard_map.46.refs_4_.refs_1_.refs_11_), channel_id=1, source_target_pairs={{0,1},{1,0},{2,3},{3,2},{4,5},{5,4},{6,7},{7,6},{8,9},{9,8},{10,11... | collective-permute-start | bytes 1572872 | tf_op jit(solution)/shard_map/ppermute | solution.py:409
  5.2 3.5 %collective-permute-start = (bf16[512,512]{1,0:T(8,128)(2,1)}, bf16[512,512]{1,0:T(8,128)(2,1)S(1)}, u32[]{:S(2)}, u32[]{:S(2)}) collective-permute-start(bf16[512,512]{1,0:T(8,128)(2,1)} %shard_map.46.refs_4_.refs_1_.refs_11_), channel_id=1, source_target_pairs={{0,2},{1,3},{2,4},{3,5},{4,6},{5,7},{8,10},{9,11},{10,12},{11,13},... | collective-permute-start | bytes 1572872 | tf_op jit(solution)/shard_map/ppermute | solution.py:415
  9.0 2.5 %copy-done.1 = bf16[5,512,2,512]{3,2,1,0:T(2,128)(2,1)S(1)} copy-done((bf16[5,512,2,512]{3,2,1,0:T(2,128)(2,1)S(1)}, bf16[5,512,2,512]{3,2,1,0:T(2,128)(2,1)}, u32[]{:S(2)}) %copy-start.1) | copy-done | bytes 5242904
  11.5 1.0 copy-done.2
  12.5 7.7 %shard_map.47 = (bf16[512,512]{1,0:T(8,128)(2,1)S(1)}, bf16[512,512]{1,0:T(8,128)(2,1)S(1)}, bf16[512,512]{1,0:T(8,128)(2,1)S(1)}, bf16[256,512]{1,0:T(8,128)(2,...) custom-call(s32[4]{0:T(128)S(1)} %pad_add_fusion.refs_0_, ...), custom_call_target="tpu_custom_call" | custom-call | flops 8800000000 | tf_op jit(solution)/shard_map/pallas_call | solution.py:37
  21.5 3.5 %collective-permute-start.2 = (bf16[512,512]{1,0:T(8,128)(2,1)S(1)}, bf16[512,512]{1,0:T(8,128)(2,1)S(1)}, u32[]{:S(2)}, u32[]{:S(2)}) collective-permute-start(bf16[512,512]{1,0:T(8,128)(2,1)S(1)} %shard_map.48.refs_4_.refs_2_.refs_12_.refs_11_), channel_id=1, source_target_pairs={{0,2},{1,3},{2,4},{3,5},{4,6},{5,7},{8,10},{9,11},{10,12},{11,13},... | collective-permute-start | bytes 1572872 | tf_op jit(solution)/shard_map/ppermute | solution.py:415
  25.5 2.4 %shard_map.49 = (bf16[256,2,512]{2,1,0:T(2,128)(2,1)S(1)}, bf16[256,2,512]{2,1,0:T(2,128)(2,1)S(1)}) custom-call(s32[4]{0:T(128)S(1)} %pad_add_fusion.refs_0_, s32[2,512]{1,0:T(2,128)S(1)} %get-tuple-element.45.refs_1_, bf16[512,2,512]{2,1,0:T(2,128)(2,1)S(1)} %get-tuple-element.46.refs_2_, bf16[512,2,512]{2,1,0:T(2,128)(2,1)S(1)} %collective-permute-done.3.refs_3_, ...), custom_call_target="tpu_custom_call" | custom-call | flops 2200000000 | tf_op jit(solution)/shard_map/pallas_call | solution.py:37
  27.9 1.6 collective-permute-start.7
  29.5 6.8 %collective-permute-done.2.refs_1_ = bf16[512,512]{1,0:T(8,128)(2,1)S(1)} collective-permute-done((bf16[512,512]{1,0:T(8,128)(2,1)S(1)}, bf16[512,512]{1,0:T(8,128)(2,1)S(1)}, u32[]{:S(2)}, u32[]{:S(2)}) %collective-permute-start.2) | collective-permute-done | bytes 524320 | tf_op jit(solution)/shard_map/ppermute | solution.py:415
  36.3 2.3 %collective-permute-done.4.refs_4_.refs_2_.refs_16_.refs_15_ = bf16[512,512]{1,0:T(8,128)(2,1)S(1)} collective-permute-done((bf16[512,512]{1,0:T(8,128)(2,1)S(1)}, bf16[512,512]{1,0:T(8,128)(2,1)S(1)}, u32[]{:S(2)}, u32[]{:S(2)}) %collective-permute-start.4) | collective-permute-done | bytes 524320 | tf_op jit(solution)/shard_map/ppermute | solution.py:409
  39.3 3.5 %collective-permute-start.6 = (bf16[512,512]{1,0:T(8,128)(2,1)S(1)}, bf16[512,512]{1,0:T(8,128)(2,1)S(1)}, u32[]{:S(2)}, u32[]{:S(2)}) collective-permute-start(bf16[512,512]{1,0:T(8,128)(2,1)S(1)} %shard_map.50.refs_4_.refs_3_.refs_13_.refs_12_.refs_11_), channel_id=1, source_target_pairs={{0,2},{1,3},{2,4},{3,5},{4,6},{5,7},{8,10},{9,11},{10,12},{11,13},... | collective-permute-start | bytes 1572872 | tf_op jit(solution)/shard_map/ppermute | solution.py:415
  43.3 1.1 shard_map.51
  44.5 1.8 %collective-permute-start.10 = (bf16[128,512]{1,0:T(8,128)(2,1)S(1)}, bf16[128,512]{1,0:T(8,128)(2,1)S(1)}, u32[]{:S(2)}, u32[]{:S(2)}) collective-permute-start(bf16[128,512]{1,0:T(8,128)(2,1)S(1)} %get-tuple-element.52.refs_3_.refs_1_), channel_id=1, source_target_pairs={{0,4},{1,5},{8,12},{9,13},{16,20},{17,21},{24,28},{25,29}} | collective-permute-start | bytes 393224 | tf_op jit(solution)/shard_map/ppermute | solution.py:498
  46.3 1.3 collective-permute-start.11
  47.6 1.3 collective-permute-start.9
  48.9 6.2 %collective-permute-done.6.refs_1_ = bf16[512,512]{1,0:T(8,128)(2,1)S(1)} collective-permute-done((bf16[512,512]{1,0:T(8,128)(2,1)S(1)}, bf16[512,512]{1,0:T(8,128)(2,1)S(1)}, u32[]{:S(2)}, u32[]{:S(2)}) %collective-permute-start.6) | collective-permute-done | bytes 524320 | tf_op jit(solution)/shard_map/ppermute | solution.py:415
  55.1 1.5 collective-permute-start.14
  56.6 1.3 collective-permute-done.10.refs_6_.refs_3_
  57.9 2.1 %collective-permute-done.11.refs_7_.refs_4_ = bf16[128,512]{1,0:T(8,128)(2,1)S(1)} collective-permute-done((bf16[128,512]{1,0:T(8,128)(2,1)S(1)}, bf16[128,512]{1,0:T(8,128)(2,1)S(1)}, u32[]{:S(2)}, u32[]{:S(2)}) %collective-permute-start.11) | collective-permute-done | bytes 131104 | tf_op jit(solution)/shard_map/ppermute | solution.py:498
  60.0 1.4 collective-permute-done.9.refs_5_.refs_2_
  63.2 1.6 collective-permute-start.16
  65.3 4.4 %collective-permute-start.13 = (bf16[512,512]{1,0:T(8,128)(2,1)S(1)}, bf16[512,512]{1,0:T(8,128)(2,1)S(1)}, u32[]{:S(2)}, u32[]{:S(2)}) collective-permute-start(bf16[512,512]{1,0:T(8,128)(2,1)S(1)} %shard_map.52.refs_5_.refs_4_.refs_14_.refs_13_.refs_12_.refs_11_), channel_id=1, source_target_pairs={{0,2},{1,3},{2,4},{3,5},{4,6},{5,7},{8,10},{9,11},{10,12},{11,13},... | collective-permute-start | bytes 1572872 | tf_op jit(solution)/shard_map/ppermute | solution.py:415
  69.7 1.6 collective-permute-start.15
  71.3 7.9 %collective-permute-done.15.refs_1_ = bf16[128,512]{1,0:T(8,128)(2,1)S(1)} collective-permute-done((bf16[128,512]{1,0:T(8,128)(2,1)S(1)}, bf16[128,512]{1,0:T(8,128)(2,1)S(1)}, u32[]{:S(2)}, u32[]{:S(2)}) %collective-permute-start.15) | collective-permute-done | bytes 131104 | tf_op jit(solution)/shard_map/ppermute | solution.py:409
  79.7 1.1 shard_map.56
  82.5 6.6 %collective-permute-done.22.refs_1_ = bf16[2,128,512]{2,1,0:T(8,128)(2,1)S(1)} collective-permute-done((bf16[2,128,512]{2,1,0:T(8,128)(2,1)S(1)}, bf16[2,128,512]{2,1,0:T(8,128)(2,1)S(1)}, u32[]{:S(2)}, u32[]{:S(2)}) %collective-permute-start.22) | collective-permute-done | bytes 262176 | tf_op jit(solution)/shard_map/ppermute | solution.py:412
  89.1 4.4 %collective-permute-start.24 = (bf16[512,512]{1,0:T(8,128)(2,1)S(1)}, bf16[512,512]{1,0:T(8,128)(2,1)S(1)}, u32[]{:S(2)}, u32[]{:S(2)}) collective-permute-start(bf16[512,512]{1,0:T(8,128)(2,1)S(1)} %shard_map.57.refs_5_.refs_14_.refs_13_.refs_12_.refs_11_), channel_id=1, source_target_pairs={{0,2},{1,3},{2,4},{3,5},{4,6},{5,7},{8,10},{9,11},{10,12},{11,13},... | collective-permute-start | bytes 1572872 | tf_op jit(solution)/shard_map/ppermute | solution.py:415
  94.9 4.1 %shard_map.60.refs_6_.refs_8_ = bf16[2568,2,512]{2,1,0:T(2,128)(2,1)S(1)} custom-call(s32[4]{0:T(128)S(1)} %pad_add_fusion.refs_0_, s32[2,512]{1,0:T(2,128)S(1)} %get-tuple-element.57.refs_1_, s32[2,512]{1,0:T(2,128)S(1)} %get-tuple-element.41.refs_2_.refs_1_, bf16[256,2,512]{2,1,0:T(2,128)(2,1)S(1)} %get-tuple-element.58.refs_3_, ...), custom_call_target="tpu_custom_call" | custom-call | flops 110000000 | tf_op jit(solution)/shard_map/pallas_call | solution.py:37
  99.0 0.8 collective-permute-start.17
  99.9 2.0 %shard_map.61 = (bf16[512,1024]{1,0:T(8,128)(2,1)S(1)}, bf16[512,2,512]{2,1,0:T(2,128)(2,1)S(1)}) custom-call(s32[4]{0:T(128)S(1)} %pad_add_fusion.refs_0_, bf16[2,512,512]{2,1,0:T(8,128)(2,1)S(1)} %copy-done.4, bf16[256,1024]{1,0:T(8,128)(2,1)S(1)} %get-tuple-element.55.refs_2_.refs_6_, bf16[256,1024]{1,0:T(8,128)(2,1)S(1)} %collective-permute-done.18.refs_3_.refs_7_, ...), custom_call_target="tpu_custom_call" | custom-call | flops 2200000000 | tf_op jit(solution)/shard_map/pallas_call | solution.py:37
  101.8 2.2 %collective-permute-done.24.refs_1_ = bf16[512,512]{1,0:T(8,128)(2,1)S(1)} collective-permute-done((bf16[512,512]{1,0:T(8,128)(2,1)S(1)}, bf16[512,512]{1,0:T(8,128)(2,1)S(1)}, u32[]{:S(2)}, u32[]{:S(2)}) %collective-permute-start.24) | collective-permute-done | bytes 524320 | tf_op jit(solution)/shard_map/ppermute | solution.py:415
  104.0 2.3 %collective-permute-done.25.refs_4_.refs_18_.refs_17_.refs_16_.refs_15_ = bf16[512,512]{1,0:T(8,128)(2,1)S(1)} collective-permute-done((bf16[512,512]{1,0:T(8,128)(2,1)S(1)}, bf16[512,512]{1,0:T(8,128)(2,1)S(1)}, u32[]{:S(2)}, u32[]{:S(2)}) %collective-permute-start.25) | collective-permute-done | bytes 524320 | tf_op jit(solution)/shard_map/ppermute | solution.py:409
  106.9 2.2 %collective-permute-start.27 = (bf16[512,512]{1,0:T(8,128)(2,1)S(1)}, bf16[512,512]{1,0:T(8,128)(2,1)S(1)}, u32[]{:S(2)}, u32[]{:S(2)}) collective-permute-start(bf16[512,512]{1,0:T(8,128)(2,1)S(1)} %shard_map.62.refs_10_.refs_14_.refs_13_.refs_12_.refs_11_), channel_id=1, source_target_pairs={{0,2},{1,3},{2,4},{3,5},{4,6},{5,7},{8,10},{9,11},{10,12},{11,13},... | collective-permute-start | bytes 1572872 | tf_op jit(solution)/shard_map/ppermute | solution.py:415
  109.7 3.5 %shard_map.63 = (bf16[512,1024]{1,0:T(8,128)(2,1)S(1)}, bf16[512,512]{1,0:T(8,128)(2,1)S(1)}, bf16[512,2,512]{2,1,0:T(2,128)(2,1)S(1)}) custom-call(s32[4]{0:T(128)S(1)} %pad_add_fusion.refs_0_, bf16[2,512,512]{2,1,0:T(8,128)(2,1)S(1)} %copy-done.4, bf16[2,512,512]{2,1,0:T(8,128)(2,1)S(1)} %copy-done, ...), custom_call_target="tpu_custom_call" | custom-call | flops 3849999872 | tf_op jit(solution)/shard_map/pallas_call | solution.py:37
  114.1 4.6 %collective-permute-done.27.refs_1_ = bf16[512,512]{1,0:T(8,128)(2,1)S(1)} collective-permute-done((bf16[512,512]{1,0:T(8,128)(2,1)S(1)}, bf16[512,512]{1,0:T(8,128)(2,1)S(1)}, u32[]{:S(2)}, u32[]{:S(2)}) %collective-permute-start.27) | collective-permute-done | bytes 524320 | tf_op jit(solution)/shard_map/ppermute | solution.py:415
  118.7 2.3 %collective-permute-done.28.refs_3_.refs_18_.refs_17_.refs_16_.refs_15_ = bf16[512,512]{1,0:T(8,128)(2,1)S(1)} collective-permute-done((bf16[512,512]{1,0:T(8,128)(2,1)S(1)}, bf16[512,512]{1,0:T(8,128)(2,1)S(1)}, u32[]{:S(2)}, u32[]{:S(2)}) %collective-permute-start.28) | collective-permute-done | bytes 524320 | tf_op jit(solution)/shard_map/ppermute | solution.py:409
  122.2 2.4 %collective-permute-start.29 = (bf16[256,512]{1,0:T(8,128)(2,1)S(1)}, bf16[256,512]{1,0:T(8,128)(2,1)S(1)}, u32[]{:S(2)}, u32[]{:S(2)}) collective-permute-start(bf16[256,512]{1,0:T(8,128)(2,1)S(1)} %slice.4), channel_id=1, source_target_pairs={{0,2},{1,3},{2,4},{3,5},{4,6},{5,7},{8,10},{9,11},{10,12},{11,13},... | collective-permute-start | bytes 786440 | tf_op jit(solution)/shard_map/ppermute | solution.py:415
  124.6 1.8 %shard_map.66 = (bf16[2560,2,512]{2,1,0:T(2,128)(2,1)}, f32[8,128]{1,0:T(8,128)S(1)}) custom-call(s32[4]{0:T(128)S(1)} %pad_add_fusion.refs_0_, s32[2,512]{1,0:T(2,128)S(1)} %get-tuple-element.41.refs_2_.refs_1_, bf16[2,512,512]{2,1,0:T(8,128)(2,1)S(1)} %shard_map.64.refs_2_, bf16[2,512,512]{2,1,0:T(8,128)(2,1)S(1)} %collective-permute-done.26.refs_3_, ...), custom_call_target="tpu_custom_call" | custom-call | flops 5500000256 | tf_op jit(solution)/shard_map/pallas_call | solution.py:37
  126.4 6.2 %shard_map.67 = (bf16[2560,2,512]{2,1,0:T(2,128)(2,1)}, f32[8,128]{1,0:T(8,128)S(1)}) custom-call(s32[4]{0:T(128)S(1)} %pad_add_fusion.refs_0_, s32[2,512]{1,0:T(2,128)S(1)} %get-tuple-element.41.refs_2_.refs_1_, bf16[2,512,512]{2,1,0:T(8,128)(2,1)S(1)} %shard_map.64.refs_2_, ...), custom_call_target="tpu_custom_call", output_to_operand_aliasing={{0}: (19, {})} | custom-call | flops 5500000256 | tf_op jit(solution)/shard_map/pallas_call | solution.py:37
  133.2 2.6 %collective-permute-start.31 = (bf16[256,512]{1,0:T(8,128)(2,1)S(1)}, bf16[256,512]{1,0:T(8,128)(2,1)S(1)}, u32[]{:S(2)}, u32[]{:S(2)}) collective-permute-start(bf16[256,512]{1,0:T(8,128)(2,1)S(1)} %shard_map.68.refs_20_.refs_14_.refs_13_), channel_id=1, source_target_pairs={{0,2},{1,3},{2,4},{3,5},{4,6},{5,7},{8,10},{9,11},{10,12},{11,13},... | collective-permute-start | bytes 786440 | tf_op jit(solution)/shard_map/ppermute | solution.py:415
  135.8 1.2 collective-permute-start.32
  137.0 6.4 %shard_map.69 = (bf16[2560,2,512]{2,1,0:T(2,128)(2,1)}, f32[8,128]{1,0:T(8,128)S(1)}) custom-call(s32[4]{0:T(128)S(1)} %pad_add_fusion.refs_0_, s32[2,512]{1,0:T(2,128)S(1)} %get-tuple-element.41.refs_2_.refs_1_, bf16[2,512,512]{2,1,0:T(8,128)(2,1)S(1)} %shard_map.64.refs_2_, ...), custom_call_target="tpu_custom_call", output_to_operand_aliasing={{0}: (19, {})} | custom-call | flops 5500000256 | tf_op jit(solution)/shard_map/pallas_call | solution.py:37
  143.4 6.2 %shard_map.70 = (bf16[2560,2,512]{2,1,0:T(2,128)(2,1)}, f32[8,128]{1,0:T(8,128)S(1)}) custom-call(s32[4]{0:T(128)S(1)} %pad_add_fusion.refs_0_, s32[2,512]{1,0:T(2,128)S(1)} %get-tuple-element.41.refs_2_.refs_1_, bf16[2,512,512]{2,1,0:T(8,128)(2,1)S(1)} %shard_map.64.refs_2_, ...), custom_call_target="tpu_custom_call", output_to_operand_aliasing={{0}: (19, {})} | custom-call | flops 5500000256 | tf_op jit(solution)/shard_map/pallas_call | solution.py:37
  150.2 1.0 collective-permute-start.33
  151.1 4.0 %shard_map.72 = (bf16[2560,2,512]{2,1,0:T(2,128)(2,1)}, f32[8,128]{1,0:T(8,128)S(1)}) custom-call(s32[4]{0:T(128)S(1)} %pad_add_fusion.refs_0_, s32[2,512]{1,0:T(2,128)S(1)} %get-tuple-element.41.refs_2_.refs_1_, bf16[2,512,512]{2,1,0:T(8,128)(2,1)S(1)} %shard_map.64.refs_2_, ...), custom_call_target="tpu_custom_call", output_to_operand_aliasing={{0}: (19, {})} | custom-call | flops 5500000256 | tf_op jit(solution)/shard_map/pallas_call | solution.py:37
  155.2 1.4 collective-permute-done.33.refs_18_
  156.6 4.6 %shard_map.73 = (bf16[2560,2,512]{2,1,0:T(2,128)(2,1)}, f32[8,128]{1,0:T(8,128)}) custom-call(s32[4]{0:T(128)S(1)} %pad_add_fusion.refs_0_, s32[2,512]{1,0:T(2,128)S(1)} %get-tuple-element.41.refs_2_.refs_1_, bf16[2,512,512]{2,1,0:T(8,128)(2,1)S(1)} %shard_map.64.refs_2_, ...), custom_call_target="tpu_custom_call", output_to_operand_aliasing={{0}: (19, {})} | custom-call | flops 5500000256 | tf_op jit(solution)/shard_map/pallas_call | solution.py:37
  (63 shorter events, 13.4 us)
Async XLA Ops:
  0.0 8.8 %copy-start.5 = (s32[2,512]{1,0:T(2,128)S(1)}, s32[2,512]{1,0:T(2,128)}, u32[]{:S(2)}) copy-start(s32[2,512]{1,0:T(2,128)} %refs_1_.3) | copy-start | bytes 12292
  2.2 18.7 %collective-permute-start.1 = (bf16[512,512]{1,0:T(8,128)(2,1)}, bf16[512,512]{1,0:T(8,128)(2,1)S(1)}, u32[]{:S(2)}, u32[]{:S(2)}) collective-permute-start(bf16[512,512]{1,0:T(8,128)(2,1)} %shard_map.46.refs_4_.refs_1_.refs_11_), channel_id=1, source_target_pairs={{0,1},{1,0},{2,3},{3,2},{4,5},{5,4},{6,7},{7,6},{8,9},{9,8},{10,11... | collective-permute-start | bytes 1572872 | tf_op jit(solution)/shard_map/ppermute | solution.py:409
  5.2 15.7 %collective-permute-start = (bf16[512,512]{1,0:T(8,128)(2,1)}, bf16[512,512]{1,0:T(8,128)(2,1)S(1)}, u32[]{:S(2)}, u32[]{:S(2)}) collective-permute-start(bf16[512,512]{1,0:T(8,128)(2,1)} %shard_map.46.refs_4_.refs_1_.refs_11_), channel_id=1, source_target_pairs={{0,2},{1,3},{2,4},{3,5},{4,6},{5,7},{8,10},{9,11},{10,12},{11,13},... | collective-permute-start | bytes 1572872 | tf_op jit(solution)/shard_map/ppermute | solution.py:415
  9.0 2.5 %copy-start.1 = (bf16[5,512,2,512]{3,2,1,0:T(2,128)(2,1)S(1)}, bf16[5,512,2,512]{3,2,1,0:T(2,128)(2,1)}, u32[]{:S(2)}) copy-start(bf16[5,512,2,512]{3,2,1,0:T(2,128)(2,1)} %param.4) | copy-start | bytes 15728644
  11.5 1.0 copy-start.2
  20.3 5.2 %collective-permute-start.3 = (bf16[512,2,512]{2,1,0:T(2,128)(2,1)S(1)}, bf16[512,2,512]{2,1,0:T(2,128)(2,1)S(1)}, u32[]{:S(2)}, u32[]{:S(2)}) collective-permute-start(bf16[512,2,512]{2,1,0:T(2,128)(2,1)S(1)} %get-tuple-element.47), channel_id=1, source_target_pairs={{0,8},{8,0},{16,24},{24,16},{1,9},{9,1},{17,25},{25,17},{2,10},{10... | collective-permute-start | bytes 3145736 | tf_op jit(solution)/shard_map/ppermute | solution.py:406
  20.4 18.3 %collective-permute-start.5 = (bf16[512,2,512]{2,1,0:T(2,128)(2,1)S(1)}, bf16[512,2,512]{2,1,0:T(2,128)(2,1)S(1)}, u32[]{:S(2)}, u32[]{:S(2)}) collective-permute-start(bf16[512,2,512]{2,1,0:T(2,128)(2,1)S(1)} %get-tuple-element.49.refs_7_), channel_id=1, source_target_pairs={{0,8},{8,0},{16,24},{24,16},{1,9},{9,1},{17,25},{25,17},{2,10},{10... | collective-permute-start | bytes 3145736 | tf_op jit(solution)/shard_map/ppermute | solution.py:406
  21.5 14.9 %collective-permute-start.2 = (bf16[512,512]{1,0:T(8,128)(2,1)S(1)}, bf16[512,512]{1,0:T(8,128)(2,1)S(1)}, u32[]{:S(2)}, u32[]{:S(2)}) collective-permute-start(bf16[512,512]{1,0:T(8,128)(2,1)S(1)} %shard_map.48.refs_4_.refs_2_.refs_12_.refs_11_), channel_id=1, source_target_pairs={{0,2},{1,3},{2,4},{3,5},{4,6},{5,7},{8,10},{9,11},{10,12},{11,13},... | collective-permute-start | bytes 1572872 | tf_op jit(solution)/shard_map/ppermute | solution.py:415
  25.0 13.7 %collective-permute-start.4 = (bf16[512,512]{1,0:T(8,128)(2,1)S(1)}, bf16[512,512]{1,0:T(8,128)(2,1)S(1)}, u32[]{:S(2)}, u32[]{:S(2)}) collective-permute-start(bf16[512,512]{1,0:T(8,128)(2,1)S(1)} %shard_map.48.refs_4_.refs_2_.refs_12_.refs_11_), channel_id=1, source_target_pairs={{0,1},{1,0},{2,3},{3,2},{4,5},{5,4},{6,7},{7,6},{8,9},{9,8},{10,11... | collective-permute-start | bytes 1572872 | tf_op jit(solution)/shard_map/ppermute | solution.py:409
  27.9 15.4 %collective-permute-start.7 = (bf16[256,2,512]{2,1,0:T(2,128)(2,1)S(1)}, bf16[256,2,512]{2,1,0:T(2,128)(2,1)S(1)}, u32[]{:S(2)}, u32[]{:S(2)}) collective-permute-start(bf16[256,2,512]{2,1,0:T(2,128)(2,1)S(1)} %get-tuple-element.51.refs_2_), channel_id=1, source_target_pairs={{0,16},{8,24},{16,0},{24,8},{1,17},{9,25},{17,1},{25,9},{2,18},{10... | collective-permute-start | bytes 1572872 | tf_op jit(solution)/shard_map/ppermute | solution.py:412
  39.3 15.8 %collective-permute-start.6 = (bf16[512,512]{1,0:T(8,128)(2,1)S(1)}, bf16[512,512]{1,0:T(8,128)(2,1)S(1)}, u32[]{:S(2)}, u32[]{:S(2)}) collective-permute-start(bf16[512,512]{1,0:T(8,128)(2,1)S(1)} %shard_map.50.refs_4_.refs_3_.refs_13_.refs_12_.refs_11_), channel_id=1, source_target_pairs={{0,2},{1,3},{2,4},{3,5},{4,6},{5,7},{8,10},{9,11},{10,12},{11,13},... | collective-permute-start | bytes 1572872 | tf_op jit(solution)/shard_map/ppermute | solution.py:415
  42.7 13.8 %collective-permute-start.8 = (bf16[512,512]{1,0:T(8,128)(2,1)S(1)}, bf16[512,512]{1,0:T(8,128)(2,1)S(1)}, u32[]{:S(2)}, u32[]{:S(2)}) collective-permute-start(bf16[512,512]{1,0:T(8,128)(2,1)S(1)} %shard_map.50.refs_4_.refs_3_.refs_13_.refs_12_.refs_11_), channel_id=1, source_target_pairs={{0,1},{1,0},{2,3},{3,2},{4,5},{5,4},{6,7},{7,6},{8,9},{9,8},{10,11... | collective-permute-start | bytes 1572872 | tf_op jit(solution)/shard_map/ppermute | solution.py:409
  44.5 13.4 %collective-permute-start.10 = (bf16[128,512]{1,0:T(8,128)(2,1)S(1)}, bf16[128,512]{1,0:T(8,128)(2,1)S(1)}, u32[]{:S(2)}, u32[]{:S(2)}) collective-permute-start(bf16[128,512]{1,0:T(8,128)(2,1)S(1)} %get-tuple-element.52.refs_3_.refs_1_), channel_id=1, source_target_pairs={{0,4},{1,5},{8,12},{9,13},{16,20},{17,21},{24,28},{25,29}} | collective-permute-start | bytes 393224 | tf_op jit(solution)/shard_map/ppermute | solution.py:498
  46.3 13.7 %collective-permute-start.11 = (bf16[128,512]{1,0:T(8,128)(2,1)S(1)}, bf16[128,512]{1,0:T(8,128)(2,1)S(1)}, u32[]{:S(2)}, u32[]{:S(2)}) collective-permute-start(bf16[128,512]{1,0:T(8,128)(2,1)S(1)} %get-tuple-element.52.refs_3_.refs_1_), channel_id=1, source_target_pairs={{0,6},{1,7},{8,14},{9,15},{16,22},{17,23},{24,30},{25,31}} | collective-permute-start | bytes 393224 | tf_op jit(solution)/shard_map/ppermute | solution.py:498
  47.6 13.8 %collective-permute-start.9 = (bf16[128,512]{1,0:T(8,128)(2,1)S(1)}, bf16[128,512]{1,0:T(8,128)(2,1)S(1)}, u32[]{:S(2)}, u32[]{:S(2)}) collective-permute-start(bf16[128,512]{1,0:T(8,128)(2,1)S(1)} %get-tuple-element.52.refs_3_.refs_1_), channel_id=1, source_target_pairs={{0,2},{1,3},{8,10},{9,11},{16,18},{17,19},{24,26},{25,27}} | collective-permute-start | bytes 393224 | tf_op jit(solution)/shard_map/ppermute | solution.py:498
  55.1 24.1 %collective-permute-start.14 = (bf16[256,2,512]{2,1,0:T(2,128)(2,1)S(1)}, bf16[256,2,512]{2,1,0:T(2,128)(2,1)S(1)}, u32[]{:S(2)}, u32[]{:S(2)}) collective-permute-start(bf16[256,2,512]{2,1,0:T(2,128)(2,1)S(1)} %get-tuple-element.48.refs_3_.refs_2_), channel_id=1, source_target_pairs={{0,16},{8,24},{16,0},{24,8},{1,17},{9,25},{17,1},{25,9},{2,18},{10... | collective-permute-start | bytes 1572872 | tf_op jit(solution)/shard_map/ppermute | solution.py:412
  63.2 17.6 %collective-permute-start.16 = (bf16[512,512]{1,0:T(8,128)(2,1)S(1)}, bf16[512,512]{1,0:T(8,128)(2,1)S(1)}, u32[]{:S(2)}, u32[]{:S(2)}) collective-permute-start(bf16[512,512]{1,0:T(8,128)(2,1)S(1)} %shard_map.54.refs_2_.refs_1_), channel_id=1, source_target_pairs={{0,16},{8,24},{16,0},{24,8},{1,17},{9,25},{17,1},{25,9},{2,18},{10... | collective-permute-start | bytes 1572872 | tf_op jit(solution)/shard_map/ppermute | solution.py:412
  64.8 16.7 %collective-permute-start.12 = (bf16[512,512]{1,0:T(8,128)(2,1)S(1)}, bf16[512,512]{1,0:T(8,128)(2,1)S(1)}, u32[]{:S(2)}, u32[]{:S(2)}) collective-permute-start(bf16[512,512]{1,0:T(8,128)(2,1)S(1)} %shard_map.52.refs_5_.refs_4_.refs_14_.refs_13_.refs_12_.refs_11_), channel_id=1, source_target_pairs={{0,1},{1,0},{2,3},{3,2},{4,5},{5,4},{6,7},{7,6},{8,9},{9,8},{10,11... | collective-permute-start | bytes 1572872 | tf_op jit(solution)/shard_map/ppermute | solution.py:409
  65.3 16.2 %collective-permute-start.13 = (bf16[512,512]{1,0:T(8,128)(2,1)S(1)}, bf16[512,512]{1,0:T(8,128)(2,1)S(1)}, u32[]{:S(2)}, u32[]{:S(2)}) collective-permute-start(bf16[512,512]{1,0:T(8,128)(2,1)S(1)} %shard_map.52.refs_5_.refs_4_.refs_14_.refs_13_.refs_12_.refs_11_), channel_id=1, source_target_pairs={{0,2},{1,3},{2,4},{3,5},{4,6},{5,7},{8,10},{9,11},{10,12},{11,13},... | collective-permute-start | bytes 1572872 | tf_op jit(solution)/shard_map/ppermute | solution.py:415
  69.7 9.4 %collective-permute-start.15 = (bf16[128,512]{1,0:T(8,128)(2,1)S(1)}, bf16[128,512]{1,0:T(8,128)(2,1)S(1)}, u32[]{:S(2)}, u32[]{:S(2)}) collective-permute-start(bf16[128,512]{1,0:T(8,128)(2,1)S(1)} %shard_map.53.refs_5_.refs_0_), channel_id=1, source_target_pairs={{0,1},{1,0},{2,3},{3,2},{4,5},{5,4},{6,7},{7,6},{8,9},{9,8},{10,11... | collective-permute-start | bytes 393224 | tf_op jit(solution)/shard_map/ppermute | solution.py:409
  79.1 14.4 %collective-permute-start.20 = (bf16[256,2,512]{2,1,0:T(2,128)(2,1)S(1)}, bf16[256,2,512]{2,1,0:T(2,128)(2,1)S(1)}, u32[]{:S(2)}, u32[]{:S(2)}) collective-permute-start(bf16[256,2,512]{2,1,0:T(2,128)(2,1)S(1)} %get-tuple-element.58.refs_3_), channel_id=1, source_target_pairs={{0,8},{8,0},{16,24},{24,16},{1,9},{9,1},{17,25},{25,17},{2,10},{10... | collective-permute-start | bytes 1572872 | tf_op jit(solution)/shard_map/ppermute | solution.py:406
  79.2 19.9 %collective-permute-start.18 = (bf16[256,1024]{1,0:T(8,128)(2,1)S(1)}, bf16[256,1024]{1,0:T(8,128)(2,1)S(1)}, u32[]{:S(2)}, u32[]{:S(2)}) collective-permute-start(bf16[256,1024]{1,0:T(8,128)(2,1)S(1)} %get-tuple-element.55.refs_2_.refs_6_), channel_id=1, source_target_pairs={{0,8},{8,0},{16,24},{24,16},{1,9},{9,1},{17,25},{25,17},{2,10},{10... | collective-permute-start | bytes 1572872 | tf_op jit(solution)/shard_map/ppermute | solution.py:406
  80.9 8.3 %collective-permute-start.22 = (bf16[2,128,512]{2,1,0:T(8,128)(2,1)S(1)}, bf16[2,128,512]{2,1,0:T(8,128)(2,1)S(1)}, u32[]{:S(2)}, u32[]{:S(2)}) collective-permute-start(bf16[2,128,512]{2,1,0:T(8,128)(2,1)S(1)} %shard_map.55.refs_4_.refs_0_), channel_id=1, source_target_pairs={{0,16},{8,24},{16,0},{24,8},{1,17},{9,25},{17,1},{25,9},{2,18},{10... | collective-permute-start | bytes 786440 | tf_op jit(solution)/shard_map/ppermute | solution.py:412
  81.5 13.4 %collective-permute-start.21 = (bf16[256,2,512]{2,1,0:T(2,128)(2,1)S(1)}, bf16[256,2,512]{2,1,0:T(2,128)(2,1)S(1)}, u32[]{:S(2)}, u32[]{:S(2)}) collective-permute-start(bf16[256,2,512]{2,1,0:T(2,128)(2,1)S(1)} %get-tuple-element.54.refs_3_.refs_5_), channel_id=1, source_target_pairs={{0,8},{8,0},{16,24},{24,16},{1,9},{9,1},{17,25},{25,17},{2,10},{10... | collective-permute-start | bytes 1572872 | tf_op jit(solution)/shard_map/ppermute | solution.py:406
  81.5 18.4 %collective-permute-start.19 = (bf16[256,1024]{1,0:T(8,128)(2,1)S(1)}, bf16[256,1024]{1,0:T(8,128)(2,1)S(1)}, u32[]{:S(2)}, u32[]{:S(2)}) collective-permute-start(bf16[256,1024]{1,0:T(8,128)(2,1)S(1)} %get-tuple-element.56.refs_4_.refs_8_), channel_id=1, source_target_pairs={{0,8},{8,0},{16,24},{24,16},{1,9},{9,1},{17,25},{25,17},{2,10},{10... | collective-permute-start | bytes 1572872 | tf_op jit(solution)/shard_map/ppermute | solution.py:406
  89.1 14.9 %collective-permute-start.24 = (bf16[512,512]{1,0:T(8,128)(2,1)S(1)}, bf16[512,512]{1,0:T(8,128)(2,1)S(1)}, u32[]{:S(2)}, u32[]{:S(2)}) collective-permute-start(bf16[512,512]{1,0:T(8,128)(2,1)S(1)} %shard_map.57.refs_5_.refs_14_.refs_13_.refs_12_.refs_11_), channel_id=1, source_target_pairs={{0,2},{1,3},{2,4},{3,5},{4,6},{5,7},{8,10},{9,11},{10,12},{11,13},... | collective-permute-start | bytes 1572872 | tf_op jit(solution)/shard_map/ppermute | solution.py:415
  93.6 12.8 %collective-permute-start.25 = (bf16[512,512]{1,0:T(8,128)(2,1)S(1)}, bf16[512,512]{1,0:T(8,128)(2,1)S(1)}, u32[]{:S(2)}, u32[]{:S(2)}) collective-permute-start(bf16[512,512]{1,0:T(8,128)(2,1)S(1)} %shard_map.57.refs_5_.refs_14_.refs_13_.refs_12_.refs_11_), channel_id=1, source_target_pairs={{0,1},{1,0},{2,3},{3,2},{4,5},{5,4},{6,7},{7,6},{8,9},{9,8},{10,11... | collective-permute-start | bytes 1572872 | tf_op jit(solution)/shard_map/ppermute | solution.py:409
  94.8 14.9 %collective-permute-start.23 = (bf16[2,2,128,512]{3,2,1,0:T(8,128)(2,1)S(1)}, bf16[2,2,128,512]{3,2,1,0:T(8,128)(2,1)S(1)}, u32[]{:S(2)}, u32[]{:S(2)}) collective-permute-start(bf16[2,2,128,512]{3,2,1,0:T(8,128)(2,1)S(1)} %shard_map.59.refs_10_.refs_4_), channel_id=1, source_target_pairs={{0,8},{8,0},{16,24},{24,16},{1,9},{9,1},{17,25},{25,17},{2,10},{10... | collective-permute-start | bytes 1572872 | tf_op jit(solution)/shard_map/ppermute | solution.py:406
  94.9 5.0 %copy-start.4 = (bf16[2,512,512]{2,1,0:T(8,128)(2,1)S(1)}, bf16[2,512,512]{2,1,0:T(8,128)(2,1)}, u32[]{:S(2)}) copy-start(bf16[2,512,512]{2,1,0:T(8,128)(2,1)} %refs_1_.5) | copy-start | bytes 3145732
  99.0 10.7 %copy-start = (bf16[2,512,512]{2,1,0:T(8,128)(2,1)S(1)}, bf16[2,512,512]{2,1,0:T(8,128)(2,1)}, u32[]{:S(2)}) copy-start(bf16[2,512,512]{2,1,0:T(8,128)(2,1)} %refs_4_.11) | copy-start | bytes 3145732
  99.0 14.4 %collective-permute-start.17 = (bf16[512,512]{1,0:T(8,128)(2,1)S(1)}, bf16[512,512]{1,0:T(8,128)(2,1)S(1)}, u32[]{:S(2)}, u32[]{:S(2)}) collective-permute-start(bf16[512,512]{1,0:T(8,128)(2,1)S(1)} %shard_map.58.refs_2_), channel_id=1, source_target_pairs={{0,16},{8,24},{16,0},{24,8},{1,17},{9,25},{17,1},{25,9},{2,18},{10... | collective-permute-start | bytes 1572872 | tf_op jit(solution)/shard_map/ppermute | solution.py:412
  106.9 11.8 %collective-permute-start.27 = (bf16[512,512]{1,0:T(8,128)(2,1)S(1)}, bf16[512,512]{1,0:T(8,128)(2,1)S(1)}, u32[]{:S(2)}, u32[]{:S(2)}) collective-permute-start(bf16[512,512]{1,0:T(8,128)(2,1)S(1)} %shard_map.62.refs_10_.refs_14_.refs_13_.refs_12_.refs_11_), channel_id=1, source_target_pairs={{0,2},{1,3},{2,4},{3,5},{4,6},{5,7},{8,10},{9,11},{10,12},{11,13},... | collective-permute-start | bytes 1572872 | tf_op jit(solution)/shard_map/ppermute | solution.py:415
  109.2 11.9 %collective-permute-start.28 = (bf16[512,512]{1,0:T(8,128)(2,1)S(1)}, bf16[512,512]{1,0:T(8,128)(2,1)S(1)}, u32[]{:S(2)}, u32[]{:S(2)}) collective-permute-start(bf16[512,512]{1,0:T(8,128)(2,1)S(1)} %shard_map.62.refs_10_.refs_14_.refs_13_.refs_12_.refs_11_), channel_id=1, source_target_pairs={{0,1},{1,0},{2,3},{3,2},{4,5},{5,4},{6,7},{7,6},{8,9},{9,8},{10,11... | collective-permute-start | bytes 1572872 | tf_op jit(solution)/shard_map/ppermute | solution.py:409
  114.0 10.5 %copy-start.3 = (bf16[512,512]{1,0:T(8,128)(2,1)S(1)}, bf16[512,512]{1,0:T(8,128)(2,1)}, u32[]{:S(2)}) copy-start(bf16[512,512]{1,0:T(8,128)(2,1)} %shard_map.46.refs_4_.refs_1_.refs_11_) | copy-start | bytes 1572868
  114.0 10.5 %collective-permute-start.26 = (bf16[2,512,512]{2,1,0:T(8,128)(2,1)S(1)}, bf16[2,512,512]{2,1,0:T(8,128)(2,1)S(1)}, u32[]{:S(2)}, u32[]{:S(2)}) collective-permute-start(bf16[2,512,512]{2,1,0:T(8,128)(2,1)S(1)} %shard_map.64.refs_2_), channel_id=1, source_target_pairs={{0,8},{8,0},{16,24},{24,16},{1,9},{9,1},{17,25},{25,17},{2,10},{10... | collective-permute-start | bytes 3145736 | tf_op jit(solution)/shard_map/ppermute | solution.py:406
  121.6 11.0 %collective-permute-start.30 = (bf16[512,512]{1,0:T(8,128)(2,1)S(1)}, bf16[512,512]{1,0:T(8,128)(2,1)S(1)}, u32[]{:S(2)}, u32[]{:S(2)}) collective-permute-start(bf16[512,512]{1,0:T(8,128)(2,1)S(1)} %shard_map.65.refs_19_.refs_14_.refs_13_.refs_12_), channel_id=1, source_target_pairs={{0,1},{1,0},{2,3},{3,2},{4,5},{5,4},{6,7},{7,6},{8,9},{9,8},{10,11... | collective-permute-start | bytes 1572872 | tf_op jit(solution)/shard_map/ppermute | solution.py:409
  122.2 10.4 %collective-permute-start.29 = (bf16[256,512]{1,0:T(8,128)(2,1)S(1)}, bf16[256,512]{1,0:T(8,128)(2,1)S(1)}, u32[]{:S(2)}, u32[]{:S(2)}) collective-permute-start(bf16[256,512]{1,0:T(8,128)(2,1)S(1)} %slice.4), channel_id=1, source_target_pairs={{0,2},{1,3},{2,4},{3,5},{4,6},{5,7},{8,10},{9,11},{10,12},{11,13},... | collective-permute-start | bytes 786440 | tf_op jit(solution)/shard_map/ppermute | solution.py:415
  133.2 16.4 %collective-permute-start.31 = (bf16[256,512]{1,0:T(8,128)(2,1)S(1)}, bf16[256,512]{1,0:T(8,128)(2,1)S(1)}, u32[]{:S(2)}, u32[]{:S(2)}) collective-permute-start(bf16[256,512]{1,0:T(8,128)(2,1)S(1)} %shard_map.68.refs_20_.refs_14_.refs_13_), channel_id=1, source_target_pairs={{0,2},{1,3},{2,4},{3,5},{4,6},{5,7},{8,10},{9,11},{10,12},{11,13},... | collective-permute-start | bytes 786440 | tf_op jit(solution)/shard_map/ppermute | solution.py:415
  135.8 13.8 %collective-permute-start.32 = (bf16[256,512]{1,0:T(8,128)(2,1)S(1)}, bf16[256,512]{1,0:T(8,128)(2,1)S(1)}, u32[]{:S(2)}, u32[]{:S(2)}) collective-permute-start(bf16[256,512]{1,0:T(8,128)(2,1)S(1)} %shard_map.68.refs_20_.refs_14_.refs_13_), channel_id=1, source_target_pairs={{0,1},{1,0},{2,3},{3,2},{4,5},{5,4},{6,7},{7,6},{8,9},{9,8},{10,11... | collective-permute-start | bytes 786440 | tf_op jit(solution)/shard_map/ppermute | solution.py:409
  150.2 6.4 %collective-permute-start.33 = (bf16[256,512]{1,0:T(8,128)(2,1)S(1)}, bf16[256,512]{1,0:T(8,128)(2,1)S(1)}, u32[]{:S(2)}, u32[]{:S(2)}) collective-permute-start(bf16[256,512]{1,0:T(8,128)(2,1)S(1)} %shard_map.71.refs_20_.refs_14_), channel_id=1, source_target_pairs={{0,1},{1,0},{2,3},{3,2},{4,5},{5,4},{6,7},{7,6},{8,9},{9,8},{10,11... | collective-permute-start | bytes 786440 | tf_op jit(solution)/shard_map/ppermute | solution.py:409

commit v6 on v5

--- a/solution.py
+++ b/solution.py
@@ -579,9 +579,9 @@
             us=5.0, mib=24,
         )
 
-    plan = [(0, gather), (1, join), (2, functools.partial(fresh, 0)), (3, head_here), (line - 1, functools.partial(old, held, "old_held")), (3, head_pair), (3, functools.partial(fresh, 1)), (line, functools.partial(old, other, "old_other")), (4, head_all), (4, scatter), (4, prep0), (5, prep1), (5, old_here)]
+    plan = [(0, gather), (1, join), (2, functools.partial(fresh, 0)), (3, head_here), (line - 1, functools.partial(old, held, "old_held")), (3, head_pair), (3, functools.partial(fresh, 1)), (line, functools.partial(old, other, "old_other")), (4, scatter), (4, prep0), (5, head_all), (5, old_here), (5, prep1)]
     for i in range(pieces):
-        plan.append((max((6, 6, 7, 7, 8, 8)[min(i, 5)], i + line - 1), functools.partial(update, i)))
+        plan.append((max((6, 6, 7, 8, 8, 8)[min(i, 5)], i + line - 1), functools.partial(update, i)))
     for k in range(last_step + 1):
         step(k)
         while plan and (plan[0][0] <= k or k == last_step):

time: 164 us -> 159 us (0.970); the launches traced: 161 us -> 158 us
  waiting for transfers between devices: 47.7 us -> 43.9 us
    ppermute x5, waiting for transfers between devices: 6.8 us -> 2.35 us  [to_chip(): lax.ppermute(value, 'prow', [(r, (r + 2 * h) % row_devices) for r in rang...]
  transfers between devices with their start and end apart: 34 -> 34, of which waited for: 14 -> 13; matrix products, arithmetic and copies ran while one was open for 0% -> 0% of each run, Pallas kernels for 33% -> 33%
where the time goes in v6:
time: 159 us; the launch traced here: 158 us
  Pallas kernels  60.4 us (38%)
  starting transfers between devices  49.5 us (31%)
  waiting for transfers between devices  43.9 us (28%)
  local copies, waits for them, and re-layouts  3.76 us (2%)
    pallas_call x28, Pallas kernels, call(): pl.pallas_call(ordered, out_shape=tuple((shape for shape, _ in outs)), in...  60.4 us
    ppermute x8, starting transfers between devices, to_next(): lax.ppermute(value, 'pcol', [(c, c + 2) for c in range(col_devices - 2)])  26.2 us
    ppermute x8, waiting for transfers between devices, to_next(): lax.ppermute(value, 'pcol', [(c, c + 2) for c in range(col_devices - 2)])  19.5 us
    ppermute x10, waiting for transfers between devices, to_neighbour(): return lax.ppermute(value, 'pcol', [(c, c ^ 1) for c in range(col_devices)])  17.3 us
    ppermute x10, starting transfers between devices, to_neighbour(): return lax.ppermute(value, 'pcol', [(c, c ^ 1) for c in range(col_devices)])  10.1 us
    ppermute x5, starting transfers between devices, to_chip(): lax.ppermute(value, 'prow', [(r, (r + 2 * h) % row_devices) for r in rang...  6.92 us
    ppermute x3, waiting for transfers between devices, fresh(): lax.ppermute(head[0], 'pcol', [(0, 2 * h), (1, 2 * h + 1)])  4.82 us
    ppermute x3, starting transfers between devices, fresh(): lax.ppermute(head[0], 'pcol', [(0, 2 * h), (1, 2 * h + 1)])  4.4 us
  transfers between devices with their start and end apart: 34, of which 13 were waited for; matrix products, arithmetic and copies ran while one was open for 0% of the time, Pallas kernels for 33%

profile of v6, /device:TPU:0, one launch (start us, length us, event | category | flops | bytes accessed | tf_op | source)
XLA Modules:
  0.0 158.3 jit_solution(9809911709808089122)
XLA Ops:
  0.0 2.2 %shard_map.46.refs_4_.refs_1_.refs_11_ = bf16[512,512]{1,0:T(8,128)(2,1)} custom-call(bf16[2560,2,512]{2,1,0:T(2,128)(2,1)} %bitcast.5), custom_call_target="tpu_custom_call" | custom-call | flops 1100000000 | tf_op jit(solution)/shard_map/pallas_call | solution.py:37
  2.2 3.0 %collective-permute-start.1 = (bf16[512,512]{1,0:T(8,128)(2,1)}, bf16[512,512]{1,0:T(8,128)(2,1)S(1)}, u32[]{:S(2)}, u32[]{:S(2)}) collective-permute-start(bf16[512,512]{1,0:T(8,128)(2,1)} %shard_map.46.refs_4_.refs_1_.refs_11_), channel_id=1, source_target_pairs={{0,1},{1,0},{2,3},{3,2},{4,5},{5,4},{6,7},{7,6},{8,9},{9,8},{10,11... | collective-permute-start | bytes 1572872 | tf_op jit(solution)/shard_map/ppermute | solution.py:409
  5.2 3.5 %collective-permute-start = (bf16[512,512]{1,0:T(8,128)(2,1)}, bf16[512,512]{1,0:T(8,128)(2,1)S(1)}, u32[]{:S(2)}, u32[]{:S(2)}) collective-permute-start(bf16[512,512]{1,0:T(8,128)(2,1)} %shard_map.46.refs_4_.refs_1_.refs_11_), channel_id=1, source_target_pairs={{0,2},{1,3},{2,4},{3,5},{4,6},{5,7},{8,10},{9,11},{10,12},{11,13},... | collective-permute-start | bytes 1572872 | tf_op jit(solution)/shard_map/ppermute | solution.py:415
  9.0 2.5 %copy-done.1 = bf16[5,512,2,512]{3,2,1,0:T(2,128)(2,1)S(1)} copy-done((bf16[5,512,2,512]{3,2,1,0:T(2,128)(2,1)S(1)}, bf16[5,512,2,512]{3,2,1,0:T(2,128)(2,1)}, u32[]{:S(2)}) %copy-start.1) | copy-done | bytes 5242904
  11.5 1.0 copy-done.2
  12.5 7.7 %shard_map.47 = (bf16[512,512]{1,0:T(8,128)(2,1)S(1)}, bf16[512,512]{1,0:T(8,128)(2,1)S(1)}, bf16[512,512]{1,0:T(8,128)(2,1)S(1)}, bf16[256,512]{1,0:T(8,128)(2,...) custom-call(s32[4]{0:T(128)S(1)} %pad_add_fusion.refs_0_, ...), custom_call_target="tpu_custom_call" | custom-call | flops 8800000000 | tf_op jit(solution)/shard_map/pallas_call | solution.py:37
  21.5 3.5 %collective-permute-start.2 = (bf16[512,512]{1,0:T(8,128)(2,1)S(1)}, bf16[512,512]{1,0:T(8,128)(2,1)S(1)}, u32[]{:S(2)}, u32[]{:S(2)}) collective-permute-start(bf16[512,512]{1,0:T(8,128)(2,1)S(1)} %shard_map.48.refs_4_.refs_2_.refs_12_.refs_11_), channel_id=1, source_target_pairs={{0,2},{1,3},{2,4},{3,5},{4,6},{5,7},{8,10},{9,11},{10,12},{11,13},... | collective-permute-start | bytes 1572872 | tf_op jit(solution)/shard_map/ppermute | solution.py:415
  25.5 2.4 %shard_map.49 = (bf16[256,2,512]{2,1,0:T(2,128)(2,1)S(1)}, bf16[256,2,512]{2,1,0:T(2,128)(2,1)S(1)}) custom-call(s32[4]{0:T(128)S(1)} %pad_add_fusion.refs_0_, s32[2,512]{1,0:T(2,128)S(1)} %get-tuple-element.45.refs_1_, bf16[512,2,512]{2,1,0:T(2,128)(2,1)S(1)} %get-tuple-element.46.refs_2_, bf16[512,2,512]{2,1,0:T(2,128)(2,1)S(1)} %collective-permute-done.3.refs_3_, ...), custom_call_target="tpu_custom_call" | custom-call | flops 2200000000 | tf_op jit(solution)/shard_map/pallas_call | solution.py:37
  27.9 1.6 collective-permute-start.7
  29.5 6.8 %collective-permute-done.2.refs_1_ = bf16[512,512]{1,0:T(8,128)(2,1)S(1)} collective-permute-done((bf16[512,512]{1,0:T(8,128)(2,1)S(1)}, bf16[512,512]{1,0:T(8,128)(2,1)S(1)}, u32[]{:S(2)}, u32[]{:S(2)}) %collective-permute-start.2) | collective-permute-done | bytes 524320 | tf_op jit(solution)/shard_map/ppermute | solution.py:415
  36.3 2.3 %collective-permute-done.4.refs_4_.refs_2_.refs_16_.refs_15_ = bf16[512,512]{1,0:T(8,128)(2,1)S(1)} collective-permute-done((bf16[512,512]{1,0:T(8,128)(2,1)S(1)}, bf16[512,512]{1,0:T(8,128)(2,1)S(1)}, u32[]{:S(2)}, u32[]{:S(2)}) %collective-permute-start.4) | collective-permute-done | bytes 524320 | tf_op jit(solution)/shard_map/ppermute | solution.py:409
  39.3 3.5 %collective-permute-start.6 = (bf16[512,512]{1,0:T(8,128)(2,1)S(1)}, bf16[512,512]{1,0:T(8,128)(2,1)S(1)}, u32[]{:S(2)}, u32[]{:S(2)}) collective-permute-start(bf16[512,512]{1,0:T(8,128)(2,1)S(1)} %shard_map.50.refs_4_.refs_3_.refs_13_.refs_12_.refs_11_), channel_id=1, source_target_pairs={{0,2},{1,3},{2,4},{3,5},{4,6},{5,7},{8,10},{9,11},{10,12},{11,13},... | collective-permute-start | bytes 1572872 | tf_op jit(solution)/shard_map/ppermute | solution.py:415
  43.3 1.1 shard_map.51
  44.5 1.8 %collective-permute-start.10 = (bf16[128,512]{1,0:T(8,128)(2,1)S(1)}, bf16[128,512]{1,0:T(8,128)(2,1)S(1)}, u32[]{:S(2)}, u32[]{:S(2)}) collective-permute-start(bf16[128,512]{1,0:T(8,128)(2,1)S(1)} %get-tuple-element.52.refs_3_.refs_1_), channel_id=1, source_target_pairs={{0,4},{1,5},{8,12},{9,13},{16,20},{17,21},{24,28},{25,29}} | collective-permute-start | bytes 393224 | tf_op jit(solution)/shard_map/ppermute | solution.py:498
  46.3 1.3 collective-permute-start.11
  47.6 1.3 collective-permute-start.9
  48.9 6.2 %collective-permute-done.6.refs_1_ = bf16[512,512]{1,0:T(8,128)(2,1)S(1)} collective-permute-done((bf16[512,512]{1,0:T(8,128)(2,1)S(1)}, bf16[512,512]{1,0:T(8,128)(2,1)S(1)}, u32[]{:S(2)}, u32[]{:S(2)}) %collective-permute-start.6) | collective-permute-done | bytes 524320 | tf_op jit(solution)/shard_map/ppermute | solution.py:415
  55.1 1.5 collective-permute-start.14
  56.6 1.3 collective-permute-done.10.refs_6_.refs_3_
  57.9 2.1 %collective-permute-done.11.refs_7_.refs_4_ = bf16[128,512]{1,0:T(8,128)(2,1)S(1)} collective-permute-done((bf16[128,512]{1,0:T(8,128)(2,1)S(1)}, bf16[128,512]{1,0:T(8,128)(2,1)S(1)}, u32[]{:S(2)}, u32[]{:S(2)}) %collective-permute-start.11) | collective-permute-done | bytes 131104 | tf_op jit(solution)/shard_map/ppermute | solution.py:498
  60.0 1.4 collective-permute-done.9.refs_5_.refs_2_
  63.2 1.6 collective-permute-start.16
  65.3 4.4 %collective-permute-start.13 = (bf16[512,512]{1,0:T(8,128)(2,1)S(1)}, bf16[512,512]{1,0:T(8,128)(2,1)S(1)}, u32[]{:S(2)}, u32[]{:S(2)}) collective-permute-start(bf16[512,512]{1,0:T(8,128)(2,1)S(1)} %shard_map.52.refs_5_.refs_4_.refs_14_.refs_13_.refs_12_.refs_11_), channel_id=1, source_target_pairs={{0,2},{1,3},{2,4},{3,5},{4,6},{5,7},{8,10},{9,11},{10,12},{11,13},... | collective-permute-start | bytes 1572872 | tf_op jit(solution)/shard_map/ppermute | solution.py:415
  69.7 1.6 %collective-permute-start.15 = (bf16[128,512]{1,0:T(8,128)(2,1)S(1)}, bf16[128,512]{1,0:T(8,128)(2,1)S(1)}, u32[]{:S(2)}, u32[]{:S(2)}) collective-permute-start(bf16[128,512]{1,0:T(8,128)(2,1)S(1)} %shard_map.53.refs_5_.refs_0_), channel_id=1, source_target_pairs={{0,1},{1,0},{2,3},{3,2},{4,5},{5,4},{6,7},{7,6},{8,9},{9,8},{10,11... | collective-permute-start | bytes 393224 | tf_op jit(solution)/shard_map/ppermute | solution.py:409
  71.3 7.9 %collective-permute-done.15.refs_1_ = bf16[128,512]{1,0:T(8,128)(2,1)S(1)} collective-permute-done((bf16[128,512]{1,0:T(8,128)(2,1)S(1)}, bf16[128,512]{1,0:T(8,128)(2,1)S(1)}, u32[]{:S(2)}, u32[]{:S(2)}) %collective-permute-start.15) | collective-permute-done | bytes 131104 | tf_op jit(solution)/shard_map/ppermute | solution.py:409
  79.7 1.1 shard_map.56
  82.0 4.4 %collective-permute-start.19 = (bf16[512,512]{1,0:T(8,128)(2,1)S(1)}, bf16[512,512]{1,0:T(8,128)(2,1)S(1)}, u32[]{:S(2)}, u32[]{:S(2)}) collective-permute-start(bf16[512,512]{1,0:T(8,128)(2,1)S(1)} %shard_map.57.refs_5_.refs_14_.refs_13_.refs_12_.refs_11_), channel_id=1, source_target_pairs={{0,2},{1,3},{2,4},{3,5},{4,6},{5,7},{8,10},{9,11},{10,12},{11,13},... | collective-permute-start | bytes 1572872 | tf_op jit(solution)/shard_map/ppermute | solution.py:415
  88.2 4.1 %shard_map.59.refs_6_.refs_8_ = bf16[2568,2,512]{2,1,0:T(2,128)(2,1)S(1)} custom-call(s32[4]{0:T(128)S(1)} %pad_add_fusion.refs_0_, s32[2,512]{1,0:T(2,128)S(1)} %get-tuple-element.58.refs_1_, s32[2,512]{1,0:T(2,128)S(1)} %get-tuple-element.41.refs_2_.refs_1_, bf16[256,2,512]{2,1,0:T(2,128)(2,1)S(1)} %get-tuple-element.59.refs_3_, ...), custom_call_target="tpu_custom_call" | custom-call | flops 110000000 | tf_op jit(solution)/shard_map/pallas_call | solution.py:37
  92.3 1.8 %collective-permute-start.17 = (bf16[512,512]{1,0:T(8,128)(2,1)S(1)}, bf16[512,512]{1,0:T(8,128)(2,1)S(1)}, u32[]{:S(2)}, u32[]{:S(2)}) collective-permute-start(bf16[512,512]{1,0:T(8,128)(2,1)S(1)} %shard_map.58.refs_10_.refs_2_), channel_id=1, source_target_pairs={{0,16},{8,24},{16,0},{24,8},{1,17},{9,25},{17,1},{25,9},{2,18},{10... | collective-permute-start | bytes 1572872 | tf_op jit(solution)/shard_map/ppermute | solution.py:412
  94.1 2.0 %shard_map.60 = (bf16[512,1024]{1,0:T(8,128)(2,1)S(1)}, bf16[512,2,512]{2,1,0:T(2,128)(2,1)S(1)}) custom-call(s32[4]{0:T(128)S(1)} %pad_add_fusion.refs_0_, bf16[2,512,512]{2,1,0:T(8,128)(2,1)S(1)} %copy-done.4, bf16[256,1024]{1,0:T(8,128)(2,1)S(1)} %get-tuple-element.56.refs_2_.refs_6_, bf16[256,1024]{1,0:T(8,128)(2,1)S(1)} %collective-permute-done.20.refs_3_.refs_7_, ...), custom_call_target="tpu_custom_call" | custom-call | flops 2200000000 | tf_op jit(solution)/shard_map/pallas_call | solution.py:37
  96.1 1.8 %collective-permute-done.19.refs_1_ = bf16[512,512]{1,0:T(8,128)(2,1)S(1)} collective-permute-done((bf16[512,512]{1,0:T(8,128)(2,1)S(1)}, bf16[512,512]{1,0:T(8,128)(2,1)S(1)}, u32[]{:S(2)}, u32[]{:S(2)}) %collective-permute-start.19) | collective-permute-done | bytes 524320 | tf_op jit(solution)/shard_map/ppermute | solution.py:415
  97.8 2.3 %collective-permute-done.24.refs_4_.refs_18_.refs_17_.refs_16_.refs_15_ = bf16[512,512]{1,0:T(8,128)(2,1)S(1)} collective-permute-done((bf16[512,512]{1,0:T(8,128)(2,1)S(1)}, bf16[512,512]{1,0:T(8,128)(2,1)S(1)}, u32[]{:S(2)}, u32[]{:S(2)}) %collective-permute-start.24) | collective-permute-done | bytes 524320 | tf_op jit(solution)/shard_map/ppermute | solution.py:409
  100.9 2.2 %collective-permute-start.27 = (bf16[512,512]{1,0:T(8,128)(2,1)S(1)}, bf16[512,512]{1,0:T(8,128)(2,1)S(1)}, u32[]{:S(2)}, u32[]{:S(2)}) collective-permute-start(bf16[512,512]{1,0:T(8,128)(2,1)S(1)} %shard_map.61.refs_2_.refs_14_.refs_13_.refs_12_.refs_11_), channel_id=1, source_target_pairs={{0,2},{1,3},{2,4},{3,5},{4,6},{5,7},{8,10},{9,11},{10,12},{11,13},... | collective-permute-start | bytes 1572872 | tf_op jit(solution)/shard_map/ppermute | solution.py:415
  103.7 2.3 %collective-permute-done.17.refs_4_ = bf16[512,512]{1,0:T(8,128)(2,1)S(1)} collective-permute-done((bf16[512,512]{1,0:T(8,128)(2,1)S(1)}, bf16[512,512]{1,0:T(8,128)(2,1)S(1)}, u32[]{:S(2)}, u32[]{:S(2)}) %collective-permute-start.17) | collective-permute-done | bytes 524320 | tf_op jit(solution)/shard_map/ppermute | solution.py:412
  106.0 0.6 shard_map.63.refs_10_.refs_2_
  106.8 3.5 %shard_map.64 = (bf16[512,1024]{1,0:T(8,128)(2,1)S(1)}, bf16[512,512]{1,0:T(8,128)(2,1)S(1)}, bf16[512,2,512]{2,1,0:T(2,128)(2,1)S(1)}) custom-call(s32[4]{0:T(128)S(1)} %pad_add_fusion.refs_0_, bf16[2,512,512]{2,1,0:T(8,128)(2,1)S(1)} %copy-done.4, bf16[2,512,512]{2,1,0:T(8,128)(2,1)S(1)} %copy-done, ...), custom_call_target="tpu_custom_call" | custom-call | flops 3849999872 | tf_op jit(solution)/shard_map/pallas_call | solution.py:37
  110.2 4.7 %collective-permute-done.27.refs_1_ = bf16[512,512]{1,0:T(8,128)(2,1)S(1)} collective-permute-done((bf16[512,512]{1,0:T(8,128)(2,1)S(1)}, bf16[512,512]{1,0:T(8,128)(2,1)S(1)}, u32[]{:S(2)}, u32[]{:S(2)}) %collective-permute-start.27) | collective-permute-done | bytes 524320 | tf_op jit(solution)/shard_map/ppermute | solution.py:415
  114.9 2.3 %collective-permute-done.28.refs_3_.refs_18_.refs_17_.refs_16_.refs_15_ = bf16[512,512]{1,0:T(8,128)(2,1)S(1)} collective-permute-done((bf16[512,512]{1,0:T(8,128)(2,1)S(1)}, bf16[512,512]{1,0:T(8,128)(2,1)S(1)}, u32[]{:S(2)}, u32[]{:S(2)}) %collective-permute-start.28) | collective-permute-done | bytes 524320 | tf_op jit(solution)/shard_map/ppermute | solution.py:409
  118.4 2.2 %collective-permute-start.29 = (bf16[256,512]{1,0:T(8,128)(2,1)S(1)}, bf16[256,512]{1,0:T(8,128)(2,1)S(1)}, u32[]{:S(2)}, u32[]{:S(2)}) collective-permute-start(bf16[256,512]{1,0:T(8,128)(2,1)S(1)} %slice.4), channel_id=1, source_target_pairs={{0,2},{1,3},{2,4},{3,5},{4,6},{5,7},{8,10},{9,11},{10,12},{11,13},... | collective-permute-start | bytes 786440 | tf_op jit(solution)/shard_map/ppermute | solution.py:415
  120.6 1.8 %shard_map.66 = (bf16[2560,2,512]{2,1,0:T(2,128)(2,1)}, f32[8,128]{1,0:T(8,128)S(1)}) custom-call(s32[4]{0:T(128)S(1)} %pad_add_fusion.refs_0_, s32[2,512]{1,0:T(2,128)S(1)} %get-tuple-element.41.refs_2_.refs_1_, bf16[2,512,512]{2,1,0:T(8,128)(2,1)S(1)} %shard_map.63.refs_10_.refs_2_, bf16[2,512,512]{2,1,0:T(8,128)(2,1)S(1)} %collective-permute-done.25.refs_3_, ...), custom_call_target="tpu_custom_call" | custom-call | flops 5500000256 | tf_op jit(solution)/shard_map/pallas_call | solution.py:37
  122.4 6.2 %shard_map.67 = (bf16[2560,2,512]{2,1,0:T(2,128)(2,1)}, f32[8,128]{1,0:T(8,128)S(1)}) custom-call(s32[4]{0:T(128)S(1)} %pad_add_fusion.refs_0_, s32[2,512]{1,0:T(2,128)S(1)} %get-tuple-element.41.refs_2_.refs_1_, bf16[2,512,512]{2,1,0:T(8,128)(2,1)S(1)} %shard_map.63.refs_10_.refs_2_, ...), custom_call_target="tpu_custom_call", output_to_operand_aliasing={{0}: (19, {})} | custom-call | flops 5500000256 | tf_op jit(solution)/shard_map/pallas_call | solution.py:37
  128.6 2.4 %collective-permute-done.30.refs_3_.refs_18_.refs_17_.refs_16_ = bf16[512,512]{1,0:T(8,128)(2,1)S(1)} collective-permute-done((bf16[512,512]{1,0:T(8,128)(2,1)S(1)}, bf16[512,512]{1,0:T(8,128)(2,1)S(1)}, u32[]{:S(2)}, u32[]{:S(2)}) %collective-permute-start.30) | collective-permute-done | bytes 524320 | tf_op jit(solution)/shard_map/ppermute | solution.py:409
  131.6 2.5 %collective-permute-start.31 = (bf16[256,512]{1,0:T(8,128)(2,1)S(1)}, bf16[256,512]{1,0:T(8,128)(2,1)S(1)}, u32[]{:S(2)}, u32[]{:S(2)}) collective-permute-start(bf16[256,512]{1,0:T(8,128)(2,1)S(1)} %shard_map.68.refs_20_.refs_14_.refs_13_), channel_id=1, source_target_pairs={{0,2},{1,3},{2,4},{3,5},{4,6},{5,7},{8,10},{9,11},{10,12},{11,13},... | collective-permute-start | bytes 786440 | tf_op jit(solution)/shard_map/ppermute | solution.py:415
  134.7 6.4 %shard_map.69 = (bf16[2560,2,512]{2,1,0:T(2,128)(2,1)}, f32[8,128]{1,0:T(8,128)S(1)}) custom-call(s32[4]{0:T(128)S(1)} %pad_add_fusion.refs_0_, s32[2,512]{1,0:T(2,128)S(1)} %get-tuple-element.41.refs_2_.refs_1_, bf16[2,512,512]{2,1,0:T(8,128)(2,1)S(1)} %shard_map.63.refs_10_.refs_2_, ...), custom_call_target="tpu_custom_call", output_to_operand_aliasing={{0}: (19, {})} | custom-call | flops 5500000256 | tf_op jit(solution)/shard_map/pallas_call | solution.py:37
  141.6 1.6 %collective-permute-start.33 = (bf16[256,512]{1,0:T(8,128)(2,1)S(1)}, bf16[256,512]{1,0:T(8,128)(2,1)S(1)}, u32[]{:S(2)}, u32[]{:S(2)}) collective-permute-start(bf16[256,512]{1,0:T(8,128)(2,1)S(1)} %shard_map.70.refs_20_.refs_14_), channel_id=1, source_target_pairs={{0,1},{1,0},{2,3},{3,2},{4,5},{5,4},{6,7},{7,6},{8,9},{9,8},{10,11... | collective-permute-start | bytes 786440 | tf_op jit(solution)/shard_map/ppermute | solution.py:409
  143.2 6.2 %shard_map.71 = (bf16[2560,2,512]{2,1,0:T(2,128)(2,1)}, f32[8,128]{1,0:T(8,128)S(1)}) custom-call(s32[4]{0:T(128)S(1)} %pad_add_fusion.refs_0_, s32[2,512]{1,0:T(2,128)S(1)} %get-tuple-element.41.refs_2_.refs_1_, bf16[2,512,512]{2,1,0:T(8,128)(2,1)S(1)} %shard_map.63.refs_10_.refs_2_, ...), custom_call_target="tpu_custom_call", output_to_operand_aliasing={{0}: (19, {})} | custom-call | flops 5500000256 | tf_op jit(solution)/shard_map/pallas_call | solution.py:37
  149.4 4.1 %shard_map.72 = (bf16[2560,2,512]{2,1,0:T(2,128)(2,1)}, f32[8,128]{1,0:T(8,128)S(1)}) custom-call(s32[4]{0:T(128)S(1)} %pad_add_fusion.refs_0_, s32[2,512]{1,0:T(2,128)S(1)} %get-tuple-element.41.refs_2_.refs_1_, bf16[2,512,512]{2,1,0:T(8,128)(2,1)S(1)} %shard_map.63.refs_10_.refs_2_, ...), custom_call_target="tpu_custom_call", output_to_operand_aliasing={{0}: (19, {})} | custom-call | flops 5500000256 | tf_op jit(solution)/shard_map/pallas_call | solution.py:37
  153.5 4.6 %shard_map.73 = (bf16[2560,2,512]{2,1,0:T(2,128)(2,1)}, f32[8,128]{1,0:T(8,128)}) custom-call(s32[4]{0:T(128)S(1)} %pad_add_fusion.refs_0_, s32[2,512]{1,0:T(2,128)S(1)} %get-tuple-element.41.refs_2_.refs_1_, bf16[2,512,512]{2,1,0:T(8,128)(2,1)S(1)} %shard_map.63.refs_10_.refs_2_, ...), custom_call_target="tpu_custom_call", output_to_operand_aliasing={{0}: (19, {})} | custom-call | flops 5500000256 | tf_op jit(solution)/shard_map/pallas_call | solution.py:37
  (63 shorter events, 13.1 us)
Async XLA Ops:
  0.0 8.8 %copy-start.5 = (s32[2,512]{1,0:T(2,128)S(1)}, s32[2,512]{1,0:T(2,128)}, u32[]{:S(2)}) copy-start(s32[2,512]{1,0:T(2,128)} %refs_1_.3) | copy-start | bytes 12292
  2.2 18.7 %collective-permute-start.1 = (bf16[512,512]{1,0:T(8,128)(2,1)}, bf16[512,512]{1,0:T(8,128)(2,1)S(1)}, u32[]{:S(2)}, u32[]{:S(2)}) collective-permute-start(bf16[512,512]{1,0:T(8,128)(2,1)} %shard_map.46.refs_4_.refs_1_.refs_11_), channel_id=1, source_target_pairs={{0,1},{1,0},{2,3},{3,2},{4,5},{5,4},{6,7},{7,6},{8,9},{9,8},{10,11... | collective-permute-start | bytes 1572872 | tf_op jit(solution)/shard_map/ppermute | solution.py:409
  5.2 15.7 %collective-permute-start = (bf16[512,512]{1,0:T(8,128)(2,1)}, bf16[512,512]{1,0:T(8,128)(2,1)S(1)}, u32[]{:S(2)}, u32[]{:S(2)}) collective-permute-start(bf16[512,512]{1,0:T(8,128)(2,1)} %shard_map.46.refs_4_.refs_1_.refs_11_), channel_id=1, source_target_pairs={{0,2},{1,3},{2,4},{3,5},{4,6},{5,7},{8,10},{9,11},{10,12},{11,13},... | collective-permute-start | bytes 1572872 | tf_op jit(solution)/shard_map/ppermute | solution.py:415
  9.0 2.5 %copy-start.1 = (bf16[5,512,2,512]{3,2,1,0:T(2,128)(2,1)S(1)}, bf16[5,512,2,512]{3,2,1,0:T(2,128)(2,1)}, u32[]{:S(2)}) copy-start(bf16[5,512,2,512]{3,2,1,0:T(2,128)(2,1)} %param.4) | copy-start | bytes 15728644
  11.5 1.0 copy-start.2
  20.3 5.2 %collective-permute-start.3 = (bf16[512,2,512]{2,1,0:T(2,128)(2,1)S(1)}, bf16[512,2,512]{2,1,0:T(2,128)(2,1)S(1)}, u32[]{:S(2)}, u32[]{:S(2)}) collective-permute-start(bf16[512,2,512]{2,1,0:T(2,128)(2,1)S(1)} %get-tuple-element.47), channel_id=1, source_target_pairs={{0,8},{8,0},{16,24},{24,16},{1,9},{9,1},{17,25},{25,17},{2,10},{10... | collective-permute-start | bytes 3145736 | tf_op jit(solution)/shard_map/ppermute | solution.py:406
  20.4 18.3 %collective-permute-start.5 = (bf16[512,2,512]{2,1,0:T(2,128)(2,1)S(1)}, bf16[512,2,512]{2,1,0:T(2,128)(2,1)S(1)}, u32[]{:S(2)}, u32[]{:S(2)}) collective-permute-start(bf16[512,2,512]{2,1,0:T(2,128)(2,1)S(1)} %get-tuple-element.49.refs_7_), channel_id=1, source_target_pairs={{0,8},{8,0},{16,24},{24,16},{1,9},{9,1},{17,25},{25,17},{2,10},{10... | collective-permute-start | bytes 3145736 | tf_op jit(solution)/shard_map/ppermute | solution.py:406
  21.5 14.9 %collective-permute-start.2 = (bf16[512,512]{1,0:T(8,128)(2,1)S(1)}, bf16[512,512]{1,0:T(8,128)(2,1)S(1)}, u32[]{:S(2)}, u32[]{:S(2)}) collective-permute-start(bf16[512,512]{1,0:T(8,128)(2,1)S(1)} %shard_map.48.refs_4_.refs_2_.refs_12_.refs_11_), channel_id=1, source_target_pairs={{0,2},{1,3},{2,4},{3,5},{4,6},{5,7},{8,10},{9,11},{10,12},{11,13},... | collective-permute-start | bytes 1572872 | tf_op jit(solution)/shard_map/ppermute | solution.py:415
  25.0 13.7 %collective-permute-start.4 = (bf16[512,512]{1,0:T(8,128)(2,1)S(1)}, bf16[512,512]{1,0:T(8,128)(2,1)S(1)}, u32[]{:S(2)}, u32[]{:S(2)}) collective-permute-start(bf16[512,512]{1,0:T(8,128)(2,1)S(1)} %shard_map.48.refs_4_.refs_2_.refs_12_.refs_11_), channel_id=1, source_target_pairs={{0,1},{1,0},{2,3},{3,2},{4,5},{5,4},{6,7},{7,6},{8,9},{9,8},{10,11... | collective-permute-start | bytes 1572872 | tf_op jit(solution)/shard_map/ppermute | solution.py:409
  27.9 15.4 %collective-permute-start.7 = (bf16[256,2,512]{2,1,0:T(2,128)(2,1)S(1)}, bf16[256,2,512]{2,1,0:T(2,128)(2,1)S(1)}, u32[]{:S(2)}, u32[]{:S(2)}) collective-permute-start(bf16[256,2,512]{2,1,0:T(2,128)(2,1)S(1)} %get-tuple-element.51.refs_2_), channel_id=1, source_target_pairs={{0,16},{8,24},{16,0},{24,8},{1,17},{9,25},{17,1},{25,9},{2,18},{10... | collective-permute-start | bytes 1572872 | tf_op jit(solution)/shard_map/ppermute | solution.py:412
  39.3 15.8 %collective-permute-start.6 = (bf16[512,512]{1,0:T(8,128)(2,1)S(1)}, bf16[512,512]{1,0:T(8,128)(2,1)S(1)}, u32[]{:S(2)}, u32[]{:S(2)}) collective-permute-start(bf16[512,512]{1,0:T(8,128)(2,1)S(1)} %shard_map.50.refs_4_.refs_3_.refs_13_.refs_12_.refs_11_), channel_id=1, source_target_pairs={{0,2},{1,3},{2,4},{3,5},{4,6},{5,7},{8,10},{9,11},{10,12},{11,13},... | collective-permute-start | bytes 1572872 | tf_op jit(solution)/shard_map/ppermute | solution.py:415
  42.7 13.8 %collective-permute-start.8 = (bf16[512,512]{1,0:T(8,128)(2,1)S(1)}, bf16[512,512]{1,0:T(8,128)(2,1)S(1)}, u32[]{:S(2)}, u32[]{:S(2)}) collective-permute-start(bf16[512,512]{1,0:T(8,128)(2,1)S(1)} %shard_map.50.refs_4_.refs_3_.refs_13_.refs_12_.refs_11_), channel_id=1, source_target_pairs={{0,1},{1,0},{2,3},{3,2},{4,5},{5,4},{6,7},{7,6},{8,9},{9,8},{10,11... | collective-permute-start | bytes 1572872 | tf_op jit(solution)/shard_map/ppermute | solution.py:409
  44.5 13.4 %collective-permute-start.10 = (bf16[128,512]{1,0:T(8,128)(2,1)S(1)}, bf16[128,512]{1,0:T(8,128)(2,1)S(1)}, u32[]{:S(2)}, u32[]{:S(2)}) collective-permute-start(bf16[128,512]{1,0:T(8,128)(2,1)S(1)} %get-tuple-element.52.refs_3_.refs_1_), channel_id=1, source_target_pairs={{0,4},{1,5},{8,12},{9,13},{16,20},{17,21},{24,28},{25,29}} | collective-permute-start | bytes 393224 | tf_op jit(solution)/shard_map/ppermute | solution.py:498
  46.3 13.7 %collective-permute-start.11 = (bf16[128,512]{1,0:T(8,128)(2,1)S(1)}, bf16[128,512]{1,0:T(8,128)(2,1)S(1)}, u32[]{:S(2)}, u32[]{:S(2)}) collective-permute-start(bf16[128,512]{1,0:T(8,128)(2,1)S(1)} %get-tuple-element.52.refs_3_.refs_1_), channel_id=1, source_target_pairs={{0,6},{1,7},{8,14},{9,15},{16,22},{17,23},{24,30},{25,31}} | collective-permute-start | bytes 393224 | tf_op jit(solution)/shard_map/ppermute | solution.py:498
  47.6 13.8 %collective-permute-start.9 = (bf16[128,512]{1,0:T(8,128)(2,1)S(1)}, bf16[128,512]{1,0:T(8,128)(2,1)S(1)}, u32[]{:S(2)}, u32[]{:S(2)}) collective-permute-start(bf16[128,512]{1,0:T(8,128)(2,1)S(1)} %get-tuple-element.52.refs_3_.refs_1_), channel_id=1, source_target_pairs={{0,2},{1,3},{8,10},{9,11},{16,18},{17,19},{24,26},{25,27}} | collective-permute-start | bytes 393224 | tf_op jit(solution)/shard_map/ppermute | solution.py:498
  55.1 24.1 %collective-permute-start.14 = (bf16[256,2,512]{2,1,0:T(2,128)(2,1)S(1)}, bf16[256,2,512]{2,1,0:T(2,128)(2,1)S(1)}, u32[]{:S(2)}, u32[]{:S(2)}) collective-permute-start(bf16[256,2,512]{2,1,0:T(2,128)(2,1)S(1)} %get-tuple-element.48.refs_3_.refs_2_), channel_id=1, source_target_pairs={{0,16},{8,24},{16,0},{24,8},{1,17},{9,25},{17,1},{25,9},{2,18},{10... | collective-permute-start | bytes 1572872 | tf_op jit(solution)/shard_map/ppermute | solution.py:412
  63.2 17.6 %collective-permute-start.16 = (bf16[512,512]{1,0:T(8,128)(2,1)S(1)}, bf16[512,512]{1,0:T(8,128)(2,1)S(1)}, u32[]{:S(2)}, u32[]{:S(2)}) collective-permute-start(bf16[512,512]{1,0:T(8,128)(2,1)S(1)} %shard_map.54.refs_2_.refs_1_), channel_id=1, source_target_pairs={{0,16},{8,24},{16,0},{24,8},{1,17},{9,25},{17,1},{25,9},{2,18},{10... | collective-permute-start | bytes 1572872 | tf_op jit(solution)/shard_map/ppermute | solution.py:412
  64.8 16.2 %collective-permute-start.12 = (bf16[512,512]{1,0:T(8,128)(2,1)S(1)}, bf16[512,512]{1,0:T(8,128)(2,1)S(1)}, u32[]{:S(2)}, u32[]{:S(2)}) collective-permute-start(bf16[512,512]{1,0:T(8,128)(2,1)S(1)} %shard_map.52.refs_5_.refs_4_.refs_14_.refs_13_.refs_12_.refs_11_), channel_id=1, source_target_pairs={{0,1},{1,0},{2,3},{3,2},{4,5},{5,4},{6,7},{7,6},{8,9},{9,8},{10,11... | collective-permute-start | bytes 1572872 | tf_op jit(solution)/shard_map/ppermute | solution.py:409
  65.3 16.2 %collective-permute-start.13 = (bf16[512,512]{1,0:T(8,128)(2,1)S(1)}, bf16[512,512]{1,0:T(8,128)(2,1)S(1)}, u32[]{:S(2)}, u32[]{:S(2)}) collective-permute-start(bf16[512,512]{1,0:T(8,128)(2,1)S(1)} %shard_map.52.refs_5_.refs_4_.refs_14_.refs_13_.refs_12_.refs_11_), channel_id=1, source_target_pairs={{0,2},{1,3},{2,4},{3,5},{4,6},{5,7},{8,10},{9,11},{10,12},{11,13},... | collective-permute-start | bytes 1572872 | tf_op jit(solution)/shard_map/ppermute | solution.py:415
  69.7 9.4 %collective-permute-start.15 = (bf16[128,512]{1,0:T(8,128)(2,1)S(1)}, bf16[128,512]{1,0:T(8,128)(2,1)S(1)}, u32[]{:S(2)}, u32[]{:S(2)}) collective-permute-start(bf16[128,512]{1,0:T(8,128)(2,1)S(1)} %shard_map.53.refs_5_.refs_0_), channel_id=1, source_target_pairs={{0,1},{1,0},{2,3},{3,2},{4,5},{5,4},{6,7},{7,6},{8,9},{9,8},{10,11... | collective-permute-start | bytes 393224 | tf_op jit(solution)/shard_map/ppermute | solution.py:409
  79.1 7.3 %collective-permute-start.22 = (bf16[256,2,512]{2,1,0:T(2,128)(2,1)S(1)}, bf16[256,2,512]{2,1,0:T(2,128)(2,1)S(1)}, u32[]{:S(2)}, u32[]{:S(2)}) collective-permute-start(bf16[256,2,512]{2,1,0:T(2,128)(2,1)S(1)} %get-tuple-element.59.refs_3_), channel_id=1, source_target_pairs={{0,8},{8,0},{16,24},{24,16},{1,9},{9,1},{17,25},{25,17},{2,10},{10... | collective-permute-start | bytes 1572872 | tf_op jit(solution)/shard_map/ppermute | solution.py:406
  79.2 13.2 %collective-permute-start.20 = (bf16[256,1024]{1,0:T(8,128)(2,1)S(1)}, bf16[256,1024]{1,0:T(8,128)(2,1)S(1)}, u32[]{:S(2)}, u32[]{:S(2)}) collective-permute-start(bf16[256,1024]{1,0:T(8,128)(2,1)S(1)} %get-tuple-element.56.refs_2_.refs_6_), channel_id=1, source_target_pairs={{0,8},{8,0},{16,24},{24,16},{1,9},{9,1},{17,25},{25,17},{2,10},{10... | collective-permute-start | bytes 1572872 | tf_op jit(solution)/shard_map/ppermute | solution.py:406
  80.9 6.2 %collective-permute-start.23 = (bf16[256,2,512]{2,1,0:T(2,128)(2,1)S(1)}, bf16[256,2,512]{2,1,0:T(2,128)(2,1)S(1)}, u32[]{:S(2)}, u32[]{:S(2)}) collective-permute-start(bf16[256,2,512]{2,1,0:T(2,128)(2,1)S(1)} %get-tuple-element.54.refs_3_.refs_5_), channel_id=1, source_target_pairs={{0,8},{8,0},{16,24},{24,16},{1,9},{9,1},{17,25},{25,17},{2,10},{10... | collective-permute-start | bytes 1572872 | tf_op jit(solution)/shard_map/ppermute | solution.py:406
  80.9 13.2 %collective-permute-start.21 = (bf16[256,1024]{1,0:T(8,128)(2,1)S(1)}, bf16[256,1024]{1,0:T(8,128)(2,1)S(1)}, u32[]{:S(2)}, u32[]{:S(2)}) collective-permute-start(bf16[256,1024]{1,0:T(8,128)(2,1)S(1)} %get-tuple-element.57.refs_4_.refs_8_), channel_id=1, source_target_pairs={{0,8},{8,0},{16,24},{24,16},{1,9},{9,1},{17,25},{25,17},{2,10},{10... | collective-permute-start | bytes 1572872 | tf_op jit(solution)/shard_map/ppermute | solution.py:406
  82.0 15.8 %collective-permute-start.19 = (bf16[512,512]{1,0:T(8,128)(2,1)S(1)}, bf16[512,512]{1,0:T(8,128)(2,1)S(1)}, u32[]{:S(2)}, u32[]{:S(2)}) collective-permute-start(bf16[512,512]{1,0:T(8,128)(2,1)S(1)} %shard_map.57.refs_5_.refs_14_.refs_13_.refs_12_.refs_11_), channel_id=1, source_target_pairs={{0,2},{1,3},{2,4},{3,5},{4,6},{5,7},{8,10},{9,11},{10,12},{11,13},... | collective-permute-start | bytes 1572872 | tf_op jit(solution)/shard_map/ppermute | solution.py:415
  86.5 13.7 %collective-permute-start.24 = (bf16[512,512]{1,0:T(8,128)(2,1)S(1)}, bf16[512,512]{1,0:T(8,128)(2,1)S(1)}, u32[]{:S(2)}, u32[]{:S(2)}) collective-permute-start(bf16[512,512]{1,0:T(8,128)(2,1)S(1)} %shard_map.57.refs_5_.refs_14_.refs_13_.refs_12_.refs_11_), channel_id=1, source_target_pairs={{0,1},{1,0},{2,3},{3,2},{4,5},{5,4},{6,7},{7,6},{8,9},{9,8},{10,11... | collective-permute-start | bytes 1572872 | tf_op jit(solution)/shard_map/ppermute | solution.py:409
  87.0 13.7 %collective-permute-start.18 = (bf16[2,128,512]{2,1,0:T(8,128)(2,1)S(1)}, bf16[2,128,512]{2,1,0:T(8,128)(2,1)S(1)}, u32[]{:S(2)}, u32[]{:S(2)}) collective-permute-start(bf16[2,128,512]{2,1,0:T(8,128)(2,1)S(1)} %shard_map.55.refs_4_.refs_0_), channel_id=1, source_target_pairs={{0,16},{8,24},{16,0},{24,8},{1,17},{9,25},{17,1},{25,9},{2,18},{10... | collective-permute-start | bytes 786440 | tf_op jit(solution)/shard_map/ppermute | solution.py:412
  88.2 5.9 %copy-start.4 = (bf16[2,512,512]{2,1,0:T(8,128)(2,1)S(1)}, bf16[2,512,512]{2,1,0:T(8,128)(2,1)}, u32[]{:S(2)}) copy-start(bf16[2,512,512]{2,1,0:T(8,128)(2,1)} %refs_1_.5) | copy-start | bytes 3145732
  92.3 13.7 %collective-permute-start.17 = (bf16[512,512]{1,0:T(8,128)(2,1)S(1)}, bf16[512,512]{1,0:T(8,128)(2,1)S(1)}, u32[]{:S(2)}, u32[]{:S(2)}) collective-permute-start(bf16[512,512]{1,0:T(8,128)(2,1)S(1)} %shard_map.58.refs_10_.refs_2_), channel_id=1, source_target_pairs={{0,16},{8,24},{16,0},{24,8},{1,17},{9,25},{17,1},{25,9},{2,18},{10... | collective-permute-start | bytes 1572872 | tf_op jit(solution)/shard_map/ppermute | solution.py:412
  96.1 10.7 %copy-start = (bf16[2,512,512]{2,1,0:T(8,128)(2,1)S(1)}, bf16[2,512,512]{2,1,0:T(8,128)(2,1)}, u32[]{:S(2)}) copy-start(bf16[2,512,512]{2,1,0:T(8,128)(2,1)} %refs_4_.11) | copy-start | bytes 3145732
  100.8 5.9 %collective-permute-start.26 = (bf16[2,2,128,512]{3,2,1,0:T(8,128)(2,1)S(1)}, bf16[2,2,128,512]{3,2,1,0:T(8,128)(2,1)S(1)}, u32[]{:S(2)}, u32[]{:S(2)}) collective-permute-start(bf16[2,2,128,512]{3,2,1,0:T(8,128)(2,1)S(1)} %shard_map.62.refs_5_.refs_4_), channel_id=1, source_target_pairs={{0,8},{8,0},{16,24},{24,16},{1,9},{9,1},{17,25},{25,17},{2,10},{10... | collective-permute-start | bytes 1572872 | tf_op jit(solution)/shard_map/ppermute | solution.py:406
  100.9 14.0 %collective-permute-start.27 = (bf16[512,512]{1,0:T(8,128)(2,1)S(1)}, bf16[512,512]{1,0:T(8,128)(2,1)S(1)}, u32[]{:S(2)}, u32[]{:S(2)}) collective-permute-start(bf16[512,512]{1,0:T(8,128)(2,1)S(1)} %shard_map.61.refs_2_.refs_14_.refs_13_.refs_12_.refs_11_), channel_id=1, source_target_pairs={{0,2},{1,3},{2,4},{3,5},{4,6},{5,7},{8,10},{9,11},{10,12},{11,13},... | collective-permute-start | bytes 1572872 | tf_op jit(solution)/shard_map/ppermute | solution.py:415
  103.1 14.1 %collective-permute-start.28 = (bf16[512,512]{1,0:T(8,128)(2,1)S(1)}, bf16[512,512]{1,0:T(8,128)(2,1)S(1)}, u32[]{:S(2)}, u32[]{:S(2)}) collective-permute-start(bf16[512,512]{1,0:T(8,128)(2,1)S(1)} %shard_map.61.refs_2_.refs_14_.refs_13_.refs_12_.refs_11_), channel_id=1, source_target_pairs={{0,1},{1,0},{2,3},{3,2},{4,5},{5,4},{6,7},{7,6},{8,9},{9,8},{10,11... | collective-permute-start | bytes 1572872 | tf_op jit(solution)/shard_map/ppermute | solution.py:409
  106.7 13.9 %collective-permute-start.25 = (bf16[2,512,512]{2,1,0:T(8,128)(2,1)S(1)}, bf16[2,512,512]{2,1,0:T(8,128)(2,1)S(1)}, u32[]{:S(2)}, u32[]{:S(2)}) collective-permute-start(bf16[2,512,512]{2,1,0:T(8,128)(2,1)S(1)} %shard_map.63.refs_10_.refs_2_), channel_id=1, source_target_pairs={{0,8},{8,0},{16,24},{24,16},{1,9},{9,1},{17,25},{25,17},{2,10},{10... | collective-permute-start | bytes 3145736 | tf_op jit(solution)/shard_map/ppermute | solution.py:406
  117.2 3.4 %copy-start.3 = (bf16[512,512]{1,0:T(8,128)(2,1)S(1)}, bf16[512,512]{1,0:T(8,128)(2,1)}, u32[]{:S(2)}) copy-start(bf16[512,512]{1,0:T(8,128)(2,1)} %shard_map.46.refs_4_.refs_1_.refs_11_) | copy-start | bytes 1572868
  117.8 13.3 %collective-permute-start.30 = (bf16[512,512]{1,0:T(8,128)(2,1)S(1)}, bf16[512,512]{1,0:T(8,128)(2,1)S(1)}, u32[]{:S(2)}, u32[]{:S(2)}) collective-permute-start(bf16[512,512]{1,0:T(8,128)(2,1)S(1)} %shard_map.65.refs_19_.refs_14_.refs_13_.refs_12_), channel_id=1, source_target_pairs={{0,1},{1,0},{2,3},{3,2},{4,5},{5,4},{6,7},{7,6},{8,9},{9,8},{10,11... | collective-permute-start | bytes 1572872 | tf_op jit(solution)/shard_map/ppermute | solution.py:409
  118.4 10.3 %collective-permute-start.29 = (bf16[256,512]{1,0:T(8,128)(2,1)S(1)}, bf16[256,512]{1,0:T(8,128)(2,1)S(1)}, u32[]{:S(2)}, u32[]{:S(2)}) collective-permute-start(bf16[256,512]{1,0:T(8,128)(2,1)S(1)} %slice.4), channel_id=1, source_target_pairs={{0,2},{1,3},{2,4},{3,5},{4,6},{5,7},{8,10},{9,11},{10,12},{11,13},... | collective-permute-start | bytes 786440 | tf_op jit(solution)/shard_map/ppermute | solution.py:415
  131.6 9.4 %collective-permute-start.31 = (bf16[256,512]{1,0:T(8,128)(2,1)S(1)}, bf16[256,512]{1,0:T(8,128)(2,1)S(1)}, u32[]{:S(2)}, u32[]{:S(2)}) collective-permute-start(bf16[256,512]{1,0:T(8,128)(2,1)S(1)} %shard_map.68.refs_20_.refs_14_.refs_13_), channel_id=1, source_target_pairs={{0,2},{1,3},{2,4},{3,5},{4,6},{5,7},{8,10},{9,11},{10,12},{11,13},... | collective-permute-start | bytes 786440 | tf_op jit(solution)/shard_map/ppermute | solution.py:415
  134.1 7.0 %collective-permute-start.32 = (bf16[256,512]{1,0:T(8,128)(2,1)S(1)}, bf16[256,512]{1,0:T(8,128)(2,1)S(1)}, u32[]{:S(2)}, u32[]{:S(2)}) collective-permute-start(bf16[256,512]{1,0:T(8,128)(2,1)S(1)} %shard_map.68.refs_20_.refs_14_.refs_13_), channel_id=1, source_target_pairs={{0,1},{1,0},{2,3},{3,2},{4,5},{5,4},{6,7},{7,6},{8,9},{9,8},{10,11... | collective-permute-start | bytes 786440 | tf_op jit(solution)/shard_map/ppermute | solution.py:409
  141.6 11.8 %collective-permute-start.33 = (bf16[256,512]{1,0:T(8,128)(2,1)S(1)}, bf16[256,512]{1,0:T(8,128)(2,1)S(1)}, u32[]{:S(2)}, u32[]{:S(2)}) collective-permute-start(bf16[256,512]{1,0:T(8,128)(2,1)S(1)} %shard_map.70.refs_20_.refs_14_), channel_id=1, source_target_pairs={{0,1},{1,0},{2,3},{3,2},{4,5},{5,4},{6,7},{7,6},{8,9},{9,8},{10,11... | collective-permute-start | bytes 786440 | tf_op jit(solution)/shard_map/ppermute | solution.py:409

commit v7 on v6

--- a/solution.py
+++ b/solution.py
@@ -209,13 +209,16 @@
             out[1] = choices[2 * h + 1][...]
 
 
-def by_place_kernel(meta, *refs):
-    out = refs[-1]
-    for h, choice in enumerate(refs[:-1]):
-
-        @pl.when(lax.div(meta[2], 2) == h)
-        def _(choice=choice):
-            out[...] = choice[...]
+def by_span_kernel(span, meta, mine, came, out):
+    first = lax.rem(lax.div(meta[2], 2), 2 * span) == 0
+
+    @pl.when(first)
+    def _():
+        out[...] = mine[...]
+
+    @pl.when(jnp.logical_not(first))
+    def _():
+        out[...] = came[...]
 
 
 def stack_kernel(*refs):
@@ -494,16 +497,29 @@
         state["fresh"] += [new, to_sibling(new)]
         state["brought"] += [brought, to_sibling(brought)]
         if head:
-            state["head"] = head + [
-                lax.ppermute(head[0], "pcol", [(0, 2 * h), (1, 2 * h + 1)]) for h in range(1, line)
-            ]
-            state["awaited"] = state.get("awaited", []) + state["head"][1:]
-
-    def head_here():
+            pass_head(head[0], 0)
+
+    spans = []
+    while 2 ** len(spans) < line:
+        spans.insert(0, 2 ** len(spans))
+
+    def pass_head(value, i):
+        if i == len(spans):
+            state["head"] = (value, to_neighbour(value))
+            return
+        starts = range(0, line - spans[i], 2 * spans[i])
+        pairs = [(2 * p + y, 2 * (p + spans[i]) + y) for p in starts for y in range(2)]
+        state["head"] = (value, lax.ppermute(value, "pcol", pairs))
+        state["awaited"] = state.get("awaited", []) + [state["head"][1]] if i == 0 else []
+
+    def head_next(i):
         (mine,) = run(
-            by_place_kernel, [(meta, SMEM)] + [(v, VMEM) for v in state["head"]], [(bf16(part, nb), VMEM)], us=0.1
-        )
-        state["head"] = (mine, to_neighbour(mine))
+            functools.partial(by_span_kernel, spans[i - 1]),
+            [(meta, SMEM)] + [(v, VMEM) for v in state["head"]],
+            [(bf16(part, nb), VMEM)],
+            us=0.1,
+        )
+        pass_head(mine, i)
 
     def head_pair():
         (pair,) = run(stack_kernel, [(v, VMEM) for v in state["head"]], [(bf16(2, part, nb), VMEM)], us=0.1)
@@ -579,7 +595,7 @@
             us=5.0, mib=24,
         )
 
-    plan = [(0, gather), (1, join), (2, functools.partial(fresh, 0)), (3, head_here), (line - 1, functools.partial(old, held, "old_held")), (3, head_pair), (3, functools.partial(fresh, 1)), (line, functools.partial(old, other, "old_other")), (4, scatter), (4, prep0), (5, head_all), (5, old_here), (5, prep1)]
+    plan = [(0, gather), (1, join), (2, functools.partial(fresh, 0)), *[(3, functools.partial(head_next, i)) for i in range(1, len(spans))], (line - 1, functools.partial(old, held, "old_held")), (3, functools.partial(fresh, 1)), (3, functools.partial(head_next, len(spans))), (line, functools.partial(old, other, "old_other")), (4, head_pair), (4, scatter), (4, prep0), (5, head_all), (5, old_here), (5, prep1)]
     for i in range(pieces):
         plan.append((max((6, 6, 7, 8, 8, 8)[min(i, 5)], i + line - 1), functools.partial(update, i)))
     for k in range(last_step + 1):

time: 159 us -> 160 us (level)
  starting transfers between devices: 49.5 us -> 57.5 us
  waiting for transfers between devices: 43.9 us -> 36.2 us
    ppermute x10, waiting for transfers between devices: 17.3 us -> 11.6 us  [to_neighbour(): return lax.ppermute(value, 'pcol', [(c, c ^ 1) for c in range(col_devices)])]
    ppermute x8, starting transfers between devices: 26.2 us -> 29.4 us  [to_next(): lax.ppermute(value, 'pcol', [(c, c + 2) for c in range(col_devices - 2)])]
    ppermute x10, starting transfers between devices: 10.1 us -> 13.1 us  [to_neighbour(): return lax.ppermute(value, 'pcol', [(c, c ^ 1) for c in range(col_devices)])]
    ppermute x3 -> x2, starting transfers between devices: 4.4 us -> 6.55 us  [pass_head(): state['head'] = (value, lax.ppermute(value, 'pcol', pairs))]
    ppermute x8, waiting for transfers between devices: 19.5 us -> 17.8 us  [to_next(): lax.ppermute(value, 'pcol', [(c, c + 2) for c in range(col_devices - 2)])]
    pallas_call x28 -> x29, Pallas kernels: 60.4 us -> 61 us  [call(): pl.pallas_call(ordered, out_shape=tuple((shape for shape, _ in outs)), in...]
    ppermute x3 -> x2, waiting for transfers between devices: 4.82 us -> 4.93 us  [pass_head(): state['head'] = (value, lax.ppermute(value, 'pcol', pairs))]
  transfers between devices with their start and end apart: 34 -> 33, of which waited for: 13 -> 12; matrix products, arithmetic and copies ran while one was open for 0% -> 0% of each run, Pallas kernels for 33% -> 33%
where the time goes in v7:
time: 160 us; the launch traced here: 159 us
  Pallas kernels  61 us (38%)
  starting transfers between devices  57.5 us (36%)
  waiting for transfers between devices  36.2 us (23%)
  local copies, waits for them, and re-layouts  3.75 us (2%)
    pallas_call x29, Pallas kernels, call(): pl.pallas_call(ordered, out_shape=tuple((shape for shape, _ in outs)), in...  61 us
    ppermute x8, starting transfers between devices, to_next(): lax.ppermute(value, 'pcol', [(c, c + 2) for c in range(col_devices - 2)])  29.4 us
    ppermute x8, waiting for transfers between devices, to_next(): lax.ppermute(value, 'pcol', [(c, c + 2) for c in range(col_devices - 2)])  17.8 us
    ppermute x10, starting transfers between devices, to_neighbour(): return lax.ppermute(value, 'pcol', [(c, c ^ 1) for c in range(col_devices)])  13.1 us
    ppermute x10, waiting for transfers between devices, to_neighbour(): return lax.ppermute(value, 'pcol', [(c, c ^ 1) for c in range(col_devices)])  11.6 us
    ppermute x5, starting transfers between devices, to_chip(): lax.ppermute(value, 'prow', [(r, (r + 2 * h) % row_devices) for r in rang...  7.05 us
    ppermute x2, starting transfers between devices, pass_head(): state['head'] = (value, lax.ppermute(value, 'pcol', pairs))  6.55 us
    ppermute x2, waiting for transfers between devices, pass_head(): state['head'] = (value, lax.ppermute(value, 'pcol', pairs))  4.93 us
  transfers between devices with their start and end apart: 33, of which 12 were waited for; matrix products, arithmetic and copies ran while one was open for 0% of the time, Pallas kernels for 33%

profile of v7, /device:TPU:0, one launch (start us, length us, event | category | flops | bytes accessed | tf_op | source)
XLA Modules:
  0.0 159.2 jit_solution(2420254068222461456)
XLA Ops:
  0.0 2.2 %shard_map.46.refs_4_.refs_1_.refs_11_ = bf16[512,512]{1,0:T(8,128)(2,1)} custom-call(bf16[2560,2,512]{2,1,0:T(2,128)(2,1)} %bitcast.5), custom_call_target="tpu_custom_call" | custom-call | flops 1100000000 | tf_op jit(solution)/shard_map/pallas_call | solution.py:37
  2.2 3.0 %collective-permute-start.1 = (bf16[512,512]{1,0:T(8,128)(2,1)}, bf16[512,512]{1,0:T(8,128)(2,1)S(1)}, u32[]{:S(2)}, u32[]{:S(2)}) collective-permute-start(bf16[512,512]{1,0:T(8,128)(2,1)} %shard_map.46.refs_4_.refs_1_.refs_11_), channel_id=1, source_target_pairs={{0,1},{1,0},{2,3},{3,2},{4,5},{5,4},{6,7},{7,6},{8,9},{9,8},{10,11... | collective-permute-start | bytes 1572872 | tf_op jit(solution)/shard_map/ppermute | solution.py:412
  5.2 3.5 %collective-permute-start = (bf16[512,512]{1,0:T(8,128)(2,1)}, bf16[512,512]{1,0:T(8,128)(2,1)S(1)}, u32[]{:S(2)}, u32[]{:S(2)}) collective-permute-start(bf16[512,512]{1,0:T(8,128)(2,1)} %shard_map.46.refs_4_.refs_1_.refs_11_), channel_id=1, source_target_pairs={{0,2},{1,3},{2,4},{3,5},{4,6},{5,7},{8,10},{9,11},{10,12},{11,13},... | collective-permute-start | bytes 1572872 | tf_op jit(solution)/shard_map/ppermute | solution.py:418
  9.0 2.5 %copy-done.1 = bf16[5,512,2,512]{3,2,1,0:T(2,128)(2,1)S(1)} copy-done((bf16[5,512,2,512]{3,2,1,0:T(2,128)(2,1)S(1)}, bf16[5,512,2,512]{3,2,1,0:T(2,128)(2,1)}, u32[]{:S(2)}) %copy-start.1) | copy-done | bytes 5242904
  11.5 1.0 copy-done.2
  12.5 7.7 %shard_map.47 = (bf16[512,512]{1,0:T(8,128)(2,1)S(1)}, bf16[512,512]{1,0:T(8,128)(2,1)S(1)}, bf16[512,512]{1,0:T(8,128)(2,1)S(1)}, bf16[256,512]{1,0:T(8,128)(2,...) custom-call(s32[4]{0:T(128)S(1)} %pad_add_fusion.refs_0_, ...), custom_call_target="tpu_custom_call" | custom-call | flops 8800000000 | tf_op jit(solution)/shard_map/pallas_call | solution.py:37
  21.5 3.5 %collective-permute-start.2 = (bf16[512,512]{1,0:T(8,128)(2,1)S(1)}, bf16[512,512]{1,0:T(8,128)(2,1)S(1)}, u32[]{:S(2)}, u32[]{:S(2)}) collective-permute-start(bf16[512,512]{1,0:T(8,128)(2,1)S(1)} %shard_map.48.refs_4_.refs_2_.refs_12_.refs_11_), channel_id=1, source_target_pairs={{0,2},{1,3},{2,4},{3,5},{4,6},{5,7},{8,10},{9,11},{10,12},{11,13},... | collective-permute-start | bytes 1572872 | tf_op jit(solution)/shard_map/ppermute | solution.py:418
  25.5 2.4 %shard_map.49 = (bf16[256,2,512]{2,1,0:T(2,128)(2,1)S(1)}, bf16[256,2,512]{2,1,0:T(2,128)(2,1)S(1)}) custom-call(s32[4]{0:T(128)S(1)} %pad_add_fusion.refs_0_, s32[2,512]{1,0:T(2,128)S(1)} %get-tuple-element.45.refs_1_, bf16[512,2,512]{2,1,0:T(2,128)(2,1)S(1)} %get-tuple-element.46.refs_2_, bf16[512,2,512]{2,1,0:T(2,128)(2,1)S(1)} %collective-permute-done.3.refs_3_, ...), custom_call_target="tpu_custom_call" | custom-call | flops 2200000000 | tf_op jit(solution)/shard_map/pallas_call | solution.py:37
  27.9 1.6 collective-permute-start.7
  29.5 6.8 %collective-permute-done.2.refs_1_ = bf16[512,512]{1,0:T(8,128)(2,1)S(1)} collective-permute-done((bf16[512,512]{1,0:T(8,128)(2,1)S(1)}, bf16[512,512]{1,0:T(8,128)(2,1)S(1)}, u32[]{:S(2)}, u32[]{:S(2)}) %collective-permute-start.2) | collective-permute-done | bytes 524320 | tf_op jit(solution)/shard_map/ppermute | solution.py:418
  36.3 2.3 %collective-permute-done.4.refs_4_.refs_2_.refs_16_.refs_15_ = bf16[512,512]{1,0:T(8,128)(2,1)S(1)} collective-permute-done((bf16[512,512]{1,0:T(8,128)(2,1)S(1)}, bf16[512,512]{1,0:T(8,128)(2,1)S(1)}, u32[]{:S(2)}, u32[]{:S(2)}) %collective-permute-start.4) | collective-permute-done | bytes 524320 | tf_op jit(solution)/shard_map/ppermute | solution.py:412
  39.3 3.5 %collective-permute-start.6 = (bf16[512,512]{1,0:T(8,128)(2,1)S(1)}, bf16[512,512]{1,0:T(8,128)(2,1)S(1)}, u32[]{:S(2)}, u32[]{:S(2)}) collective-permute-start(bf16[512,512]{1,0:T(8,128)(2,1)S(1)} %shard_map.50.refs_4_.refs_3_.refs_13_.refs_12_.refs_11_), channel_id=1, source_target_pairs={{0,2},{1,3},{2,4},{3,5},{4,6},{5,7},{8,10},{9,11},{10,12},{11,13},... | collective-permute-start | bytes 1572872 | tf_op jit(solution)/shard_map/ppermute | solution.py:418
  43.3 1.1 shard_map.51
  44.5 1.8 %collective-permute-start.9 = (bf16[128,512]{1,0:T(8,128)(2,1)S(1)}, bf16[128,512]{1,0:T(8,128)(2,1)S(1)}, u32[]{:S(2)}, u32[]{:S(2)}) collective-permute-start(bf16[128,512]{1,0:T(8,128)(2,1)S(1)} %get-tuple-element.52.refs_3_.refs_1_), channel_id=1, source_target_pairs={{0,4},{1,5},{8,12},{9,13},{16,20},{17,21},{24,28},{25,29}} | collective-permute-start | bytes 393224 | tf_op jit(solution)/shard_map/ppermute | solution.py:512
  46.3 1.6 collective-permute-start.13
  47.8 6.5 %collective-permute-done.6.refs_1_ = bf16[512,512]{1,0:T(8,128)(2,1)S(1)} collective-permute-done((bf16[512,512]{1,0:T(8,128)(2,1)S(1)}, bf16[512,512]{1,0:T(8,128)(2,1)S(1)}, u32[]{:S(2)}, u32[]{:S(2)}) %collective-permute-start.6) | collective-permute-done | bytes 524320 | tf_op jit(solution)/shard_map/ppermute | solution.py:418
  54.4 0.9 collective-permute-done.8.refs_4_.refs_3_.refs_17_.refs_16_.refs_15_
  56.9 0.6 shard_map.54.refs_4_.refs_1_
  57.6 1.6 collective-permute-start.14
  59.6 3.0 %collective-permute-start.11 = (bf16[512,512]{1,0:T(8,128)(2,1)S(1)}, bf16[512,512]{1,0:T(8,128)(2,1)S(1)}, u32[]{:S(2)}, u32[]{:S(2)}) collective-permute-start(bf16[512,512]{1,0:T(8,128)(2,1)S(1)} %shard_map.52.refs_3_.refs_4_.refs_14_.refs_13_.refs_12_.refs_11_), channel_id=1, source_target_pairs={{0,2},{1,3},{2,4},{3,5},{4,6},{5,7},{8,10},{9,11},{10,12},{11,13},... | collective-permute-start | bytes 1572872 | tf_op jit(solution)/shard_map/ppermute | solution.py:418
  62.7 4.7 %collective-permute-start.12 = (bf16[128,512]{1,0:T(8,128)(2,1)S(1)}, bf16[128,512]{1,0:T(8,128)(2,1)S(1)}, u32[]{:S(2)}, u32[]{:S(2)}) collective-permute-start(bf16[128,512]{1,0:T(8,128)(2,1)S(1)} %shard_map.53.refs_5_.refs_1_), channel_id=1, source_target_pairs={{0,2},{1,3},{4,6},{5,7},{8,10},{9,11},{12,14},{13,15},{16,18},{17,... | collective-permute-start | bytes 393224 | tf_op jit(solution)/shard_map/ppermute | solution.py:512
  67.5 1.1 shard_map.55
  68.6 4.4 %collective-permute-done.12.refs_2_ = bf16[128,512]{1,0:T(8,128)(2,1)S(1)} collective-permute-done((bf16[128,512]{1,0:T(8,128)(2,1)S(1)}, bf16[128,512]{1,0:T(8,128)(2,1)S(1)}, u32[]{:S(2)}, u32[]{:S(2)}) %collective-permute-start.12) | collective-permute-done | bytes 131104 | tf_op jit(solution)/shard_map/ppermute | solution.py:512
  74.3 1.5 collective-permute-start.16
  76.4 3.7 %collective-permute-done.16.refs_1_ = bf16[128,512]{1,0:T(8,128)(2,1)S(1)} collective-permute-done((bf16[128,512]{1,0:T(8,128)(2,1)S(1)}, bf16[128,512]{1,0:T(8,128)(2,1)S(1)}, u32[]{:S(2)}, u32[]{:S(2)}) %collective-permute-start.16) | collective-permute-done | bytes 131104 | tf_op jit(solution)/shard_map/ppermute | solution.py:412
  80.1 4.4 %collective-permute-start.18 = (bf16[512,512]{1,0:T(8,128)(2,1)S(1)}, bf16[512,512]{1,0:T(8,128)(2,1)S(1)}, u32[]{:S(2)}, u32[]{:S(2)}) collective-permute-start(bf16[512,512]{1,0:T(8,128)(2,1)S(1)} %shard_map.57.refs_5_.refs_14_.refs_13_.refs_12_.refs_11_), channel_id=1, source_target_pairs={{0,2},{1,3},{2,4},{3,5},{4,6},{5,7},{8,10},{9,11},{10,12},{11,13},... | collective-permute-start | bytes 1572872 | tf_op jit(solution)/shard_map/ppermute | solution.py:418
  84.6 1.6 collective-permute-start.23
  87.4 4.1 %shard_map.60.refs_6_.refs_8_ = bf16[2568,2,512]{2,1,0:T(2,128)(2,1)S(1)} custom-call(s32[4]{0:T(128)S(1)} %pad_add_fusion.refs_0_, s32[2,512]{1,0:T(2,128)S(1)} %get-tuple-element.58.refs_1_, s32[2,512]{1,0:T(2,128)S(1)} %get-tuple-element.41.refs_2_.refs_1_, bf16[256,2,512]{2,1,0:T(2,128)(2,1)S(1)} %get-tuple-element.59.refs_3_, ...), custom_call_target="tpu_custom_call" | custom-call | flops 110000000 | tf_op jit(solution)/shard_map/pallas_call | solution.py:37
  91.5 1.8 %collective-permute-start.15 = (bf16[512,512]{1,0:T(8,128)(2,1)S(1)}, bf16[512,512]{1,0:T(8,128)(2,1)S(1)}, u32[]{:S(2)}, u32[]{:S(2)}) collective-permute-start(bf16[512,512]{1,0:T(8,128)(2,1)S(1)} %shard_map.58.refs_2_), channel_id=1, source_target_pairs={{0,16},{8,24},{16,0},{24,8},{1,17},{9,25},{17,1},{25,9},{2,18},{10... | collective-permute-start | bytes 1572872 | tf_op jit(solution)/shard_map/ppermute | solution.py:415
  93.3 2.0 %shard_map.61 = (bf16[512,1024]{1,0:T(8,128)(2,1)S(1)}, bf16[512,2,512]{2,1,0:T(2,128)(2,1)S(1)}) custom-call(s32[4]{0:T(128)S(1)} %pad_add_fusion.refs_0_, bf16[2,512,512]{2,1,0:T(8,128)(2,1)S(1)} %copy-done.4, bf16[256,1024]{1,0:T(8,128)(2,1)S(1)} %get-tuple-element.56.refs_2_.refs_6_, bf16[256,1024]{1,0:T(8,128)(2,1)S(1)} %collective-permute-done.19.refs_3_.refs_7_, ...), custom_call_target="tpu_custom_call" | custom-call | flops 2200000000 | tf_op jit(solution)/shard_map/pallas_call | solution.py:37
  95.5 2.3 %collective-permute-done.23.refs_4_.refs_18_.refs_17_.refs_16_.refs_15_ = bf16[512,512]{1,0:T(8,128)(2,1)S(1)} collective-permute-done((bf16[512,512]{1,0:T(8,128)(2,1)S(1)}, bf16[512,512]{1,0:T(8,128)(2,1)S(1)}, u32[]{:S(2)}, u32[]{:S(2)}) %collective-permute-start.23) | collective-permute-done | bytes 524320 | tf_op jit(solution)/shard_map/ppermute | solution.py:412
  98.5 3.4 %collective-permute-start.26 = (bf16[512,512]{1,0:T(8,128)(2,1)S(1)}, bf16[512,512]{1,0:T(8,128)(2,1)S(1)}, u32[]{:S(2)}, u32[]{:S(2)}) collective-permute-start(bf16[512,512]{1,0:T(8,128)(2,1)S(1)} %shard_map.62.refs_2_.refs_14_.refs_13_.refs_12_.refs_11_), channel_id=1, source_target_pairs={{0,2},{1,3},{2,4},{3,5},{4,6},{5,7},{8,10},{9,11},{10,12},{11,13},... | collective-permute-start | bytes 1572872 | tf_op jit(solution)/shard_map/ppermute | solution.py:418
  102.0 1.6 collective-permute-start.27
  103.6 1.8 %collective-permute-done.15.refs_4_ = bf16[512,512]{1,0:T(8,128)(2,1)S(1)} collective-permute-done((bf16[512,512]{1,0:T(8,128)(2,1)S(1)}, bf16[512,512]{1,0:T(8,128)(2,1)S(1)}, u32[]{:S(2)}, u32[]{:S(2)}) %collective-permute-start.15) | collective-permute-done | bytes 524320 | tf_op jit(solution)/shard_map/ppermute | solution.py:415
  105.4 0.6 shard_map.64.refs_10_.refs_2_
  106.1 3.5 %shard_map.65 = (bf16[512,1024]{1,0:T(8,128)(2,1)S(1)}, bf16[512,512]{1,0:T(8,128)(2,1)S(1)}, bf16[512,2,512]{2,1,0:T(2,128)(2,1)S(1)}) custom-call(s32[4]{0:T(128)S(1)} %pad_add_fusion.refs_0_, bf16[2,512,512]{2,1,0:T(8,128)(2,1)S(1)} %copy-done.4, bf16[2,512,512]{2,1,0:T(8,128)(2,1)S(1)} %copy-done, ...), custom_call_target="tpu_custom_call" | custom-call | flops 3849999872 | tf_op jit(solution)/shard_map/pallas_call | solution.py:37
  109.6 4.2 %collective-permute-done.26.refs_1_ = bf16[512,512]{1,0:T(8,128)(2,1)S(1)} collective-permute-done((bf16[512,512]{1,0:T(8,128)(2,1)S(1)}, bf16[512,512]{1,0:T(8,128)(2,1)S(1)}, u32[]{:S(2)}, u32[]{:S(2)}) %collective-permute-start.26) | collective-permute-done | bytes 524320 | tf_op jit(solution)/shard_map/ppermute | solution.py:418
  113.8 2.3 %collective-permute-done.27.refs_3_.refs_18_.refs_17_.refs_16_.refs_15_ = bf16[512,512]{1,0:T(8,128)(2,1)S(1)} collective-permute-done((bf16[512,512]{1,0:T(8,128)(2,1)S(1)}, bf16[512,512]{1,0:T(8,128)(2,1)S(1)}, u32[]{:S(2)}, u32[]{:S(2)}) %collective-permute-start.27) | collective-permute-done | bytes 524320 | tf_op jit(solution)/shard_map/ppermute | solution.py:412
  116.7 1.6 collective-permute-start.29
  118.3 4.4 %collective-permute-start.28 = (bf16[256,512]{1,0:T(8,128)(2,1)S(1)}, bf16[256,512]{1,0:T(8,128)(2,1)S(1)}, u32[]{:S(2)}, u32[]{:S(2)}) collective-permute-start(bf16[256,512]{1,0:T(8,128)(2,1)S(1)} %slice.4), channel_id=1, source_target_pairs={{0,2},{1,3},{2,4},{3,5},{4,6},{5,7},{8,10},{9,11},{10,12},{11,13},... | collective-permute-start | bytes 786440 | tf_op jit(solution)/shard_map/ppermute | solution.py:418
  122.7 1.8 %shard_map.67 = (bf16[2560,2,512]{2,1,0:T(2,128)(2,1)}, f32[8,128]{1,0:T(8,128)S(1)}) custom-call(s32[4]{0:T(128)S(1)} %pad_add_fusion.refs_0_, s32[2,512]{1,0:T(2,128)S(1)} %get-tuple-element.41.refs_2_.refs_1_, bf16[2,512,512]{2,1,0:T(8,128)(2,1)S(1)} %shard_map.64.refs_10_.refs_2_, bf16[2,512,512]{2,1,0:T(8,128)(2,1)S(1)} %collective-permute-done.24.refs_3_, ...), custom_call_target="tpu_custom_call" | custom-call | flops 5500000256 | tf_op jit(solution)/shard_map/pallas_call | solution.py:37
  124.5 6.2 %shard_map.68 = (bf16[2560,2,512]{2,1,0:T(2,128)(2,1)}, f32[8,128]{1,0:T(8,128)S(1)}) custom-call(s32[4]{0:T(128)S(1)} %pad_add_fusion.refs_0_, s32[2,512]{1,0:T(2,128)S(1)} %get-tuple-element.41.refs_2_.refs_1_, bf16[2,512,512]{2,1,0:T(8,128)(2,1)S(1)} %shard_map.64.refs_10_.refs_2_, ...), custom_call_target="tpu_custom_call", output_to_operand_aliasing={{0}: (19, {})} | custom-call | flops 5500000256 | tf_op jit(solution)/shard_map/pallas_call | solution.py:37
  131.3 3.6 %collective-permute-start.30 = (bf16[256,512]{1,0:T(8,128)(2,1)S(1)}, bf16[256,512]{1,0:T(8,128)(2,1)S(1)}, u32[]{:S(2)}, u32[]{:S(2)}) collective-permute-start(bf16[256,512]{1,0:T(8,128)(2,1)S(1)} %shard_map.69.refs_20_.refs_14_.refs_13_), channel_id=1, source_target_pairs={{0,2},{1,3},{2,4},{3,5},{4,6},{5,7},{8,10},{9,11},{10,12},{11,13},... | collective-permute-start | bytes 786440 | tf_op jit(solution)/shard_map/ppermute | solution.py:418
  134.9 1.6 collective-permute-start.31
  136.5 6.4 %shard_map.70 = (bf16[2560,2,512]{2,1,0:T(2,128)(2,1)}, f32[8,128]{1,0:T(8,128)S(1)}) custom-call(s32[4]{0:T(128)S(1)} %pad_add_fusion.refs_0_, s32[2,512]{1,0:T(2,128)S(1)} %get-tuple-element.41.refs_2_.refs_1_, bf16[2,512,512]{2,1,0:T(8,128)(2,1)S(1)} %shard_map.64.refs_10_.refs_2_, ...), custom_call_target="tpu_custom_call", output_to_operand_aliasing={{0}: (19, {})} | custom-call | flops 5500000256 | tf_op jit(solution)/shard_map/pallas_call | solution.py:37
  144.1 6.2 %shard_map.72 = (bf16[2560,2,512]{2,1,0:T(2,128)(2,1)}, f32[8,128]{1,0:T(8,128)S(1)}) custom-call(s32[4]{0:T(128)S(1)} %pad_add_fusion.refs_0_, s32[2,512]{1,0:T(2,128)S(1)} %get-tuple-element.41.refs_2_.refs_1_, bf16[2,512,512]{2,1,0:T(8,128)(2,1)S(1)} %shard_map.64.refs_10_.refs_2_, ...), custom_call_target="tpu_custom_call", output_to_operand_aliasing={{0}: (19, {})} | custom-call | flops 5500000256 | tf_op jit(solution)/shard_map/pallas_call | solution.py:37
  150.3 4.1 %shard_map.73 = (bf16[2560,2,512]{2,1,0:T(2,128)(2,1)}, f32[8,128]{1,0:T(8,128)S(1)}) custom-call(s32[4]{0:T(128)S(1)} %pad_add_fusion.refs_0_, s32[2,512]{1,0:T(2,128)S(1)} %get-tuple-element.41.refs_2_.refs_1_, bf16[2,512,512]{2,1,0:T(8,128)(2,1)S(1)} %shard_map.64.refs_10_.refs_2_, ...), custom_call_target="tpu_custom_call", output_to_operand_aliasing={{0}: (19, {})} | custom-call | flops 5500000256 | tf_op jit(solution)/shard_map/pallas_call | solution.py:37
  154.3 4.6 %shard_map.74 = (bf16[2560,2,512]{2,1,0:T(2,128)(2,1)}, f32[8,128]{1,0:T(8,128)}) custom-call(s32[4]{0:T(128)S(1)} %pad_add_fusion.refs_0_, s32[2,512]{1,0:T(2,128)S(1)} %get-tuple-element.41.refs_2_.refs_1_, bf16[2,512,512]{2,1,0:T(8,128)(2,1)S(1)} %shard_map.64.refs_10_.refs_2_, ...), custom_call_target="tpu_custom_call", output_to_operand_aliasing={{0}: (19, {})} | custom-call | flops 5500000256 | tf_op jit(solution)/shard_map/pallas_call | solution.py:37
  (62 shorter events, 11.7 us)
Async XLA Ops:
  0.0 8.8 %copy-start.5 = (s32[2,512]{1,0:T(2,128)S(1)}, s32[2,512]{1,0:T(2,128)}, u32[]{:S(2)}) copy-start(s32[2,512]{1,0:T(2,128)} %refs_1_.3) | copy-start | bytes 12292
  2.2 18.7 %collective-permute-start.1 = (bf16[512,512]{1,0:T(8,128)(2,1)}, bf16[512,512]{1,0:T(8,128)(2,1)S(1)}, u32[]{:S(2)}, u32[]{:S(2)}) collective-permute-start(bf16[512,512]{1,0:T(8,128)(2,1)} %shard_map.46.refs_4_.refs_1_.refs_11_), channel_id=1, source_target_pairs={{0,1},{1,0},{2,3},{3,2},{4,5},{5,4},{6,7},{7,6},{8,9},{9,8},{10,11... | collective-permute-start | bytes 1572872 | tf_op jit(solution)/shard_map/ppermute | solution.py:412
  5.2 15.7 %collective-permute-start = (bf16[512,512]{1,0:T(8,128)(2,1)}, bf16[512,512]{1,0:T(8,128)(2,1)S(1)}, u32[]{:S(2)}, u32[]{:S(2)}) collective-permute-start(bf16[512,512]{1,0:T(8,128)(2,1)} %shard_map.46.refs_4_.refs_1_.refs_11_), channel_id=1, source_target_pairs={{0,2},{1,3},{2,4},{3,5},{4,6},{5,7},{8,10},{9,11},{10,12},{11,13},... | collective-permute-start | bytes 1572872 | tf_op jit(solution)/shard_map/ppermute | solution.py:418
  9.0 2.5 %copy-start.1 = (bf16[5,512,2,512]{3,2,1,0:T(2,128)(2,1)S(1)}, bf16[5,512,2,512]{3,2,1,0:T(2,128)(2,1)}, u32[]{:S(2)}) copy-start(bf16[5,512,2,512]{3,2,1,0:T(2,128)(2,1)} %param.4) | copy-start | bytes 15728644
  11.5 1.0 copy-start.2
  20.3 5.2 %collective-permute-start.3 = (bf16[512,2,512]{2,1,0:T(2,128)(2,1)S(1)}, bf16[512,2,512]{2,1,0:T(2,128)(2,1)S(1)}, u32[]{:S(2)}, u32[]{:S(2)}) collective-permute-start(bf16[512,2,512]{2,1,0:T(2,128)(2,1)S(1)} %get-tuple-element.47), channel_id=1, source_target_pairs={{0,8},{8,0},{16,24},{24,16},{1,9},{9,1},{17,25},{25,17},{2,10},{10... | collective-permute-start | bytes 3145736 | tf_op jit(solution)/shard_map/ppermute | solution.py:409
  20.4 18.3 %collective-permute-start.5 = (bf16[512,2,512]{2,1,0:T(2,128)(2,1)S(1)}, bf16[512,2,512]{2,1,0:T(2,128)(2,1)S(1)}, u32[]{:S(2)}, u32[]{:S(2)}) collective-permute-start(bf16[512,2,512]{2,1,0:T(2,128)(2,1)S(1)} %get-tuple-element.49.refs_7_), channel_id=1, source_target_pairs={{0,8},{8,0},{16,24},{24,16},{1,9},{9,1},{17,25},{25,17},{2,10},{10... | collective-permute-start | bytes 3145736 | tf_op jit(solution)/shard_map/ppermute | solution.py:409
  21.5 14.9 %collective-permute-start.2 = (bf16[512,512]{1,0:T(8,128)(2,1)S(1)}, bf16[512,512]{1,0:T(8,128)(2,1)S(1)}, u32[]{:S(2)}, u32[]{:S(2)}) collective-permute-start(bf16[512,512]{1,0:T(8,128)(2,1)S(1)} %shard_map.48.refs_4_.refs_2_.refs_12_.refs_11_), channel_id=1, source_target_pairs={{0,2},{1,3},{2,4},{3,5},{4,6},{5,7},{8,10},{9,11},{10,12},{11,13},... | collective-permute-start | bytes 1572872 | tf_op jit(solution)/shard_map/ppermute | solution.py:418
  25.0 13.7 %collective-permute-start.4 = (bf16[512,512]{1,0:T(8,128)(2,1)S(1)}, bf16[512,512]{1,0:T(8,128)(2,1)S(1)}, u32[]{:S(2)}, u32[]{:S(2)}) collective-permute-start(bf16[512,512]{1,0:T(8,128)(2,1)S(1)} %shard_map.48.refs_4_.refs_2_.refs_12_.refs_11_), channel_id=1, source_target_pairs={{0,1},{1,0},{2,3},{3,2},{4,5},{5,4},{6,7},{7,6},{8,9},{9,8},{10,11... | collective-permute-start | bytes 1572872 | tf_op jit(solution)/shard_map/ppermute | solution.py:412
  27.9 15.4 %collective-permute-start.7 = (bf16[256,2,512]{2,1,0:T(2,128)(2,1)S(1)}, bf16[256,2,512]{2,1,0:T(2,128)(2,1)S(1)}, u32[]{:S(2)}, u32[]{:S(2)}) collective-permute-start(bf16[256,2,512]{2,1,0:T(2,128)(2,1)S(1)} %get-tuple-element.51.refs_2_), channel_id=1, source_target_pairs={{0,16},{8,24},{16,0},{24,8},{1,17},{9,25},{17,1},{25,9},{2,18},{10... | collective-permute-start | bytes 1572872 | tf_op jit(solution)/shard_map/ppermute | solution.py:415
  39.3 15.1 %collective-permute-start.6 = (bf16[512,512]{1,0:T(8,128)(2,1)S(1)}, bf16[512,512]{1,0:T(8,128)(2,1)S(1)}, u32[]{:S(2)}, u32[]{:S(2)}) collective-permute-start(bf16[512,512]{1,0:T(8,128)(2,1)S(1)} %shard_map.50.refs_4_.refs_3_.refs_13_.refs_12_.refs_11_), channel_id=1, source_target_pairs={{0,2},{1,3},{2,4},{3,5},{4,6},{5,7},{8,10},{9,11},{10,12},{11,13},... | collective-permute-start | bytes 1572872 | tf_op jit(solution)/shard_map/ppermute | solution.py:418
  42.7 12.5 %collective-permute-start.8 = (bf16[512,512]{1,0:T(8,128)(2,1)S(1)}, bf16[512,512]{1,0:T(8,128)(2,1)S(1)}, u32[]{:S(2)}, u32[]{:S(2)}) collective-permute-start(bf16[512,512]{1,0:T(8,128)(2,1)S(1)} %shard_map.50.refs_4_.refs_3_.refs_13_.refs_12_.refs_11_), channel_id=1, source_target_pairs={{0,1},{1,0},{2,3},{3,2},{4,5},{5,4},{6,7},{7,6},{8,9},{9,8},{10,11... | collective-permute-start | bytes 1572872 | tf_op jit(solution)/shard_map/ppermute | solution.py:412
  44.5 11.3 %collective-permute-start.9 = (bf16[128,512]{1,0:T(8,128)(2,1)S(1)}, bf16[128,512]{1,0:T(8,128)(2,1)S(1)}, u32[]{:S(2)}, u32[]{:S(2)}) collective-permute-start(bf16[128,512]{1,0:T(8,128)(2,1)S(1)} %get-tuple-element.52.refs_3_.refs_1_), channel_id=1, source_target_pairs={{0,4},{1,5},{8,12},{9,13},{16,20},{17,21},{24,28},{25,29}} | collective-permute-start | bytes 393224 | tf_op jit(solution)/shard_map/ppermute | solution.py:512
  46.3 16.5 %collective-permute-start.13 = (bf16[256,2,512]{2,1,0:T(2,128)(2,1)S(1)}, bf16[256,2,512]{2,1,0:T(2,128)(2,1)S(1)}, u32[]{:S(2)}, u32[]{:S(2)}) collective-permute-start(bf16[256,2,512]{2,1,0:T(2,128)(2,1)S(1)} %get-tuple-element.48.refs_3_.refs_2_), channel_id=1, source_target_pairs={{0,16},{8,24},{16,0},{24,8},{1,17},{9,25},{17,1},{25,9},{2,18},{10... | collective-permute-start | bytes 1572872 | tf_op jit(solution)/shard_map/ppermute | solution.py:415
  57.6 16.1 %collective-permute-start.14 = (bf16[512,512]{1,0:T(8,128)(2,1)S(1)}, bf16[512,512]{1,0:T(8,128)(2,1)S(1)}, u32[]{:S(2)}, u32[]{:S(2)}) collective-permute-start(bf16[512,512]{1,0:T(8,128)(2,1)S(1)} %shard_map.54.refs_4_.refs_1_), channel_id=1, source_target_pairs={{0,16},{8,24},{16,0},{24,8},{1,17},{9,25},{17,1},{25,9},{2,18},{10... | collective-permute-start | bytes 1572872 | tf_op jit(solution)/shard_map/ppermute | solution.py:415
  59.1 15.1 %collective-permute-start.10 = (bf16[512,512]{1,0:T(8,128)(2,1)S(1)}, bf16[512,512]{1,0:T(8,128)(2,1)S(1)}, u32[]{:S(2)}, u32[]{:S(2)}) collective-permute-start(bf16[512,512]{1,0:T(8,128)(2,1)S(1)} %shard_map.52.refs_3_.refs_4_.refs_14_.refs_13_.refs_12_.refs_11_), channel_id=1, source_target_pairs={{0,1},{1,0},{2,3},{3,2},{4,5},{5,4},{6,7},{7,6},{8,9},{9,8},{10,11... | collective-permute-start | bytes 1572872 | tf_op jit(solution)/shard_map/ppermute | solution.py:412
  59.6 14.7 %collective-permute-start.11 = (bf16[512,512]{1,0:T(8,128)(2,1)S(1)}, bf16[512,512]{1,0:T(8,128)(2,1)S(1)}, u32[]{:S(2)}, u32[]{:S(2)}) collective-permute-start(bf16[512,512]{1,0:T(8,128)(2,1)S(1)} %shard_map.52.refs_3_.refs_4_.refs_14_.refs_13_.refs_12_.refs_11_), channel_id=1, source_target_pairs={{0,2},{1,3},{2,4},{3,5},{4,6},{5,7},{8,10},{9,11},{10,12},{11,13},... | collective-permute-start | bytes 1572872 | tf_op jit(solution)/shard_map/ppermute | solution.py:418
  62.6 21.9 %collective-permute-start.21 = (bf16[256,2,512]{2,1,0:T(2,128)(2,1)S(1)}, bf16[256,2,512]{2,1,0:T(2,128)(2,1)S(1)}, u32[]{:S(2)}, u32[]{:S(2)}) collective-permute-start(bf16[256,2,512]{2,1,0:T(2,128)(2,1)S(1)} %get-tuple-element.59.refs_3_), channel_id=1, source_target_pairs={{0,8},{8,0},{16,24},{24,16},{1,9},{9,1},{17,25},{25,17},{2,10},{10... | collective-permute-start | bytes 1572872 | tf_op jit(solution)/shard_map/ppermute | solution.py:409
  62.7 10.3 %collective-permute-start.12 = (bf16[128,512]{1,0:T(8,128)(2,1)S(1)}, bf16[128,512]{1,0:T(8,128)(2,1)S(1)}, u32[]{:S(2)}, u32[]{:S(2)}) collective-permute-start(bf16[128,512]{1,0:T(8,128)(2,1)S(1)} %shard_map.53.refs_5_.refs_1_), channel_id=1, source_target_pairs={{0,2},{1,3},{4,6},{5,7},{8,10},{9,11},{12,14},{13,15},{16,18},{17,... | collective-permute-start | bytes 393224 | tf_op jit(solution)/shard_map/ppermute | solution.py:512
  73.0 18.5 %collective-permute-start.19 = (bf16[256,1024]{1,0:T(8,128)(2,1)S(1)}, bf16[256,1024]{1,0:T(8,128)(2,1)S(1)}, u32[]{:S(2)}, u32[]{:S(2)}) collective-permute-start(bf16[256,1024]{1,0:T(8,128)(2,1)S(1)} %get-tuple-element.56.refs_2_.refs_6_), channel_id=1, source_target_pairs={{0,8},{8,0},{16,24},{24,16},{1,9},{9,1},{17,25},{25,17},{2,10},{10... | collective-permute-start | bytes 1572872 | tf_op jit(solution)/shard_map/ppermute | solution.py:409
  73.6 13.2 %collective-permute-start.22 = (bf16[256,2,512]{2,1,0:T(2,128)(2,1)S(1)}, bf16[256,2,512]{2,1,0:T(2,128)(2,1)S(1)}, u32[]{:S(2)}, u32[]{:S(2)}) collective-permute-start(bf16[256,2,512]{2,1,0:T(2,128)(2,1)S(1)} %get-tuple-element.54.refs_3_.refs_5_), channel_id=1, source_target_pairs={{0,8},{8,0},{16,24},{24,16},{1,9},{9,1},{17,25},{25,17},{2,10},{10... | collective-permute-start | bytes 1572872 | tf_op jit(solution)/shard_map/ppermute | solution.py:409
  74.2 19.1 %collective-permute-start.20 = (bf16[256,1024]{1,0:T(8,128)(2,1)S(1)}, bf16[256,1024]{1,0:T(8,128)(2,1)S(1)}, u32[]{:S(2)}, u32[]{:S(2)}) collective-permute-start(bf16[256,1024]{1,0:T(8,128)(2,1)S(1)} %get-tuple-element.57.refs_4_.refs_8_), channel_id=1, source_target_pairs={{0,8},{8,0},{16,24},{24,16},{1,9},{9,1},{17,25},{25,17},{2,10},{10... | collective-permute-start | bytes 1572872 | tf_op jit(solution)/shard_map/ppermute | solution.py:409
  74.3 5.8 %collective-permute-start.16 = (bf16[128,512]{1,0:T(8,128)(2,1)S(1)}, bf16[128,512]{1,0:T(8,128)(2,1)S(1)}, u32[]{:S(2)}, u32[]{:S(2)}) collective-permute-start(bf16[128,512]{1,0:T(8,128)(2,1)S(1)} %shard_map.56.refs_3_.refs_0_), channel_id=1, source_target_pairs={{0,1},{1,0},{2,3},{3,2},{4,5},{5,4},{6,7},{7,6},{8,9},{9,8},{10,11... | collective-permute-start | bytes 393224 | tf_op jit(solution)/shard_map/ppermute | solution.py:412
  80.1 15.4 %collective-permute-start.18 = (bf16[512,512]{1,0:T(8,128)(2,1)S(1)}, bf16[512,512]{1,0:T(8,128)(2,1)S(1)}, u32[]{:S(2)}, u32[]{:S(2)}) collective-permute-start(bf16[512,512]{1,0:T(8,128)(2,1)S(1)} %shard_map.57.refs_5_.refs_14_.refs_13_.refs_12_.refs_11_), channel_id=1, source_target_pairs={{0,2},{1,3},{2,4},{3,5},{4,6},{5,7},{8,10},{9,11},{10,12},{11,13},... | collective-permute-start | bytes 1572872 | tf_op jit(solution)/shard_map/ppermute | solution.py:418
  84.6 13.3 %collective-permute-start.23 = (bf16[512,512]{1,0:T(8,128)(2,1)S(1)}, bf16[512,512]{1,0:T(8,128)(2,1)S(1)}, u32[]{:S(2)}, u32[]{:S(2)}) collective-permute-start(bf16[512,512]{1,0:T(8,128)(2,1)S(1)} %shard_map.57.refs_5_.refs_14_.refs_13_.refs_12_.refs_11_), channel_id=1, source_target_pairs={{0,1},{1,0},{2,3},{3,2},{4,5},{5,4},{6,7},{7,6},{8,9},{9,8},{10,11... | collective-permute-start | bytes 1572872 | tf_op jit(solution)/shard_map/ppermute | solution.py:412
  86.8 11.6 %collective-permute-start.17 = (bf16[2,128,512]{2,1,0:T(8,128)(2,1)S(1)}, bf16[2,128,512]{2,1,0:T(8,128)(2,1)S(1)}, u32[]{:S(2)}, u32[]{:S(2)}) collective-permute-start(bf16[2,128,512]{2,1,0:T(8,128)(2,1)S(1)} %shard_map.59.refs_10_.refs_0_), channel_id=1, source_target_pairs={{0,16},{8,24},{16,0},{24,8},{1,17},{9,25},{17,1},{25,9},{2,18},{10... | collective-permute-start | bytes 786440 | tf_op jit(solution)/shard_map/ppermute | solution.py:415
  87.4 5.9 %copy-start.4 = (bf16[2,512,512]{2,1,0:T(8,128)(2,1)S(1)}, bf16[2,512,512]{2,1,0:T(8,128)(2,1)}, u32[]{:S(2)}) copy-start(bf16[2,512,512]{2,1,0:T(8,128)(2,1)} %refs_1_.5) | copy-start | bytes 3145732
  91.5 13.9 %collective-permute-start.15 = (bf16[512,512]{1,0:T(8,128)(2,1)S(1)}, bf16[512,512]{1,0:T(8,128)(2,1)S(1)}, u32[]{:S(2)}, u32[]{:S(2)}) collective-permute-start(bf16[512,512]{1,0:T(8,128)(2,1)S(1)} %shard_map.58.refs_2_), channel_id=1, source_target_pairs={{0,16},{8,24},{16,0},{24,8},{1,17},{9,25},{17,1},{25,9},{2,18},{10... | collective-permute-start | bytes 1572872 | tf_op jit(solution)/shard_map/ppermute | solution.py:415
  95.3 10.9 %copy-start = (bf16[2,512,512]{2,1,0:T(8,128)(2,1)S(1)}, bf16[2,512,512]{2,1,0:T(8,128)(2,1)}, u32[]{:S(2)}) copy-start(bf16[2,512,512]{2,1,0:T(8,128)(2,1)} %refs_4_.11) | copy-start | bytes 3145732
  98.5 7.7 %collective-permute-start.25 = (bf16[2,2,128,512]{3,2,1,0:T(8,128)(2,1)S(1)}, bf16[2,2,128,512]{3,2,1,0:T(8,128)(2,1)S(1)}, u32[]{:S(2)}, u32[]{:S(2)}) collective-permute-start(bf16[2,2,128,512]{3,2,1,0:T(8,128)(2,1)S(1)} %shard_map.63.refs_5_.refs_4_), channel_id=1, source_target_pairs={{0,8},{8,0},{16,24},{24,16},{1,9},{9,1},{17,25},{25,17},{2,10},{10... | collective-permute-start | bytes 1572872 | tf_op jit(solution)/shard_map/ppermute | solution.py:409
  98.5 15.2 %collective-permute-start.26 = (bf16[512,512]{1,0:T(8,128)(2,1)S(1)}, bf16[512,512]{1,0:T(8,128)(2,1)S(1)}, u32[]{:S(2)}, u32[]{:S(2)}) collective-permute-start(bf16[512,512]{1,0:T(8,128)(2,1)S(1)} %shard_map.62.refs_2_.refs_14_.refs_13_.refs_12_.refs_11_), channel_id=1, source_target_pairs={{0,2},{1,3},{2,4},{3,5},{4,6},{5,7},{8,10},{9,11},{10,12},{11,13},... | collective-permute-start | bytes 1572872 | tf_op jit(solution)/shard_map/ppermute | solution.py:418
  102.0 14.1 %collective-permute-start.27 = (bf16[512,512]{1,0:T(8,128)(2,1)S(1)}, bf16[512,512]{1,0:T(8,128)(2,1)S(1)}, u32[]{:S(2)}, u32[]{:S(2)}) collective-permute-start(bf16[512,512]{1,0:T(8,128)(2,1)S(1)} %shard_map.62.refs_2_.refs_14_.refs_13_.refs_12_.refs_11_), channel_id=1, source_target_pairs={{0,1},{1,0},{2,3},{3,2},{4,5},{5,4},{6,7},{7,6},{8,9},{9,8},{10,11... | collective-permute-start | bytes 1572872 | tf_op jit(solution)/shard_map/ppermute | solution.py:412
  106.0 16.6 %collective-permute-start.24 = (bf16[2,512,512]{2,1,0:T(8,128)(2,1)S(1)}, bf16[2,512,512]{2,1,0:T(8,128)(2,1)S(1)}, u32[]{:S(2)}, u32[]{:S(2)}) collective-permute-start(bf16[2,512,512]{2,1,0:T(8,128)(2,1)S(1)} %shard_map.64.refs_10_.refs_2_), channel_id=1, source_target_pairs={{0,8},{8,0},{16,24},{24,16},{1,9},{9,1},{17,25},{25,17},{2,10},{10... | collective-permute-start | bytes 3145736 | tf_op jit(solution)/shard_map/ppermute | solution.py:409
  116.1 6.6 %copy-start.3 = (bf16[512,512]{1,0:T(8,128)(2,1)S(1)}, bf16[512,512]{1,0:T(8,128)(2,1)}, u32[]{:S(2)}) copy-start(bf16[512,512]{1,0:T(8,128)(2,1)} %shard_map.46.refs_4_.refs_1_.refs_11_) | copy-start | bytes 1572868
  116.7 14.0 %collective-permute-start.29 = (bf16[512,512]{1,0:T(8,128)(2,1)S(1)}, bf16[512,512]{1,0:T(8,128)(2,1)S(1)}, u32[]{:S(2)}, u32[]{:S(2)}) collective-permute-start(bf16[512,512]{1,0:T(8,128)(2,1)S(1)} %shard_map.66.refs_19_.refs_14_.refs_13_.refs_12_), channel_id=1, source_target_pairs={{0,1},{1,0},{2,3},{3,2},{4,5},{5,4},{6,7},{7,6},{8,9},{9,8},{10,11... | collective-permute-start | bytes 1572872 | tf_op jit(solution)/shard_map/ppermute | solution.py:412
  118.3 12.4 %collective-permute-start.28 = (bf16[256,512]{1,0:T(8,128)(2,1)S(1)}, bf16[256,512]{1,0:T(8,128)(2,1)S(1)}, u32[]{:S(2)}, u32[]{:S(2)}) collective-permute-start(bf16[256,512]{1,0:T(8,128)(2,1)S(1)} %slice.4), channel_id=1, source_target_pairs={{0,2},{1,3},{2,4},{3,5},{4,6},{5,7},{8,10},{9,11},{10,12},{11,13},... | collective-permute-start | bytes 786440 | tf_op jit(solution)/shard_map/ppermute | solution.py:418
  131.3 11.7 %collective-permute-start.30 = (bf16[256,512]{1,0:T(8,128)(2,1)S(1)}, bf16[256,512]{1,0:T(8,128)(2,1)S(1)}, u32[]{:S(2)}, u32[]{:S(2)}) collective-permute-start(bf16[256,512]{1,0:T(8,128)(2,1)S(1)} %shard_map.69.refs_20_.refs_14_.refs_13_), channel_id=1, source_target_pairs={{0,2},{1,3},{2,4},{3,5},{4,6},{5,7},{8,10},{9,11},{10,12},{11,13},... | collective-permute-start | bytes 786440 | tf_op jit(solution)/shard_map/ppermute | solution.py:418
  134.9 8.0 %collective-permute-start.31 = (bf16[256,512]{1,0:T(8,128)(2,1)S(1)}, bf16[256,512]{1,0:T(8,128)(2,1)S(1)}, u32[]{:S(2)}, u32[]{:S(2)}) collective-permute-start(bf16[256,512]{1,0:T(8,128)(2,1)S(1)} %shard_map.69.refs_20_.refs_14_.refs_13_), channel_id=1, source_target_pairs={{0,1},{1,0},{2,3},{3,2},{4,5},{5,4},{6,7},{7,6},{8,9},{9,8},{10,11... | collective-permute-start | bytes 786440 | tf_op jit(solution)/shard_map/ppermute | solution.py:412
  143.5 10.8 %collective-permute-start.32 = (bf16[256,512]{1,0:T(8,128)(2,1)S(1)}, bf16[256,512]{1,0:T(8,128)(2,1)S(1)}, u32[]{:S(2)}, u32[]{:S(2)}) collective-permute-start(bf16[256,512]{1,0:T(8,128)(2,1)S(1)} %shard_map.71.refs_20_.refs_14_), channel_id=1, source_target_pairs={{0,1},{1,0},{2,3},{3,2},{4,5},{5,4},{6,7},{7,6},{8,9},{9,8},{10,11... | collective-permute-start | bytes 786440 | tf_op jit(solution)/shard_map/ppermute | solution.py:412

commit v8 on v6

--- a/solution.py
+++ b/solution.py
@@ -315,18 +315,20 @@
 
 
 def update_kernel(
-    begin, line, meta, goal, old, old_sibling, upper, up0, up1, up0_panel, tiles, top0, top1, *rest
+    begin, line, sizes, meta, goal, old, old_sibling, upper, up0, up1, up0_panel, tiles, top0, top1, *rest
 ):
-    held, other = rest[:line], rest[line : 2 * line]
+    spans = len(sizes) * line
+    held, other = rest[:spans], rest[spans : 2 * spans]
     out, token, panels, block, result, panel_sem, block_sem, out_sem = rest[-8:]
     row, core, column = meta[0], meta[1], meta[2]
     side, place = lax.rem(column, 2), lax.div(column, 2)
     count, cb, nb = block.shape
     rows_of = pl.ds(begin, count)
 
-    def panel_copy(h, which):
-        source = (held, other)[which][h].at[pl.ds(0, count)]
-        return pltpu.make_async_copy(source, panels.at[lax.rem(side + which, 2)], panel_sem.at[which])
+    def panel_copy(i, h, which):
+        source = (held, other)[which][i * line + h].at[pl.ds(0, sizes[i])]
+        target = panels.at[lax.rem(side + which, 2), pl.ds(sum(sizes[:i]), sizes[i])]
+        return pltpu.make_async_copy(source, target, panel_sem.at[i, which])
 
     load = pltpu.make_async_copy(tiles.at[rows_of], block, block_sem)
     load.start()
@@ -334,12 +336,14 @@
 
         @pl.when(place == h)
         def _(h=h):
-            panel_copy(h, 0).start()
-            panel_copy(h, 1).start()
+            for i in range(len(sizes)):
+                panel_copy(i, h, 0).start()
+                panel_copy(i, h, 1).start()
 
     def arrived():
-        panel_copy(0, 0).wait()
-        panel_copy(0, 1).wait()
+        for i in range(len(sizes)):
+            panel_copy(i, 0, 0).wait()
+            panel_copy(i, 0, 1).wait()
 
     def from_factors():
         here = begin + lax.broadcasted_iota(I32, (count, nb), 0)
@@ -557,31 +561,33 @@
             us=3.5, mib=16,
         )
 
-    def update(i):
+    def update(i, group=1):
         operands = [(meta, SMEM), (state["goal"], VMEM)] + [(v, VMEM) for v in state["old"]] + [(upper, VMEM)]
         operands += [(state[name], VMEM) for name in ("up0", "up1", "up0_panel")]
         operands += [(state[name], ANY) for name in ("moved", "top0", "top1")]
-        operands += [(v, ANY) for v in held[i : i + line] + other[i : i + line]]
+        places = [p + h for p in range(i, i + group) for h in range(line)]
+        operands += [(values[p], ANY) for values in (held, other) for p in places]
         aliases = {}
         if "result" in state:
             aliases = {len(operands): 0}
             operands.append((state["result"], ANY))
-        count = sizes[i]
+        count = sum(sizes[i : i + group])
         state["result"], _ = run(
-            functools.partial(update_kernel, begins[i], line),
+            functools.partial(update_kernel, begins[i], line, tuple(sizes[i : i + group])),
             operands,
             [(bf16(rows, cb, nb), ANY), (jax.ShapeDtypeStruct((8, 128), F32), VMEM)],
             scratch=[
                 pltpu.VMEM((2, count, nb), BF16), pltpu.VMEM((count, cb, nb), BF16),
-                pltpu.VMEM((count, cb, nb), BF16), DMA((2,)), DMA, DMA,
+                pltpu.VMEM((count, cb, nb), BF16), DMA((group, 2)), DMA, DMA,
             ],
             aliases=aliases,
             us=5.0, mib=24,
         )
 
     plan = [(0, gather), (1, join), (2, functools.partial(fresh, 0)), (3, head_here), (line - 1, functools.partial(old, held, "old_held")), (3, head_pair), (3, functools.partial(fresh, 1)), (line, functools.partial(old, other, "old_other")), (4, scatter), (4, prep0), (5, head_all), (5, old_here), (5, prep1)]
-    for i in range(pieces):
-        plan.append((max((6, 6, 7, 8, 8, 8)[min(i, 5)], i + line - 1), functools.partial(update, i)))
+    for i in range(pieces - 2):
+        plan.append((max(6 + i // 2, i + line - 1) if i < 3 else last_step, functools.partial(update, i)))
+    plan.append((last_step, functools.partial(update, pieces - 2, 2)))
     for k in range(last_step + 1):
         step(k)
         while plan and (plan[0][0] <= k or k == last_step):

time: 159 us -> 157 us (0.987)
  Pallas kernels: 60.4 us -> 58.5 us
    pallas_call x28 -> x27, Pallas kernels: 60.4 us -> 58.5 us  [call(): pl.pallas_call(ordered, out_shape=tuple((shape for shape, _ in outs)), in...]
  transfers between devices with their start and end apart: 34 -> 34, of which waited for: 13 -> 13; matrix products, arithmetic and copies ran while one was open for 0% -> 0% of each run, Pallas kernels for 33% -> 31%
where the time goes in v8:
time: 157 us; the launch traced here: 156 us
  Pallas kernels  58.5 us (37%)
  starting transfers between devices  49.5 us (32%)
  waiting for transfers between devices  43.9 us (28%)
  local copies, waits for them, and re-layouts  3.76 us (2%)
    pallas_call x27, Pallas kernels, call(): pl.pallas_call(ordered, out_shape=tuple((shape for shape, _ in outs)), in...  58.5 us
    ppermute x8, starting transfers between devices, to_next(): lax.ppermute(value, 'pcol', [(c, c + 2) for c in range(col_devices - 2)])  26.2 us
    ppermute x8, waiting for transfers between devices, to_next(): lax.ppermute(value, 'pcol', [(c, c + 2) for c in range(col_devices - 2)])  19.5 us
    ppermute x10, waiting for transfers between devices, to_neighbour(): return lax.ppermute(value, 'pcol', [(c, c ^ 1) for c in range(col_devices)])  17.3 us
    ppermute x10, starting transfers between devices, to_neighbour(): return lax.ppermute(value, 'pcol', [(c, c ^ 1) for c in range(col_devices)])  10.1 us
    ppermute x5, starting transfers between devices, to_chip(): lax.ppermute(value, 'prow', [(r, (r + 2 * h) % row_devices) for r in rang...  6.92 us
    ppermute x3, waiting for transfers between devices, fresh(): lax.ppermute(head[0], 'pcol', [(0, 2 * h), (1, 2 * h + 1)])  4.82 us
    ppermute x3, starting transfers between devices, fresh(): lax.ppermute(head[0], 'pcol', [(0, 2 * h), (1, 2 * h + 1)])  4.4 us
  transfers between devices with their start and end apart: 34, of which 13 were waited for; matrix products, arithmetic and copies ran while one was open for 0% of the time, Pallas kernels for 31%

profile of v8, /device:TPU:0, one launch (start us, length us, event | category | flops | bytes accessed | tf_op | source)
XLA Modules:
  0.0 156.4 jit_solution(12616382626379893862)
XLA Ops:
  0.0 2.2 %shard_map.46.refs_4_.refs_1_.refs_11_ = bf16[512,512]{1,0:T(8,128)(2,1)} custom-call(bf16[2560,2,512]{2,1,0:T(2,128)(2,1)} %bitcast.5), custom_call_target="tpu_custom_call" | custom-call | flops 1100000000 | tf_op jit(solution)/shard_map/pallas_call | solution.py:37
  2.2 3.0 %collective-permute-start.1 = (bf16[512,512]{1,0:T(8,128)(2,1)}, bf16[512,512]{1,0:T(8,128)(2,1)S(1)}, u32[]{:S(2)}, u32[]{:S(2)}) collective-permute-start(bf16[512,512]{1,0:T(8,128)(2,1)} %shard_map.46.refs_4_.refs_1_.refs_11_), channel_id=1, source_target_pairs={{0,1},{1,0},{2,3},{3,2},{4,5},{5,4},{6,7},{7,6},{8,9},{9,8},{10,11... | collective-permute-start | bytes 1572872 | tf_op jit(solution)/shard_map/ppermute | solution.py:413
  5.2 3.5 %collective-permute-start = (bf16[512,512]{1,0:T(8,128)(2,1)}, bf16[512,512]{1,0:T(8,128)(2,1)S(1)}, u32[]{:S(2)}, u32[]{:S(2)}) collective-permute-start(bf16[512,512]{1,0:T(8,128)(2,1)} %shard_map.46.refs_4_.refs_1_.refs_11_), channel_id=1, source_target_pairs={{0,2},{1,3},{2,4},{3,5},{4,6},{5,7},{8,10},{9,11},{10,12},{11,13},... | collective-permute-start | bytes 1572872 | tf_op jit(solution)/shard_map/ppermute | solution.py:419
  9.0 2.5 %copy-done.1 = bf16[5,512,2,512]{3,2,1,0:T(2,128)(2,1)S(1)} copy-done((bf16[5,512,2,512]{3,2,1,0:T(2,128)(2,1)S(1)}, bf16[5,512,2,512]{3,2,1,0:T(2,128)(2,1)}, u32[]{:S(2)}) %copy-start.1) | copy-done | bytes 5242904
  11.5 1.0 copy-done.2
  12.5 7.7 %shard_map.47 = (bf16[512,512]{1,0:T(8,128)(2,1)S(1)}, bf16[512,512]{1,0:T(8,128)(2,1)S(1)}, bf16[512,512]{1,0:T(8,128)(2,1)S(1)}, bf16[256,512]{1,0:T(8,128)(2,...) custom-call(s32[4]{0:T(128)S(1)} %pad_add_fusion.refs_0_, ...), custom_call_target="tpu_custom_call" | custom-call | flops 8800000000 | tf_op jit(solution)/shard_map/pallas_call | solution.py:37
  21.5 3.5 %collective-permute-start.2 = (bf16[512,512]{1,0:T(8,128)(2,1)S(1)}, bf16[512,512]{1,0:T(8,128)(2,1)S(1)}, u32[]{:S(2)}, u32[]{:S(2)}) collective-permute-start(bf16[512,512]{1,0:T(8,128)(2,1)S(1)} %shard_map.48.refs_4_.refs_2_.refs_12_.refs_11_), channel_id=1, source_target_pairs={{0,2},{1,3},{2,4},{3,5},{4,6},{5,7},{8,10},{9,11},{10,12},{11,13},... | collective-permute-start | bytes 1572872 | tf_op jit(solution)/shard_map/ppermute | solution.py:419
  25.5 2.4 %shard_map.49 = (bf16[256,2,512]{2,1,0:T(2,128)(2,1)S(1)}, bf16[256,2,512]{2,1,0:T(2,128)(2,1)S(1)}) custom-call(s32[4]{0:T(128)S(1)} %pad_add_fusion.refs_0_, s32[2,512]{1,0:T(2,128)S(1)} %get-tuple-element.43.refs_1_, bf16[512,2,512]{2,1,0:T(2,128)(2,1)S(1)} %get-tuple-element.44.refs_2_, bf16[512,2,512]{2,1,0:T(2,128)(2,1)S(1)} %collective-permute-done.3.refs_3_, ...), custom_call_target="tpu_custom_call" | custom-call | flops 2200000000 | tf_op jit(solution)/shard_map/pallas_call | solution.py:37
  27.9 1.6 collective-permute-start.7
  29.5 6.8 %collective-permute-done.2.refs_1_ = bf16[512,512]{1,0:T(8,128)(2,1)S(1)} collective-permute-done((bf16[512,512]{1,0:T(8,128)(2,1)S(1)}, bf16[512,512]{1,0:T(8,128)(2,1)S(1)}, u32[]{:S(2)}, u32[]{:S(2)}) %collective-permute-start.2) | collective-permute-done | bytes 524320 | tf_op jit(solution)/shard_map/ppermute | solution.py:419
  36.3 2.3 %collective-permute-done.4.refs_4_.refs_2_.refs_16_.refs_15_ = bf16[512,512]{1,0:T(8,128)(2,1)S(1)} collective-permute-done((bf16[512,512]{1,0:T(8,128)(2,1)S(1)}, bf16[512,512]{1,0:T(8,128)(2,1)S(1)}, u32[]{:S(2)}, u32[]{:S(2)}) %collective-permute-start.4) | collective-permute-done | bytes 524320 | tf_op jit(solution)/shard_map/ppermute | solution.py:413
  39.3 3.5 %collective-permute-start.6 = (bf16[512,512]{1,0:T(8,128)(2,1)S(1)}, bf16[512,512]{1,0:T(8,128)(2,1)S(1)}, u32[]{:S(2)}, u32[]{:S(2)}) collective-permute-start(bf16[512,512]{1,0:T(8,128)(2,1)S(1)} %shard_map.50.refs_4_.refs_3_.refs_13_.refs_12_.refs_11_), channel_id=1, source_target_pairs={{0,2},{1,3},{2,4},{3,5},{4,6},{5,7},{8,10},{9,11},{10,12},{11,13},... | collective-permute-start | bytes 1572872 | tf_op jit(solution)/shard_map/ppermute | solution.py:419
  43.3 1.1 shard_map.51
  44.5 1.8 %collective-permute-start.10 = (bf16[128,512]{1,0:T(8,128)(2,1)S(1)}, bf16[128,512]{1,0:T(8,128)(2,1)S(1)}, u32[]{:S(2)}, u32[]{:S(2)}) collective-permute-start(bf16[128,512]{1,0:T(8,128)(2,1)S(1)} %get-tuple-element.50.refs_3_.refs_1_), channel_id=1, source_target_pairs={{0,4},{1,5},{8,12},{9,13},{16,20},{17,21},{24,28},{25,29}} | collective-permute-start | bytes 393224 | tf_op jit(solution)/shard_map/ppermute | solution.py:502
  46.3 1.3 collective-permute-start.11
  47.6 1.3 collective-permute-start.9
  48.9 6.2 %collective-permute-done.6.refs_1_ = bf16[512,512]{1,0:T(8,128)(2,1)S(1)} collective-permute-done((bf16[512,512]{1,0:T(8,128)(2,1)S(1)}, bf16[512,512]{1,0:T(8,128)(2,1)S(1)}, u32[]{:S(2)}, u32[]{:S(2)}) %collective-permute-start.6) | collective-permute-done | bytes 524320 | tf_op jit(solution)/shard_map/ppermute | solution.py:419
  55.1 1.5 collective-permute-start.14
  56.6 1.3 collective-permute-done.10.refs_6_.refs_3_
  57.9 2.1 %collective-permute-done.11.refs_7_.refs_4_ = bf16[128,512]{1,0:T(8,128)(2,1)S(1)} collective-permute-done((bf16[128,512]{1,0:T(8,128)(2,1)S(1)}, bf16[128,512]{1,0:T(8,128)(2,1)S(1)}, u32[]{:S(2)}, u32[]{:S(2)}) %collective-permute-start.11) | collective-permute-done | bytes 131104 | tf_op jit(solution)/shard_map/ppermute | solution.py:502
  60.0 1.4 collective-permute-done.9.refs_5_.refs_2_
  62.6 0.6 shard_map.54.refs_2_.refs_1_
  63.2 1.6 collective-permute-start.16
  65.3 4.4 %collective-permute-start.13 = (bf16[512,512]{1,0:T(8,128)(2,1)S(1)}, bf16[512,512]{1,0:T(8,128)(2,1)S(1)}, u32[]{:S(2)}, u32[]{:S(2)}) collective-permute-start(bf16[512,512]{1,0:T(8,128)(2,1)S(1)} %shard_map.52.refs_5_.refs_4_.refs_14_.refs_13_.refs_12_.refs_11_), channel_id=1, source_target_pairs={{0,2},{1,3},{2,4},{3,5},{4,6},{5,7},{8,10},{9,11},{10,12},{11,13},... | collective-permute-start | bytes 1572872 | tf_op jit(solution)/shard_map/ppermute | solution.py:419
  69.7 1.6 %collective-permute-start.15 = (bf16[128,512]{1,0:T(8,128)(2,1)S(1)}, bf16[128,512]{1,0:T(8,128)(2,1)S(1)}, u32[]{:S(2)}, u32[]{:S(2)}) collective-permute-start(bf16[128,512]{1,0:T(8,128)(2,1)S(1)} %shard_map.53.refs_5_.refs_0_), channel_id=1, source_target_pairs={{0,1},{1,0},{2,3},{3,2},{4,5},{5,4},{6,7},{7,6},{8,9},{9,8},{10,11... | collective-permute-start | bytes 393224 | tf_op jit(solution)/shard_map/ppermute | solution.py:413
  71.3 7.9 %collective-permute-done.15.refs_1_ = bf16[128,512]{1,0:T(8,128)(2,1)S(1)} collective-permute-done((bf16[128,512]{1,0:T(8,128)(2,1)S(1)}, bf16[128,512]{1,0:T(8,128)(2,1)S(1)}, u32[]{:S(2)}, u32[]{:S(2)}) %collective-permute-start.15) | collective-permute-done | bytes 131104 | tf_op jit(solution)/shard_map/ppermute | solution.py:413
  79.7 1.1 shard_map.56
  82.0 4.4 %collective-permute-start.19 = (bf16[512,512]{1,0:T(8,128)(2,1)S(1)}, bf16[512,512]{1,0:T(8,128)(2,1)S(1)}, u32[]{:S(2)}, u32[]{:S(2)}) collective-permute-start(bf16[512,512]{1,0:T(8,128)(2,1)S(1)} %shard_map.57.refs_5_.refs_14_.refs_13_.refs_12_.refs_11_), channel_id=1, source_target_pairs={{0,2},{1,3},{2,4},{3,5},{4,6},{5,7},{8,10},{9,11},{10,12},{11,13},... | collective-permute-start | bytes 1572872 | tf_op jit(solution)/shard_map/ppermute | solution.py:419
  88.2 4.1 %shard_map.59.refs_6_.refs_8_ = bf16[2568,2,512]{2,1,0:T(2,128)(2,1)S(1)} custom-call(s32[4]{0:T(128)S(1)} %pad_add_fusion.refs_0_, s32[2,512]{1,0:T(2,128)S(1)} %get-tuple-element.56.refs_1_, s32[2,512]{1,0:T(2,128)S(1)} %get-tuple-element.39.refs_2_.refs_1_, bf16[256,2,512]{2,1,0:T(2,128)(2,1)S(1)} %get-tuple-element.57.refs_3_, ...), custom_call_target="tpu_custom_call" | custom-call | flops 110000000 | tf_op jit(solution)/shard_map/pallas_call | solution.py:37
  92.3 1.8 %collective-permute-start.17 = (bf16[512,512]{1,0:T(8,128)(2,1)S(1)}, bf16[512,512]{1,0:T(8,128)(2,1)S(1)}, u32[]{:S(2)}, u32[]{:S(2)}) collective-permute-start(bf16[512,512]{1,0:T(8,128)(2,1)S(1)} %shard_map.58.refs_10_.refs_2_), channel_id=1, source_target_pairs={{0,16},{8,24},{16,0},{24,8},{1,17},{9,25},{17,1},{25,9},{2,18},{10... | collective-permute-start | bytes 1572872 | tf_op jit(solution)/shard_map/ppermute | solution.py:416
  94.1 2.0 %shard_map.60 = (bf16[512,1024]{1,0:T(8,128)(2,1)S(1)}, bf16[512,2,512]{2,1,0:T(2,128)(2,1)S(1)}) custom-call(s32[4]{0:T(128)S(1)} %pad_add_fusion.refs_0_, bf16[2,512,512]{2,1,0:T(8,128)(2,1)S(1)} %copy-done.4, bf16[256,1024]{1,0:T(8,128)(2,1)S(1)} %get-tuple-element.54.refs_2_.refs_6_, bf16[256,1024]{1,0:T(8,128)(2,1)S(1)} %collective-permute-done.20.refs_3_.refs_7_, ...), custom_call_target="tpu_custom_call" | custom-call | flops 2200000000 | tf_op jit(solution)/shard_map/pallas_call | solution.py:37
  96.1 1.8 %collective-permute-done.19.refs_1_ = bf16[512,512]{1,0:T(8,128)(2,1)S(1)} collective-permute-done((bf16[512,512]{1,0:T(8,128)(2,1)S(1)}, bf16[512,512]{1,0:T(8,128)(2,1)S(1)}, u32[]{:S(2)}, u32[]{:S(2)}) %collective-permute-start.19) | collective-permute-done | bytes 524320 | tf_op jit(solution)/shard_map/ppermute | solution.py:419
  97.8 2.3 %collective-permute-done.24.refs_4_.refs_18_.refs_17_.refs_16_.refs_19_ = bf16[512,512]{1,0:T(8,128)(2,1)S(1)} collective-permute-done((bf16[512,512]{1,0:T(8,128)(2,1)S(1)}, bf16[512,512]{1,0:T(8,128)(2,1)S(1)}, u32[]{:S(2)}, u32[]{:S(2)}) %collective-permute-start.24) | collective-permute-done | bytes 524320 | tf_op jit(solution)/shard_map/ppermute | solution.py:413
  100.9 2.2 %collective-permute-start.27 = (bf16[512,512]{1,0:T(8,128)(2,1)S(1)}, bf16[512,512]{1,0:T(8,128)(2,1)S(1)}, u32[]{:S(2)}, u32[]{:S(2)}) collective-permute-start(bf16[512,512]{1,0:T(8,128)(2,1)S(1)} %shard_map.61.refs_2_.refs_14_.refs_13_.refs_12_.refs_15_), channel_id=1, source_target_pairs={{0,2},{1,3},{2,4},{3,5},{4,6},{5,7},{8,10},{9,11},{10,12},{11,13},... | collective-permute-start | bytes 1572872 | tf_op jit(solution)/shard_map/ppermute | solution.py:419
  103.7 2.3 %collective-permute-done.17.refs_4_ = bf16[512,512]{1,0:T(8,128)(2,1)S(1)} collective-permute-done((bf16[512,512]{1,0:T(8,128)(2,1)S(1)}, bf16[512,512]{1,0:T(8,128)(2,1)S(1)}, u32[]{:S(2)}, u32[]{:S(2)}) %collective-permute-start.17) | collective-permute-done | bytes 524320 | tf_op jit(solution)/shard_map/ppermute | solution.py:416
  106.0 0.6 shard_map.63.refs_10_.refs_2_
  106.8 3.5 %shard_map.64 = (bf16[512,1024]{1,0:T(8,128)(2,1)S(1)}, bf16[512,512]{1,0:T(8,128)(2,1)S(1)}, bf16[512,2,512]{2,1,0:T(2,128)(2,1)S(1)}) custom-call(s32[4]{0:T(128)S(1)} %pad_add_fusion.refs_0_, bf16[2,512,512]{2,1,0:T(8,128)(2,1)S(1)} %copy-done.4, bf16[2,512,512]{2,1,0:T(8,128)(2,1)S(1)} %copy-done, ...), custom_call_target="tpu_custom_call" | custom-call | flops 3849999872 | tf_op jit(solution)/shard_map/pallas_call | solution.py:37
  110.2 4.7 %collective-permute-done.27.refs_1_ = bf16[512,512]{1,0:T(8,128)(2,1)S(1)} collective-permute-done((bf16[512,512]{1,0:T(8,128)(2,1)S(1)}, bf16[512,512]{1,0:T(8,128)(2,1)S(1)}, u32[]{:S(2)}, u32[]{:S(2)}) %collective-permute-start.27) | collective-permute-done | bytes 524320 | tf_op jit(solution)/shard_map/ppermute | solution.py:419
  114.9 2.3 %collective-permute-done.28.refs_3_.refs_18_.refs_17_.refs_20_.refs_23_ = bf16[512,512]{1,0:T(8,128)(2,1)S(1)} collective-permute-done((bf16[512,512]{1,0:T(8,128)(2,1)S(1)}, bf16[512,512]{1,0:T(8,128)(2,1)S(1)}, u32[]{:S(2)}, u32[]{:S(2)}) %collective-permute-start.28) | collective-permute-done | bytes 524320 | tf_op jit(solution)/shard_map/ppermute | solution.py:413
  118.4 2.2 %collective-permute-start.29 = (bf16[256,512]{1,0:T(8,128)(2,1)S(1)}, bf16[256,512]{1,0:T(8,128)(2,1)S(1)}, u32[]{:S(2)}, u32[]{:S(2)}) collective-permute-start(bf16[256,512]{1,0:T(8,128)(2,1)S(1)} %slice.4), channel_id=1, source_target_pairs={{0,2},{1,3},{2,4},{3,5},{4,6},{5,7},{8,10},{9,11},{10,12},{11,13},... | collective-permute-start | bytes 786440 | tf_op jit(solution)/shard_map/ppermute | solution.py:419
  120.6 1.8 %shard_map.66 = (bf16[2560,2,512]{2,1,0:T(2,128)(2,1)}, f32[8,128]{1,0:T(8,128)S(1)}) custom-call(s32[4]{0:T(128)S(1)} %pad_add_fusion.refs_0_, s32[2,512]{1,0:T(2,128)S(1)} %get-tuple-element.39.refs_2_.refs_1_, bf16[2,512,512]{2,1,0:T(8,128)(2,1)S(1)} %shard_map.63.refs_10_.refs_2_, bf16[2,512,512]{2,1,0:T(8,128)(2,1)S(1)} %collective-permute-done.25.refs_3_, ...), custom_call_target="tpu_custom_call" | custom-call | flops 5500000256 | tf_op jit(solution)/shard_map/pallas_call | solution.py:37
  122.4 6.2 %shard_map.67 = (bf16[2560,2,512]{2,1,0:T(2,128)(2,1)}, f32[8,128]{1,0:T(8,128)S(1)}) custom-call(s32[4]{0:T(128)S(1)} %pad_add_fusion.refs_0_, s32[2,512]{1,0:T(2,128)S(1)} %get-tuple-element.39.refs_2_.refs_1_, bf16[2,512,512]{2,1,0:T(8,128)(2,1)S(1)} %shard_map.63.refs_10_.refs_2_, ...), custom_call_target="tpu_custom_call", output_to_operand_aliasing={{0}: (19, {})} | custom-call | flops 5500000256 | tf_op jit(solution)/shard_map/pallas_call | solution.py:37
  128.6 2.4 %collective-permute-done.30.refs_3_.refs_18_.refs_21_.refs_24_ = bf16[512,512]{1,0:T(8,128)(2,1)S(1)} collective-permute-done((bf16[512,512]{1,0:T(8,128)(2,1)S(1)}, bf16[512,512]{1,0:T(8,128)(2,1)S(1)}, u32[]{:S(2)}, u32[]{:S(2)}) %collective-permute-start.30) | collective-permute-done | bytes 524320 | tf_op jit(solution)/shard_map/ppermute | solution.py:413
  131.6 2.5 %collective-permute-start.31 = (bf16[256,512]{1,0:T(8,128)(2,1)S(1)}, bf16[256,512]{1,0:T(8,128)(2,1)S(1)}, u32[]{:S(2)}, u32[]{:S(2)}) collective-permute-start(bf16[256,512]{1,0:T(8,128)(2,1)S(1)} %shard_map.68.refs_20_.refs_14_.refs_17_), channel_id=1, source_target_pairs={{0,2},{1,3},{2,4},{3,5},{4,6},{5,7},{8,10},{9,11},{10,12},{11,13},... | collective-permute-start | bytes 786440 | tf_op jit(solution)/shard_map/ppermute | solution.py:419
  134.7 6.4 %shard_map.69 = (bf16[2560,2,512]{2,1,0:T(2,128)(2,1)}, f32[8,128]{1,0:T(8,128)S(1)}) custom-call(s32[4]{0:T(128)S(1)} %pad_add_fusion.refs_0_, s32[2,512]{1,0:T(2,128)S(1)} %get-tuple-element.39.refs_2_.refs_1_, bf16[2,512,512]{2,1,0:T(8,128)(2,1)S(1)} %shard_map.63.refs_10_.refs_2_, ...), custom_call_target="tpu_custom_call", output_to_operand_aliasing={{0}: (19, {})} | custom-call | flops 5500000256 | tf_op jit(solution)/shard_map/pallas_call | solution.py:37
  141.6 1.6 %collective-permute-start.33 = (bf16[256,512]{1,0:T(8,128)(2,1)S(1)}, bf16[256,512]{1,0:T(8,128)(2,1)S(1)}, u32[]{:S(2)}, u32[]{:S(2)}) collective-permute-start(bf16[256,512]{1,0:T(8,128)(2,1)S(1)} %shard_map.70.refs_20_.refs_18_), channel_id=1, source_target_pairs={{0,1},{1,0},{2,3},{3,2},{4,5},{5,4},{6,7},{7,6},{8,9},{9,8},{10,11... | collective-permute-start | bytes 786440 | tf_op jit(solution)/shard_map/ppermute | solution.py:413
  143.2 6.2 %shard_map.71 = (bf16[2560,2,512]{2,1,0:T(2,128)(2,1)}, f32[8,128]{1,0:T(8,128)S(1)}) custom-call(s32[4]{0:T(128)S(1)} %pad_add_fusion.refs_0_, s32[2,512]{1,0:T(2,128)S(1)} %get-tuple-element.39.refs_2_.refs_1_, bf16[2,512,512]{2,1,0:T(8,128)(2,1)S(1)} %shard_map.63.refs_10_.refs_2_, ...), custom_call_target="tpu_custom_call", output_to_operand_aliasing={{0}: (19, {})} | custom-call | flops 5500000256 | tf_op jit(solution)/shard_map/pallas_call | solution.py:37
  149.4 6.8 %shard_map.72 = (bf16[2560,2,512]{2,1,0:T(2,128)(2,1)}, f32[8,128]{1,0:T(8,128)}) custom-call(s32[4]{0:T(128)S(1)} %pad_add_fusion.refs_0_, s32[2,512]{1,0:T(2,128)S(1)} %get-tuple-element.39.refs_2_.refs_1_, bf16[2,512,512]{2,1,0:T(8,128)(2,1)S(1)} %shard_map.63.refs_10_.refs_2_, ...), custom_call_target="tpu_custom_call", output_to_operand_aliasing={{0}: (27, {})} | custom-call | flops 5500000256 | tf_op jit(solution)/shard_map/pallas_call | solution.py:37
  (62 shorter events, 12.5 us)
Async XLA Ops:
  0.0 8.8 %copy-start.5 = (s32[2,512]{1,0:T(2,128)S(1)}, s32[2,512]{1,0:T(2,128)}, u32[]{:S(2)}) copy-start(s32[2,512]{1,0:T(2,128)} %refs_1_.3) | copy-start | bytes 12292
  2.2 18.7 %collective-permute-start.1 = (bf16[512,512]{1,0:T(8,128)(2,1)}, bf16[512,512]{1,0:T(8,128)(2,1)S(1)}, u32[]{:S(2)}, u32[]{:S(2)}) collective-permute-start(bf16[512,512]{1,0:T(8,128)(2,1)} %shard_map.46.refs_4_.refs_1_.refs_11_), channel_id=1, source_target_pairs={{0,1},{1,0},{2,3},{3,2},{4,5},{5,4},{6,7},{7,6},{8,9},{9,8},{10,11... | collective-permute-start | bytes 1572872 | tf_op jit(solution)/shard_map/ppermute | solution.py:413
  5.2 15.7 %collective-permute-start = (bf16[512,512]{1,0:T(8,128)(2,1)}, bf16[512,512]{1,0:T(8,128)(2,1)S(1)}, u32[]{:S(2)}, u32[]{:S(2)}) collective-permute-start(bf16[512,512]{1,0:T(8,128)(2,1)} %shard_map.46.refs_4_.refs_1_.refs_11_), channel_id=1, source_target_pairs={{0,2},{1,3},{2,4},{3,5},{4,6},{5,7},{8,10},{9,11},{10,12},{11,13},... | collective-permute-start | bytes 1572872 | tf_op jit(solution)/shard_map/ppermute | solution.py:419
  9.0 2.5 %copy-start.1 = (bf16[5,512,2,512]{3,2,1,0:T(2,128)(2,1)S(1)}, bf16[5,512,2,512]{3,2,1,0:T(2,128)(2,1)}, u32[]{:S(2)}) copy-start(bf16[5,512,2,512]{3,2,1,0:T(2,128)(2,1)} %param.4) | copy-start | bytes 15728644
  11.5 1.0 copy-start.2
  20.3 5.2 %collective-permute-start.3 = (bf16[512,2,512]{2,1,0:T(2,128)(2,1)S(1)}, bf16[512,2,512]{2,1,0:T(2,128)(2,1)S(1)}, u32[]{:S(2)}, u32[]{:S(2)}) collective-permute-start(bf16[512,2,512]{2,1,0:T(2,128)(2,1)S(1)} %get-tuple-element.45), channel_id=1, source_target_pairs={{0,8},{8,0},{16,24},{24,16},{1,9},{9,1},{17,25},{25,17},{2,10},{10... | collective-permute-start | bytes 3145736 | tf_op jit(solution)/shard_map/ppermute | solution.py:410
  20.4 18.3 %collective-permute-start.5 = (bf16[512,2,512]{2,1,0:T(2,128)(2,1)S(1)}, bf16[512,2,512]{2,1,0:T(2,128)(2,1)S(1)}, u32[]{:S(2)}, u32[]{:S(2)}) collective-permute-start(bf16[512,2,512]{2,1,0:T(2,128)(2,1)S(1)} %get-tuple-element.47.refs_7_), channel_id=1, source_target_pairs={{0,8},{8,0},{16,24},{24,16},{1,9},{9,1},{17,25},{25,17},{2,10},{10... | collective-permute-start | bytes 3145736 | tf_op jit(solution)/shard_map/ppermute | solution.py:410
  21.5 14.9 %collective-permute-start.2 = (bf16[512,512]{1,0:T(8,128)(2,1)S(1)}, bf16[512,512]{1,0:T(8,128)(2,1)S(1)}, u32[]{:S(2)}, u32[]{:S(2)}) collective-permute-start(bf16[512,512]{1,0:T(8,128)(2,1)S(1)} %shard_map.48.refs_4_.refs_2_.refs_12_.refs_11_), channel_id=1, source_target_pairs={{0,2},{1,3},{2,4},{3,5},{4,6},{5,7},{8,10},{9,11},{10,12},{11,13},... | collective-permute-start | bytes 1572872 | tf_op jit(solution)/shard_map/ppermute | solution.py:419
  25.0 13.7 %collective-permute-start.4 = (bf16[512,512]{1,0:T(8,128)(2,1)S(1)}, bf16[512,512]{1,0:T(8,128)(2,1)S(1)}, u32[]{:S(2)}, u32[]{:S(2)}) collective-permute-start(bf16[512,512]{1,0:T(8,128)(2,1)S(1)} %shard_map.48.refs_4_.refs_2_.refs_12_.refs_11_), channel_id=1, source_target_pairs={{0,1},{1,0},{2,3},{3,2},{4,5},{5,4},{6,7},{7,6},{8,9},{9,8},{10,11... | collective-permute-start | bytes 1572872 | tf_op jit(solution)/shard_map/ppermute | solution.py:413
  27.9 15.4 %collective-permute-start.7 = (bf16[256,2,512]{2,1,0:T(2,128)(2,1)S(1)}, bf16[256,2,512]{2,1,0:T(2,128)(2,1)S(1)}, u32[]{:S(2)}, u32[]{:S(2)}) collective-permute-start(bf16[256,2,512]{2,1,0:T(2,128)(2,1)S(1)} %get-tuple-element.49.refs_2_), channel_id=1, source_target_pairs={{0,16},{8,24},{16,0},{24,8},{1,17},{9,25},{17,1},{25,9},{2,18},{10... | collective-permute-start | bytes 1572872 | tf_op jit(solution)/shard_map/ppermute | solution.py:416
  39.3 15.8 %collective-permute-start.6 = (bf16[512,512]{1,0:T(8,128)(2,1)S(1)}, bf16[512,512]{1,0:T(8,128)(2,1)S(1)}, u32[]{:S(2)}, u32[]{:S(2)}) collective-permute-start(bf16[512,512]{1,0:T(8,128)(2,1)S(1)} %shard_map.50.refs_4_.refs_3_.refs_13_.refs_12_.refs_11_), channel_id=1, source_target_pairs={{0,2},{1,3},{2,4},{3,5},{4,6},{5,7},{8,10},{9,11},{10,12},{11,13},... | collective-permute-start | bytes 1572872 | tf_op jit(solution)/shard_map/ppermute | solution.py:419
  42.7 13.8 %collective-permute-start.8 = (bf16[512,512]{1,0:T(8,128)(2,1)S(1)}, bf16[512,512]{1,0:T(8,128)(2,1)S(1)}, u32[]{:S(2)}, u32[]{:S(2)}) collective-permute-start(bf16[512,512]{1,0:T(8,128)(2,1)S(1)} %shard_map.50.refs_4_.refs_3_.refs_13_.refs_12_.refs_11_), channel_id=1, source_target_pairs={{0,1},{1,0},{2,3},{3,2},{4,5},{5,4},{6,7},{7,6},{8,9},{9,8},{10,11... | collective-permute-start | bytes 1572872 | tf_op jit(solution)/shard_map/ppermute | solution.py:413
  44.5 13.4 %collective-permute-start.10 = (bf16[128,512]{1,0:T(8,128)(2,1)S(1)}, bf16[128,512]{1,0:T(8,128)(2,1)S(1)}, u32[]{:S(2)}, u32[]{:S(2)}) collective-permute-start(bf16[128,512]{1,0:T(8,128)(2,1)S(1)} %get-tuple-element.50.refs_3_.refs_1_), channel_id=1, source_target_pairs={{0,4},{1,5},{8,12},{9,13},{16,20},{17,21},{24,28},{25,29}} | collective-permute-start | bytes 393224 | tf_op jit(solution)/shard_map/ppermute | solution.py:502
  46.3 13.7 %collective-permute-start.11 = (bf16[128,512]{1,0:T(8,128)(2,1)S(1)}, bf16[128,512]{1,0:T(8,128)(2,1)S(1)}, u32[]{:S(2)}, u32[]{:S(2)}) collective-permute-start(bf16[128,512]{1,0:T(8,128)(2,1)S(1)} %get-tuple-element.50.refs_3_.refs_1_), channel_id=1, source_target_pairs={{0,6},{1,7},{8,14},{9,15},{16,22},{17,23},{24,30},{25,31}} | collective-permute-start | bytes 393224 | tf_op jit(solution)/shard_map/ppermute | solution.py:502
  47.6 13.8 %collective-permute-start.9 = (bf16[128,512]{1,0:T(8,128)(2,1)S(1)}, bf16[128,512]{1,0:T(8,128)(2,1)S(1)}, u32[]{:S(2)}, u32[]{:S(2)}) collective-permute-start(bf16[128,512]{1,0:T(8,128)(2,1)S(1)} %get-tuple-element.50.refs_3_.refs_1_), channel_id=1, source_target_pairs={{0,2},{1,3},{8,10},{9,11},{16,18},{17,19},{24,26},{25,27}} | collective-permute-start | bytes 393224 | tf_op jit(solution)/shard_map/ppermute | solution.py:502
  55.1 24.1 %collective-permute-start.14 = (bf16[256,2,512]{2,1,0:T(2,128)(2,1)S(1)}, bf16[256,2,512]{2,1,0:T(2,128)(2,1)S(1)}, u32[]{:S(2)}, u32[]{:S(2)}) collective-permute-start(bf16[256,2,512]{2,1,0:T(2,128)(2,1)S(1)} %get-tuple-element.46.refs_3_.refs_2_), channel_id=1, source_target_pairs={{0,16},{8,24},{16,0},{24,8},{1,17},{9,25},{17,1},{25,9},{2,18},{10... | collective-permute-start | bytes 1572872 | tf_op jit(solution)/shard_map/ppermute | solution.py:416
  63.2 17.6 %collective-permute-start.16 = (bf16[512,512]{1,0:T(8,128)(2,1)S(1)}, bf16[512,512]{1,0:T(8,128)(2,1)S(1)}, u32[]{:S(2)}, u32[]{:S(2)}) collective-permute-start(bf16[512,512]{1,0:T(8,128)(2,1)S(1)} %shard_map.54.refs_2_.refs_1_), channel_id=1, source_target_pairs={{0,16},{8,24},{16,0},{24,8},{1,17},{9,25},{17,1},{25,9},{2,18},{10... | collective-permute-start | bytes 1572872 | tf_op jit(solution)/shard_map/ppermute | solution.py:416
  64.8 16.2 %collective-permute-start.12 = (bf16[512,512]{1,0:T(8,128)(2,1)S(1)}, bf16[512,512]{1,0:T(8,128)(2,1)S(1)}, u32[]{:S(2)}, u32[]{:S(2)}) collective-permute-start(bf16[512,512]{1,0:T(8,128)(2,1)S(1)} %shard_map.52.refs_5_.refs_4_.refs_14_.refs_13_.refs_12_.refs_11_), channel_id=1, source_target_pairs={{0,1},{1,0},{2,3},{3,2},{4,5},{5,4},{6,7},{7,6},{8,9},{9,8},{10,11... | collective-permute-start | bytes 1572872 | tf_op jit(solution)/shard_map/ppermute | solution.py:413
  65.3 16.2 %collective-permute-start.13 = (bf16[512,512]{1,0:T(8,128)(2,1)S(1)}, bf16[512,512]{1,0:T(8,128)(2,1)S(1)}, u32[]{:S(2)}, u32[]{:S(2)}) collective-permute-start(bf16[512,512]{1,0:T(8,128)(2,1)S(1)} %shard_map.52.refs_5_.refs_4_.refs_14_.refs_13_.refs_12_.refs_11_), channel_id=1, source_target_pairs={{0,2},{1,3},{2,4},{3,5},{4,6},{5,7},{8,10},{9,11},{10,12},{11,13},... | collective-permute-start | bytes 1572872 | tf_op jit(solution)/shard_map/ppermute | solution.py:419
  69.7 9.4 %collective-permute-start.15 = (bf16[128,512]{1,0:T(8,128)(2,1)S(1)}, bf16[128,512]{1,0:T(8,128)(2,1)S(1)}, u32[]{:S(2)}, u32[]{:S(2)}) collective-permute-start(bf16[128,512]{1,0:T(8,128)(2,1)S(1)} %shard_map.53.refs_5_.refs_0_), channel_id=1, source_target_pairs={{0,1},{1,0},{2,3},{3,2},{4,5},{5,4},{6,7},{7,6},{8,9},{9,8},{10,11... | collective-permute-start | bytes 393224 | tf_op jit(solution)/shard_map/ppermute | solution.py:413
  79.1 7.3 %collective-permute-start.22 = (bf16[256,2,512]{2,1,0:T(2,128)(2,1)S(1)}, bf16[256,2,512]{2,1,0:T(2,128)(2,1)S(1)}, u32[]{:S(2)}, u32[]{:S(2)}) collective-permute-start(bf16[256,2,512]{2,1,0:T(2,128)(2,1)S(1)} %get-tuple-element.57.refs_3_), channel_id=1, source_target_pairs={{0,8},{8,0},{16,24},{24,16},{1,9},{9,1},{17,25},{25,17},{2,10},{10... | collective-permute-start | bytes 1572872 | tf_op jit(solution)/shard_map/ppermute | solution.py:410
  79.2 13.2 %collective-permute-start.20 = (bf16[256,1024]{1,0:T(8,128)(2,1)S(1)}, bf16[256,1024]{1,0:T(8,128)(2,1)S(1)}, u32[]{:S(2)}, u32[]{:S(2)}) collective-permute-start(bf16[256,1024]{1,0:T(8,128)(2,1)S(1)} %get-tuple-element.54.refs_2_.refs_6_), channel_id=1, source_target_pairs={{0,8},{8,0},{16,24},{24,16},{1,9},{9,1},{17,25},{25,17},{2,10},{10... | collective-permute-start | bytes 1572872 | tf_op jit(solution)/shard_map/ppermute | solution.py:410
  80.9 6.2 %collective-permute-start.23 = (bf16[256,2,512]{2,1,0:T(2,128)(2,1)S(1)}, bf16[256,2,512]{2,1,0:T(2,128)(2,1)S(1)}, u32[]{:S(2)}, u32[]{:S(2)}) collective-permute-start(bf16[256,2,512]{2,1,0:T(2,128)(2,1)S(1)} %get-tuple-element.52.refs_3_.refs_5_), channel_id=1, source_target_pairs={{0,8},{8,0},{16,24},{24,16},{1,9},{9,1},{17,25},{25,17},{2,10},{10... | collective-permute-start | bytes 1572872 | tf_op jit(solution)/shard_map/ppermute | solution.py:410
  80.9 13.2 %collective-permute-start.21 = (bf16[256,1024]{1,0:T(8,128)(2,1)S(1)}, bf16[256,1024]{1,0:T(8,128)(2,1)S(1)}, u32[]{:S(2)}, u32[]{:S(2)}) collective-permute-start(bf16[256,1024]{1,0:T(8,128)(2,1)S(1)} %get-tuple-element.55.refs_4_.refs_8_), channel_id=1, source_target_pairs={{0,8},{8,0},{16,24},{24,16},{1,9},{9,1},{17,25},{25,17},{2,10},{10... | collective-permute-start | bytes 1572872 | tf_op jit(solution)/shard_map/ppermute | solution.py:410
  82.0 15.8 %collective-permute-start.19 = (bf16[512,512]{1,0:T(8,128)(2,1)S(1)}, bf16[512,512]{1,0:T(8,128)(2,1)S(1)}, u32[]{:S(2)}, u32[]{:S(2)}) collective-permute-start(bf16[512,512]{1,0:T(8,128)(2,1)S(1)} %shard_map.57.refs_5_.refs_14_.refs_13_.refs_12_.refs_11_), channel_id=1, source_target_pairs={{0,2},{1,3},{2,4},{3,5},{4,6},{5,7},{8,10},{9,11},{10,12},{11,13},... | collective-permute-start | bytes 1572872 | tf_op jit(solution)/shard_map/ppermute | solution.py:419
  86.5 13.7 %collective-permute-start.24 = (bf16[512,512]{1,0:T(8,128)(2,1)S(1)}, bf16[512,512]{1,0:T(8,128)(2,1)S(1)}, u32[]{:S(2)}, u32[]{:S(2)}) collective-permute-start(bf16[512,512]{1,0:T(8,128)(2,1)S(1)} %shard_map.57.refs_5_.refs_14_.refs_13_.refs_12_.refs_11_), channel_id=1, source_target_pairs={{0,1},{1,0},{2,3},{3,2},{4,5},{5,4},{6,7},{7,6},{8,9},{9,8},{10,11... | collective-permute-start | bytes 1572872 | tf_op jit(solution)/shard_map/ppermute | solution.py:413
  87.0 13.7 %collective-permute-start.18 = (bf16[2,128,512]{2,1,0:T(8,128)(2,1)S(1)}, bf16[2,128,512]{2,1,0:T(8,128)(2,1)S(1)}, u32[]{:S(2)}, u32[]{:S(2)}) collective-permute-start(bf16[2,128,512]{2,1,0:T(8,128)(2,1)S(1)} %shard_map.55.refs_4_.refs_0_), channel_id=1, source_target_pairs={{0,16},{8,24},{16,0},{24,8},{1,17},{9,25},{17,1},{25,9},{2,18},{10... | collective-permute-start | bytes 786440 | tf_op jit(solution)/shard_map/ppermute | solution.py:416
  88.2 5.9 %copy-start.4 = (bf16[2,512,512]{2,1,0:T(8,128)(2,1)S(1)}, bf16[2,512,512]{2,1,0:T(8,128)(2,1)}, u32[]{:S(2)}) copy-start(bf16[2,512,512]{2,1,0:T(8,128)(2,1)} %refs_1_.5) | copy-start | bytes 3145732
  92.3 13.7 %collective-permute-start.17 = (bf16[512,512]{1,0:T(8,128)(2,1)S(1)}, bf16[512,512]{1,0:T(8,128)(2,1)S(1)}, u32[]{:S(2)}, u32[]{:S(2)}) collective-permute-start(bf16[512,512]{1,0:T(8,128)(2,1)S(1)} %shard_map.58.refs_10_.refs_2_), channel_id=1, source_target_pairs={{0,16},{8,24},{16,0},{24,8},{1,17},{9,25},{17,1},{25,9},{2,18},{10... | collective-permute-start | bytes 1572872 | tf_op jit(solution)/shard_map/ppermute | solution.py:416
  96.1 10.7 %copy-start = (bf16[2,512,512]{2,1,0:T(8,128)(2,1)S(1)}, bf16[2,512,512]{2,1,0:T(8,128)(2,1)}, u32[]{:S(2)}) copy-start(bf16[2,512,512]{2,1,0:T(8,128)(2,1)} %refs_4_.9) | copy-start | bytes 3145732
  100.8 5.9 %collective-permute-start.26 = (bf16[2,2,128,512]{3,2,1,0:T(8,128)(2,1)S(1)}, bf16[2,2,128,512]{3,2,1,0:T(8,128)(2,1)S(1)}, u32[]{:S(2)}, u32[]{:S(2)}) collective-permute-start(bf16[2,2,128,512]{3,2,1,0:T(8,128)(2,1)S(1)} %shard_map.62.refs_5_.refs_4_), channel_id=1, source_target_pairs={{0,8},{8,0},{16,24},{24,16},{1,9},{9,1},{17,25},{25,17},{2,10},{10... | collective-permute-start | bytes 1572872 | tf_op jit(solution)/shard_map/ppermute | solution.py:410
  100.9 14.0 %collective-permute-start.27 = (bf16[512,512]{1,0:T(8,128)(2,1)S(1)}, bf16[512,512]{1,0:T(8,128)(2,1)S(1)}, u32[]{:S(2)}, u32[]{:S(2)}) collective-permute-start(bf16[512,512]{1,0:T(8,128)(2,1)S(1)} %shard_map.61.refs_2_.refs_14_.refs_13_.refs_12_.refs_15_), channel_id=1, source_target_pairs={{0,2},{1,3},{2,4},{3,5},{4,6},{5,7},{8,10},{9,11},{10,12},{11,13},... | collective-permute-start | bytes 1572872 | tf_op jit(solution)/shard_map/ppermute | solution.py:419
  103.1 14.1 %collective-permute-start.28 = (bf16[512,512]{1,0:T(8,128)(2,1)S(1)}, bf16[512,512]{1,0:T(8,128)(2,1)S(1)}, u32[]{:S(2)}, u32[]{:S(2)}) collective-permute-start(bf16[512,512]{1,0:T(8,128)(2,1)S(1)} %shard_map.61.refs_2_.refs_14_.refs_13_.refs_12_.refs_15_), channel_id=1, source_target_pairs={{0,1},{1,0},{2,3},{3,2},{4,5},{5,4},{6,7},{7,6},{8,9},{9,8},{10,11... | collective-permute-start | bytes 1572872 | tf_op jit(solution)/shard_map/ppermute | solution.py:413
  106.7 13.9 %collective-permute-start.25 = (bf16[2,512,512]{2,1,0:T(8,128)(2,1)S(1)}, bf16[2,512,512]{2,1,0:T(8,128)(2,1)S(1)}, u32[]{:S(2)}, u32[]{:S(2)}) collective-permute-start(bf16[2,512,512]{2,1,0:T(8,128)(2,1)S(1)} %shard_map.63.refs_10_.refs_2_), channel_id=1, source_target_pairs={{0,8},{8,0},{16,24},{24,16},{1,9},{9,1},{17,25},{25,17},{2,10},{10... | collective-permute-start | bytes 3145736 | tf_op jit(solution)/shard_map/ppermute | solution.py:410
  117.2 3.4 %copy-start.3 = (bf16[512,512]{1,0:T(8,128)(2,1)S(1)}, bf16[512,512]{1,0:T(8,128)(2,1)}, u32[]{:S(2)}) copy-start(bf16[512,512]{1,0:T(8,128)(2,1)} %shard_map.46.refs_4_.refs_1_.refs_11_) | copy-start | bytes 1572868
  117.8 13.3 %collective-permute-start.30 = (bf16[512,512]{1,0:T(8,128)(2,1)S(1)}, bf16[512,512]{1,0:T(8,128)(2,1)S(1)}, u32[]{:S(2)}, u32[]{:S(2)}) collective-permute-start(bf16[512,512]{1,0:T(8,128)(2,1)S(1)} %shard_map.65.refs_19_.refs_14_.refs_13_.refs_16_), channel_id=1, source_target_pairs={{0,1},{1,0},{2,3},{3,2},{4,5},{5,4},{6,7},{7,6},{8,9},{9,8},{10,11... | collective-permute-start | bytes 1572872 | tf_op jit(solution)/shard_map/ppermute | solution.py:413
  118.4 10.3 %collective-permute-start.29 = (bf16[256,512]{1,0:T(8,128)(2,1)S(1)}, bf16[256,512]{1,0:T(8,128)(2,1)S(1)}, u32[]{:S(2)}, u32[]{:S(2)}) collective-permute-start(bf16[256,512]{1,0:T(8,128)(2,1)S(1)} %slice.4), channel_id=1, source_target_pairs={{0,2},{1,3},{2,4},{3,5},{4,6},{5,7},{8,10},{9,11},{10,12},{11,13},... | collective-permute-start | bytes 786440 | tf_op jit(solution)/shard_map/ppermute | solution.py:419
  131.6 9.4 %collective-permute-start.31 = (bf16[256,512]{1,0:T(8,128)(2,1)S(1)}, bf16[256,512]{1,0:T(8,128)(2,1)S(1)}, u32[]{:S(2)}, u32[]{:S(2)}) collective-permute-start(bf16[256,512]{1,0:T(8,128)(2,1)S(1)} %shard_map.68.refs_20_.refs_14_.refs_17_), channel_id=1, source_target_pairs={{0,2},{1,3},{2,4},{3,5},{4,6},{5,7},{8,10},{9,11},{10,12},{11,13},... | collective-permute-start | bytes 786440 | tf_op jit(solution)/shard_map/ppermute | solution.py:419
  134.1 7.0 %collective-permute-start.32 = (bf16[256,512]{1,0:T(8,128)(2,1)S(1)}, bf16[256,512]{1,0:T(8,128)(2,1)S(1)}, u32[]{:S(2)}, u32[]{:S(2)}) collective-permute-start(bf16[256,512]{1,0:T(8,128)(2,1)S(1)} %shard_map.68.refs_20_.refs_14_.refs_17_), channel_id=1, source_target_pairs={{0,1},{1,0},{2,3},{3,2},{4,5},{5,4},{6,7},{7,6},{8,9},{9,8},{10,11... | collective-permute-start | bytes 786440 | tf_op jit(solution)/shard_map/ppermute | solution.py:413
  141.6 7.8 %collective-permute-start.33 = (bf16[256,512]{1,0:T(8,128)(2,1)S(1)}, bf16[256,512]{1,0:T(8,128)(2,1)S(1)}, u32[]{:S(2)}, u32[]{:S(2)}) collective-permute-start(bf16[256,512]{1,0:T(8,128)(2,1)S(1)} %shard_map.70.refs_20_.refs_18_), channel_id=1, source_target_pairs={{0,1},{1,0},{2,3},{3,2},{4,5},{5,4},{6,7},{7,6},{8,9},{9,8},{10,11... | collective-permute-start | bytes 786440 | tf_op jit(solution)/shard_map/ppermute | solution.py:413

commit v9 on v8

--- a/solution.py
+++ b/solution.py
@@ -586,7 +586,7 @@
 
     plan = [(0, gather), (1, join), (2, functools.partial(fresh, 0)), (3, head_here), (line - 1, functools.partial(old, held, "old_held")), (3, head_pair), (3, functools.partial(fresh, 1)), (line, functools.partial(old, other, "old_other")), (4, scatter), (4, prep0), (5, head_all), (5, old_here), (5, prep1)]
     for i in range(pieces - 2):
-        plan.append((max(6 + i // 2, i + line - 1) if i < 3 else last_step, functools.partial(update, i)))
+        plan.append((max(5 + i, i + line - 1) if i < 3 else last_step, functools.partial(update, i)))
     plan.append((last_step, functools.partial(update, pieces - 2, 2)))
     for k in range(last_step + 1):
         step(k)

time: 157 us -> 168 us (1.070)
  starting transfers between devices: 49.5 us -> 55.3 us
  waiting for transfers between devices: 43.9 us -> 47 us
  local copies, waits for them, and re-layouts: 3.76 us -> 5.59 us
    ppermute x8, waiting for transfers between devices: 19.5 us -> 6.11 us  [to_next(): lax.ppermute(value, 'pcol', [(c, c + 2) for c in range(col_devices - 2)])]
    ppermute x10, waiting for transfers between devices: 17.3 us -> 27 us  [to_neighbour(): return lax.ppermute(value, 'pcol', [(c, c ^ 1) for c in range(col_devices)])]
    ppermute x5, waiting for transfers between devices: 2.35 us -> 7.91 us  [to_chip(): lax.ppermute(value, 'prow', [(r, (r + 2 * h) % row_devices) for r in rang...]
    ppermute x10, starting transfers between devices: 10.1 us -> 12.6 us  [to_neighbour(): return lax.ppermute(value, 'pcol', [(c, c ^ 1) for c in range(col_devices)])]
    ppermute x8, starting transfers between devices: 26.2 us -> 28.5 us  [to_next(): lax.ppermute(value, 'pcol', [(c, c + 2) for c in range(col_devices - 2)])]
    unnamed x12 -> x16, local copies, waits for them, and re-layouts: 3.55 us -> 5.38 us
  transfers between devices with their start and end apart: 34 -> 34, of which waited for: 13 -> 13; matrix products, arithmetic and copies ran while one was open for 0% -> 0% of each run, Pallas kernels for 31% -> 28%
where the time goes in v9:
time: 168 us; the launch traced here: 167 us
  Pallas kernels  58.6 us (35%)
  starting transfers between devices  55.3 us (33%)
  waiting for transfers between devices  47 us (28%)
  local copies, waits for them, and re-layouts  5.59 us (3%)
    pallas_call x27, Pallas kernels, call(): pl.pallas_call(ordered, out_shape=tuple((shape for shape, _ in outs)), in...  58.6 us
    ppermute x8, starting transfers between devices, to_next(): lax.ppermute(value, 'pcol', [(c, c + 2) for c in range(col_devices - 2)])  28.5 us
    ppermute x10, waiting for transfers between devices, to_neighbour(): return lax.ppermute(value, 'pcol', [(c, c ^ 1) for c in range(col_devices)])  27 us
    ppermute x10, starting transfers between devices, to_neighbour(): return lax.ppermute(value, 'pcol', [(c, c ^ 1) for c in range(col_devices)])  12.6 us
    ppermute x5, waiting for transfers between devices, to_chip(): lax.ppermute(value, 'prow', [(r, (r + 2 * h) % row_devices) for r in rang...  7.91 us
    ppermute x5, starting transfers between devices, to_chip(): lax.ppermute(value, 'prow', [(r, (r + 2 * h) % row_devices) for r in rang...  6.7 us
    ppermute x8, waiting for transfers between devices, to_next(): lax.ppermute(value, 'pcol', [(c, c + 2) for c in range(col_devices - 2)])  6.11 us
    ppermute x3, waiting for transfers between devices, fresh(): lax.ppermute(head[0], 'pcol', [(0, 2 * h), (1, 2 * h + 1)])  6.03 us
  transfers between devices with their start and end apart: 34, of which 13 were waited for; matrix products, arithmetic and copies ran while one was open for 0% of the time, Pallas kernels for 28%

profile of v9, /device:TPU:0, one launch (start us, length us, event | category | flops | bytes accessed | tf_op | source)
XLA Modules:
  0.0 167.2 jit_solution(12039014661502872849)
XLA Ops:
  0.0 2.2 %shard_map.46.refs_4_.refs_1_.refs_11_ = bf16[512,512]{1,0:T(8,128)(2,1)} custom-call(bf16[2560,2,512]{2,1,0:T(2,128)(2,1)} %bitcast.5), custom_call_target="tpu_custom_call" | custom-call | flops 1100000000 | tf_op jit(solution)/shard_map/pallas_call | solution.py:37
  2.2 3.0 %collective-permute-start.1 = (bf16[512,512]{1,0:T(8,128)(2,1)}, bf16[512,512]{1,0:T(8,128)(2,1)S(1)}, u32[]{:S(2)}, u32[]{:S(2)}) collective-permute-start(bf16[512,512]{1,0:T(8,128)(2,1)} %shard_map.46.refs_4_.refs_1_.refs_11_), channel_id=1, source_target_pairs={{0,1},{1,0},{2,3},{3,2},{4,5},{5,4},{6,7},{7,6},{8,9},{9,8},{10,11... | collective-permute-start | bytes 1572872 | tf_op jit(solution)/shard_map/ppermute | solution.py:413
  5.2 3.5 %collective-permute-start = (bf16[512,512]{1,0:T(8,128)(2,1)}, bf16[512,512]{1,0:T(8,128)(2,1)S(1)}, u32[]{:S(2)}, u32[]{:S(2)}) collective-permute-start(bf16[512,512]{1,0:T(8,128)(2,1)} %shard_map.46.refs_4_.refs_1_.refs_11_), channel_id=1, source_target_pairs={{0,2},{1,3},{2,4},{3,5},{4,6},{5,7},{8,10},{9,11},{10,12},{11,13},... | collective-permute-start | bytes 1572872 | tf_op jit(solution)/shard_map/ppermute | solution.py:419
  9.0 2.5 %copy-done.1 = bf16[5,512,2,512]{3,2,1,0:T(2,128)(2,1)S(1)} copy-done((bf16[5,512,2,512]{3,2,1,0:T(2,128)(2,1)S(1)}, bf16[5,512,2,512]{3,2,1,0:T(2,128)(2,1)}, u32[]{:S(2)}) %copy-start.1) | copy-done | bytes 5242904
  11.5 1.0 copy-done.2
  12.5 7.7 %shard_map.47 = (bf16[512,512]{1,0:T(8,128)(2,1)S(1)}, bf16[512,512]{1,0:T(8,128)(2,1)S(1)}, bf16[512,512]{1,0:T(8,128)(2,1)S(1)}, bf16[256,512]{1,0:T(8,128)(2,...) custom-call(s32[4]{0:T(128)S(1)} %pad_add_fusion.refs_0_, ...), custom_call_target="tpu_custom_call" | custom-call | flops 8800000000 | tf_op jit(solution)/shard_map/pallas_call | solution.py:37
  21.7 1.0 copy-done.7
  23.9 3.5 %collective-permute-start.2 = (bf16[512,512]{1,0:T(8,128)(2,1)S(1)}, bf16[512,512]{1,0:T(8,128)(2,1)S(1)}, u32[]{:S(2)}, u32[]{:S(2)}) collective-permute-start(bf16[512,512]{1,0:T(8,128)(2,1)S(1)} %shard_map.48.refs_4_.refs_2_.refs_12_.refs_11_), channel_id=1, source_target_pairs={{0,2},{1,3},{2,4},{3,5},{4,6},{5,7},{8,10},{9,11},{10,12},{11,13},... | collective-permute-start | bytes 1572872 | tf_op jit(solution)/shard_map/ppermute | solution.py:419
  27.4 2.4 %shard_map.49 = (bf16[256,2,512]{2,1,0:T(2,128)(2,1)S(1)}, bf16[256,2,512]{2,1,0:T(2,128)(2,1)S(1)}) custom-call(s32[4]{0:T(128)S(1)} %pad_add_fusion.refs_0_, s32[2,512]{1,0:T(2,128)S(1)} %get-tuple-element.43.refs_1_, bf16[512,2,512]{2,1,0:T(2,128)(2,1)S(1)} %get-tuple-element.44.refs_2_, bf16[512,2,512]{2,1,0:T(2,128)(2,1)S(1)} %collective-permute-done.3.refs_3_, ...), custom_call_target="tpu_custom_call" | custom-call | flops 2200000000 | tf_op jit(solution)/shard_map/pallas_call | solution.py:37
  29.8 1.6 collective-permute-start.7
  31.3 5.9 %collective-permute-done.4.refs_4_.refs_2_.refs_16_.refs_15_ = bf16[512,512]{1,0:T(8,128)(2,1)S(1)} collective-permute-done((bf16[512,512]{1,0:T(8,128)(2,1)S(1)}, bf16[512,512]{1,0:T(8,128)(2,1)S(1)}, u32[]{:S(2)}, u32[]{:S(2)}) %collective-permute-start.4) | collective-permute-done | bytes 524320 | tf_op jit(solution)/shard_map/ppermute | solution.py:413
  37.3 1.2 collective-permute-done.2.refs_1_
  39.1 1.6 collective-permute-start.8
  40.6 4.4 %collective-permute-start.6 = (bf16[512,512]{1,0:T(8,128)(2,1)S(1)}, bf16[512,512]{1,0:T(8,128)(2,1)S(1)}, u32[]{:S(2)}, u32[]{:S(2)}) collective-permute-start(bf16[512,512]{1,0:T(8,128)(2,1)S(1)} %shard_map.50.refs_4_.refs_3_.refs_13_.refs_12_.refs_11_), channel_id=1, source_target_pairs={{0,2},{1,3},{2,4},{3,5},{4,6},{5,7},{8,10},{9,11},{10,12},{11,13},... | collective-permute-start | bytes 1572872 | tf_op jit(solution)/shard_map/ppermute | solution.py:419
  45.1 1.1 shard_map.51
  46.2 2.0 %collective-permute-start.11 = (bf16[128,512]{1,0:T(8,128)(2,1)S(1)}, bf16[128,512]{1,0:T(8,128)(2,1)S(1)}, u32[]{:S(2)}, u32[]{:S(2)}) collective-permute-start(bf16[128,512]{1,0:T(8,128)(2,1)S(1)} %get-tuple-element.50.refs_3_.refs_1_), channel_id=1, source_target_pairs={{0,6},{1,7},{8,14},{9,15},{16,22},{17,23},{24,30},{25,31}} | collective-permute-start | bytes 393224 | tf_op jit(solution)/shard_map/ppermute | solution.py:502
  48.2 1.8 %collective-permute-start.10 = (bf16[128,512]{1,0:T(8,128)(2,1)S(1)}, bf16[128,512]{1,0:T(8,128)(2,1)S(1)}, u32[]{:S(2)}, u32[]{:S(2)}) collective-permute-start(bf16[128,512]{1,0:T(8,128)(2,1)S(1)} %get-tuple-element.50.refs_3_.refs_1_), channel_id=1, source_target_pairs={{0,4},{1,5},{8,12},{9,13},{16,20},{17,21},{24,28},{25,29}} | collective-permute-start | bytes 393224 | tf_op jit(solution)/shard_map/ppermute | solution.py:502
  50.1 1.3 collective-permute-start.9
  51.9 1.5 collective-permute-start.14
  53.4 4.0 %collective-permute-done.6.refs_1_ = bf16[512,512]{1,0:T(8,128)(2,1)S(1)} collective-permute-done((bf16[512,512]{1,0:T(8,128)(2,1)S(1)}, bf16[512,512]{1,0:T(8,128)(2,1)S(1)}, u32[]{:S(2)}, u32[]{:S(2)}) %collective-permute-start.6) | collective-permute-done | bytes 524320 | tf_op jit(solution)/shard_map/ppermute | solution.py:419
  57.4 2.8 %collective-permute-done.11.refs_7_.refs_4_ = bf16[128,512]{1,0:T(8,128)(2,1)S(1)} collective-permute-done((bf16[128,512]{1,0:T(8,128)(2,1)S(1)}, bf16[128,512]{1,0:T(8,128)(2,1)S(1)}, u32[]{:S(2)}, u32[]{:S(2)}) %collective-permute-start.11) | collective-permute-done | bytes 131104 | tf_op jit(solution)/shard_map/ppermute | solution.py:502
  60.2 1.8 %collective-permute-done.10.refs_6_.refs_3_ = bf16[128,512]{1,0:T(8,128)(2,1)S(1)} collective-permute-done((bf16[128,512]{1,0:T(8,128)(2,1)S(1)}, bf16[128,512]{1,0:T(8,128)(2,1)S(1)}, u32[]{:S(2)}, u32[]{:S(2)}) %collective-permute-start.10) | collective-permute-done | bytes 131104 | tf_op jit(solution)/shard_map/ppermute | solution.py:502
  62.0 1.4 collective-permute-done.9.refs_5_.refs_2_
  65.2 1.6 collective-permute-start.16
  66.8 4.4 %collective-permute-start.13 = (bf16[512,512]{1,0:T(8,128)(2,1)S(1)}, bf16[512,512]{1,0:T(8,128)(2,1)S(1)}, u32[]{:S(2)}, u32[]{:S(2)}) collective-permute-start(bf16[512,512]{1,0:T(8,128)(2,1)S(1)} %shard_map.52.refs_5_.refs_4_.refs_14_.refs_13_.refs_12_.refs_11_), channel_id=1, source_target_pairs={{0,2},{1,3},{2,4},{3,5},{4,6},{5,7},{8,10},{9,11},{10,12},{11,13},... | collective-permute-start | bytes 1572872 | tf_op jit(solution)/shard_map/ppermute | solution.py:419
  71.8 1.5 collective-permute-start.15
  73.3 11.8 %collective-permute-done.15.refs_1_ = bf16[128,512]{1,0:T(8,128)(2,1)S(1)} collective-permute-done((bf16[128,512]{1,0:T(8,128)(2,1)S(1)}, bf16[128,512]{1,0:T(8,128)(2,1)S(1)}, u32[]{:S(2)}, u32[]{:S(2)}) %collective-permute-start.15) | collective-permute-done | bytes 131104 | tf_op jit(solution)/shard_map/ppermute | solution.py:413
  85.7 1.1 shard_map.56
  88.5 2.2 %collective-permute-start.19 = (bf16[512,512]{1,0:T(8,128)(2,1)S(1)}, bf16[512,512]{1,0:T(8,128)(2,1)S(1)}, u32[]{:S(2)}, u32[]{:S(2)}) collective-permute-start(bf16[512,512]{1,0:T(8,128)(2,1)S(1)} %shard_map.57.refs_5_.refs_14_.refs_13_.refs_12_.refs_11_), channel_id=1, source_target_pairs={{0,2},{1,3},{2,4},{3,5},{4,6},{5,7},{8,10},{9,11},{10,12},{11,13},... | collective-permute-start | bytes 1572872 | tf_op jit(solution)/shard_map/ppermute | solution.py:419
  92.0 1.5 collective-permute-start.18
  93.5 4.1 %shard_map.59.refs_6_.refs_8_ = bf16[2568,2,512]{2,1,0:T(2,128)(2,1)S(1)} custom-call(s32[4]{0:T(128)S(1)} %pad_add_fusion.refs_0_, s32[2,512]{1,0:T(2,128)S(1)} %get-tuple-element.56.refs_1_, s32[2,512]{1,0:T(2,128)S(1)} %get-tuple-element.39.refs_2_.refs_1_, bf16[256,2,512]{2,1,0:T(2,128)(2,1)S(1)} %get-tuple-element.57.refs_3_, ...), custom_call_target="tpu_custom_call" | custom-call | flops 110000000 | tf_op jit(solution)/shard_map/pallas_call | solution.py:37
  97.6 2.0 %shard_map.60 = (bf16[512,1024]{1,0:T(8,128)(2,1)S(1)}, bf16[512,2,512]{2,1,0:T(2,128)(2,1)S(1)}) custom-call(s32[4]{0:T(128)S(1)} %pad_add_fusion.refs_0_, bf16[2,512,512]{2,1,0:T(8,128)(2,1)S(1)} %copy-done.4, bf16[256,1024]{1,0:T(8,128)(2,1)S(1)} %get-tuple-element.54.refs_2_.refs_6_, bf16[256,1024]{1,0:T(8,128)(2,1)S(1)} %collective-permute-done.20.refs_3_.refs_7_, ...), custom_call_target="tpu_custom_call" | custom-call | flops 2200000000 | tf_op jit(solution)/shard_map/pallas_call | solution.py:37
  99.6 2.3 %collective-permute-done.24.refs_4_.refs_18_.refs_17_.refs_16_.refs_19_ = bf16[512,512]{1,0:T(8,128)(2,1)S(1)} collective-permute-done((bf16[512,512]{1,0:T(8,128)(2,1)S(1)}, bf16[512,512]{1,0:T(8,128)(2,1)S(1)}, u32[]{:S(2)}, u32[]{:S(2)}) %collective-permute-start.24) | collective-permute-done | bytes 524320 | tf_op jit(solution)/shard_map/ppermute | solution.py:413
  102.5 7.9 %collective-permute-done.18.refs_1_ = bf16[2,128,512]{2,1,0:T(8,128)(2,1)S(1)} collective-permute-done((bf16[2,128,512]{2,1,0:T(8,128)(2,1)S(1)}, bf16[2,128,512]{2,1,0:T(8,128)(2,1)S(1)}, u32[]{:S(2)}, u32[]{:S(2)}) %collective-permute-start.18) | collective-permute-done | bytes 262176 | tf_op jit(solution)/shard_map/ppermute | solution.py:416
  111.7 1.5 collective-permute-start.28
  113.2 2.2 %collective-permute-start.27 = (bf16[512,512]{1,0:T(8,128)(2,1)S(1)}, bf16[512,512]{1,0:T(8,128)(2,1)S(1)}, u32[]{:S(2)}, u32[]{:S(2)}) collective-permute-start(bf16[512,512]{1,0:T(8,128)(2,1)S(1)} %shard_map.61.refs_2_.refs_14_.refs_13_.refs_12_.refs_15_), channel_id=1, source_target_pairs={{0,2},{1,3},{2,4},{3,5},{4,6},{5,7},{8,10},{9,11},{10,12},{11,13},... | collective-permute-start | bytes 1572872 | tf_op jit(solution)/shard_map/ppermute | solution.py:419
  115.4 3.5 %shard_map.64 = (bf16[512,1024]{1,0:T(8,128)(2,1)S(1)}, bf16[512,512]{1,0:T(8,128)(2,1)S(1)}, bf16[512,2,512]{2,1,0:T(2,128)(2,1)S(1)}) custom-call(s32[4]{0:T(128)S(1)} %pad_add_fusion.refs_0_, bf16[2,512,512]{2,1,0:T(8,128)(2,1)S(1)} %copy-done.4, bf16[2,512,512]{2,1,0:T(8,128)(2,1)S(1)} %copy-done, ...), custom_call_target="tpu_custom_call" | custom-call | flops 3849999872 | tf_op jit(solution)/shard_map/pallas_call | solution.py:37
  118.9 1.8 %shard_map.65 = (bf16[2560,2,512]{2,1,0:T(2,128)(2,1)}, f32[8,128]{1,0:T(8,128)S(1)}) custom-call(s32[4]{0:T(128)S(1)} %pad_add_fusion.refs_0_, s32[2,512]{1,0:T(2,128)S(1)} %get-tuple-element.39.refs_2_.refs_1_, bf16[2,512,512]{2,1,0:T(8,128)(2,1)S(1)} %shard_map.63.refs_10_.refs_2_, bf16[2,512,512]{2,1,0:T(8,128)(2,1)S(1)} %collective-permute-done.25.refs_3_, ...), custom_call_target="tpu_custom_call" | custom-call | flops 5500000256 | tf_op jit(solution)/shard_map/pallas_call | solution.py:37
  120.8 4.8 %collective-permute-done.28.refs_3_.refs_18_.refs_17_.refs_20_.refs_23_ = bf16[512,512]{1,0:T(8,128)(2,1)S(1)} collective-permute-done((bf16[512,512]{1,0:T(8,128)(2,1)S(1)}, bf16[512,512]{1,0:T(8,128)(2,1)S(1)}, u32[]{:S(2)}, u32[]{:S(2)}) %collective-permute-start.28) | collective-permute-done | bytes 524320 | tf_op jit(solution)/shard_map/ppermute | solution.py:413
  127.8 4.3 %collective-permute-start.29 = (bf16[256,512]{1,0:T(8,128)(2,1)S(1)}, bf16[256,512]{1,0:T(8,128)(2,1)S(1)}, u32[]{:S(2)}, u32[]{:S(2)}) collective-permute-start(bf16[256,512]{1,0:T(8,128)(2,1)S(1)} %slice.4), channel_id=1, source_target_pairs={{0,2},{1,3},{2,4},{3,5},{4,6},{5,7},{8,10},{9,11},{10,12},{11,13},... | collective-permute-start | bytes 786440 | tf_op jit(solution)/shard_map/ppermute | solution.py:419
  132.1 6.2 %shard_map.67 = (bf16[2560,2,512]{2,1,0:T(2,128)(2,1)}, f32[8,128]{1,0:T(8,128)S(1)}) custom-call(s32[4]{0:T(128)S(1)} %pad_add_fusion.refs_0_, s32[2,512]{1,0:T(2,128)S(1)} %get-tuple-element.39.refs_2_.refs_1_, bf16[2,512,512]{2,1,0:T(8,128)(2,1)S(1)} %shard_map.63.refs_10_.refs_2_, ...), custom_call_target="tpu_custom_call", output_to_operand_aliasing={{0}: (19, {})} | custom-call | flops 5500000256 | tf_op jit(solution)/shard_map/pallas_call | solution.py:37
  138.3 1.6 collective-permute-done.30.refs_3_.refs_18_.refs_21_.refs_24_
  140.4 1.0 collective-permute-start.32
  141.4 4.0 %collective-permute-start.31 = (bf16[256,512]{1,0:T(8,128)(2,1)S(1)}, bf16[256,512]{1,0:T(8,128)(2,1)S(1)}, u32[]{:S(2)}, u32[]{:S(2)}) collective-permute-start(bf16[256,512]{1,0:T(8,128)(2,1)S(1)} %shard_map.68.refs_20_.refs_14_.refs_17_), channel_id=1, source_target_pairs={{0,2},{1,3},{2,4},{3,5},{4,6},{5,7},{8,10},{9,11},{10,12},{11,13},... | collective-permute-start | bytes 786440 | tf_op jit(solution)/shard_map/ppermute | solution.py:419
  145.4 6.4 %shard_map.69 = (bf16[2560,2,512]{2,1,0:T(2,128)(2,1)}, f32[8,128]{1,0:T(8,128)S(1)}) custom-call(s32[4]{0:T(128)S(1)} %pad_add_fusion.refs_0_, s32[2,512]{1,0:T(2,128)S(1)} %get-tuple-element.39.refs_2_.refs_1_, bf16[2,512,512]{2,1,0:T(8,128)(2,1)S(1)} %shard_map.63.refs_10_.refs_2_, ...), custom_call_target="tpu_custom_call", output_to_operand_aliasing={{0}: (19, {})} | custom-call | flops 5500000256 | tf_op jit(solution)/shard_map/pallas_call | solution.py:37
  152.4 1.6 collective-permute-start.33
  154.0 6.2 %shard_map.71 = (bf16[2560,2,512]{2,1,0:T(2,128)(2,1)}, f32[8,128]{1,0:T(8,128)S(1)}) custom-call(s32[4]{0:T(128)S(1)} %pad_add_fusion.refs_0_, s32[2,512]{1,0:T(2,128)S(1)} %get-tuple-element.39.refs_2_.refs_1_, bf16[2,512,512]{2,1,0:T(8,128)(2,1)S(1)} %shard_map.63.refs_10_.refs_2_, ...), custom_call_target="tpu_custom_call", output_to_operand_aliasing={{0}: (19, {})} | custom-call | flops 5500000256 | tf_op jit(solution)/shard_map/pallas_call | solution.py:37
  160.2 6.8 %shard_map.72 = (bf16[2560,2,512]{2,1,0:T(2,128)(2,1)}, f32[8,128]{1,0:T(8,128)}) custom-call(s32[4]{0:T(128)S(1)} %pad_add_fusion.refs_0_, s32[2,512]{1,0:T(2,128)S(1)} %get-tuple-element.39.refs_2_.refs_1_, bf16[2,512,512]{2,1,0:T(8,128)(2,1)S(1)} %shard_map.63.refs_10_.refs_2_, ...), custom_call_target="tpu_custom_call", output_to_operand_aliasing={{0}: (27, {})} | custom-call | flops 5500000256 | tf_op jit(solution)/shard_map/pallas_call | solution.py:37
  (66 shorter events, 14.9 us)
Async XLA Ops:
  0.0 8.8 %copy-start.5 = (s32[2,512]{1,0:T(2,128)S(1)}, s32[2,512]{1,0:T(2,128)}, u32[]{:S(2)}) copy-start(s32[2,512]{1,0:T(2,128)} %refs_1_.3) | copy-start | bytes 12292
  2.2 18.7 %collective-permute-start.1 = (bf16[512,512]{1,0:T(8,128)(2,1)}, bf16[512,512]{1,0:T(8,128)(2,1)S(1)}, u32[]{:S(2)}, u32[]{:S(2)}) collective-permute-start(bf16[512,512]{1,0:T(8,128)(2,1)} %shard_map.46.refs_4_.refs_1_.refs_11_), channel_id=1, source_target_pairs={{0,1},{1,0},{2,3},{3,2},{4,5},{5,4},{6,7},{7,6},{8,9},{9,8},{10,11... | collective-permute-start | bytes 1572872 | tf_op jit(solution)/shard_map/ppermute | solution.py:413
  5.2 15.7 %collective-permute-start = (bf16[512,512]{1,0:T(8,128)(2,1)}, bf16[512,512]{1,0:T(8,128)(2,1)S(1)}, u32[]{:S(2)}, u32[]{:S(2)}) collective-permute-start(bf16[512,512]{1,0:T(8,128)(2,1)} %shard_map.46.refs_4_.refs_1_.refs_11_), channel_id=1, source_target_pairs={{0,2},{1,3},{2,4},{3,5},{4,6},{5,7},{8,10},{9,11},{10,12},{11,13},... | collective-permute-start | bytes 1572872 | tf_op jit(solution)/shard_map/ppermute | solution.py:419
  9.0 2.5 %copy-start.1 = (bf16[5,512,2,512]{3,2,1,0:T(2,128)(2,1)S(1)}, bf16[5,512,2,512]{3,2,1,0:T(2,128)(2,1)}, u32[]{:S(2)}) copy-start(bf16[5,512,2,512]{3,2,1,0:T(2,128)(2,1)} %param.4) | copy-start | bytes 15728644
  11.5 1.0 copy-start.2
  20.3 7.1 %collective-permute-start.3 = (bf16[512,2,512]{2,1,0:T(2,128)(2,1)S(1)}, bf16[512,2,512]{2,1,0:T(2,128)(2,1)S(1)}, u32[]{:S(2)}, u32[]{:S(2)}) collective-permute-start(bf16[512,2,512]{2,1,0:T(2,128)(2,1)S(1)} %get-tuple-element.45), channel_id=1, source_target_pairs={{0,8},{8,0},{16,24},{24,16},{1,9},{9,1},{17,25},{25,17},{2,10},{10... | collective-permute-start | bytes 3145736 | tf_op jit(solution)/shard_map/ppermute | solution.py:410
  20.4 18.1 %collective-permute-start.5 = (bf16[512,2,512]{2,1,0:T(2,128)(2,1)S(1)}, bf16[512,2,512]{2,1,0:T(2,128)(2,1)S(1)}, u32[]{:S(2)}, u32[]{:S(2)}) collective-permute-start(bf16[512,2,512]{2,1,0:T(2,128)(2,1)S(1)} %get-tuple-element.47.refs_7_), channel_id=1, source_target_pairs={{0,8},{8,0},{16,24},{24,16},{1,9},{9,1},{17,25},{25,17},{2,10},{10... | collective-permute-start | bytes 3145736 | tf_op jit(solution)/shard_map/ppermute | solution.py:410
  20.9 0.8 copy-start.6
  21.7 1.0 copy-start.7
  23.3 14.0 %collective-permute-start.4 = (bf16[512,512]{1,0:T(8,128)(2,1)S(1)}, bf16[512,512]{1,0:T(8,128)(2,1)S(1)}, u32[]{:S(2)}, u32[]{:S(2)}) collective-permute-start(bf16[512,512]{1,0:T(8,128)(2,1)S(1)} %shard_map.48.refs_4_.refs_2_.refs_12_.refs_11_), channel_id=1, source_target_pairs={{0,1},{1,0},{2,3},{3,2},{4,5},{5,4},{6,7},{7,6},{8,9},{9,8},{10,11... | collective-permute-start | bytes 1572872 | tf_op jit(solution)/shard_map/ppermute | solution.py:413
  23.9 14.6 %collective-permute-start.2 = (bf16[512,512]{1,0:T(8,128)(2,1)S(1)}, bf16[512,512]{1,0:T(8,128)(2,1)S(1)}, u32[]{:S(2)}, u32[]{:S(2)}) collective-permute-start(bf16[512,512]{1,0:T(8,128)(2,1)S(1)} %shard_map.48.refs_4_.refs_2_.refs_12_.refs_11_), channel_id=1, source_target_pairs={{0,2},{1,3},{2,4},{3,5},{4,6},{5,7},{8,10},{9,11},{10,12},{11,13},... | collective-permute-start | bytes 1572872 | tf_op jit(solution)/shard_map/ppermute | solution.py:419
  29.8 15.3 %collective-permute-start.7 = (bf16[256,2,512]{2,1,0:T(2,128)(2,1)S(1)}, bf16[256,2,512]{2,1,0:T(2,128)(2,1)S(1)}, u32[]{:S(2)}, u32[]{:S(2)}) collective-permute-start(bf16[256,2,512]{2,1,0:T(2,128)(2,1)S(1)} %get-tuple-element.49.refs_2_), channel_id=1, source_target_pairs={{0,16},{8,24},{16,0},{24,8},{1,17},{9,25},{17,1},{25,9},{2,18},{10... | collective-permute-start | bytes 1572872 | tf_op jit(solution)/shard_map/ppermute | solution.py:416
  39.1 12.8 %collective-permute-start.8 = (bf16[512,512]{1,0:T(8,128)(2,1)S(1)}, bf16[512,512]{1,0:T(8,128)(2,1)S(1)}, u32[]{:S(2)}, u32[]{:S(2)}) collective-permute-start(bf16[512,512]{1,0:T(8,128)(2,1)S(1)} %shard_map.50.refs_4_.refs_3_.refs_13_.refs_12_.refs_11_), channel_id=1, source_target_pairs={{0,1},{1,0},{2,3},{3,2},{4,5},{5,4},{6,7},{7,6},{8,9},{9,8},{10,11... | collective-permute-start | bytes 1572872 | tf_op jit(solution)/shard_map/ppermute | solution.py:413
  40.6 16.7 %collective-permute-start.6 = (bf16[512,512]{1,0:T(8,128)(2,1)S(1)}, bf16[512,512]{1,0:T(8,128)(2,1)S(1)}, u32[]{:S(2)}, u32[]{:S(2)}) collective-permute-start(bf16[512,512]{1,0:T(8,128)(2,1)S(1)} %shard_map.50.refs_4_.refs_3_.refs_13_.refs_12_.refs_11_), channel_id=1, source_target_pairs={{0,2},{1,3},{2,4},{3,5},{4,6},{5,7},{8,10},{9,11},{10,12},{11,13},... | collective-permute-start | bytes 1572872 | tf_op jit(solution)/shard_map/ppermute | solution.py:419
  46.2 14.0 %collective-permute-start.11 = (bf16[128,512]{1,0:T(8,128)(2,1)S(1)}, bf16[128,512]{1,0:T(8,128)(2,1)S(1)}, u32[]{:S(2)}, u32[]{:S(2)}) collective-permute-start(bf16[128,512]{1,0:T(8,128)(2,1)S(1)} %get-tuple-element.50.refs_3_.refs_1_), channel_id=1, source_target_pairs={{0,6},{1,7},{8,14},{9,15},{16,22},{17,23},{24,30},{25,31}} | collective-permute-start | bytes 393224 | tf_op jit(solution)/shard_map/ppermute | solution.py:502
  48.2 13.8 %collective-permute-start.10 = (bf16[128,512]{1,0:T(8,128)(2,1)S(1)}, bf16[128,512]{1,0:T(8,128)(2,1)S(1)}, u32[]{:S(2)}, u32[]{:S(2)}) collective-permute-start(bf16[128,512]{1,0:T(8,128)(2,1)S(1)} %get-tuple-element.50.refs_3_.refs_1_), channel_id=1, source_target_pairs={{0,4},{1,5},{8,12},{9,13},{16,20},{17,21},{24,28},{25,29}} | collective-permute-start | bytes 393224 | tf_op jit(solution)/shard_map/ppermute | solution.py:502
  50.1 13.3 %collective-permute-start.9 = (bf16[128,512]{1,0:T(8,128)(2,1)S(1)}, bf16[128,512]{1,0:T(8,128)(2,1)S(1)}, u32[]{:S(2)}, u32[]{:S(2)}) collective-permute-start(bf16[128,512]{1,0:T(8,128)(2,1)S(1)} %get-tuple-element.50.refs_3_.refs_1_), channel_id=1, source_target_pairs={{0,2},{1,3},{8,10},{9,11},{16,18},{17,19},{24,26},{25,27}} | collective-permute-start | bytes 393224 | tf_op jit(solution)/shard_map/ppermute | solution.py:502
  51.9 33.2 %collective-permute-start.14 = (bf16[256,2,512]{2,1,0:T(2,128)(2,1)S(1)}, bf16[256,2,512]{2,1,0:T(2,128)(2,1)S(1)}, u32[]{:S(2)}, u32[]{:S(2)}) collective-permute-start(bf16[256,2,512]{2,1,0:T(2,128)(2,1)S(1)} %get-tuple-element.46.refs_3_.refs_2_), channel_id=1, source_target_pairs={{0,16},{8,24},{16,0},{24,8},{1,17},{9,25},{17,1},{25,9},{2,18},{10... | collective-permute-start | bytes 1572872 | tf_op jit(solution)/shard_map/ppermute | solution.py:416
  65.2 21.6 %collective-permute-start.16 = (bf16[512,512]{1,0:T(8,128)(2,1)S(1)}, bf16[512,512]{1,0:T(8,128)(2,1)S(1)}, u32[]{:S(2)}, u32[]{:S(2)}) collective-permute-start(bf16[512,512]{1,0:T(8,128)(2,1)S(1)} %shard_map.54.refs_2_.refs_1_), channel_id=1, source_target_pairs={{0,16},{8,24},{16,0},{24,8},{1,17},{9,25},{17,1},{25,9},{2,18},{10... | collective-permute-start | bytes 1572872 | tf_op jit(solution)/shard_map/ppermute | solution.py:416
  66.8 20.1 %collective-permute-start.13 = (bf16[512,512]{1,0:T(8,128)(2,1)S(1)}, bf16[512,512]{1,0:T(8,128)(2,1)S(1)}, u32[]{:S(2)}, u32[]{:S(2)}) collective-permute-start(bf16[512,512]{1,0:T(8,128)(2,1)S(1)} %shard_map.52.refs_5_.refs_4_.refs_14_.refs_13_.refs_12_.refs_11_), channel_id=1, source_target_pairs={{0,2},{1,3},{2,4},{3,5},{4,6},{5,7},{8,10},{9,11},{10,12},{11,13},... | collective-permute-start | bytes 1572872 | tf_op jit(solution)/shard_map/ppermute | solution.py:419
  71.2 16.2 %collective-permute-start.12 = (bf16[512,512]{1,0:T(8,128)(2,1)S(1)}, bf16[512,512]{1,0:T(8,128)(2,1)S(1)}, u32[]{:S(2)}, u32[]{:S(2)}) collective-permute-start(bf16[512,512]{1,0:T(8,128)(2,1)S(1)} %shard_map.52.refs_5_.refs_4_.refs_14_.refs_13_.refs_12_.refs_11_), channel_id=1, source_target_pairs={{0,1},{1,0},{2,3},{3,2},{4,5},{5,4},{6,7},{7,6},{8,9},{9,8},{10,11... | collective-permute-start | bytes 1572872 | tf_op jit(solution)/shard_map/ppermute | solution.py:413
  71.8 13.3 %collective-permute-start.15 = (bf16[128,512]{1,0:T(8,128)(2,1)S(1)}, bf16[128,512]{1,0:T(8,128)(2,1)S(1)}, u32[]{:S(2)}, u32[]{:S(2)}) collective-permute-start(bf16[128,512]{1,0:T(8,128)(2,1)S(1)} %shard_map.53.refs_5_.refs_0_), channel_id=1, source_target_pairs={{0,1},{1,0},{2,3},{3,2},{4,5},{5,4},{6,7},{7,6},{8,9},{9,8},{10,11... | collective-permute-start | bytes 393224 | tf_op jit(solution)/shard_map/ppermute | solution.py:413
  85.1 3.5 %collective-permute-start.22 = (bf16[256,2,512]{2,1,0:T(2,128)(2,1)S(1)}, bf16[256,2,512]{2,1,0:T(2,128)(2,1)S(1)}, u32[]{:S(2)}, u32[]{:S(2)}) collective-permute-start(bf16[256,2,512]{2,1,0:T(2,128)(2,1)S(1)} %get-tuple-element.57.refs_3_), channel_id=1, source_target_pairs={{0,8},{8,0},{16,24},{24,16},{1,9},{9,1},{17,25},{25,17},{2,10},{10... | collective-permute-start | bytes 1572872 | tf_op jit(solution)/shard_map/ppermute | solution.py:410
  85.1 6.3 %collective-permute-start.20 = (bf16[256,1024]{1,0:T(8,128)(2,1)S(1)}, bf16[256,1024]{1,0:T(8,128)(2,1)S(1)}, u32[]{:S(2)}, u32[]{:S(2)}) collective-permute-start(bf16[256,1024]{1,0:T(8,128)(2,1)S(1)} %get-tuple-element.54.refs_2_.refs_6_), channel_id=1, source_target_pairs={{0,8},{8,0},{16,24},{24,16},{1,9},{9,1},{17,25},{25,17},{2,10},{10... | collective-permute-start | bytes 1572872 | tf_op jit(solution)/shard_map/ppermute | solution.py:410
  86.8 5.2 %collective-permute-start.23 = (bf16[256,2,512]{2,1,0:T(2,128)(2,1)S(1)}, bf16[256,2,512]{2,1,0:T(2,128)(2,1)S(1)}, u32[]{:S(2)}, u32[]{:S(2)}) collective-permute-start(bf16[256,2,512]{2,1,0:T(2,128)(2,1)S(1)} %get-tuple-element.52.refs_3_.refs_5_), channel_id=1, source_target_pairs={{0,8},{8,0},{16,24},{24,16},{1,9},{9,1},{17,25},{25,17},{2,10},{10... | collective-permute-start | bytes 1572872 | tf_op jit(solution)/shard_map/ppermute | solution.py:410
  86.9 10.7 %collective-permute-start.21 = (bf16[256,1024]{1,0:T(8,128)(2,1)S(1)}, bf16[256,1024]{1,0:T(8,128)(2,1)S(1)}, u32[]{:S(2)}, u32[]{:S(2)}) collective-permute-start(bf16[256,1024]{1,0:T(8,128)(2,1)S(1)} %get-tuple-element.55.refs_4_.refs_8_), channel_id=1, source_target_pairs={{0,8},{8,0},{16,24},{24,16},{1,9},{9,1},{17,25},{25,17},{2,10},{10... | collective-permute-start | bytes 1572872 | tf_op jit(solution)/shard_map/ppermute | solution.py:410
  88.0 14.0 %collective-permute-start.24 = (bf16[512,512]{1,0:T(8,128)(2,1)S(1)}, bf16[512,512]{1,0:T(8,128)(2,1)S(1)}, u32[]{:S(2)}, u32[]{:S(2)}) collective-permute-start(bf16[512,512]{1,0:T(8,128)(2,1)S(1)} %shard_map.57.refs_5_.refs_14_.refs_13_.refs_12_.refs_11_), channel_id=1, source_target_pairs={{0,1},{1,0},{2,3},{3,2},{4,5},{5,4},{6,7},{7,6},{8,9},{9,8},{10,11... | collective-permute-start | bytes 1572872 | tf_op jit(solution)/shard_map/ppermute | solution.py:413
  88.5 13.4 %collective-permute-start.19 = (bf16[512,512]{1,0:T(8,128)(2,1)S(1)}, bf16[512,512]{1,0:T(8,128)(2,1)S(1)}, u32[]{:S(2)}, u32[]{:S(2)}) collective-permute-start(bf16[512,512]{1,0:T(8,128)(2,1)S(1)} %shard_map.57.refs_5_.refs_14_.refs_13_.refs_12_.refs_11_), channel_id=1, source_target_pairs={{0,2},{1,3},{2,4},{3,5},{4,6},{5,7},{8,10},{9,11},{10,12},{11,13},... | collective-permute-start | bytes 1572872 | tf_op jit(solution)/shard_map/ppermute | solution.py:419
  91.4 19.1 %collective-permute-start.17 = (bf16[512,512]{1,0:T(8,128)(2,1)S(1)}, bf16[512,512]{1,0:T(8,128)(2,1)S(1)}, u32[]{:S(2)}, u32[]{:S(2)}) collective-permute-start(bf16[512,512]{1,0:T(8,128)(2,1)S(1)} %shard_map.58.refs_10_.refs_2_), channel_id=1, source_target_pairs={{0,16},{8,24},{16,0},{24,8},{1,17},{9,25},{17,1},{25,9},{2,18},{10... | collective-permute-start | bytes 1572872 | tf_op jit(solution)/shard_map/ppermute | solution.py:416
  92.0 18.4 %collective-permute-start.18 = (bf16[2,128,512]{2,1,0:T(8,128)(2,1)S(1)}, bf16[2,128,512]{2,1,0:T(8,128)(2,1)S(1)}, u32[]{:S(2)}, u32[]{:S(2)}) collective-permute-start(bf16[2,128,512]{2,1,0:T(8,128)(2,1)S(1)} %shard_map.55.refs_4_.refs_0_), channel_id=1, source_target_pairs={{0,16},{8,24},{16,0},{24,8},{1,17},{9,25},{17,1},{25,9},{2,18},{10... | collective-permute-start | bytes 786440 | tf_op jit(solution)/shard_map/ppermute | solution.py:416
  93.5 4.1 %copy-start.4 = (bf16[2,512,512]{2,1,0:T(8,128)(2,1)S(1)}, bf16[2,512,512]{2,1,0:T(8,128)(2,1)}, u32[]{:S(2)}) copy-start(bf16[2,512,512]{2,1,0:T(8,128)(2,1)} %refs_1_.5) | copy-start | bytes 3145732
  99.6 15.8 %copy-start = (bf16[2,512,512]{2,1,0:T(8,128)(2,1)S(1)}, bf16[2,512,512]{2,1,0:T(8,128)(2,1)}, u32[]{:S(2)}) copy-start(bf16[2,512,512]{2,1,0:T(8,128)(2,1)} %refs_4_.9) | copy-start | bytes 3145732
  111.1 7.8 %collective-permute-start.25 = (bf16[2,512,512]{2,1,0:T(8,128)(2,1)S(1)}, bf16[2,512,512]{2,1,0:T(8,128)(2,1)S(1)}, u32[]{:S(2)}, u32[]{:S(2)}) collective-permute-start(bf16[2,512,512]{2,1,0:T(8,128)(2,1)S(1)} %shard_map.63.refs_10_.refs_2_), channel_id=1, source_target_pairs={{0,8},{8,0},{16,24},{24,16},{1,9},{9,1},{17,25},{25,17},{2,10},{10... | collective-permute-start | bytes 3145736 | tf_op jit(solution)/shard_map/ppermute | solution.py:410
  111.2 4.2 %collective-permute-start.26 = (bf16[2,2,128,512]{3,2,1,0:T(8,128)(2,1)S(1)}, bf16[2,2,128,512]{3,2,1,0:T(8,128)(2,1)S(1)}, u32[]{:S(2)}, u32[]{:S(2)}) collective-permute-start(bf16[2,2,128,512]{3,2,1,0:T(8,128)(2,1)S(1)} %shard_map.62.refs_5_.refs_4_), channel_id=1, source_target_pairs={{0,8},{8,0},{16,24},{24,16},{1,9},{9,1},{17,25},{25,17},{2,10},{10... | collective-permute-start | bytes 1572872 | tf_op jit(solution)/shard_map/ppermute | solution.py:410
  111.7 13.9 %collective-permute-start.28 = (bf16[512,512]{1,0:T(8,128)(2,1)S(1)}, bf16[512,512]{1,0:T(8,128)(2,1)S(1)}, u32[]{:S(2)}, u32[]{:S(2)}) collective-permute-start(bf16[512,512]{1,0:T(8,128)(2,1)S(1)} %shard_map.61.refs_2_.refs_14_.refs_13_.refs_12_.refs_15_), channel_id=1, source_target_pairs={{0,1},{1,0},{2,3},{3,2},{4,5},{5,4},{6,7},{7,6},{8,9},{9,8},{10,11... | collective-permute-start | bytes 1572872 | tf_op jit(solution)/shard_map/ppermute | solution.py:413
  113.2 13.3 %collective-permute-start.27 = (bf16[512,512]{1,0:T(8,128)(2,1)S(1)}, bf16[512,512]{1,0:T(8,128)(2,1)S(1)}, u32[]{:S(2)}, u32[]{:S(2)}) collective-permute-start(bf16[512,512]{1,0:T(8,128)(2,1)S(1)} %shard_map.61.refs_2_.refs_14_.refs_13_.refs_12_.refs_15_), channel_id=1, source_target_pairs={{0,2},{1,3},{2,4},{3,5},{4,6},{5,7},{8,10},{9,11},{10,12},{11,13},... | collective-permute-start | bytes 1572872 | tf_op jit(solution)/shard_map/ppermute | solution.py:419
  115.4 3.5 %copy-start.3 = (bf16[512,512]{1,0:T(8,128)(2,1)S(1)}, bf16[512,512]{1,0:T(8,128)(2,1)}, u32[]{:S(2)}) copy-start(bf16[512,512]{1,0:T(8,128)(2,1)} %shard_map.46.refs_4_.refs_1_.refs_11_) | copy-start | bytes 1572868
  127.1 12.8 %collective-permute-start.30 = (bf16[512,512]{1,0:T(8,128)(2,1)S(1)}, bf16[512,512]{1,0:T(8,128)(2,1)S(1)}, u32[]{:S(2)}, u32[]{:S(2)}) collective-permute-start(bf16[512,512]{1,0:T(8,128)(2,1)S(1)} %shard_map.66.refs_20_.refs_14_.refs_13_.refs_16_), channel_id=1, source_target_pairs={{0,1},{1,0},{2,3},{3,2},{4,5},{5,4},{6,7},{7,6},{8,9},{9,8},{10,11... | collective-permute-start | bytes 1572872 | tf_op jit(solution)/shard_map/ppermute | solution.py:413
  127.8 10.5 %collective-permute-start.29 = (bf16[256,512]{1,0:T(8,128)(2,1)S(1)}, bf16[256,512]{1,0:T(8,128)(2,1)S(1)}, u32[]{:S(2)}, u32[]{:S(2)}) collective-permute-start(bf16[256,512]{1,0:T(8,128)(2,1)S(1)} %slice.4), channel_id=1, source_target_pairs={{0,2},{1,3},{2,4},{3,5},{4,6},{5,7},{8,10},{9,11},{10,12},{11,13},... | collective-permute-start | bytes 786440 | tf_op jit(solution)/shard_map/ppermute | solution.py:419
  140.4 11.4 %collective-permute-start.32 = (bf16[256,512]{1,0:T(8,128)(2,1)S(1)}, bf16[256,512]{1,0:T(8,128)(2,1)S(1)}, u32[]{:S(2)}, u32[]{:S(2)}) collective-permute-start(bf16[256,512]{1,0:T(8,128)(2,1)S(1)} %shard_map.68.refs_20_.refs_14_.refs_17_), channel_id=1, source_target_pairs={{0,1},{1,0},{2,3},{3,2},{4,5},{5,4},{6,7},{7,6},{8,9},{9,8},{10,11... | collective-permute-start | bytes 786440 | tf_op jit(solution)/shard_map/ppermute | solution.py:413
  141.4 10.4 %collective-permute-start.31 = (bf16[256,512]{1,0:T(8,128)(2,1)S(1)}, bf16[256,512]{1,0:T(8,128)(2,1)S(1)}, u32[]{:S(2)}, u32[]{:S(2)}) collective-permute-start(bf16[256,512]{1,0:T(8,128)(2,1)S(1)} %shard_map.68.refs_20_.refs_14_.refs_17_), channel_id=1, source_target_pairs={{0,2},{1,3},{2,4},{3,5},{4,6},{5,7},{8,10},{9,11},{10,12},{11,13},... | collective-permute-start | bytes 786440 | tf_op jit(solution)/shard_map/ppermute | solution.py:419
  152.4 7.8 %collective-permute-start.33 = (bf16[256,512]{1,0:T(8,128)(2,1)S(1)}, bf16[256,512]{1,0:T(8,128)(2,1)S(1)}, u32[]{:S(2)}, u32[]{:S(2)}) collective-permute-start(bf16[256,512]{1,0:T(8,128)(2,1)S(1)} %shard_map.70.refs_20_.refs_18_), channel_id=1, source_target_pairs={{0,1},{1,0},{2,3},{3,2},{4,5},{5,4},{6,7},{7,6},{8,9},{9,8},{10,11... | collective-permute-start | bytes 786440 | tf_op jit(solution)/shard_map/ppermute | solution.py:413

commit v10 on v8

--- a/solution.py
+++ b/solution.py
@@ -584,7 +584,7 @@
             us=5.0, mib=24,
         )
 
-    plan = [(0, gather), (1, join), (2, functools.partial(fresh, 0)), (3, head_here), (line - 1, functools.partial(old, held, "old_held")), (3, head_pair), (3, functools.partial(fresh, 1)), (line, functools.partial(old, other, "old_other")), (4, scatter), (4, prep0), (5, head_all), (5, old_here), (5, prep1)]
+    plan = [(0, gather), (1, join), (2, functools.partial(fresh, 0)), (3, head_here), (3, head_pair), (3, functools.partial(fresh, 1)), (line, functools.partial(old, held, "old_held")), (line, functools.partial(old, other, "old_other")), (4, scatter), (4, prep0), (5, head_all), (5, old_here), (5, prep1)]
     for i in range(pieces - 2):
         plan.append((max(6 + i // 2, i + line - 1) if i < 3 else last_step, functools.partial(update, i)))
     plan.append((last_step, functools.partial(update, pieces - 2, 2)))

time: 157 us -> 165 us (1.051)
  waiting for transfers between devices: 43.9 us -> 49 us
  local copies, waits for them, and re-layouts: 3.76 us -> 5.59 us
    ppermute x5, waiting for transfers between devices: 2.35 us -> 16.2 us  [to_chip(): lax.ppermute(value, 'prow', [(r, (r + 2 * h) % row_devices) for r in rang...]
    ppermute x8, waiting for transfers between devices: 19.5 us -> 12.9 us  [to_next(): lax.ppermute(value, 'pcol', [(c, c + 2) for c in range(col_devices - 2)])]
    ppermute x3, starting transfers between devices: 4.4 us -> 7.49 us  [fresh(): lax.ppermute(head[0], 'pcol', [(0, 2 * h), (1, 2 * h + 1)])]
    ppermute x8, starting transfers between devices: 26.2 us -> 23.7 us  [to_next(): lax.ppermute(value, 'pcol', [(c, c + 2) for c in range(col_devices - 2)])]
    ppermute x3, waiting for transfers between devices: 4.82 us -> 2.48 us  [fresh(): lax.ppermute(head[0], 'pcol', [(0, 2 * h), (1, 2 * h + 1)])]
    unnamed x12 -> x16, local copies, waits for them, and re-layouts: 3.55 us -> 5.38 us
  transfers between devices with their start and end apart: 34 -> 34, of which waited for: 13 -> 12; matrix products, arithmetic and copies ran while one was open for 0% -> 0% of each run, Pallas kernels for 31% -> 30%
where the time goes in v10:
time: 165 us; the launch traced here: 164 us
  Pallas kernels  58.5 us (35%)
  starting transfers between devices  49.6 us (30%)
  waiting for transfers between devices  49 us (30%)
  local copies, waits for them, and re-layouts  5.59 us (3%)
    pallas_call x27, Pallas kernels, call(): pl.pallas_call(ordered, out_shape=tuple((shape for shape, _ in outs)), in...  58.5 us
    ppermute x8, starting transfers between devices, to_next(): lax.ppermute(value, 'pcol', [(c, c + 2) for c in range(col_devices - 2)])  23.7 us
    ppermute x10, waiting for transfers between devices, to_neighbour(): return lax.ppermute(value, 'pcol', [(c, c ^ 1) for c in range(col_devices)])  17.5 us
    ppermute x5, waiting for transfers between devices, to_chip(): lax.ppermute(value, 'prow', [(r, (r + 2 * h) % row_devices) for r in rang...  16.2 us
    ppermute x8, waiting for transfers between devices, to_next(): lax.ppermute(value, 'pcol', [(c, c + 2) for c in range(col_devices - 2)])  12.9 us
    ppermute x10, starting transfers between devices, to_neighbour(): return lax.ppermute(value, 'pcol', [(c, c ^ 1) for c in range(col_devices)])  10.1 us
    ppermute x3, starting transfers between devices, fresh(): lax.ppermute(head[0], 'pcol', [(0, 2 * h), (1, 2 * h + 1)])  7.49 us
    ppermute x5, starting transfers between devices, to_chip(): lax.ppermute(value, 'prow', [(r, (r + 2 * h) % row_devices) for r in rang...  6.92 us
  transfers between devices with their start and end apart: 34, of which 12 were waited for; matrix products, arithmetic and copies ran while one was open for 0% of the time, Pallas kernels for 30%

profile of v10, /device:TPU:0, one launch (start us, length us, event | category | flops | bytes accessed | tf_op | source)
XLA Modules:
  0.0 163.5 jit_solution(5750866323227069282)
XLA Ops:
  0.0 2.2 %shard_map.46.refs_4_.refs_1_.refs_11_ = bf16[512,512]{1,0:T(8,128)(2,1)} custom-call(bf16[2560,2,512]{2,1,0:T(2,128)(2,1)} %bitcast.5), custom_call_target="tpu_custom_call" | custom-call | flops 1100000000 | tf_op jit(solution)/shard_map/pallas_call | solution.py:37
  2.2 3.0 %collective-permute-start.1 = (bf16[512,512]{1,0:T(8,128)(2,1)}, bf16[512,512]{1,0:T(8,128)(2,1)S(1)}, u32[]{:S(2)}, u32[]{:S(2)}) collective-permute-start(bf16[512,512]{1,0:T(8,128)(2,1)} %shard_map.46.refs_4_.refs_1_.refs_11_), channel_id=1, source_target_pairs={{0,1},{1,0},{2,3},{3,2},{4,5},{5,4},{6,7},{7,6},{8,9},{9,8},{10,11... | collective-permute-start | bytes 1572872 | tf_op jit(solution)/shard_map/ppermute | solution.py:413
  5.2 3.5 %collective-permute-start = (bf16[512,512]{1,0:T(8,128)(2,1)}, bf16[512,512]{1,0:T(8,128)(2,1)S(1)}, u32[]{:S(2)}, u32[]{:S(2)}) collective-permute-start(bf16[512,512]{1,0:T(8,128)(2,1)} %shard_map.46.refs_4_.refs_1_.refs_11_), channel_id=1, source_target_pairs={{0,2},{1,3},{2,4},{3,5},{4,6},{5,7},{8,10},{9,11},{10,12},{11,13},... | collective-permute-start | bytes 1572872 | tf_op jit(solution)/shard_map/ppermute | solution.py:419
  9.0 2.5 %copy-done.1 = bf16[5,512,2,512]{3,2,1,0:T(2,128)(2,1)S(1)} copy-done((bf16[5,512,2,512]{3,2,1,0:T(2,128)(2,1)S(1)}, bf16[5,512,2,512]{3,2,1,0:T(2,128)(2,1)}, u32[]{:S(2)}) %copy-start.1) | copy-done | bytes 5242904
  11.5 1.0 copy-done.2
  12.5 7.7 %shard_map.47 = (bf16[512,512]{1,0:T(8,128)(2,1)S(1)}, bf16[512,512]{1,0:T(8,128)(2,1)S(1)}, bf16[512,512]{1,0:T(8,128)(2,1)S(1)}, bf16[256,512]{1,0:T(8,128)(2,...) custom-call(s32[4]{0:T(128)S(1)} %pad_add_fusion.refs_0_, ...), custom_call_target="tpu_custom_call" | custom-call | flops 8800000000 | tf_op jit(solution)/shard_map/pallas_call | solution.py:37
  20.9 0.8 copy-done.6
  21.7 1.0 copy-done.7
  23.3 3.5 %collective-permute-start.2 = (bf16[512,512]{1,0:T(8,128)(2,1)S(1)}, bf16[512,512]{1,0:T(8,128)(2,1)S(1)}, u32[]{:S(2)}, u32[]{:S(2)}) collective-permute-start(bf16[512,512]{1,0:T(8,128)(2,1)S(1)} %shard_map.48.refs_4_.refs_2_.refs_12_.refs_11_), channel_id=1, source_target_pairs={{0,2},{1,3},{2,4},{3,5},{4,6},{5,7},{8,10},{9,11},{10,12},{11,13},... | collective-permute-start | bytes 1572872 | tf_op jit(solution)/shard_map/ppermute | solution.py:419
  27.4 2.4 %shard_map.49 = (bf16[256,2,512]{2,1,0:T(2,128)(2,1)S(1)}, bf16[256,2,512]{2,1,0:T(2,128)(2,1)S(1)}) custom-call(s32[4]{0:T(128)S(1)} %pad_add_fusion.refs_0_, s32[2,512]{1,0:T(2,128)S(1)} %get-tuple-element.43.refs_1_, bf16[512,2,512]{2,1,0:T(2,128)(2,1)S(1)} %get-tuple-element.44.refs_2_, bf16[512,2,512]{2,1,0:T(2,128)(2,1)S(1)} %collective-permute-done.3.refs_3_, ...), custom_call_target="tpu_custom_call" | custom-call | flops 2200000000 | tf_op jit(solution)/shard_map/pallas_call | solution.py:37
  29.8 1.6 collective-permute-start.7
  31.3 6.8 %collective-permute-done.2.refs_1_ = bf16[512,512]{1,0:T(8,128)(2,1)S(1)} collective-permute-done((bf16[512,512]{1,0:T(8,128)(2,1)S(1)}, bf16[512,512]{1,0:T(8,128)(2,1)S(1)}, u32[]{:S(2)}, u32[]{:S(2)}) %collective-permute-start.2) | collective-permute-done | bytes 524320 | tf_op jit(solution)/shard_map/ppermute | solution.py:419
  38.2 2.3 %collective-permute-done.4.refs_4_.refs_2_.refs_16_.refs_15_ = bf16[512,512]{1,0:T(8,128)(2,1)S(1)} collective-permute-done((bf16[512,512]{1,0:T(8,128)(2,1)S(1)}, bf16[512,512]{1,0:T(8,128)(2,1)S(1)}, u32[]{:S(2)}, u32[]{:S(2)}) %collective-permute-start.4) | collective-permute-done | bytes 524320 | tf_op jit(solution)/shard_map/ppermute | solution.py:413
  41.1 3.5 %collective-permute-start.6 = (bf16[512,512]{1,0:T(8,128)(2,1)S(1)}, bf16[512,512]{1,0:T(8,128)(2,1)S(1)}, u32[]{:S(2)}, u32[]{:S(2)}) collective-permute-start(bf16[512,512]{1,0:T(8,128)(2,1)S(1)} %shard_map.50.refs_4_.refs_3_.refs_13_.refs_12_.refs_11_), channel_id=1, source_target_pairs={{0,2},{1,3},{2,4},{3,5},{4,6},{5,7},{8,10},{9,11},{10,12},{11,13},... | collective-permute-start | bytes 1572872 | tf_op jit(solution)/shard_map/ppermute | solution.py:419
  45.2 1.5 collective-permute-start.13
  46.7 1.1 shard_map.51
  47.8 1.8 %collective-permute-start.10 = (bf16[128,512]{1,0:T(8,128)(2,1)S(1)}, bf16[128,512]{1,0:T(8,128)(2,1)S(1)}, u32[]{:S(2)}, u32[]{:S(2)}) collective-permute-start(bf16[128,512]{1,0:T(8,128)(2,1)S(1)} %get-tuple-element.50.refs_3_.refs_1_), channel_id=1, source_target_pairs={{0,4},{1,5},{8,12},{9,13},{16,20},{17,21},{24,28},{25,29}} | collective-permute-start | bytes 393224 | tf_op jit(solution)/shard_map/ppermute | solution.py:502
  49.6 1.3 collective-permute-start.11
  50.9 6.0 %collective-permute-done.6.refs_1_ = bf16[512,512]{1,0:T(8,128)(2,1)S(1)} collective-permute-done((bf16[512,512]{1,0:T(8,128)(2,1)S(1)}, bf16[512,512]{1,0:T(8,128)(2,1)S(1)}, u32[]{:S(2)}, u32[]{:S(2)}) %collective-permute-start.6) | collective-permute-done | bytes 524320 | tf_op jit(solution)/shard_map/ppermute | solution.py:419
  56.9 4.4 %collective-permute-start.9 = (bf16[128,512]{1,0:T(8,128)(2,1)S(1)}, bf16[128,512]{1,0:T(8,128)(2,1)S(1)}, u32[]{:S(2)}, u32[]{:S(2)}) collective-permute-start(bf16[128,512]{1,0:T(8,128)(2,1)S(1)} %get-tuple-element.50.refs_3_.refs_1_), channel_id=1, source_target_pairs={{0,2},{1,3},{8,10},{9,11},{16,18},{17,19},{24,26},{25,27}} | collective-permute-start | bytes 393224 | tf_op jit(solution)/shard_map/ppermute | solution.py:502
  61.8 2.0 %collective-permute-done.9.refs_5_.refs_2_ = bf16[128,512]{1,0:T(8,128)(2,1)S(1)} collective-permute-done((bf16[128,512]{1,0:T(8,128)(2,1)S(1)}, bf16[128,512]{1,0:T(8,128)(2,1)S(1)}, u32[]{:S(2)}, u32[]{:S(2)}) %collective-permute-start.9) | collective-permute-done | bytes 131104 | tf_op jit(solution)/shard_map/ppermute | solution.py:502
  64.4 4.4 %collective-permute-start.12 = (bf16[512,512]{1,0:T(8,128)(2,1)S(1)}, bf16[512,512]{1,0:T(8,128)(2,1)S(1)}, u32[]{:S(2)}, u32[]{:S(2)}) collective-permute-start(bf16[512,512]{1,0:T(8,128)(2,1)S(1)} %shard_map.52.refs_5_.refs_4_.refs_14_.refs_13_.refs_12_.refs_11_), channel_id=1, source_target_pairs={{0,2},{1,3},{2,4},{3,5},{4,6},{5,7},{8,10},{9,11},{10,12},{11,13},... | collective-permute-start | bytes 1572872 | tf_op jit(solution)/shard_map/ppermute | solution.py:419
  70.0 1.6 collective-permute-start.14
  71.5 10.8 %collective-permute-done.14.refs_1_ = bf16[128,512]{1,0:T(8,128)(2,1)S(1)} collective-permute-done((bf16[128,512]{1,0:T(8,128)(2,1)S(1)}, bf16[128,512]{1,0:T(8,128)(2,1)S(1)}, u32[]{:S(2)}, u32[]{:S(2)}) %collective-permute-start.14) | collective-permute-done | bytes 131104 | tf_op jit(solution)/shard_map/ppermute | solution.py:413
  82.4 1.1 shard_map.55
  84.8 2.2 %collective-permute-start.19 = (bf16[512,512]{1,0:T(8,128)(2,1)S(1)}, bf16[512,512]{1,0:T(8,128)(2,1)S(1)}, u32[]{:S(2)}, u32[]{:S(2)}) collective-permute-start(bf16[512,512]{1,0:T(8,128)(2,1)S(1)} %shard_map.56.refs_5_.refs_14_.refs_13_.refs_12_.refs_11_), channel_id=1, source_target_pairs={{0,2},{1,3},{2,4},{3,5},{4,6},{5,7},{8,10},{9,11},{10,12},{11,13},... | collective-permute-start | bytes 1572872 | tf_op jit(solution)/shard_map/ppermute | solution.py:419
  87.0 0.6 shard_map.57.refs_5_.refs_1_
  87.6 1.6 collective-permute-start.16
  90.2 0.6 shard_map.58.refs_10_.refs_2_
  90.9 4.1 %shard_map.59.refs_6_.refs_8_ = bf16[2568,2,512]{2,1,0:T(2,128)(2,1)S(1)} custom-call(s32[4]{0:T(128)S(1)} %pad_add_fusion.refs_0_, s32[2,512]{1,0:T(2,128)S(1)} %get-tuple-element.56.refs_1_, s32[2,512]{1,0:T(2,128)S(1)} %get-tuple-element.39.refs_2_.refs_1_, bf16[256,2,512]{2,1,0:T(2,128)(2,1)S(1)} %get-tuple-element.57.refs_3_, ...), custom_call_target="tpu_custom_call" | custom-call | flops 110000000 | tf_op jit(solution)/shard_map/pallas_call | solution.py:37
  95.0 1.8 %collective-permute-start.17 = (bf16[512,512]{1,0:T(8,128)(2,1)S(1)}, bf16[512,512]{1,0:T(8,128)(2,1)S(1)}, u32[]{:S(2)}, u32[]{:S(2)}) collective-permute-start(bf16[512,512]{1,0:T(8,128)(2,1)S(1)} %shard_map.58.refs_10_.refs_2_), channel_id=1, source_target_pairs={{0,16},{8,24},{16,0},{24,8},{1,17},{9,25},{17,1},{25,9},{2,18},{10... | collective-permute-start | bytes 1572872 | tf_op jit(solution)/shard_map/ppermute | solution.py:416
  96.8 2.0 %shard_map.60 = (bf16[512,1024]{1,0:T(8,128)(2,1)S(1)}, bf16[512,2,512]{2,1,0:T(2,128)(2,1)S(1)}) custom-call(s32[4]{0:T(128)S(1)} %pad_add_fusion.refs_0_, bf16[2,512,512]{2,1,0:T(8,128)(2,1)S(1)} %copy-done.4, bf16[256,1024]{1,0:T(8,128)(2,1)S(1)} %get-tuple-element.54.refs_2_.refs_6_, bf16[256,1024]{1,0:T(8,128)(2,1)S(1)} %collective-permute-done.20.refs_3_.refs_7_, ...), custom_call_target="tpu_custom_call" | custom-call | flops 2200000000 | tf_op jit(solution)/shard_map/pallas_call | solution.py:37
  98.7 3.7 %collective-permute-done.16.refs_5_.refs_3_ = bf16[512,512]{1,0:T(8,128)(2,1)S(1)} collective-permute-done((bf16[512,512]{1,0:T(8,128)(2,1)S(1)}, bf16[512,512]{1,0:T(8,128)(2,1)S(1)}, u32[]{:S(2)}, u32[]{:S(2)}) %collective-permute-start.16) | collective-permute-done | bytes 524320 | tf_op jit(solution)/shard_map/ppermute | solution.py:416
  103.5 4.6 %collective-permute-done.18.refs_1_ = bf16[2,128,512]{2,1,0:T(8,128)(2,1)S(1)} collective-permute-done((bf16[2,128,512]{2,1,0:T(8,128)(2,1)S(1)}, bf16[2,128,512]{2,1,0:T(8,128)(2,1)S(1)}, u32[]{:S(2)}, u32[]{:S(2)}) %collective-permute-start.18) | collective-permute-done | bytes 262176 | tf_op jit(solution)/shard_map/ppermute | solution.py:416
  108.2 1.9 %collective-permute-start.27 = (bf16[512,512]{1,0:T(8,128)(2,1)S(1)}, bf16[512,512]{1,0:T(8,128)(2,1)S(1)}, u32[]{:S(2)}, u32[]{:S(2)}) collective-permute-start(bf16[512,512]{1,0:T(8,128)(2,1)S(1)} %shard_map.61.refs_2_.refs_14_.refs_13_.refs_12_.refs_15_), channel_id=1, source_target_pairs={{0,2},{1,3},{2,4},{3,5},{4,6},{5,7},{8,10},{9,11},{10,12},{11,13},... | collective-permute-start | bytes 1572872 | tf_op jit(solution)/shard_map/ppermute | solution.py:419
  110.7 7.9 %collective-permute-done.17.refs_4_ = bf16[512,512]{1,0:T(8,128)(2,1)S(1)} collective-permute-done((bf16[512,512]{1,0:T(8,128)(2,1)S(1)}, bf16[512,512]{1,0:T(8,128)(2,1)S(1)}, u32[]{:S(2)}, u32[]{:S(2)}) %collective-permute-start.17) | collective-permute-done | bytes 524320 | tf_op jit(solution)/shard_map/ppermute | solution.py:416
  118.5 0.6 shard_map.63.refs_10_.refs_2_
  119.3 3.5 %shard_map.64 = (bf16[512,1024]{1,0:T(8,128)(2,1)S(1)}, bf16[512,512]{1,0:T(8,128)(2,1)S(1)}, bf16[512,2,512]{2,1,0:T(2,128)(2,1)S(1)}) custom-call(s32[4]{0:T(128)S(1)} %pad_add_fusion.refs_0_, bf16[2,512,512]{2,1,0:T(8,128)(2,1)S(1)} %copy-done.4, bf16[2,512,512]{2,1,0:T(8,128)(2,1)S(1)} %copy-done, ...), custom_call_target="tpu_custom_call" | custom-call | flops 3849999872 | tf_op jit(solution)/shard_map/pallas_call | solution.py:37
  122.8 1.4 collective-permute-done.28.refs_3_.refs_18_.refs_17_.refs_20_.refs_23_
  125.3 2.2 %collective-permute-start.29 = (bf16[256,512]{1,0:T(8,128)(2,1)S(1)}, bf16[256,512]{1,0:T(8,128)(2,1)S(1)}, u32[]{:S(2)}, u32[]{:S(2)}) collective-permute-start(bf16[256,512]{1,0:T(8,128)(2,1)S(1)} %slice.4), channel_id=1, source_target_pairs={{0,2},{1,3},{2,4},{3,5},{4,6},{5,7},{8,10},{9,11},{10,12},{11,13},... | collective-permute-start | bytes 786440 | tf_op jit(solution)/shard_map/ppermute | solution.py:419
  127.6 1.8 %shard_map.66 = (bf16[2560,2,512]{2,1,0:T(2,128)(2,1)}, f32[8,128]{1,0:T(8,128)S(1)}) custom-call(s32[4]{0:T(128)S(1)} %pad_add_fusion.refs_0_, s32[2,512]{1,0:T(2,128)S(1)} %get-tuple-element.39.refs_2_.refs_1_, bf16[2,512,512]{2,1,0:T(8,128)(2,1)S(1)} %shard_map.63.refs_10_.refs_2_, bf16[2,512,512]{2,1,0:T(8,128)(2,1)S(1)} %collective-permute-done.25.refs_3_, ...), custom_call_target="tpu_custom_call" | custom-call | flops 5500000256 | tf_op jit(solution)/shard_map/pallas_call | solution.py:37
  129.4 6.2 %shard_map.67 = (bf16[2560,2,512]{2,1,0:T(2,128)(2,1)}, f32[8,128]{1,0:T(8,128)S(1)}) custom-call(s32[4]{0:T(128)S(1)} %pad_add_fusion.refs_0_, s32[2,512]{1,0:T(2,128)S(1)} %get-tuple-element.39.refs_2_.refs_1_, bf16[2,512,512]{2,1,0:T(8,128)(2,1)S(1)} %shard_map.63.refs_10_.refs_2_, ...), custom_call_target="tpu_custom_call", output_to_operand_aliasing={{0}: (19, {})} | custom-call | flops 5500000256 | tf_op jit(solution)/shard_map/pallas_call | solution.py:37
  135.6 2.4 %collective-permute-done.30.refs_3_.refs_18_.refs_21_.refs_24_ = bf16[512,512]{1,0:T(8,128)(2,1)S(1)} collective-permute-done((bf16[512,512]{1,0:T(8,128)(2,1)S(1)}, bf16[512,512]{1,0:T(8,128)(2,1)S(1)}, u32[]{:S(2)}, u32[]{:S(2)}) %collective-permute-start.30) | collective-permute-done | bytes 524320 | tf_op jit(solution)/shard_map/ppermute | solution.py:413
  138.6 2.6 %collective-permute-start.31 = (bf16[256,512]{1,0:T(8,128)(2,1)S(1)}, bf16[256,512]{1,0:T(8,128)(2,1)S(1)}, u32[]{:S(2)}, u32[]{:S(2)}) collective-permute-start(bf16[256,512]{1,0:T(8,128)(2,1)S(1)} %shard_map.68.refs_20_.refs_14_.refs_17_), channel_id=1, source_target_pairs={{0,2},{1,3},{2,4},{3,5},{4,6},{5,7},{8,10},{9,11},{10,12},{11,13},... | collective-permute-start | bytes 786440 | tf_op jit(solution)/shard_map/ppermute | solution.py:419
  141.7 6.4 %shard_map.69 = (bf16[2560,2,512]{2,1,0:T(2,128)(2,1)}, f32[8,128]{1,0:T(8,128)S(1)}) custom-call(s32[4]{0:T(128)S(1)} %pad_add_fusion.refs_0_, s32[2,512]{1,0:T(2,128)S(1)} %get-tuple-element.39.refs_2_.refs_1_, bf16[2,512,512]{2,1,0:T(8,128)(2,1)S(1)} %shard_map.63.refs_10_.refs_2_, ...), custom_call_target="tpu_custom_call", output_to_operand_aliasing={{0}: (19, {})} | custom-call | flops 5500000256 | tf_op jit(solution)/shard_map/pallas_call | solution.py:37
  148.7 1.6 collective-permute-start.33
  150.3 6.2 %shard_map.71 = (bf16[2560,2,512]{2,1,0:T(2,128)(2,1)}, f32[8,128]{1,0:T(8,128)S(1)}) custom-call(s32[4]{0:T(128)S(1)} %pad_add_fusion.refs_0_, s32[2,512]{1,0:T(2,128)S(1)} %get-tuple-element.39.refs_2_.refs_1_, bf16[2,512,512]{2,1,0:T(8,128)(2,1)S(1)} %shard_map.63.refs_10_.refs_2_, ...), custom_call_target="tpu_custom_call", output_to_operand_aliasing={{0}: (19, {})} | custom-call | flops 5500000256 | tf_op jit(solution)/shard_map/pallas_call | solution.py:37
  156.5 6.8 %shard_map.72 = (bf16[2560,2,512]{2,1,0:T(2,128)(2,1)}, f32[8,128]{1,0:T(8,128)}) custom-call(s32[4]{0:T(128)S(1)} %pad_add_fusion.refs_0_, s32[2,512]{1,0:T(2,128)S(1)} %get-tuple-element.39.refs_2_.refs_1_, bf16[2,512,512]{2,1,0:T(8,128)(2,1)S(1)} %shard_map.63.refs_10_.refs_2_, ...), custom_call_target="tpu_custom_call", output_to_operand_aliasing={{0}: (27, {})} | custom-call | flops 5500000256 | tf_op jit(solution)/shard_map/pallas_call | solution.py:37
  (66 shorter events, 12.3 us)
Async XLA Ops:
  0.0 8.8 %copy-start.5 = (s32[2,512]{1,0:T(2,128)S(1)}, s32[2,512]{1,0:T(2,128)}, u32[]{:S(2)}) copy-start(s32[2,512]{1,0:T(2,128)} %refs_1_.3) | copy-start | bytes 12292
  2.2 18.7 %collective-permute-start.1 = (bf16[512,512]{1,0:T(8,128)(2,1)}, bf16[512,512]{1,0:T(8,128)(2,1)S(1)}, u32[]{:S(2)}, u32[]{:S(2)}) collective-permute-start(bf16[512,512]{1,0:T(8,128)(2,1)} %shard_map.46.refs_4_.refs_1_.refs_11_), channel_id=1, source_target_pairs={{0,1},{1,0},{2,3},{3,2},{4,5},{5,4},{6,7},{7,6},{8,9},{9,8},{10,11... | collective-permute-start | bytes 1572872 | tf_op jit(solution)/shard_map/ppermute | solution.py:413
  5.2 15.7 %collective-permute-start = (bf16[512,512]{1,0:T(8,128)(2,1)}, bf16[512,512]{1,0:T(8,128)(2,1)S(1)}, u32[]{:S(2)}, u32[]{:S(2)}) collective-permute-start(bf16[512,512]{1,0:T(8,128)(2,1)} %shard_map.46.refs_4_.refs_1_.refs_11_), channel_id=1, source_target_pairs={{0,2},{1,3},{2,4},{3,5},{4,6},{5,7},{8,10},{9,11},{10,12},{11,13},... | collective-permute-start | bytes 1572872 | tf_op jit(solution)/shard_map/ppermute | solution.py:419
  9.0 2.5 %copy-start.1 = (bf16[5,512,2,512]{3,2,1,0:T(2,128)(2,1)S(1)}, bf16[5,512,2,512]{3,2,1,0:T(2,128)(2,1)}, u32[]{:S(2)}) copy-start(bf16[5,512,2,512]{3,2,1,0:T(2,128)(2,1)} %param.4) | copy-start | bytes 15728644
  11.5 1.0 copy-start.2
  20.3 7.1 %collective-permute-start.3 = (bf16[512,2,512]{2,1,0:T(2,128)(2,1)S(1)}, bf16[512,2,512]{2,1,0:T(2,128)(2,1)S(1)}, u32[]{:S(2)}, u32[]{:S(2)}) collective-permute-start(bf16[512,2,512]{2,1,0:T(2,128)(2,1)S(1)} %get-tuple-element.45), channel_id=1, source_target_pairs={{0,8},{8,0},{16,24},{24,16},{1,9},{9,1},{17,25},{25,17},{2,10},{10... | collective-permute-start | bytes 3145736 | tf_op jit(solution)/shard_map/ppermute | solution.py:410
  20.4 20.1 %collective-permute-start.5 = (bf16[512,2,512]{2,1,0:T(2,128)(2,1)S(1)}, bf16[512,2,512]{2,1,0:T(2,128)(2,1)S(1)}, u32[]{:S(2)}, u32[]{:S(2)}) collective-permute-start(bf16[512,2,512]{2,1,0:T(2,128)(2,1)S(1)} %get-tuple-element.47.refs_7_), channel_id=1, source_target_pairs={{0,8},{8,0},{16,24},{24,16},{1,9},{9,1},{17,25},{25,17},{2,10},{10... | collective-permute-start | bytes 3145736 | tf_op jit(solution)/shard_map/ppermute | solution.py:410
  20.9 0.8 copy-start.6
  21.7 1.0 copy-start.7
  23.3 14.9 %collective-permute-start.2 = (bf16[512,512]{1,0:T(8,128)(2,1)S(1)}, bf16[512,512]{1,0:T(8,128)(2,1)S(1)}, u32[]{:S(2)}, u32[]{:S(2)}) collective-permute-start(bf16[512,512]{1,0:T(8,128)(2,1)S(1)} %shard_map.48.refs_4_.refs_2_.refs_12_.refs_11_), channel_id=1, source_target_pairs={{0,2},{1,3},{2,4},{3,5},{4,6},{5,7},{8,10},{9,11},{10,12},{11,13},... | collective-permute-start | bytes 1572872 | tf_op jit(solution)/shard_map/ppermute | solution.py:419
  26.8 13.7 %collective-permute-start.4 = (bf16[512,512]{1,0:T(8,128)(2,1)S(1)}, bf16[512,512]{1,0:T(8,128)(2,1)S(1)}, u32[]{:S(2)}, u32[]{:S(2)}) collective-permute-start(bf16[512,512]{1,0:T(8,128)(2,1)S(1)} %shard_map.48.refs_4_.refs_2_.refs_12_.refs_11_), channel_id=1, source_target_pairs={{0,1},{1,0},{2,3},{3,2},{4,5},{5,4},{6,7},{7,6},{8,9},{9,8},{10,11... | collective-permute-start | bytes 1572872 | tf_op jit(solution)/shard_map/ppermute | solution.py:413
  29.8 16.9 %collective-permute-start.7 = (bf16[256,2,512]{2,1,0:T(2,128)(2,1)S(1)}, bf16[256,2,512]{2,1,0:T(2,128)(2,1)S(1)}, u32[]{:S(2)}, u32[]{:S(2)}) collective-permute-start(bf16[256,2,512]{2,1,0:T(2,128)(2,1)S(1)} %get-tuple-element.49.refs_2_), channel_id=1, source_target_pairs={{0,16},{8,24},{16,0},{24,8},{1,17},{9,25},{17,1},{25,9},{2,18},{10... | collective-permute-start | bytes 1572872 | tf_op jit(solution)/shard_map/ppermute | solution.py:416
  41.1 15.8 %collective-permute-start.6 = (bf16[512,512]{1,0:T(8,128)(2,1)S(1)}, bf16[512,512]{1,0:T(8,128)(2,1)S(1)}, u32[]{:S(2)}, u32[]{:S(2)}) collective-permute-start(bf16[512,512]{1,0:T(8,128)(2,1)S(1)} %shard_map.50.refs_4_.refs_3_.refs_13_.refs_12_.refs_11_), channel_id=1, source_target_pairs={{0,2},{1,3},{2,4},{3,5},{4,6},{5,7},{8,10},{9,11},{10,12},{11,13},... | collective-permute-start | bytes 1572872 | tf_op jit(solution)/shard_map/ppermute | solution.py:419
  44.6 16.7 %collective-permute-start.8 = (bf16[512,512]{1,0:T(8,128)(2,1)S(1)}, bf16[512,512]{1,0:T(8,128)(2,1)S(1)}, u32[]{:S(2)}, u32[]{:S(2)}) collective-permute-start(bf16[512,512]{1,0:T(8,128)(2,1)S(1)} %shard_map.50.refs_4_.refs_3_.refs_13_.refs_12_.refs_11_), channel_id=1, source_target_pairs={{0,1},{1,0},{2,3},{3,2},{4,5},{5,4},{6,7},{7,6},{8,9},{9,8},{10,11... | collective-permute-start | bytes 1572872 | tf_op jit(solution)/shard_map/ppermute | solution.py:413
  45.2 37.2 %collective-permute-start.13 = (bf16[256,2,512]{2,1,0:T(2,128)(2,1)S(1)}, bf16[256,2,512]{2,1,0:T(2,128)(2,1)S(1)}, u32[]{:S(2)}, u32[]{:S(2)}) collective-permute-start(bf16[256,2,512]{2,1,0:T(2,128)(2,1)S(1)} %get-tuple-element.46.refs_3_.refs_2_), channel_id=1, source_target_pairs={{0,16},{8,24},{16,0},{24,8},{1,17},{9,25},{17,1},{25,9},{2,18},{10... | collective-permute-start | bytes 1572872 | tf_op jit(solution)/shard_map/ppermute | solution.py:416
  47.8 13.5 %collective-permute-start.10 = (bf16[128,512]{1,0:T(8,128)(2,1)S(1)}, bf16[128,512]{1,0:T(8,128)(2,1)S(1)}, u32[]{:S(2)}, u32[]{:S(2)}) collective-permute-start(bf16[128,512]{1,0:T(8,128)(2,1)S(1)} %get-tuple-element.50.refs_3_.refs_1_), channel_id=1, source_target_pairs={{0,4},{1,5},{8,12},{9,13},{16,20},{17,21},{24,28},{25,29}} | collective-permute-start | bytes 393224 | tf_op jit(solution)/shard_map/ppermute | solution.py:502
  49.6 12.2 %collective-permute-start.11 = (bf16[128,512]{1,0:T(8,128)(2,1)S(1)}, bf16[128,512]{1,0:T(8,128)(2,1)S(1)}, u32[]{:S(2)}, u32[]{:S(2)}) collective-permute-start(bf16[128,512]{1,0:T(8,128)(2,1)S(1)} %get-tuple-element.50.refs_3_.refs_1_), channel_id=1, source_target_pairs={{0,6},{1,7},{8,14},{9,15},{16,22},{17,23},{24,30},{25,31}} | collective-permute-start | bytes 393224 | tf_op jit(solution)/shard_map/ppermute | solution.py:502
  56.9 6.9 %collective-permute-start.9 = (bf16[128,512]{1,0:T(8,128)(2,1)S(1)}, bf16[128,512]{1,0:T(8,128)(2,1)S(1)}, u32[]{:S(2)}, u32[]{:S(2)}) collective-permute-start(bf16[128,512]{1,0:T(8,128)(2,1)S(1)} %get-tuple-element.50.refs_3_.refs_1_), channel_id=1, source_target_pairs={{0,2},{1,3},{8,10},{9,11},{16,18},{17,19},{24,26},{25,27}} | collective-permute-start | bytes 393224 | tf_op jit(solution)/shard_map/ppermute | solution.py:502
  64.4 19.7 %collective-permute-start.12 = (bf16[512,512]{1,0:T(8,128)(2,1)S(1)}, bf16[512,512]{1,0:T(8,128)(2,1)S(1)}, u32[]{:S(2)}, u32[]{:S(2)}) collective-permute-start(bf16[512,512]{1,0:T(8,128)(2,1)S(1)} %shard_map.52.refs_5_.refs_4_.refs_14_.refs_13_.refs_12_.refs_11_), channel_id=1, source_target_pairs={{0,2},{1,3},{2,4},{3,5},{4,6},{5,7},{8,10},{9,11},{10,12},{11,13},... | collective-permute-start | bytes 1572872 | tf_op jit(solution)/shard_map/ppermute | solution.py:419
  68.8 15.4 %collective-permute-start.15 = (bf16[512,512]{1,0:T(8,128)(2,1)S(1)}, bf16[512,512]{1,0:T(8,128)(2,1)S(1)}, u32[]{:S(2)}, u32[]{:S(2)}) collective-permute-start(bf16[512,512]{1,0:T(8,128)(2,1)S(1)} %shard_map.52.refs_5_.refs_4_.refs_14_.refs_13_.refs_12_.refs_11_), channel_id=1, source_target_pairs={{0,1},{1,0},{2,3},{3,2},{4,5},{5,4},{6,7},{7,6},{8,9},{9,8},{10,11... | collective-permute-start | bytes 1572872 | tf_op jit(solution)/shard_map/ppermute | solution.py:413
  70.0 12.4 %collective-permute-start.14 = (bf16[128,512]{1,0:T(8,128)(2,1)S(1)}, bf16[128,512]{1,0:T(8,128)(2,1)S(1)}, u32[]{:S(2)}, u32[]{:S(2)}) collective-permute-start(bf16[128,512]{1,0:T(8,128)(2,1)S(1)} %shard_map.53.refs_0_.refs_2_), channel_id=1, source_target_pairs={{0,1},{1,0},{2,3},{3,2},{4,5},{5,4},{6,7},{7,6},{8,9},{9,8},{10,11... | collective-permute-start | bytes 393224 | tf_op jit(solution)/shard_map/ppermute | solution.py:413
  71.5 16.1 %collective-permute-start.22 = (bf16[256,2,512]{2,1,0:T(2,128)(2,1)S(1)}, bf16[256,2,512]{2,1,0:T(2,128)(2,1)S(1)}, u32[]{:S(2)}, u32[]{:S(2)}) collective-permute-start(bf16[256,2,512]{2,1,0:T(2,128)(2,1)S(1)} %get-tuple-element.57.refs_3_), channel_id=1, source_target_pairs={{0,8},{8,0},{16,24},{24,16},{1,9},{9,1},{17,25},{25,17},{2,10},{10... | collective-permute-start | bytes 1572872 | tf_op jit(solution)/shard_map/ppermute | solution.py:410
  82.4 6.8 %collective-permute-start.20 = (bf16[256,1024]{1,0:T(8,128)(2,1)S(1)}, bf16[256,1024]{1,0:T(8,128)(2,1)S(1)}, u32[]{:S(2)}, u32[]{:S(2)}) collective-permute-start(bf16[256,1024]{1,0:T(8,128)(2,1)S(1)} %get-tuple-element.54.refs_2_.refs_6_), channel_id=1, source_target_pairs={{0,8},{8,0},{16,24},{24,16},{1,9},{9,1},{17,25},{25,17},{2,10},{10... | collective-permute-start | bytes 1572872 | tf_op jit(solution)/shard_map/ppermute | solution.py:410
  83.5 6.2 %collective-permute-start.23 = (bf16[256,2,512]{2,1,0:T(2,128)(2,1)S(1)}, bf16[256,2,512]{2,1,0:T(2,128)(2,1)S(1)}, u32[]{:S(2)}, u32[]{:S(2)}) collective-permute-start(bf16[256,2,512]{2,1,0:T(2,128)(2,1)S(1)} %get-tuple-element.52.refs_3_.refs_5_), channel_id=1, source_target_pairs={{0,8},{8,0},{16,24},{24,16},{1,9},{9,1},{17,25},{25,17},{2,10},{10... | collective-permute-start | bytes 1572872 | tf_op jit(solution)/shard_map/ppermute | solution.py:410
  84.1 10.9 %collective-permute-start.21 = (bf16[256,1024]{1,0:T(8,128)(2,1)S(1)}, bf16[256,1024]{1,0:T(8,128)(2,1)S(1)}, u32[]{:S(2)}, u32[]{:S(2)}) collective-permute-start(bf16[256,1024]{1,0:T(8,128)(2,1)S(1)} %get-tuple-element.55.refs_4_.refs_8_), channel_id=1, source_target_pairs={{0,8},{8,0},{16,24},{24,16},{1,9},{9,1},{17,25},{25,17},{2,10},{10... | collective-permute-start | bytes 1572872 | tf_op jit(solution)/shard_map/ppermute | solution.py:410
  84.8 17.7 %collective-permute-start.19 = (bf16[512,512]{1,0:T(8,128)(2,1)S(1)}, bf16[512,512]{1,0:T(8,128)(2,1)S(1)}, u32[]{:S(2)}, u32[]{:S(2)}) collective-permute-start(bf16[512,512]{1,0:T(8,128)(2,1)S(1)} %shard_map.56.refs_5_.refs_14_.refs_13_.refs_12_.refs_11_), channel_id=1, source_target_pairs={{0,2},{1,3},{2,4},{3,5},{4,6},{5,7},{8,10},{9,11},{10,12},{11,13},... | collective-permute-start | bytes 1572872 | tf_op jit(solution)/shard_map/ppermute | solution.py:419
  87.6 14.8 %collective-permute-start.16 = (bf16[512,512]{1,0:T(8,128)(2,1)S(1)}, bf16[512,512]{1,0:T(8,128)(2,1)S(1)}, u32[]{:S(2)}, u32[]{:S(2)}) collective-permute-start(bf16[512,512]{1,0:T(8,128)(2,1)S(1)} %shard_map.57.refs_5_.refs_1_), channel_id=1, source_target_pairs={{0,16},{8,24},{16,0},{24,8},{1,17},{9,25},{17,1},{25,9},{2,18},{10... | collective-permute-start | bytes 1572872 | tf_op jit(solution)/shard_map/ppermute | solution.py:416
  89.2 13.7 %collective-permute-start.24 = (bf16[512,512]{1,0:T(8,128)(2,1)S(1)}, bf16[512,512]{1,0:T(8,128)(2,1)S(1)}, u32[]{:S(2)}, u32[]{:S(2)}) collective-permute-start(bf16[512,512]{1,0:T(8,128)(2,1)S(1)} %shard_map.56.refs_5_.refs_14_.refs_13_.refs_12_.refs_11_), channel_id=1, source_target_pairs={{0,1},{1,0},{2,3},{3,2},{4,5},{5,4},{6,7},{7,6},{8,9},{9,8},{10,11... | collective-permute-start | bytes 1572872 | tf_op jit(solution)/shard_map/ppermute | solution.py:413
  89.7 18.4 %collective-permute-start.18 = (bf16[2,128,512]{2,1,0:T(8,128)(2,1)S(1)}, bf16[2,128,512]{2,1,0:T(8,128)(2,1)S(1)}, u32[]{:S(2)}, u32[]{:S(2)}) collective-permute-start(bf16[2,128,512]{2,1,0:T(8,128)(2,1)S(1)} %shard_map.54.refs_4_.refs_0_), channel_id=1, source_target_pairs={{0,16},{8,24},{16,0},{24,8},{1,17},{9,25},{17,1},{25,9},{2,18},{10... | collective-permute-start | bytes 786440 | tf_op jit(solution)/shard_map/ppermute | solution.py:416
  90.9 5.9 %copy-start.4 = (bf16[2,512,512]{2,1,0:T(8,128)(2,1)S(1)}, bf16[2,512,512]{2,1,0:T(8,128)(2,1)}, u32[]{:S(2)}) copy-start(bf16[2,512,512]{2,1,0:T(8,128)(2,1)} %refs_1_.5) | copy-start | bytes 3145732
  95.0 23.6 %collective-permute-start.17 = (bf16[512,512]{1,0:T(8,128)(2,1)S(1)}, bf16[512,512]{1,0:T(8,128)(2,1)S(1)}, u32[]{:S(2)}, u32[]{:S(2)}) collective-permute-start(bf16[512,512]{1,0:T(8,128)(2,1)S(1)} %shard_map.58.refs_10_.refs_2_), channel_id=1, source_target_pairs={{0,16},{8,24},{16,0},{24,8},{1,17},{9,25},{17,1},{25,9},{2,18},{10... | collective-permute-start | bytes 1572872 | tf_op jit(solution)/shard_map/ppermute | solution.py:416
  98.7 20.5 %copy-start = (bf16[2,512,512]{2,1,0:T(8,128)(2,1)S(1)}, bf16[2,512,512]{2,1,0:T(8,128)(2,1)}, u32[]{:S(2)}) copy-start(bf16[2,512,512]{2,1,0:T(8,128)(2,1)} %refs_4_.9) | copy-start | bytes 3145732
  108.1 11.1 %collective-permute-start.26 = (bf16[2,2,128,512]{3,2,1,0:T(8,128)(2,1)S(1)}, bf16[2,2,128,512]{3,2,1,0:T(8,128)(2,1)S(1)}, u32[]{:S(2)}, u32[]{:S(2)}) collective-permute-start(bf16[2,2,128,512]{3,2,1,0:T(8,128)(2,1)S(1)} %shard_map.62.refs_5_.refs_4_), channel_id=1, source_target_pairs={{0,8},{8,0},{16,24},{24,16},{1,9},{9,1},{17,25},{25,17},{2,10},{10... | collective-permute-start | bytes 1572872 | tf_op jit(solution)/shard_map/ppermute | solution.py:410
  108.2 14.6 %collective-permute-start.27 = (bf16[512,512]{1,0:T(8,128)(2,1)S(1)}, bf16[512,512]{1,0:T(8,128)(2,1)S(1)}, u32[]{:S(2)}, u32[]{:S(2)}) collective-permute-start(bf16[512,512]{1,0:T(8,128)(2,1)S(1)} %shard_map.61.refs_2_.refs_14_.refs_13_.refs_12_.refs_15_), channel_id=1, source_target_pairs={{0,2},{1,3},{2,4},{3,5},{4,6},{5,7},{8,10},{9,11},{10,12},{11,13},... | collective-permute-start | bytes 1572872 | tf_op jit(solution)/shard_map/ppermute | solution.py:419
  110.1 14.1 %collective-permute-start.28 = (bf16[512,512]{1,0:T(8,128)(2,1)S(1)}, bf16[512,512]{1,0:T(8,128)(2,1)S(1)}, u32[]{:S(2)}, u32[]{:S(2)}) collective-permute-start(bf16[512,512]{1,0:T(8,128)(2,1)S(1)} %shard_map.61.refs_2_.refs_14_.refs_13_.refs_12_.refs_15_), channel_id=1, source_target_pairs={{0,1},{1,0},{2,3},{3,2},{4,5},{5,4},{6,7},{7,6},{8,9},{9,8},{10,11... | collective-permute-start | bytes 1572872 | tf_op jit(solution)/shard_map/ppermute | solution.py:413
  119.2 8.4 %collective-permute-start.25 = (bf16[2,512,512]{2,1,0:T(8,128)(2,1)S(1)}, bf16[2,512,512]{2,1,0:T(8,128)(2,1)S(1)}, u32[]{:S(2)}, u32[]{:S(2)}) collective-permute-start(bf16[2,512,512]{2,1,0:T(8,128)(2,1)S(1)} %shard_map.63.refs_10_.refs_2_), channel_id=1, source_target_pairs={{0,8},{8,0},{16,24},{24,16},{1,9},{9,1},{17,25},{25,17},{2,10},{10... | collective-permute-start | bytes 3145736 | tf_op jit(solution)/shard_map/ppermute | solution.py:410
  124.2 3.4 %copy-start.3 = (bf16[512,512]{1,0:T(8,128)(2,1)S(1)}, bf16[512,512]{1,0:T(8,128)(2,1)}, u32[]{:S(2)}) copy-start(bf16[512,512]{1,0:T(8,128)(2,1)} %shard_map.46.refs_4_.refs_1_.refs_11_) | copy-start | bytes 1572868
  124.8 13.3 %collective-permute-start.30 = (bf16[512,512]{1,0:T(8,128)(2,1)S(1)}, bf16[512,512]{1,0:T(8,128)(2,1)S(1)}, u32[]{:S(2)}, u32[]{:S(2)}) collective-permute-start(bf16[512,512]{1,0:T(8,128)(2,1)S(1)} %shard_map.65.refs_19_.refs_14_.refs_13_.refs_16_), channel_id=1, source_target_pairs={{0,1},{1,0},{2,3},{3,2},{4,5},{5,4},{6,7},{7,6},{8,9},{9,8},{10,11... | collective-permute-start | bytes 1572872 | tf_op jit(solution)/shard_map/ppermute | solution.py:413
  125.3 10.3 %collective-permute-start.29 = (bf16[256,512]{1,0:T(8,128)(2,1)S(1)}, bf16[256,512]{1,0:T(8,128)(2,1)S(1)}, u32[]{:S(2)}, u32[]{:S(2)}) collective-permute-start(bf16[256,512]{1,0:T(8,128)(2,1)S(1)} %slice.4), channel_id=1, source_target_pairs={{0,2},{1,3},{2,4},{3,5},{4,6},{5,7},{8,10},{9,11},{10,12},{11,13},... | collective-permute-start | bytes 786440 | tf_op jit(solution)/shard_map/ppermute | solution.py:419
  138.6 9.5 %collective-permute-start.31 = (bf16[256,512]{1,0:T(8,128)(2,1)S(1)}, bf16[256,512]{1,0:T(8,128)(2,1)S(1)}, u32[]{:S(2)}, u32[]{:S(2)}) collective-permute-start(bf16[256,512]{1,0:T(8,128)(2,1)S(1)} %shard_map.68.refs_20_.refs_14_.refs_17_), channel_id=1, source_target_pairs={{0,2},{1,3},{2,4},{3,5},{4,6},{5,7},{8,10},{9,11},{10,12},{11,13},... | collective-permute-start | bytes 786440 | tf_op jit(solution)/shard_map/ppermute | solution.py:419
  141.2 7.0 %collective-permute-start.32 = (bf16[256,512]{1,0:T(8,128)(2,1)S(1)}, bf16[256,512]{1,0:T(8,128)(2,1)S(1)}, u32[]{:S(2)}, u32[]{:S(2)}) collective-permute-start(bf16[256,512]{1,0:T(8,128)(2,1)S(1)} %shard_map.68.refs_20_.refs_14_.refs_17_), channel_id=1, source_target_pairs={{0,1},{1,0},{2,3},{3,2},{4,5},{5,4},{6,7},{7,6},{8,9},{9,8},{10,11... | collective-permute-start | bytes 786440 | tf_op jit(solution)/shard_map/ppermute | solution.py:413
  148.7 7.8 %collective-permute-start.33 = (bf16[256,512]{1,0:T(8,128)(2,1)S(1)}, bf16[256,512]{1,0:T(8,128)(2,1)S(1)}, u32[]{:S(2)}, u32[]{:S(2)}) collective-permute-start(bf16[256,512]{1,0:T(8,128)(2,1)S(1)} %shard_map.70.refs_20_.refs_18_), channel_id=1, source_target_pairs={{0,1},{1,0},{2,3},{3,2},{4,5},{5,4},{6,7},{7,6},{8,9},{9,8},{10,11... | collective-permute-start | bytes 786440 | tf_op jit(solution)/shard_map/ppermute | solution.py:413

commit v11 on v8

--- a/solution.py
+++ b/solution.py
@@ -349,8 +349,11 @@
         here = begin + lax.broadcasted_iota(I32, (count, nb), 0)
         pick = jnp.where(here == goal[pl.ds(core, 1), :], 1.0, 0.0)
         pick_sibling = jnp.where(here == goal[pl.ds(1 - core, 1), :], 1.0, 0.0)
-        moved = jnp.sum(pick + pick_sibling, axis=1, keepdims=True) > 0.5
         pick, pick_sibling = pick.astype(BF16), pick_sibling.astype(BF16)
+        lanes = min(nb, 128)
+        ones = jnp.ones((nb, lanes), BF16)
+        found = dot(pick, ones) + dot(pick_sibling, ones)
+        moved = jnp.concatenate([found] * (nb // lanes), axis=1) > 0.5
         arrived()
         whole = []
         for k in range(2):

time: 157 us -> 160 us (1.019)
  Pallas kernels: 58.5 us -> 61.5 us
    pallas_call x27, Pallas kernels: 58.5 us -> 61.5 us  [call(): pl.pallas_call(ordered, out_shape=tuple((shape for shape, _ in outs)), in...]
  transfers between devices with their start and end apart: 34 -> 34, of which waited for: 13 -> 13; matrix products, arithmetic and copies ran while one was open for 0% -> 0% of each run, Pallas kernels for 31% -> 32%
where the time goes in v11:
time: 160 us; the launch traced here: 159 us
  Pallas kernels  61.5 us (38%)
  starting transfers between devices  49.5 us (31%)
  waiting for transfers between devices  43.2 us (27%)
  local copies, waits for them, and re-layouts  3.76 us (2%)
    pallas_call x27, Pallas kernels, call(): pl.pallas_call(ordered, out_shape=tuple((shape for shape, _ in outs)), in...  61.5 us
    ppermute x8, starting transfers between devices, to_next(): lax.ppermute(value, 'pcol', [(c, c + 2) for c in range(col_devices - 2)])  26.2 us
    ppermute x8, waiting for transfers between devices, to_next(): lax.ppermute(value, 'pcol', [(c, c + 2) for c in range(col_devices - 2)])  19.5 us
    ppermute x10, waiting for transfers between devices, to_neighbour(): return lax.ppermute(value, 'pcol', [(c, c ^ 1) for c in range(col_devices)])  16.6 us
    ppermute x10, starting transfers between devices, to_neighbour(): return lax.ppermute(value, 'pcol', [(c, c ^ 1) for c in range(col_devices)])  10.1 us
    ppermute x5, starting transfers between devices, to_chip(): lax.ppermute(value, 'prow', [(r, (r + 2 * h) % row_devices) for r in rang...  6.92 us
    ppermute x3, waiting for transfers between devices, fresh(): lax.ppermute(head[0], 'pcol', [(0, 2 * h), (1, 2 * h + 1)])  4.82 us
    ppermute x3, starting transfers between devices, fresh(): lax.ppermute(head[0], 'pcol', [(0, 2 * h), (1, 2 * h + 1)])  4.4 us
  transfers between devices with their start and end apart: 34, of which 13 were waited for; matrix products, arithmetic and copies ran while one was open for 0% of the time, Pallas kernels for 32%

profile of v11, /device:TPU:0, one launch (start us, length us, event | category | flops | bytes accessed | tf_op | source)
XLA Modules:
  0.0 158.7 jit_solution(1092387338669499767)
XLA Ops:
  0.0 2.2 %shard_map.46.refs_4_.refs_1_.refs_11_ = bf16[512,512]{1,0:T(8,128)(2,1)} custom-call(bf16[2560,2,512]{2,1,0:T(2,128)(2,1)} %bitcast.5), custom_call_target="tpu_custom_call" | custom-call | flops 1100000000 | tf_op jit(solution)/shard_map/pallas_call | solution.py:37
  2.2 3.0 %collective-permute-start.1 = (bf16[512,512]{1,0:T(8,128)(2,1)}, bf16[512,512]{1,0:T(8,128)(2,1)S(1)}, u32[]{:S(2)}, u32[]{:S(2)}) collective-permute-start(bf16[512,512]{1,0:T(8,128)(2,1)} %shard_map.46.refs_4_.refs_1_.refs_11_), channel_id=1, source_target_pairs={{0,1},{1,0},{2,3},{3,2},{4,5},{5,4},{6,7},{7,6},{8,9},{9,8},{10,11... | collective-permute-start | bytes 1572872 | tf_op jit(solution)/shard_map/ppermute | solution.py:416
  5.2 3.5 %collective-permute-start = (bf16[512,512]{1,0:T(8,128)(2,1)}, bf16[512,512]{1,0:T(8,128)(2,1)S(1)}, u32[]{:S(2)}, u32[]{:S(2)}) collective-permute-start(bf16[512,512]{1,0:T(8,128)(2,1)} %shard_map.46.refs_4_.refs_1_.refs_11_), channel_id=1, source_target_pairs={{0,2},{1,3},{2,4},{3,5},{4,6},{5,7},{8,10},{9,11},{10,12},{11,13},... | collective-permute-start | bytes 1572872 | tf_op jit(solution)/shard_map/ppermute | solution.py:422
  9.0 2.5 %copy-done.1 = bf16[5,512,2,512]{3,2,1,0:T(2,128)(2,1)S(1)} copy-done((bf16[5,512,2,512]{3,2,1,0:T(2,128)(2,1)S(1)}, bf16[5,512,2,512]{3,2,1,0:T(2,128)(2,1)}, u32[]{:S(2)}) %copy-start.1) | copy-done | bytes 5242904
  11.5 1.0 copy-done.2
  12.5 7.7 %shard_map.47 = (bf16[512,512]{1,0:T(8,128)(2,1)S(1)}, bf16[512,512]{1,0:T(8,128)(2,1)S(1)}, bf16[512,512]{1,0:T(8,128)(2,1)S(1)}, bf16[256,512]{1,0:T(8,128)(2,...) custom-call(s32[4]{0:T(128)S(1)} %pad_add_fusion.refs_0_, ...), custom_call_target="tpu_custom_call" | custom-call | flops 8800000000 | tf_op jit(solution)/shard_map/pallas_call | solution.py:37
  21.5 3.5 %collective-permute-start.2 = (bf16[512,512]{1,0:T(8,128)(2,1)S(1)}, bf16[512,512]{1,0:T(8,128)(2,1)S(1)}, u32[]{:S(2)}, u32[]{:S(2)}) collective-permute-start(bf16[512,512]{1,0:T(8,128)(2,1)S(1)} %shard_map.48.refs_4_.refs_2_.refs_12_.refs_11_), channel_id=1, source_target_pairs={{0,2},{1,3},{2,4},{3,5},{4,6},{5,7},{8,10},{9,11},{10,12},{11,13},... | collective-permute-start | bytes 1572872 | tf_op jit(solution)/shard_map/ppermute | solution.py:422
  25.5 2.4 %shard_map.49 = (bf16[256,2,512]{2,1,0:T(2,128)(2,1)S(1)}, bf16[256,2,512]{2,1,0:T(2,128)(2,1)S(1)}) custom-call(s32[4]{0:T(128)S(1)} %pad_add_fusion.refs_0_, s32[2,512]{1,0:T(2,128)S(1)} %get-tuple-element.43.refs_1_, bf16[512,2,512]{2,1,0:T(2,128)(2,1)S(1)} %get-tuple-element.44.refs_2_, bf16[512,2,512]{2,1,0:T(2,128)(2,1)S(1)} %collective-permute-done.3.refs_3_, ...), custom_call_target="tpu_custom_call" | custom-call | flops 2200000000 | tf_op jit(solution)/shard_map/pallas_call | solution.py:37
  27.9 1.6 collective-permute-start.7
  29.5 6.8 %collective-permute-done.2.refs_1_ = bf16[512,512]{1,0:T(8,128)(2,1)S(1)} collective-permute-done((bf16[512,512]{1,0:T(8,128)(2,1)S(1)}, bf16[512,512]{1,0:T(8,128)(2,1)S(1)}, u32[]{:S(2)}, u32[]{:S(2)}) %collective-permute-start.2) | collective-permute-done | bytes 524320 | tf_op jit(solution)/shard_map/ppermute | solution.py:422
  36.3 2.3 %collective-permute-done.4.refs_4_.refs_2_.refs_16_.refs_15_ = bf16[512,512]{1,0:T(8,128)(2,1)S(1)} collective-permute-done((bf16[512,512]{1,0:T(8,128)(2,1)S(1)}, bf16[512,512]{1,0:T(8,128)(2,1)S(1)}, u32[]{:S(2)}, u32[]{:S(2)}) %collective-permute-start.4) | collective-permute-done | bytes 524320 | tf_op jit(solution)/shard_map/ppermute | solution.py:416
  39.3 3.5 %collective-permute-start.6 = (bf16[512,512]{1,0:T(8,128)(2,1)S(1)}, bf16[512,512]{1,0:T(8,128)(2,1)S(1)}, u32[]{:S(2)}, u32[]{:S(2)}) collective-permute-start(bf16[512,512]{1,0:T(8,128)(2,1)S(1)} %shard_map.50.refs_4_.refs_3_.refs_13_.refs_12_.refs_11_), channel_id=1, source_target_pairs={{0,2},{1,3},{2,4},{3,5},{4,6},{5,7},{8,10},{9,11},{10,12},{11,13},... | collective-permute-start | bytes 1572872 | tf_op jit(solution)/shard_map/ppermute | solution.py:422
  43.3 1.1 shard_map.51
  44.5 1.8 %collective-permute-start.10 = (bf16[128,512]{1,0:T(8,128)(2,1)S(1)}, bf16[128,512]{1,0:T(8,128)(2,1)S(1)}, u32[]{:S(2)}, u32[]{:S(2)}) collective-permute-start(bf16[128,512]{1,0:T(8,128)(2,1)S(1)} %get-tuple-element.50.refs_3_.refs_1_), channel_id=1, source_target_pairs={{0,4},{1,5},{8,12},{9,13},{16,20},{17,21},{24,28},{25,29}} | collective-permute-start | bytes 393224 | tf_op jit(solution)/shard_map/ppermute | solution.py:505
  46.3 1.3 collective-permute-start.11
  47.6 1.3 collective-permute-start.9
  48.9 6.2 %collective-permute-done.6.refs_1_ = bf16[512,512]{1,0:T(8,128)(2,1)S(1)} collective-permute-done((bf16[512,512]{1,0:T(8,128)(2,1)S(1)}, bf16[512,512]{1,0:T(8,128)(2,1)S(1)}, u32[]{:S(2)}, u32[]{:S(2)}) %collective-permute-start.6) | collective-permute-done | bytes 524320 | tf_op jit(solution)/shard_map/ppermute | solution.py:422
  55.1 1.5 collective-permute-start.14
  56.6 1.3 collective-permute-done.10.refs_6_.refs_3_
  57.9 2.1 %collective-permute-done.11.refs_7_.refs_4_ = bf16[128,512]{1,0:T(8,128)(2,1)S(1)} collective-permute-done((bf16[128,512]{1,0:T(8,128)(2,1)S(1)}, bf16[128,512]{1,0:T(8,128)(2,1)S(1)}, u32[]{:S(2)}, u32[]{:S(2)}) %collective-permute-start.11) | collective-permute-done | bytes 131104 | tf_op jit(solution)/shard_map/ppermute | solution.py:505
  60.0 1.4 collective-permute-done.9.refs_5_.refs_2_
  62.6 0.6 shard_map.54.refs_2_.refs_1_
  63.2 1.6 collective-permute-start.16
  65.3 4.4 %collective-permute-start.13 = (bf16[512,512]{1,0:T(8,128)(2,1)S(1)}, bf16[512,512]{1,0:T(8,128)(2,1)S(1)}, u32[]{:S(2)}, u32[]{:S(2)}) collective-permute-start(bf16[512,512]{1,0:T(8,128)(2,1)S(1)} %shard_map.52.refs_5_.refs_4_.refs_14_.refs_13_.refs_12_.refs_11_), channel_id=1, source_target_pairs={{0,2},{1,3},{2,4},{3,5},{4,6},{5,7},{8,10},{9,11},{10,12},{11,13},... | collective-permute-start | bytes 1572872 | tf_op jit(solution)/shard_map/ppermute | solution.py:422
  69.7 1.6 collective-permute-start.15
  71.3 7.9 %collective-permute-done.15.refs_1_ = bf16[128,512]{1,0:T(8,128)(2,1)S(1)} collective-permute-done((bf16[128,512]{1,0:T(8,128)(2,1)S(1)}, bf16[128,512]{1,0:T(8,128)(2,1)S(1)}, u32[]{:S(2)}, u32[]{:S(2)}) %collective-permute-start.15) | collective-permute-done | bytes 131104 | tf_op jit(solution)/shard_map/ppermute | solution.py:416
  79.7 1.1 shard_map.56
  82.0 4.4 %collective-permute-start.19 = (bf16[512,512]{1,0:T(8,128)(2,1)S(1)}, bf16[512,512]{1,0:T(8,128)(2,1)S(1)}, u32[]{:S(2)}, u32[]{:S(2)}) collective-permute-start(bf16[512,512]{1,0:T(8,128)(2,1)S(1)} %shard_map.57.refs_5_.refs_14_.refs_13_.refs_12_.refs_11_), channel_id=1, source_target_pairs={{0,2},{1,3},{2,4},{3,5},{4,6},{5,7},{8,10},{9,11},{10,12},{11,13},... | collective-permute-start | bytes 1572872 | tf_op jit(solution)/shard_map/ppermute | solution.py:422
  88.2 4.1 %shard_map.59.refs_6_.refs_8_ = bf16[2568,2,512]{2,1,0:T(2,128)(2,1)S(1)} custom-call(s32[4]{0:T(128)S(1)} %pad_add_fusion.refs_0_, s32[2,512]{1,0:T(2,128)S(1)} %get-tuple-element.56.refs_1_, s32[2,512]{1,0:T(2,128)S(1)} %get-tuple-element.39.refs_2_.refs_1_, bf16[256,2,512]{2,1,0:T(2,128)(2,1)S(1)} %get-tuple-element.57.refs_3_, ...), custom_call_target="tpu_custom_call" | custom-call | flops 110000000 | tf_op jit(solution)/shard_map/pallas_call | solution.py:37
  92.3 1.8 %collective-permute-start.17 = (bf16[512,512]{1,0:T(8,128)(2,1)S(1)}, bf16[512,512]{1,0:T(8,128)(2,1)S(1)}, u32[]{:S(2)}, u32[]{:S(2)}) collective-permute-start(bf16[512,512]{1,0:T(8,128)(2,1)S(1)} %shard_map.58.refs_10_.refs_2_), channel_id=1, source_target_pairs={{0,16},{8,24},{16,0},{24,8},{1,17},{9,25},{17,1},{25,9},{2,18},{10... | collective-permute-start | bytes 1572872 | tf_op jit(solution)/shard_map/ppermute | solution.py:419
  94.1 2.0 %shard_map.60 = (bf16[512,1024]{1,0:T(8,128)(2,1)S(1)}, bf16[512,2,512]{2,1,0:T(2,128)(2,1)S(1)}) custom-call(s32[4]{0:T(128)S(1)} %pad_add_fusion.refs_0_, bf16[2,512,512]{2,1,0:T(8,128)(2,1)S(1)} %copy-done.4, bf16[256,1024]{1,0:T(8,128)(2,1)S(1)} %get-tuple-element.54.refs_2_.refs_6_, bf16[256,1024]{1,0:T(8,128)(2,1)S(1)} %collective-permute-done.20.refs_3_.refs_7_, ...), custom_call_target="tpu_custom_call" | custom-call | flops 2200000000 | tf_op jit(solution)/shard_map/pallas_call | solution.py:37
  96.1 1.8 %collective-permute-done.19.refs_1_ = bf16[512,512]{1,0:T(8,128)(2,1)S(1)} collective-permute-done((bf16[512,512]{1,0:T(8,128)(2,1)S(1)}, bf16[512,512]{1,0:T(8,128)(2,1)S(1)}, u32[]{:S(2)}, u32[]{:S(2)}) %collective-permute-start.19) | collective-permute-done | bytes 524320 | tf_op jit(solution)/shard_map/ppermute | solution.py:422
  97.8 2.3 %collective-permute-done.24.refs_4_.refs_18_.refs_17_.refs_16_.refs_19_ = bf16[512,512]{1,0:T(8,128)(2,1)S(1)} collective-permute-done((bf16[512,512]{1,0:T(8,128)(2,1)S(1)}, bf16[512,512]{1,0:T(8,128)(2,1)S(1)}, u32[]{:S(2)}, u32[]{:S(2)}) %collective-permute-start.24) | collective-permute-done | bytes 524320 | tf_op jit(solution)/shard_map/ppermute | solution.py:416
  100.9 2.2 %collective-permute-start.27 = (bf16[512,512]{1,0:T(8,128)(2,1)S(1)}, bf16[512,512]{1,0:T(8,128)(2,1)S(1)}, u32[]{:S(2)}, u32[]{:S(2)}) collective-permute-start(bf16[512,512]{1,0:T(8,128)(2,1)S(1)} %shard_map.61.refs_2_.refs_14_.refs_13_.refs_12_.refs_15_), channel_id=1, source_target_pairs={{0,2},{1,3},{2,4},{3,5},{4,6},{5,7},{8,10},{9,11},{10,12},{11,13},... | collective-permute-start | bytes 1572872 | tf_op jit(solution)/shard_map/ppermute | solution.py:422
  103.7 2.3 %collective-permute-done.17.refs_4_ = bf16[512,512]{1,0:T(8,128)(2,1)S(1)} collective-permute-done((bf16[512,512]{1,0:T(8,128)(2,1)S(1)}, bf16[512,512]{1,0:T(8,128)(2,1)S(1)}, u32[]{:S(2)}, u32[]{:S(2)}) %collective-permute-start.17) | collective-permute-done | bytes 524320 | tf_op jit(solution)/shard_map/ppermute | solution.py:419
  106.0 0.6 shard_map.63.refs_10_.refs_2_
  106.8 3.5 %shard_map.64 = (bf16[512,1024]{1,0:T(8,128)(2,1)S(1)}, bf16[512,512]{1,0:T(8,128)(2,1)S(1)}, bf16[512,2,512]{2,1,0:T(2,128)(2,1)S(1)}) custom-call(s32[4]{0:T(128)S(1)} %pad_add_fusion.refs_0_, bf16[2,512,512]{2,1,0:T(8,128)(2,1)S(1)} %copy-done.4, bf16[2,512,512]{2,1,0:T(8,128)(2,1)S(1)} %copy-done, ...), custom_call_target="tpu_custom_call" | custom-call | flops 3849999872 | tf_op jit(solution)/shard_map/pallas_call | solution.py:37
  110.2 4.7 %collective-permute-done.27.refs_1_ = bf16[512,512]{1,0:T(8,128)(2,1)S(1)} collective-permute-done((bf16[512,512]{1,0:T(8,128)(2,1)S(1)}, bf16[512,512]{1,0:T(8,128)(2,1)S(1)}, u32[]{:S(2)}, u32[]{:S(2)}) %collective-permute-start.27) | collective-permute-done | bytes 524320 | tf_op jit(solution)/shard_map/ppermute | solution.py:422
  114.9 2.3 %collective-permute-done.28.refs_3_.refs_18_.refs_17_.refs_20_.refs_23_ = bf16[512,512]{1,0:T(8,128)(2,1)S(1)} collective-permute-done((bf16[512,512]{1,0:T(8,128)(2,1)S(1)}, bf16[512,512]{1,0:T(8,128)(2,1)S(1)}, u32[]{:S(2)}, u32[]{:S(2)}) %collective-permute-start.28) | collective-permute-done | bytes 524320 | tf_op jit(solution)/shard_map/ppermute | solution.py:416
  118.4 2.2 %collective-permute-start.29 = (bf16[256,512]{1,0:T(8,128)(2,1)S(1)}, bf16[256,512]{1,0:T(8,128)(2,1)S(1)}, u32[]{:S(2)}, u32[]{:S(2)}) collective-permute-start(bf16[256,512]{1,0:T(8,128)(2,1)S(1)} %slice.4), channel_id=1, source_target_pairs={{0,2},{1,3},{2,4},{3,5},{4,6},{5,7},{8,10},{9,11},{10,12},{11,13},... | collective-permute-start | bytes 786440 | tf_op jit(solution)/shard_map/ppermute | solution.py:422
  120.6 1.8 %shard_map.66 = (bf16[2560,2,512]{2,1,0:T(2,128)(2,1)}, f32[8,128]{1,0:T(8,128)S(1)}) custom-call(s32[4]{0:T(128)S(1)} %pad_add_fusion.refs_0_, s32[2,512]{1,0:T(2,128)S(1)} %get-tuple-element.39.refs_2_.refs_1_, bf16[2,512,512]{2,1,0:T(8,128)(2,1)S(1)} %shard_map.63.refs_10_.refs_2_, bf16[2,512,512]{2,1,0:T(8,128)(2,1)S(1)} %collective-permute-done.25.refs_3_, ...), custom_call_target="tpu_custom_call" | custom-call | flops 5500000256 | tf_op jit(solution)/shard_map/pallas_call | solution.py:37
  122.4 6.9 %shard_map.67 = (bf16[2560,2,512]{2,1,0:T(2,128)(2,1)}, f32[8,128]{1,0:T(8,128)S(1)}) custom-call(s32[4]{0:T(128)S(1)} %pad_add_fusion.refs_0_, s32[2,512]{1,0:T(2,128)S(1)} %get-tuple-element.39.refs_2_.refs_1_, bf16[2,512,512]{2,1,0:T(8,128)(2,1)S(1)} %shard_map.63.refs_10_.refs_2_, ...), custom_call_target="tpu_custom_call", output_to_operand_aliasing={{0}: (19, {})} | custom-call | flops 5500000256 | tf_op jit(solution)/shard_map/pallas_call | solution.py:37
  129.3 1.8 %collective-permute-done.30.refs_3_.refs_18_.refs_21_.refs_24_ = bf16[512,512]{1,0:T(8,128)(2,1)S(1)} collective-permute-done((bf16[512,512]{1,0:T(8,128)(2,1)S(1)}, bf16[512,512]{1,0:T(8,128)(2,1)S(1)}, u32[]{:S(2)}, u32[]{:S(2)}) %collective-permute-start.30) | collective-permute-done | bytes 524320 | tf_op jit(solution)/shard_map/ppermute | solution.py:416
  131.6 2.5 %collective-permute-start.31 = (bf16[256,512]{1,0:T(8,128)(2,1)S(1)}, bf16[256,512]{1,0:T(8,128)(2,1)S(1)}, u32[]{:S(2)}, u32[]{:S(2)}) collective-permute-start(bf16[256,512]{1,0:T(8,128)(2,1)S(1)} %shard_map.68.refs_20_.refs_14_.refs_17_), channel_id=1, source_target_pairs={{0,2},{1,3},{2,4},{3,5},{4,6},{5,7},{8,10},{9,11},{10,12},{11,13},... | collective-permute-start | bytes 786440 | tf_op jit(solution)/shard_map/ppermute | solution.py:422
  134.7 7.1 %shard_map.69 = (bf16[2560,2,512]{2,1,0:T(2,128)(2,1)}, f32[8,128]{1,0:T(8,128)S(1)}) custom-call(s32[4]{0:T(128)S(1)} %pad_add_fusion.refs_0_, s32[2,512]{1,0:T(2,128)S(1)} %get-tuple-element.39.refs_2_.refs_1_, bf16[2,512,512]{2,1,0:T(8,128)(2,1)S(1)} %shard_map.63.refs_10_.refs_2_, ...), custom_call_target="tpu_custom_call", output_to_operand_aliasing={{0}: (19, {})} | custom-call | flops 5500000256 | tf_op jit(solution)/shard_map/pallas_call | solution.py:37
  142.3 1.6 collective-permute-start.33
  143.9 6.9 %shard_map.71 = (bf16[2560,2,512]{2,1,0:T(2,128)(2,1)}, f32[8,128]{1,0:T(8,128)S(1)}) custom-call(s32[4]{0:T(128)S(1)} %pad_add_fusion.refs_0_, s32[2,512]{1,0:T(2,128)S(1)} %get-tuple-element.39.refs_2_.refs_1_, bf16[2,512,512]{2,1,0:T(8,128)(2,1)S(1)} %shard_map.63.refs_10_.refs_2_, ...), custom_call_target="tpu_custom_call", output_to_operand_aliasing={{0}: (19, {})} | custom-call | flops 5500000256 | tf_op jit(solution)/shard_map/pallas_call | solution.py:37
  150.8 7.8 %shard_map.72 = (bf16[2560,2,512]{2,1,0:T(2,128)(2,1)}, f32[8,128]{1,0:T(8,128)}) custom-call(s32[4]{0:T(128)S(1)} %pad_add_fusion.refs_0_, s32[2,512]{1,0:T(2,128)S(1)} %get-tuple-element.39.refs_2_.refs_1_, bf16[2,512,512]{2,1,0:T(8,128)(2,1)S(1)} %shard_map.63.refs_10_.refs_2_, ...), custom_call_target="tpu_custom_call", output_to_operand_aliasing={{0}: (27, {})} | custom-call | flops 5500000256 | tf_op jit(solution)/shard_map/pallas_call | solution.py:37
  (62 shorter events, 12.5 us)
Async XLA Ops:
  0.0 8.8 %copy-start.5 = (s32[2,512]{1,0:T(2,128)S(1)}, s32[2,512]{1,0:T(2,128)}, u32[]{:S(2)}) copy-start(s32[2,512]{1,0:T(2,128)} %refs_1_.3) | copy-start | bytes 12292
  2.2 18.7 %collective-permute-start.1 = (bf16[512,512]{1,0:T(8,128)(2,1)}, bf16[512,512]{1,0:T(8,128)(2,1)S(1)}, u32[]{:S(2)}, u32[]{:S(2)}) collective-permute-start(bf16[512,512]{1,0:T(8,128)(2,1)} %shard_map.46.refs_4_.refs_1_.refs_11_), channel_id=1, source_target_pairs={{0,1},{1,0},{2,3},{3,2},{4,5},{5,4},{6,7},{7,6},{8,9},{9,8},{10,11... | collective-permute-start | bytes 1572872 | tf_op jit(solution)/shard_map/ppermute | solution.py:416
  5.2 15.7 %collective-permute-start = (bf16[512,512]{1,0:T(8,128)(2,1)}, bf16[512,512]{1,0:T(8,128)(2,1)S(1)}, u32[]{:S(2)}, u32[]{:S(2)}) collective-permute-start(bf16[512,512]{1,0:T(8,128)(2,1)} %shard_map.46.refs_4_.refs_1_.refs_11_), channel_id=1, source_target_pairs={{0,2},{1,3},{2,4},{3,5},{4,6},{5,7},{8,10},{9,11},{10,12},{11,13},... | collective-permute-start | bytes 1572872 | tf_op jit(solution)/shard_map/ppermute | solution.py:422
  9.0 2.5 %copy-start.1 = (bf16[5,512,2,512]{3,2,1,0:T(2,128)(2,1)S(1)}, bf16[5,512,2,512]{3,2,1,0:T(2,128)(2,1)}, u32[]{:S(2)}) copy-start(bf16[5,512,2,512]{3,2,1,0:T(2,128)(2,1)} %param.4) | copy-start | bytes 15728644
  11.5 1.0 copy-start.2
  20.3 5.2 %collective-permute-start.3 = (bf16[512,2,512]{2,1,0:T(2,128)(2,1)S(1)}, bf16[512,2,512]{2,1,0:T(2,128)(2,1)S(1)}, u32[]{:S(2)}, u32[]{:S(2)}) collective-permute-start(bf16[512,2,512]{2,1,0:T(2,128)(2,1)S(1)} %get-tuple-element.45), channel_id=1, source_target_pairs={{0,8},{8,0},{16,24},{24,16},{1,9},{9,1},{17,25},{25,17},{2,10},{10... | collective-permute-start | bytes 3145736 | tf_op jit(solution)/shard_map/ppermute | solution.py:413
  20.4 18.3 %collective-permute-start.5 = (bf16[512,2,512]{2,1,0:T(2,128)(2,1)S(1)}, bf16[512,2,512]{2,1,0:T(2,128)(2,1)S(1)}, u32[]{:S(2)}, u32[]{:S(2)}) collective-permute-start(bf16[512,2,512]{2,1,0:T(2,128)(2,1)S(1)} %get-tuple-element.47.refs_7_), channel_id=1, source_target_pairs={{0,8},{8,0},{16,24},{24,16},{1,9},{9,1},{17,25},{25,17},{2,10},{10... | collective-permute-start | bytes 3145736 | tf_op jit(solution)/shard_map/ppermute | solution.py:413
  21.5 14.9 %collective-permute-start.2 = (bf16[512,512]{1,0:T(8,128)(2,1)S(1)}, bf16[512,512]{1,0:T(8,128)(2,1)S(1)}, u32[]{:S(2)}, u32[]{:S(2)}) collective-permute-start(bf16[512,512]{1,0:T(8,128)(2,1)S(1)} %shard_map.48.refs_4_.refs_2_.refs_12_.refs_11_), channel_id=1, source_target_pairs={{0,2},{1,3},{2,4},{3,5},{4,6},{5,7},{8,10},{9,11},{10,12},{11,13},... | collective-permute-start | bytes 1572872 | tf_op jit(solution)/shard_map/ppermute | solution.py:422
  25.0 13.7 %collective-permute-start.4 = (bf16[512,512]{1,0:T(8,128)(2,1)S(1)}, bf16[512,512]{1,0:T(8,128)(2,1)S(1)}, u32[]{:S(2)}, u32[]{:S(2)}) collective-permute-start(bf16[512,512]{1,0:T(8,128)(2,1)S(1)} %shard_map.48.refs_4_.refs_2_.refs_12_.refs_11_), channel_id=1, source_target_pairs={{0,1},{1,0},{2,3},{3,2},{4,5},{5,4},{6,7},{7,6},{8,9},{9,8},{10,11... | collective-permute-start | bytes 1572872 | tf_op jit(solution)/shard_map/ppermute | solution.py:416
  27.9 15.4 %collective-permute-start.7 = (bf16[256,2,512]{2,1,0:T(2,128)(2,1)S(1)}, bf16[256,2,512]{2,1,0:T(2,128)(2,1)S(1)}, u32[]{:S(2)}, u32[]{:S(2)}) collective-permute-start(bf16[256,2,512]{2,1,0:T(2,128)(2,1)S(1)} %get-tuple-element.49.refs_2_), channel_id=1, source_target_pairs={{0,16},{8,24},{16,0},{24,8},{1,17},{9,25},{17,1},{25,9},{2,18},{10... | collective-permute-start | bytes 1572872 | tf_op jit(solution)/shard_map/ppermute | solution.py:419
  39.3 15.8 %collective-permute-start.6 = (bf16[512,512]{1,0:T(8,128)(2,1)S(1)}, bf16[512,512]{1,0:T(8,128)(2,1)S(1)}, u32[]{:S(2)}, u32[]{:S(2)}) collective-permute-start(bf16[512,512]{1,0:T(8,128)(2,1)S(1)} %shard_map.50.refs_4_.refs_3_.refs_13_.refs_12_.refs_11_), channel_id=1, source_target_pairs={{0,2},{1,3},{2,4},{3,5},{4,6},{5,7},{8,10},{9,11},{10,12},{11,13},... | collective-permute-start | bytes 1572872 | tf_op jit(solution)/shard_map/ppermute | solution.py:422
  42.7 13.8 %collective-permute-start.8 = (bf16[512,512]{1,0:T(8,128)(2,1)S(1)}, bf16[512,512]{1,0:T(8,128)(2,1)S(1)}, u32[]{:S(2)}, u32[]{:S(2)}) collective-permute-start(bf16[512,512]{1,0:T(8,128)(2,1)S(1)} %shard_map.50.refs_4_.refs_3_.refs_13_.refs_12_.refs_11_), channel_id=1, source_target_pairs={{0,1},{1,0},{2,3},{3,2},{4,5},{5,4},{6,7},{7,6},{8,9},{9,8},{10,11... | collective-permute-start | bytes 1572872 | tf_op jit(solution)/shard_map/ppermute | solution.py:416
  44.5 13.4 %collective-permute-start.10 = (bf16[128,512]{1,0:T(8,128)(2,1)S(1)}, bf16[128,512]{1,0:T(8,128)(2,1)S(1)}, u32[]{:S(2)}, u32[]{:S(2)}) collective-permute-start(bf16[128,512]{1,0:T(8,128)(2,1)S(1)} %get-tuple-element.50.refs_3_.refs_1_), channel_id=1, source_target_pairs={{0,4},{1,5},{8,12},{9,13},{16,20},{17,21},{24,28},{25,29}} | collective-permute-start | bytes 393224 | tf_op jit(solution)/shard_map/ppermute | solution.py:505
  46.3 13.7 %collective-permute-start.11 = (bf16[128,512]{1,0:T(8,128)(2,1)S(1)}, bf16[128,512]{1,0:T(8,128)(2,1)S(1)}, u32[]{:S(2)}, u32[]{:S(2)}) collective-permute-start(bf16[128,512]{1,0:T(8,128)(2,1)S(1)} %get-tuple-element.50.refs_3_.refs_1_), channel_id=1, source_target_pairs={{0,6},{1,7},{8,14},{9,15},{16,22},{17,23},{24,30},{25,31}} | collective-permute-start | bytes 393224 | tf_op jit(solution)/shard_map/ppermute | solution.py:505
  47.6 13.8 %collective-permute-start.9 = (bf16[128,512]{1,0:T(8,128)(2,1)S(1)}, bf16[128,512]{1,0:T(8,128)(2,1)S(1)}, u32[]{:S(2)}, u32[]{:S(2)}) collective-permute-start(bf16[128,512]{1,0:T(8,128)(2,1)S(1)} %get-tuple-element.50.refs_3_.refs_1_), channel_id=1, source_target_pairs={{0,2},{1,3},{8,10},{9,11},{16,18},{17,19},{24,26},{25,27}} | collective-permute-start | bytes 393224 | tf_op jit(solution)/shard_map/ppermute | solution.py:505
  55.1 24.1 %collective-permute-start.14 = (bf16[256,2,512]{2,1,0:T(2,128)(2,1)S(1)}, bf16[256,2,512]{2,1,0:T(2,128)(2,1)S(1)}, u32[]{:S(2)}, u32[]{:S(2)}) collective-permute-start(bf16[256,2,512]{2,1,0:T(2,128)(2,1)S(1)} %get-tuple-element.46.refs_3_.refs_2_), channel_id=1, source_target_pairs={{0,16},{8,24},{16,0},{24,8},{1,17},{9,25},{17,1},{25,9},{2,18},{10... | collective-permute-start | bytes 1572872 | tf_op jit(solution)/shard_map/ppermute | solution.py:419
  63.2 17.6 %collective-permute-start.16 = (bf16[512,512]{1,0:T(8,128)(2,1)S(1)}, bf16[512,512]{1,0:T(8,128)(2,1)S(1)}, u32[]{:S(2)}, u32[]{:S(2)}) collective-permute-start(bf16[512,512]{1,0:T(8,128)(2,1)S(1)} %shard_map.54.refs_2_.refs_1_), channel_id=1, source_target_pairs={{0,16},{8,24},{16,0},{24,8},{1,17},{9,25},{17,1},{25,9},{2,18},{10... | collective-permute-start | bytes 1572872 | tf_op jit(solution)/shard_map/ppermute | solution.py:419
  64.8 16.2 %collective-permute-start.12 = (bf16[512,512]{1,0:T(8,128)(2,1)S(1)}, bf16[512,512]{1,0:T(8,128)(2,1)S(1)}, u32[]{:S(2)}, u32[]{:S(2)}) collective-permute-start(bf16[512,512]{1,0:T(8,128)(2,1)S(1)} %shard_map.52.refs_5_.refs_4_.refs_14_.refs_13_.refs_12_.refs_11_), channel_id=1, source_target_pairs={{0,1},{1,0},{2,3},{3,2},{4,5},{5,4},{6,7},{7,6},{8,9},{9,8},{10,11... | collective-permute-start | bytes 1572872 | tf_op jit(solution)/shard_map/ppermute | solution.py:416
  65.3 16.2 %collective-permute-start.13 = (bf16[512,512]{1,0:T(8,128)(2,1)S(1)}, bf16[512,512]{1,0:T(8,128)(2,1)S(1)}, u32[]{:S(2)}, u32[]{:S(2)}) collective-permute-start(bf16[512,512]{1,0:T(8,128)(2,1)S(1)} %shard_map.52.refs_5_.refs_4_.refs_14_.refs_13_.refs_12_.refs_11_), channel_id=1, source_target_pairs={{0,2},{1,3},{2,4},{3,5},{4,6},{5,7},{8,10},{9,11},{10,12},{11,13},... | collective-permute-start | bytes 1572872 | tf_op jit(solution)/shard_map/ppermute | solution.py:422
  69.7 9.4 %collective-permute-start.15 = (bf16[128,512]{1,0:T(8,128)(2,1)S(1)}, bf16[128,512]{1,0:T(8,128)(2,1)S(1)}, u32[]{:S(2)}, u32[]{:S(2)}) collective-permute-start(bf16[128,512]{1,0:T(8,128)(2,1)S(1)} %shard_map.53.refs_5_.refs_0_), channel_id=1, source_target_pairs={{0,1},{1,0},{2,3},{3,2},{4,5},{5,4},{6,7},{7,6},{8,9},{9,8},{10,11... | collective-permute-start | bytes 393224 | tf_op jit(solution)/shard_map/ppermute | solution.py:416
  79.1 7.3 %collective-permute-start.22 = (bf16[256,2,512]{2,1,0:T(2,128)(2,1)S(1)}, bf16[256,2,512]{2,1,0:T(2,128)(2,1)S(1)}, u32[]{:S(2)}, u32[]{:S(2)}) collective-permute-start(bf16[256,2,512]{2,1,0:T(2,128)(2,1)S(1)} %get-tuple-element.57.refs_3_), channel_id=1, source_target_pairs={{0,8},{8,0},{16,24},{24,16},{1,9},{9,1},{17,25},{25,17},{2,10},{10... | collective-permute-start | bytes 1572872 | tf_op jit(solution)/shard_map/ppermute | solution.py:413
  79.2 13.1 %collective-permute-start.20 = (bf16[256,1024]{1,0:T(8,128)(2,1)S(1)}, bf16[256,1024]{1,0:T(8,128)(2,1)S(1)}, u32[]{:S(2)}, u32[]{:S(2)}) collective-permute-start(bf16[256,1024]{1,0:T(8,128)(2,1)S(1)} %get-tuple-element.54.refs_2_.refs_6_), channel_id=1, source_target_pairs={{0,8},{8,0},{16,24},{24,16},{1,9},{9,1},{17,25},{25,17},{2,10},{10... | collective-permute-start | bytes 1572872 | tf_op jit(solution)/shard_map/ppermute | solution.py:413
  80.9 6.2 %collective-permute-start.23 = (bf16[256,2,512]{2,1,0:T(2,128)(2,1)S(1)}, bf16[256,2,512]{2,1,0:T(2,128)(2,1)S(1)}, u32[]{:S(2)}, u32[]{:S(2)}) collective-permute-start(bf16[256,2,512]{2,1,0:T(2,128)(2,1)S(1)} %get-tuple-element.52.refs_3_.refs_5_), channel_id=1, source_target_pairs={{0,8},{8,0},{16,24},{24,16},{1,9},{9,1},{17,25},{25,17},{2,10},{10... | collective-permute-start | bytes 1572872 | tf_op jit(solution)/shard_map/ppermute | solution.py:413
  80.9 13.2 %collective-permute-start.21 = (bf16[256,1024]{1,0:T(8,128)(2,1)S(1)}, bf16[256,1024]{1,0:T(8,128)(2,1)S(1)}, u32[]{:S(2)}, u32[]{:S(2)}) collective-permute-start(bf16[256,1024]{1,0:T(8,128)(2,1)S(1)} %get-tuple-element.55.refs_4_.refs_8_), channel_id=1, source_target_pairs={{0,8},{8,0},{16,24},{24,16},{1,9},{9,1},{17,25},{25,17},{2,10},{10... | collective-permute-start | bytes 1572872 | tf_op jit(solution)/shard_map/ppermute | solution.py:413
  82.0 15.8 %collective-permute-start.19 = (bf16[512,512]{1,0:T(8,128)(2,1)S(1)}, bf16[512,512]{1,0:T(8,128)(2,1)S(1)}, u32[]{:S(2)}, u32[]{:S(2)}) collective-permute-start(bf16[512,512]{1,0:T(8,128)(2,1)S(1)} %shard_map.57.refs_5_.refs_14_.refs_13_.refs_12_.refs_11_), channel_id=1, source_target_pairs={{0,2},{1,3},{2,4},{3,5},{4,6},{5,7},{8,10},{9,11},{10,12},{11,13},... | collective-permute-start | bytes 1572872 | tf_op jit(solution)/shard_map/ppermute | solution.py:422
  86.5 13.7 %collective-permute-start.24 = (bf16[512,512]{1,0:T(8,128)(2,1)S(1)}, bf16[512,512]{1,0:T(8,128)(2,1)S(1)}, u32[]{:S(2)}, u32[]{:S(2)}) collective-permute-start(bf16[512,512]{1,0:T(8,128)(2,1)S(1)} %shard_map.57.refs_5_.refs_14_.refs_13_.refs_12_.refs_11_), channel_id=1, source_target_pairs={{0,1},{1,0},{2,3},{3,2},{4,5},{5,4},{6,7},{7,6},{8,9},{9,8},{10,11... | collective-permute-start | bytes 1572872 | tf_op jit(solution)/shard_map/ppermute | solution.py:416
  87.0 13.7 %collective-permute-start.18 = (bf16[2,128,512]{2,1,0:T(8,128)(2,1)S(1)}, bf16[2,128,512]{2,1,0:T(8,128)(2,1)S(1)}, u32[]{:S(2)}, u32[]{:S(2)}) collective-permute-start(bf16[2,128,512]{2,1,0:T(8,128)(2,1)S(1)} %shard_map.55.refs_4_.refs_0_), channel_id=1, source_target_pairs={{0,16},{8,24},{16,0},{24,8},{1,17},{9,25},{17,1},{25,9},{2,18},{10... | collective-permute-start | bytes 786440 | tf_op jit(solution)/shard_map/ppermute | solution.py:419
  88.2 5.9 %copy-start.4 = (bf16[2,512,512]{2,1,0:T(8,128)(2,1)S(1)}, bf16[2,512,512]{2,1,0:T(8,128)(2,1)}, u32[]{:S(2)}) copy-start(bf16[2,512,512]{2,1,0:T(8,128)(2,1)} %refs_1_.5) | copy-start | bytes 3145732
  92.3 13.7 %collective-permute-start.17 = (bf16[512,512]{1,0:T(8,128)(2,1)S(1)}, bf16[512,512]{1,0:T(8,128)(2,1)S(1)}, u32[]{:S(2)}, u32[]{:S(2)}) collective-permute-start(bf16[512,512]{1,0:T(8,128)(2,1)S(1)} %shard_map.58.refs_10_.refs_2_), channel_id=1, source_target_pairs={{0,16},{8,24},{16,0},{24,8},{1,17},{9,25},{17,1},{25,9},{2,18},{10... | collective-permute-start | bytes 1572872 | tf_op jit(solution)/shard_map/ppermute | solution.py:419
  96.1 10.7 %copy-start = (bf16[2,512,512]{2,1,0:T(8,128)(2,1)S(1)}, bf16[2,512,512]{2,1,0:T(8,128)(2,1)}, u32[]{:S(2)}) copy-start(bf16[2,512,512]{2,1,0:T(8,128)(2,1)} %refs_4_.9) | copy-start | bytes 3145732
  100.8 5.9 %collective-permute-start.26 = (bf16[2,2,128,512]{3,2,1,0:T(8,128)(2,1)S(1)}, bf16[2,2,128,512]{3,2,1,0:T(8,128)(2,1)S(1)}, u32[]{:S(2)}, u32[]{:S(2)}) collective-permute-start(bf16[2,2,128,512]{3,2,1,0:T(8,128)(2,1)S(1)} %shard_map.62.refs_5_.refs_4_), channel_id=1, source_target_pairs={{0,8},{8,0},{16,24},{24,16},{1,9},{9,1},{17,25},{25,17},{2,10},{10... | collective-permute-start | bytes 1572872 | tf_op jit(solution)/shard_map/ppermute | solution.py:413
  100.9 14.0 %collective-permute-start.27 = (bf16[512,512]{1,0:T(8,128)(2,1)S(1)}, bf16[512,512]{1,0:T(8,128)(2,1)S(1)}, u32[]{:S(2)}, u32[]{:S(2)}) collective-permute-start(bf16[512,512]{1,0:T(8,128)(2,1)S(1)} %shard_map.61.refs_2_.refs_14_.refs_13_.refs_12_.refs_15_), channel_id=1, source_target_pairs={{0,2},{1,3},{2,4},{3,5},{4,6},{5,7},{8,10},{9,11},{10,12},{11,13},... | collective-permute-start | bytes 1572872 | tf_op jit(solution)/shard_map/ppermute | solution.py:422
  103.1 14.1 %collective-permute-start.28 = (bf16[512,512]{1,0:T(8,128)(2,1)S(1)}, bf16[512,512]{1,0:T(8,128)(2,1)S(1)}, u32[]{:S(2)}, u32[]{:S(2)}) collective-permute-start(bf16[512,512]{1,0:T(8,128)(2,1)S(1)} %shard_map.61.refs_2_.refs_14_.refs_13_.refs_12_.refs_15_), channel_id=1, source_target_pairs={{0,1},{1,0},{2,3},{3,2},{4,5},{5,4},{6,7},{7,6},{8,9},{9,8},{10,11... | collective-permute-start | bytes 1572872 | tf_op jit(solution)/shard_map/ppermute | solution.py:416
  106.7 13.9 %collective-permute-start.25 = (bf16[2,512,512]{2,1,0:T(8,128)(2,1)S(1)}, bf16[2,512,512]{2,1,0:T(8,128)(2,1)S(1)}, u32[]{:S(2)}, u32[]{:S(2)}) collective-permute-start(bf16[2,512,512]{2,1,0:T(8,128)(2,1)S(1)} %shard_map.63.refs_10_.refs_2_), channel_id=1, source_target_pairs={{0,8},{8,0},{16,24},{24,16},{1,9},{9,1},{17,25},{25,17},{2,10},{10... | collective-permute-start | bytes 3145736 | tf_op jit(solution)/shard_map/ppermute | solution.py:413
  117.2 3.4 %copy-start.3 = (bf16[512,512]{1,0:T(8,128)(2,1)S(1)}, bf16[512,512]{1,0:T(8,128)(2,1)}, u32[]{:S(2)}) copy-start(bf16[512,512]{1,0:T(8,128)(2,1)} %shard_map.46.refs_4_.refs_1_.refs_11_) | copy-start | bytes 1572868
  117.8 13.3 %collective-permute-start.30 = (bf16[512,512]{1,0:T(8,128)(2,1)S(1)}, bf16[512,512]{1,0:T(8,128)(2,1)S(1)}, u32[]{:S(2)}, u32[]{:S(2)}) collective-permute-start(bf16[512,512]{1,0:T(8,128)(2,1)S(1)} %shard_map.65.refs_19_.refs_14_.refs_13_.refs_16_), channel_id=1, source_target_pairs={{0,1},{1,0},{2,3},{3,2},{4,5},{5,4},{6,7},{7,6},{8,9},{9,8},{10,11... | collective-permute-start | bytes 1572872 | tf_op jit(solution)/shard_map/ppermute | solution.py:416
  118.4 10.9 %collective-permute-start.29 = (bf16[256,512]{1,0:T(8,128)(2,1)S(1)}, bf16[256,512]{1,0:T(8,128)(2,1)S(1)}, u32[]{:S(2)}, u32[]{:S(2)}) collective-permute-start(bf16[256,512]{1,0:T(8,128)(2,1)S(1)} %slice.4), channel_id=1, source_target_pairs={{0,2},{1,3},{2,4},{3,5},{4,6},{5,7},{8,10},{9,11},{10,12},{11,13},... | collective-permute-start | bytes 786440 | tf_op jit(solution)/shard_map/ppermute | solution.py:422
  131.6 10.1 %collective-permute-start.31 = (bf16[256,512]{1,0:T(8,128)(2,1)S(1)}, bf16[256,512]{1,0:T(8,128)(2,1)S(1)}, u32[]{:S(2)}, u32[]{:S(2)}) collective-permute-start(bf16[256,512]{1,0:T(8,128)(2,1)S(1)} %shard_map.68.refs_20_.refs_14_.refs_17_), channel_id=1, source_target_pairs={{0,2},{1,3},{2,4},{3,5},{4,6},{5,7},{8,10},{9,11},{10,12},{11,13},... | collective-permute-start | bytes 786440 | tf_op jit(solution)/shard_map/ppermute | solution.py:422
  134.1 7.7 %collective-permute-start.32 = (bf16[256,512]{1,0:T(8,128)(2,1)S(1)}, bf16[256,512]{1,0:T(8,128)(2,1)S(1)}, u32[]{:S(2)}, u32[]{:S(2)}) collective-permute-start(bf16[256,512]{1,0:T(8,128)(2,1)S(1)} %shard_map.68.refs_20_.refs_14_.refs_17_), channel_id=1, source_target_pairs={{0,1},{1,0},{2,3},{3,2},{4,5},{5,4},{6,7},{7,6},{8,9},{9,8},{10,11... | collective-permute-start | bytes 786440 | tf_op jit(solution)/shard_map/ppermute | solution.py:416
  142.3 8.4 %collective-permute-start.33 = (bf16[256,512]{1,0:T(8,128)(2,1)S(1)}, bf16[256,512]{1,0:T(8,128)(2,1)S(1)}, u32[]{:S(2)}, u32[]{:S(2)}) collective-permute-start(bf16[256,512]{1,0:T(8,128)(2,1)S(1)} %shard_map.70.refs_20_.refs_18_), channel_id=1, source_target_pairs={{0,1},{1,0},{2,3},{3,2},{4,5},{5,4},{6,7},{7,6},{8,9},{9,8},{10,11... | collective-permute-start | bytes 786440 | tf_op jit(solution)/shard_map/ppermute | solution.py:416
